TPU v7x, 32 devices: a whole 2x2x4 slice. The times are simulated.
32 devices in a mesh: roll: 2 (over y), dom: 4 (over z), blk: 4 (over x, core).
Axes of the slice: x: 2, y: 2, z: 4, core: 2. Of those that a mesh axis runs over, the one named last changes fastest.
Arguments:
- basis: bfloat16 [256, 4, 128, 128], P('blk', 'dom', 'roll'), parts along dimension 2
- zone: int32 [4, 128, 128], P('dom', 'roll'), parts along dimension 1, may hold values from 0 to 15
- cond_table: float32 [16], replicated, may hold values from 0.1 to 0.4
- heat_table: float32 [16], replicated, may hold values from 0.25 to 1
Outputs:
- applied: bfloat16 [512, 4, 64, 128], P('roll', 'dom', 'blk'), parts along dimension 0
- reduced: float32 [256, 512], P(('dom', 'blk'), 'roll'), parts along dimension 1
There are 2 independent parts, one for each index of `roll`. A program takes and returns all parts, laid end to end along the dimension named above; an argument that names none is the same for every part. Nothing has to cross between parts.
All inputs are finite; a program needn't handle non-finite values.
Results may differ from a plain program's by a relative error of at most 0.0035.
Values may be sent and summed in bfloat16 or wider, within the bound.
No kernel may reach another device: no remote copies, remote signals or barrier semaphores. Data moves between devices by JAX's collectives and lax.ppermute only.
A program may use at most 64 MiB of HBM per device.

v0:
```python
import jax
import jax.numpy as jnp
from jax import lax
from jax.sharding import PartitionSpec as P

ZONES = 16


def with_halo(cells, sides, width):
    for axis, dim in sides:
        count = lax.axis_size(axis)
        ends = count - 1
        head = lax.slice_in_dim(cells, 0, width, axis=dim)
        tail = lax.slice_in_dim(cells, cells.shape[dim] - width, cells.shape[dim], axis=dim)
        cells = jnp.concatenate(
            [
                lax.ppermute(tail, axis, [(i, (i + 1) % count) for i in range(ends)]),
                cells,
                lax.ppermute(head, axis, [((i + 1) % count, i) for i in range(ends)]),
            ],
            axis=dim,
        )
    return cells


def table_lookup(zone, table):
    result = jnp.zeros(zone.shape, jnp.float32)
    for which in range(ZONES):
        result = jnp.where(zone == which, table[which], result)
    return result


def shifted(grid, axis, start):
    result = grid
    for which in range(3):
        dim = grid.ndim - 3 + which
        extent = grid.shape[dim]
        lower = start if which == axis else 1
        result = lax.slice_in_dim(result, lower, lower + extent - 2, axis=dim)
    return result


def apply_operator(padded, cond, heat):
    values = padded.astype(jnp.float32)
    center = values[:, 1:-1, 1:-1, 1:-1]
    own = cond[1:-1, 1:-1, 1:-1]
    total = heat * center
    for axis in range(3):
        for start in (0, 2):
            face = 0.5 * (own + shifted(cond, axis, start))
            total = total + face * (center - shifted(values, axis, start))
    return total


def per_device(basis, zone, cond_table, heat_table):
    cond = lax.optimization_barrier(table_lookup(zone, cond_table).astype(jnp.bfloat16))
    heat = table_lookup(zone, heat_table)
    columns = basis.shape[0] * lax.axis_size("blk")
    planes = basis.shape[1]
    weight = 1.0 / (lax.axis_size("dom") * planes * basis.shape[2] * basis.shape[3])
    stacked = jnp.concatenate([basis, cond[None]], 0)
    padded = with_halo(stacked, (("dom", 1),), 1)
    padded = jnp.pad(padded, ((0, 0), (0, 0), (1, 1), (1, 1)))
    image = apply_operator(padded[:-1], padded[-1].astype(jnp.float32), heat).astype(jnp.bfloat16)
    basis_local, local_image = (
        lax.all_to_all(basis, "blk", split_axis=2, concat_axis=0, tiled=True),
        lax.all_to_all(image, "blk", split_axis=2, concat_axis=0, tiled=True),
    )
    flat_basis = basis_local.reshape(columns, -1)
    flat_image = local_image.reshape(columns, -1)
    product = lax.dot_general(
        flat_basis, flat_image, (((1,), (1,)), ((), ())), preferred_element_type=jnp.float32
    )
    reduced = lax.psum_scatter(product * weight, ("dom", "blk"), scatter_dimension=0, tiled=True)
    return (local_image, reduced)


def solution(mesh):
    placed = (P("blk", "dom", "roll", None), P("dom", "roll", None), P(), P())
    return jax.shard_map(
        per_device,
        mesh=mesh,
        in_specs=placed,
        out_specs=(P("roll", "dom", "blk", None), P(("dom", "blk"), "roll")),
        check_vma=False,
    )
```

profile of v0, /device:TPU:0, one launch (start us, length us, event | category | flops | bytes accessed | tf_op | source)
XLA Modules:
  0.0 172.4 jit_solution(1354798945172810719)
XLA Ops:
  7.2 2.0 %fusion.33 = (f32[1]{0:T(128)}, f32[1]{0:T(128)}, f32[1]{0:T(128)}, f32[1]{0:T(128)}, f32[1]{0:T(128)}, /*index=5*/f32[1]{0:T(128)}, f32[1]{0:T(128)}, f32[1]{0:...) fusion(f32[16]{0:T(128)} %param.7), kind=kLoop, calls=%fused_computation.68 | loop fusion | bytes 128 | tf_op jit(solution)/shard_map/slice | solution.py:29
  9.1 2.0 %fusion.32 = (bf16[1]{0:T(256)(128)(2,1)}, bf16[1]{0:T(256)(128)(2,1)}, bf16[1]{0:T(256)(128)(2,1)}, bf16[1]{0:T(256)(128)(2,1)}, bf16[1]{0:T(256)(128)(2,1)}, /...) fusion(f32[16]{0:T(128)} %param.6), kind=kLoop, calls=%fused_computation.67 | loop fusion | bytes 64 | tf_op jit(solution)/shard_map/slice | solution.py:29
  11.1 10.9 %select_bitcast_fusion = (f32[64,128]{1,0:T(8,128)S(1)}, pred[1,64,128]{2,1,0:T(8,128)(4,1)S(1)}, pred[1,64,128]{2,1,0:T(8,128)(4,1)S(1)}, pred[1,64,128]{2,1,0:...) fusion(f32[]{:T(128)} %bitcast.15, f32[]{:T(128)} %bitcast.14, ...), kind=kLoop, calls=%fused_computation.50 | loop fusion | flops 262144 | bytes 196672 | tf_op jit(solution)/shard_map/mul | solution.py:47
  22.0 10.1 %select_convert_fusion = bf16[1,64,128]{2,1,0:T(8,128)(2,1)S(1)} fusion(pred[1,64,128]{2,1,0:T(8,128)(4,1)S(1)} %get-tuple-element.32, pred[1,64,128]{2,1,0:T(8,128)(4,1)S(1)} %get-tuple-element.31, pred[1,64,128]{2,1,0:T(8,128)(4,1)S(1)} %get-tuple-element.30, pred[1,64,128]{2,1,0:T(8,128)(4,1)S(1)} %get-tuple-element.29, ...), kind=kLoop, calls=%fused_computation.49 | loop fusion | flops 131072 | bytes 147488 | tf_op jit(solution)/shard_map/convert_element_type | solution.py:56
  32.1 1.3 pad_maximum_fusion.1
  33.4 5.0 %collective-permute-start = (bf16[65,1,64,128]{3,2,1,0:T(8,128)(2,1)S(1)}, bf16[65,1,64,128]{3,2,1,0:T(8,128)(2,1)S(1)}, u32[]{:S(2)}, u32[]{:S(2)}) collective-permute-start(bf16[65,1,64,128]{3,2,1,0:T(8,128)(2,1)S(1)} %pad_maximum_fusion.1), channel_id=1, source_target_pairs={{0,4},{4,8},{8,12},{1,5},{5,9},{9,13},{2,6},{6,10},{10,14},{3,7},{... | collective-permute-start | bytes 3194888 | tf_op jit(solution)/shard_map/ppermute | solution.py:17
  38.4 1.3 collective-permute-start.1
  39.7 2.9 %copy.49 = bf16[64,1,64,128]{3,0,1,2:T(8,128)(2,1)} copy(bf16[64,1,64,128]{3,2,1,0:T(8,128)(2,1)} %param.4) | data formatting | bytes 2097152 | tf_op args[0]
  42.6 4.3 %all-to-all-start.1 = ((bf16[64,1,64,128]{3,0,1,2:T(8,128)(2,1)}), bf16[64,1,64,128]{3,0,1,2:T(8,128)(2,1)}, u32[]{:S(2)}, u32[]{:S(2)}) async-start(bf16[64,1,64,128]{3,0,1,2:T(8,128)(2,1)} %copy.49), calls=%async_computation.1 | async-start | bytes 2097152 | tf_op jit(solution)/shard_map/all_to_all | solution.py:66
  46.9 0.1 copy.43
  47.0 14.1 %collective-permute-done = bf16[65,1,64,128]{3,2,1,0:T(8,128)(2,1)S(1)} collective-permute-done((bf16[65,1,64,128]{3,2,1,0:T(8,128)(2,1)S(1)}, bf16[65,1,64,128]{3,2,1,0:T(8,128)(2,1)S(1)}, u32[]{:S(2)}, u32[]{:S(2)}) %collective-permute-start) | collective-permute-done | bytes 1064992 | tf_op jit(solution)/shard_map/ppermute | solution.py:17
  61.1 0.0 copy-start
  61.1 1.0 copy-done
  62.1 3.3 %collective-permute-done.1 = bf16[65,1,64,128]{3,2,1,0:T(8,128)(2,1)} collective-permute-done((bf16[65,1,64,128]{3,2,1,0:T(8,128)(2,1)S(1)}, bf16[65,1,64,128]{3,2,1,0:T(8,128)(2,1)}, u32[]{:S(2)}, u32[]{:S(2)}) %collective-permute-start.1) | collective-permute-done | bytes 1064992 | tf_op jit(solution)/shard_map/ppermute | solution.py:19
  65.4 2.1 %pad_maximum_fusion = bf16[65,3,64,128]{3,2,1,0:T(8,128)(2,1)S(1)} fusion(bf16[65,1,64,128]{3,2,1,0:T(8,128)(2,1)} %collective-permute-done.1, bf16[1,1,64,128]{3,2,1,0:T(8,128)(2,1)S(1)} %bitcast.82, bf16[64,1,64,128]{3,2,1,0:T(8,128)(2,1)} %param.4, bf16[65,1,64,128]{3,2,1,0:T(8,128)(2,1)} %copy-done), kind=kLoop, calls=%fused_computation.21 | loop fusion | flops 4792320 | bytes 6389760 | tf_op jit(solution)/shard_map/concatenate | solution.py:15
  67.4 6.4 %copy.44 = bf16[65,3,64,128]{2,3,1,0:T(8,128)(2,1)} copy(bf16[65,3,64,128]{3,2,1,0:T(8,128)(2,1)S(1)} %pad_maximum_fusion) | data formatting | bytes 6389760 | tf_op jit(solution)/shard_map/concatenate | solution.py:15
  73.9 6.1 %slice_convert_fusion = f32[64,3,66,130]{2,3,1,0:T(8,128)S(1)} fusion(bf16[65,3,64,128]{2,3,1,0:T(8,128)(2,1)} %copy.44), kind=kLoop, calls=%fused_computation | loop fusion | flops 1647360 | bytes 9784320 | tf_op jit(solution)/shard_map/convert_element_type | solution.py:44
  80.0 1.0 fusion.19
  81.0 0.2 fusion.31
  81.2 7.1 %fusion.2 = bf16[64,1,64,128]{2,3,1,0:T(8,128)(2,1)S(1)} fusion(f32[64,3,66,130]{2,3,1,0:T(8,128)S(1)} %slice_convert_fusion, f32[64,128]{0,1:T(8,128)S(1)} %get-tuple-element.38, f32[64,128]{0,1:T(8,128)S(1)} %get-tuple-element.34, f32[64,128]{0,1:T(8,128)S(1)} %get-tuple-element.35, f32[64,128]{0,1:T(8,128)S(1)} %get-tuple-element.36, ...), kind=kLoop, calls=%fused_computation.5 | loop fusion | flops 10485760 | bytes 15958016 | tf_op jit(solution)/shard_map/convert_element_type | solution.py:64
  88.3 2.3 %copy.45 = bf16[64,1,64,128]{3,0,1,2:T(8,128)(2,1)} copy(bf16[64,1,64,128]{2,3,1,0:T(8,128)(2,1)S(1)} %fusion.2) | data formatting | bytes 2097152 | tf_op jit(solution)/shard_map/convert_element_type | solution.py:64
  90.7 0.0 all-to-all-done.1
  90.7 3.5 %all-to-all-start = ((bf16[64,1,64,128]{3,0,1,2:T(8,128)(2,1)}), bf16[64,1,64,128]{3,0,1,2:T(8,128)(2,1)S(1)}, u32[]{:S(2)}, u32[]{:S(2)}) async-start(bf16[64,1,64,128]{3,0,1,2:T(8,128)(2,1)} %copy.45), calls=%async_computation | async-start | bytes 2097152 | tf_op jit(solution)/shard_map/all_to_all | solution.py:67
  94.2 0.2 reduce-scatter.4.cloned.1.call-start
  94.4 1.9 %copy.50 = bf16[64,1,64,128]{3,2,0,1:T(8,128)(2,1)S(1)} copy(bf16[64,1,64,128]{3,0,1,2:T(8,128)(2,1)} %all-to-all-done.1) | data formatting | bytes 2097152 | tf_op jit(solution)/shard_map/all_to_all | solution.py:66
  96.3 0.2 copy.51
  96.5 12.1 %all-to-all-done = bf16[64,1,64,128]{3,0,1,2:T(8,128)(2,1)S(1)} async-done(((bf16[64,1,64,128]{3,0,1,2:T(8,128)(2,1)}), bf16[64,1,64,128]{3,0,1,2:T(8,128)(2,1)S(1)}, u32[]{:S(2)}, u32[]{:S(2)}) %all-to-all-start) | async-done | bytes 1048608 | tf_op jit(solution)/shard_map/all_to_all | solution.py:67
  108.6 0.7 copy.46
  109.3 0.2 copy.47
  109.5 0.0 copy-start.1
  109.5 0.5 fusion.13
  110.0 0.8 copy.54
  110.8 0.0 reduce-scatter.4.cloned.1.call-update
  110.9 54.7 %reduce-scatter.4.cloned.1.call-done = f32[16,256]{1,0:T(8,128)} async-done(((f32[256,256]{1,0:T(8,128)}), f32[16,256]{1,0:T(8,128)}) %reduce-scatter.4.cloned.1.call-update) | async-done | bytes 16400
  165.5 0.0 copy-done.1
Async XLA Ops:
  33.4 27.7 %collective-permute-start = (bf16[65,1,64,128]{3,2,1,0:T(8,128)(2,1)S(1)}, bf16[65,1,64,128]{3,2,1,0:T(8,128)(2,1)S(1)}, u32[]{:S(2)}, u32[]{:S(2)}) collective-permute-start(bf16[65,1,64,128]{3,2,1,0:T(8,128)(2,1)S(1)} %pad_maximum_fusion.1), channel_id=1, source_target_pairs={{0,4},{4,8},{8,12},{1,5},{5,9},{9,13},{2,6},{6,10},{10,14},{3,7},{... | collective-permute-start | bytes 3194888 | tf_op jit(solution)/shard_map/ppermute | solution.py:17
  38.4 27.0 %collective-permute-start.1 = (bf16[65,1,64,128]{3,2,1,0:T(8,128)(2,1)S(1)}, bf16[65,1,64,128]{3,2,1,0:T(8,128)(2,1)}, u32[]{:S(2)}, u32[]{:S(2)}) collective-permute-start(bf16[65,1,64,128]{3,2,1,0:T(8,128)(2,1)S(1)} %pad_maximum_fusion.1), channel_id=1, source_target_pairs={{4,0},{8,4},{12,8},{5,1},{9,5},{13,9},{6,2},{10,6},{14,10},{7,3},{... | collective-permute-start | bytes 3194888 | tf_op jit(solution)/shard_map/ppermute | solution.py:19
  42.6 48.0 %all-to-all-start.1 = ((bf16[64,1,64,128]{3,0,1,2:T(8,128)(2,1)}), bf16[64,1,64,128]{3,0,1,2:T(8,128)(2,1)}, u32[]{:S(2)}, u32[]{:S(2)}) async-start(bf16[64,1,64,128]{3,0,1,2:T(8,128)(2,1)} %copy.49), calls=%async_computation.1 | async-start | bytes 2097152 | tf_op jit(solution)/shard_map/all_to_all | solution.py:66
  61.1 1.0 copy-start
  90.7 18.0 %all-to-all-start = ((bf16[64,1,64,128]{3,0,1,2:T(8,128)(2,1)}), bf16[64,1,64,128]{3,0,1,2:T(8,128)(2,1)S(1)}, u32[]{:S(2)}, u32[]{:S(2)}) async-start(bf16[64,1,64,128]{3,0,1,2:T(8,128)(2,1)} %copy.45), calls=%async_computation | async-start | bytes 2097152 | tf_op jit(solution)/shard_map/all_to_all | solution.py:67
  94.2 71.3 %reduce-scatter.4.cloned.1.call-start = ((), (), s32[]{:S(2)}) async-start(), calls=%async_computation.3 | async-start | bytes 278528
  109.5 56.0 %copy-start.1 = (bf16[4,64,1,16,128]{4,3,1,0,2:T(8,128)(2,1)}, bf16[4,64,1,16,128]{4,3,1,0,2:T(8,128)(2,1)S(1)}, u32[]{:S(2)}) copy-start(bf16[4,64,1,16,128]{4,3,1,0,2:T(8,128)(2,1)S(1)} %copy.47) | copy-start | bytes 3145732
Sparse Core Ops, SparseCore 0:
  111.0 54.4 reduce-scatter.3
where the time goes:
time: 173 us; the launch traced here: 172 us
  waiting for transfers between devices  84.1 us (49%)
  other arithmetic  38.8 us (22%)
  local copies, waits for them, and re-layouts  20.5 us (12%)
  starting transfers between devices  14.3 us (8%)
  between operations  14.2 us (8%)
    unnamed x2, waiting for transfers between devices  54.7 us
    ppermute x1, waiting for transfers between devices, with_halo(): lax.ppermute(tail, axis, [(i, (i + 1) % count) for i in range(ends)])  14.1 us
    all_to_all x1, waiting for transfers between devices, per_device(): lax.all_to_all(image, 'blk', split_axis=2, concat_axis=0, tiled=True)  12.1 us
    mul x1, other arithmetic, apply_operator(): total = heat * center  10.9 us
    convert_element_type x1, other arithmetic, per_device(): table_lookup(zone, cond_table).astype(jnp.bfloat16)  10.1 us
    convert_element_type x1, other arithmetic, per_device(): apply_operator(padded[:-1], padded[-1].astype(jnp.float32), heat)  7.14 us
    concatenate x1, local copies, waits for them, and re-layouts, with_halo(): jnp.concatenate([lax.ppermute(tail, axis, [(i, (i + 1) % count) for i in...  6.43 us
    convert_element_type x1, other arithmetic, apply_operator(): values = padded.astype(jnp.float32)  6.11 us
  transfers between devices with their start and end apart: 5, of which 4 were waited for; matrix products, arithmetic and copies ran while one was open for 18% of the time, Pallas kernels for 0%

commit v1 on v0

v1 whole, which is shorter than its diff:
```python
import functools

import jax
import jax.numpy as jnp
from jax import lax
from jax.experimental import pallas as pl
from jax.experimental.pallas import tpu as pltpu
from jax.sharding import PartitionSpec as P

ZONES = 16
F32 = jnp.float32
BF16 = jnp.bfloat16


def lookup(zone, table_ref):
    result = jnp.zeros(zone.shape, F32)
    for which in range(ZONES):
        result = jnp.where(zone == which, table_ref[which], result)
    return result


def cond_of(zone, table_ref):
    return lookup(zone, table_ref).astype(BF16).astype(F32)


def prepare_kernel(blocks, basis_ref, zone_ref, cond_ref, *refs):
    centers, slabs, mains, edges, (wide, turned, cond_pad, sems) = (
        refs[0:2], refs[2:4], refs[4:2 + blocks], refs[2 + blocks:2 * blocks], refs[2 * blocks:],
    )
    columns, _, ny, nz = basis_ref.shape
    rows = ny // blocks
    me = lax.axis_index("blk")
    for c in range(columns):
        wide[c * ny:(c + 1) * ny, :] = basis_ref[c, 0].astype(F32)
    zero = jnp.zeros((columns, nz), BF16)
    turned[0] = zero
    turned[ny + 1] = zero
    for y in range(ny):
        turned[y + 1] = wide[pl.ds(y, columns, stride=ny), :].astype(BF16)
    mine = zone_ref[0, pl.ds(pl.multiple_of(me * rows, rows), rows), :]
    own = cond_of(mine, cond_ref)
    cond_pad[...] = jnp.concatenate([own, jnp.zeros((columns - rows, nz), F32)], 0).astype(BF16)

    copies = []

    def send(source, target):
        copy = pltpu.make_async_copy(source, target, sems.at[len(copies)])
        copy.start()
        copies.append(copy)

    for s in range(blocks):
        first = (me ^ s) * rows
        if s < 2:
            send(turned.at[pl.ds(first, rows + 2)], centers[s])
            send(turned.at[pl.ds(first + 1, rows)], slabs[s].at[pl.ds(0, rows)])
        else:
            send(turned.at[pl.ds(first + 1, rows)], mains[s - 2])
            send(turned.at[pl.ds(first, 1)], edges[s - 2].at[pl.ds(0, 1)])
            send(turned.at[pl.ds(first + rows + 1, 1)], edges[s - 2].at[pl.ds(1, 1)])
    send(cond_pad, slabs[0].at[rows])
    for copy in copies:
        copy.wait()


def prepare(basis, zone, cond_table, blocks):
    columns, _, ny, nz = basis.shape
    rows = ny // blocks

    def out(n):
        return jax.ShapeDtypeStruct((n, columns, nz), BF16)

    vmem = pl.BlockSpec(memory_space=pltpu.VMEM)
    smem = pl.BlockSpec(memory_space=pltpu.SMEM)
    shapes = [out(rows + 2)] * 2 + [out(rows + 1), out(rows)] + [out(rows)] * (blocks - 2) + [out(2)] * (blocks - 2)
    results = pl.pallas_call(
        functools.partial(prepare_kernel, blocks),
        out_shape=shapes,
        in_specs=[vmem, vmem, smem],
        out_specs=[pl.BlockSpec(memory_space=pl.ANY)] * len(shapes),
        scratch_shapes=[
            pltpu.VMEM((columns * ny, nz), F32),
            pltpu.VMEM((ny + 2, columns, nz), BF16),
            pltpu.VMEM((columns, nz), BF16),
            pltpu.SemaphoreType.DMA((3 * blocks,)),
        ],
        compiler_params=pltpu.CompilerParams(vmem_limit_bytes=16 << 20),
    )(basis, zone, cond_table)
    return results[0:2], results[2:4], results[4:2 + blocks], results[2 + blocks:]


def apply_kernel(blocks, weight, zone_ref, cond_ref, heat_ref, *refs):
    centers, mains, edges, ups, downs = (
        refs[0:2], refs[2:blocks], refs[blocks:2 * blocks - 2],
        refs[2 * blocks - 2:3 * blocks - 2], refs[3 * blocks - 2:4 * blocks - 2],
    )
    applied_ref, gram_ref, cond_pad, coef, left, right, wide = refs[4 * blocks - 2:]
    _, columns, nz = ups[1].shape
    rows = ups[1].shape[0]
    ny = zone_ref.shape[1]
    me = lax.axis_index("blk")
    slab = lax.axis_index("dom")
    slabs = lax.axis_size("dom")

    cond_pad[0:8, :] = jnp.zeros((8, nz), F32)
    cond_pad[8:8 + ny, :] = cond_of(zone_ref[0], cond_ref)
    cond_pad[8 + ny:16 + ny, :] = jnp.zeros((8, nz), F32)
    base = pl.multiple_of(me * rows, 8)
    near = cond_pad[pl.ds(base, rows + 16), :]
    own = near[8:8 + rows]
    lane = lax.broadcasted_iota(jnp.int32, (rows, nz), 1)
    above = jnp.where(slab == slabs - 1, 0.0, ups[0][rows].astype(F32)[:rows])
    below = jnp.where(slab == 0, 0.0, downs[0][rows].astype(F32)[:rows])
    beside = (
        jnp.where(lane == 0, 0.0, pltpu.roll(own, 1, 1)),
        jnp.where(lane == nz - 1, 0.0, pltpu.roll(own, nz - 1, 1)),
    )
    coef[0] = lookup(zone_ref[0, pl.ds(base, rows), :], heat_ref)
    for which, other in enumerate((below, above, near[7:7 + rows], near[9:9 + rows], *beside)):
        coef[1 + which] = 0.5 * (own + other)

    lane = lax.broadcasted_iota(jnp.int32, (columns, nz), 1)
    first, last = lane == 0, lane == nz - 1
    for y in range(rows):
        face = [jnp.broadcast_to(coef[k, y:y + 1, :], (columns, nz)) for k in range(7)]
        for s in range(blocks):
            def row(at):
                if s < 2:
                    return centers[s][at + 1]
                if at < 0:
                    return edges[s - 2][0]
                return mains[s - 2][at] if at < rows else edges[s - 2][1]

            raw = row(y)
            v = raw.astype(F32)
            total = face[0] * v
            total += face[1] * (v - downs[s][y].astype(F32))
            total += face[2] * (v - ups[s][y].astype(F32))
            total += face[3] * (v - row(y - 1).astype(F32))
            total += face[4] * (v - row(y + 1).astype(F32))
            total += face[5] * (v - jnp.where(first, 0.0, pltpu.roll(v, 1, 1)))
            total += face[6] * (v - jnp.where(last, 0.0, pltpu.roll(v, nz - 1, 1)))
            image = total.astype(BF16)
            start = (me ^ s) * columns
            where = pl.ds(pl.multiple_of(start, columns), columns)
            left[where, y * nz:(y + 1) * nz] = raw
            right[where, y * nz:(y + 1) * nz] = image
            wide[pl.ds(start * rows + y, columns, stride=rows), :] = image.astype(F32)
    gram_ref[...] = weight * lax.dot_general(
        left[...], right[...], (((1,), (1,)), ((), ())), preferred_element_type=F32
    )
    for c in range(blocks * columns):
        applied_ref[c, 0] = wide[c * rows:(c + 1) * rows, :].astype(BF16)


def apply(zone, cond_table, heat_table, centers, mains, edges, ups, downs, weight):
    blocks = len(ups)
    rows, columns, nz = ups[1].shape
    ny = zone.shape[1]
    total = blocks * columns
    vmem = pl.BlockSpec(memory_space=pltpu.VMEM)
    smem = pl.BlockSpec(memory_space=pltpu.SMEM)
    pieces = (*centers, *mains, *edges, *ups, *downs)
    return pl.pallas_call(
        functools.partial(apply_kernel, blocks, weight),
        out_shape=(
            jax.ShapeDtypeStruct((total, 1, rows, nz), BF16),
            jax.ShapeDtypeStruct((total, total), F32),
        ),
        in_specs=[vmem, smem, smem] + [vmem] * len(pieces),
        out_specs=(vmem, vmem),
        scratch_shapes=[
            pltpu.VMEM((ny + 16, nz), F32),
            pltpu.VMEM((7, rows, nz), F32),
            pltpu.VMEM((total, rows * nz), BF16),
            pltpu.VMEM((total, rows * nz), BF16),
            pltpu.VMEM((total * rows, nz), F32),
        ],
        compiler_params=pltpu.CompilerParams(vmem_limit_bytes=32 << 20),
    )(zone, cond_table, heat_table, *pieces)


def per_device(basis, zone, cond_table, heat_table):
    blocks = lax.axis_size("blk")
    slabs = lax.axis_size("dom")
    columns = basis.shape[0] * blocks
    weight = 1.0 / (slabs * basis.shape[1] * basis.shape[2] * basis.shape[3])
    axes = ("dom", "blk")

    def across(array, s):
        return lax.ppermute(array, "blk", [(i, i ^ s) for i in range(blocks)])

    def along(array, step, s):
        pairs = [
            (d * blocks + b, (d + step) * blocks + (b ^ s))
            for d in range(slabs) if 0 <= d + step < slabs for b in range(blocks)
        ]
        return lax.ppermute(array, axes, pairs)

    centers, slab_rows, mains, edges = prepare(basis, zone, cond_table, blocks)
    mains = [across(main, s + 2) for s, main in enumerate(mains)]
    ups = [along(array, -1, s) for s, array in enumerate(slab_rows)]
    downs = [along(array, 1, s) for s, array in enumerate(slab_rows)]
    centers = [centers[0], across(centers[1], 1)]
    edges = [across(edge, s + 2) for s, edge in enumerate(edges)]
    ups += [along(main, -1, 0) for main in mains]
    downs += [along(main, 1, 0) for main in mains]
    applied, gram = apply(zone, cond_table, heat_table, centers, mains, edges, ups, downs, weight)
    parts = slabs * blocks
    shares = gram.reshape(parts, columns // parts, columns)
    shares = lax.all_to_all(shares, axes, split_axis=0, concat_axis=0, tiled=True)
    return applied, shares.sum(0)


def solution(mesh):
    placed = (P("blk", "dom", "roll", None), P("dom", "roll", None), P(), P())
    return jax.shard_map(
        per_device,
        mesh=mesh,
        in_specs=placed,
        out_specs=(P("roll", "dom", "blk", None), P(("dom", "blk"), "roll")),
        check_vma=False,
    )
```

time: 173 us -> 68 us (0.39)
  waiting for transfers between devices: 84.1 us -> 14.1 us
  other arithmetic: 38.8 us -> 0.63 us
  local copies, waits for them, and re-layouts: 20.5 us -> 2.64 us
  starting transfers between devices: 14.3 us -> 28.7 us
  blocking collectives: 0 us -> 13.7 us
  between operations: 14.2 us -> 0.78 us
  Pallas kernels: 0 us -> 7.05 us
    unnamed x2 -> x0, waiting for transfers between devices: 54.7 us -> none
    convert_element_type x4 -> x0, other arithmetic: 24.3 us -> none  [the longest x1 10.1 us: per_device(): table_lookup(zone, cond_table).astype(jnp.bfloat16)]
    ppermute x2 -> x13, starting transfers between devices: 6.29 us -> 28.7 us  [the longest x8 22.1 us: along(): return lax.ppermute(array, axes, pairs)]
    all_to_all x0 -> x1, blocking collectives: none -> 13.7 us  [per_device(): lax.all_to_all(shares, axes, split_axis=0, concat_axis=0, tiled=True)]
    all_to_all x2 -> x0, waiting for transfers between devices: 12.1 us -> none  [the longest x1 12.1 us: per_device(): lax.all_to_all(image, 'blk', split_axis=2, concat_axis=0, tiled=True)]
    mul x2 -> x0, other arithmetic: 11.1 us -> none  [the longest x1 10.9 us: apply_operator(): total = heat * center]
    all_to_all x2 -> x0, starting transfers between devices: 7.77 us -> none  [the longest x1 4.25 us: per_device(): lax.all_to_all(basis, 'blk', split_axis=2, concat_axis=0, tiled=True)]
    pallas_call x0 -> x2, Pallas kernels: none -> 7.05 us  [the longest x1 4.8 us: apply(): pl.pallas_call(functools.partial(apply_kernel, blocks, weight), out_shape...]
  transfers between devices with their start and end apart: 5 -> 13, of which waited for: 4 -> 6; matrix products, arithmetic and copies ran while one was open for 18% -> 0% of each run, Pallas kernels for 0% -> 0%
where the time goes in v1:
time: 68 us; the launch traced here: 67.6 us
  starting transfers between devices  28.7 us (42%)
  waiting for transfers between devices  14.1 us (21%)
  blocking collectives  13.7 us (20%)
  Pallas kernels  7.05 us (10%)
  local copies, waits for them, and re-layouts  2.64 us (4%)
  between operations  0.78 us (1%)
    ppermute x8, starting transfers between devices, along(): return lax.ppermute(array, axes, pairs)  22.1 us
    all_to_all x1, blocking collectives, per_device(): lax.all_to_all(shares, axes, split_axis=0, concat_axis=0, tiled=True)  13.7 us
    ppermute x8, waiting for transfers between devices, along(): return lax.ppermute(array, axes, pairs)  12 us
    ppermute x5, starting transfers between devices, across(): return lax.ppermute(array, 'blk', [(i, i ^ s) for i in range(blocks)])  6.53 us
    pallas_call x1, Pallas kernels, apply(): pl.pallas_call(functools.partial(apply_kernel, blocks, weight), out_shape...  4.8 us
    unnamed x10, local copies, waits for them, and re-layouts  2.64 us
    pallas_call x1, Pallas kernels, prepare(): pl.pallas_call(functools.partial(prepare_kernel, blocks), out_shape=shape...  2.26 us
    ppermute x5, waiting for transfers between devices, across(): return lax.ppermute(array, 'blk', [(i, i ^ s) for i in range(blocks)])  2.07 us
  transfers between devices with their start and end apart: 13, of which 6 were waited for; matrix products, arithmetic and copies ran while one was open for 0% of the time, Pallas kernels for 0%

profile of v1, /device:TPU:0, one launch (start us, length us, event | category | flops | bytes accessed | tf_op | source)
XLA Modules:
  0.0 67.6 jit_solution(9610993085923634820)
XLA Ops:
  0.6 0.0 copy-start
  0.6 1.2 %copy-done = bf16[64,1,64,128]{3,2,1,0:T(8,128)(2,1)S(1)} copy-done((bf16[64,1,64,128]{3,2,1,0:T(8,128)(2,1)S(1)}, bf16[64,1,64,128]{3,2,1,0:T(8,128)(2,1)}, u32[]{:S(2)}) %copy-start) | copy-done | bytes 1048600
  1.9 0.0 copy-start.1
  1.9 0.8 %copy-done.1 = s32[1,64,128]{2,1,0:T(8,128)S(1)} copy-done((s32[1,64,128]{2,1,0:T(8,128)S(1)}, s32[1,64,128]{2,1,0:T(8,128)}, u32[]{:S(2)}) %copy-start.1) | copy-done | bytes 32792
  2.6 0.0 copy-start.3
  2.6 0.7 copy-done.3
  3.3 0.0 copy-start.2
  3.3 2.3 %shard_map.59 = (bf16[18,64,128]{2,1,0:T(8,128)(2,1)S(1)}, bf16[18,64,128]{2,1,0:T(8,128)(2,1)S(1)}, bf16[17,64,128]{2,1,0:T(8,128)(2,1)S(1)}, bf16[16,64,128]{2...) custom-call(bf16[64,1,64,128]{3,2,1,0:T(8,128)(2,1)S(1)} %copy-done,, ...), custom_call_target="tpu_custom_call" | custom-call | tf_op jit(solution)/shard_map/pallas_call | solution.py:75
  5.5 3.0 %collective-permute-start.1 = (bf16[16,64,128]{2,1,0:T(8,128)(2,1)S(1)}, bf16[16,64,128]{2,1,0:T(8,128)(2,1)S(1)}, u32[]{:S(2)}, u32[]{:S(2)}) collective-permute-start(bf16[16,64,128]{2,1,0:T(8,128)(2,1)S(1)} %get-tuple-element.14), channel_id=1, source_target_pairs={{0,2},{1,3},{2,0},{3,1},{4,6},{5,7},{6,4},{7,5},{8,10},{9,11},{10,... | collective-permute-start | bytes 786440 | tf_op jit(solution)/shard_map/ppermute | solution.py:190
  8.5 0.1 collective-permute-start.3
  8.6 0.8 %collective-permute-start.4 = (bf16[2,64,128]{2,1,0:T(8,128)(2,1)S(1)}, bf16[2,64,128]{2,1,0:T(8,128)(2,1)S(1)}, u32[]{:S(2)}, u32[]{:S(2)}) collective-permute-start(bf16[2,64,128]{2,1,0:T(8,128)(2,1)S(1)} %get-tuple-element.17), channel_id=1, source_target_pairs={{0,3},{1,2},{2,1},{3,0},{4,7},{5,6},{6,5},{7,4},{8,11},{9,10},{10,... | collective-permute-start | bytes 98312 | tf_op jit(solution)/shard_map/ppermute | solution.py:190
  9.4 0.9 %collective-permute-start.2 = (bf16[16,64,128]{2,1,0:T(8,128)(2,1)S(1)}, bf16[16,64,128]{2,1,0:T(8,128)(2,1)S(1)}, u32[]{:S(2)}, u32[]{:S(2)}) collective-permute-start(bf16[16,64,128]{2,1,0:T(8,128)(2,1)S(1)} %get-tuple-element.15), channel_id=1, source_target_pairs={{0,3},{1,2},{2,1},{3,0},{4,7},{5,6},{6,5},{7,4},{8,11},{9,10},{10,... | collective-permute-start | bytes 786440 | tf_op jit(solution)/shard_map/ppermute | solution.py:190
  10.4 3.9 %collective-permute-start.9 = (bf16[17,64,128]{2,1,0:T(8,128)(2,1)S(1)}, bf16[17,64,128]{2,1,0:T(8,128)(2,1)S(1)}, u32[]{:S(2)}, u32[]{:S(2)}) collective-permute-start(bf16[17,64,128]{2,1,0:T(8,128)(2,1)S(1)} %get-tuple-element.18), channel_id=1, source_target_pairs={{0,4},{1,5},{2,6},{3,7},{4,8},{5,9},{6,10},{7,11},{8,12},{9,13},{1... | collective-permute-start | bytes 835592 | tf_op jit(solution)/shard_map/ppermute | solution.py:197
  14.3 2.1 %collective-permute-done.3.refs_4_ = bf16[2,64,128]{2,1,0:T(8,128)(2,1)S(1)} collective-permute-done((bf16[2,64,128]{2,1,0:T(8,128)(2,1)S(1)}, bf16[2,64,128]{2,1,0:T(8,128)(2,1)S(1)}, u32[]{:S(2)}, u32[]{:S(2)}) %collective-permute-start.3) | collective-permute-done | bytes 32800 | tf_op jit(solution)/shard_map/ppermute | solution.py:190
  16.4 1.3 %collective-permute-start.5 = (bf16[17,64,128]{2,1,0:T(8,128)(2,1)S(1)}, bf16[17,64,128]{2,1,0:T(8,128)(2,1)S(1)}, u32[]{:S(2)}, u32[]{:S(2)}) collective-permute-start(bf16[17,64,128]{2,1,0:T(8,128)(2,1)S(1)} %get-tuple-element.18), channel_id=1, source_target_pairs={{4,0},{5,1},{6,2},{7,3},{8,4},{9,5},{10,6},{11,7},{12,8},{13,9},{1... | collective-permute-start | bytes 835592 | tf_op jit(solution)/shard_map/ppermute | solution.py:197
  17.7 0.0 collective-permute-done.4.refs_5_
  17.7 3.2 %collective-permute-start.10 = (bf16[16,64,128]{2,1,0:T(8,128)(2,1)S(1)}, bf16[16,64,128]{2,1,0:T(8,128)(2,1)S(1)}, u32[]{:S(2)}, u32[]{:S(2)}) collective-permute-start(bf16[16,64,128]{2,1,0:T(8,128)(2,1)S(1)} %get-tuple-element.19), channel_id=1, source_target_pairs={{0,5},{1,4},{2,7},{3,6},{4,9},{5,8},{6,11},{7,10},{8,13},{9,12},{1... | collective-permute-start | bytes 786440 | tf_op jit(solution)/shard_map/ppermute | solution.py:197
  20.9 0.0 collective-permute-done.1.refs_2_
  20.9 1.3 %collective-permute-start.6 = (bf16[16,64,128]{2,1,0:T(8,128)(2,1)S(1)}, bf16[16,64,128]{2,1,0:T(8,128)(2,1)S(1)}, u32[]{:S(2)}, u32[]{:S(2)}) collective-permute-start(bf16[16,64,128]{2,1,0:T(8,128)(2,1)S(1)} %get-tuple-element.19), channel_id=1, source_target_pairs={{4,1},{5,0},{6,3},{7,2},{8,5},{9,4},{10,7},{11,6},{12,9},{13,8},{1... | collective-permute-start | bytes 786440 | tf_op jit(solution)/shard_map/ppermute | solution.py:197
  22.2 0.0 collective-permute-done.2.refs_3_
  22.2 0.0 copy-start.4
  22.2 1.7 %collective-permute-start = (bf16[18,64,128]{2,1,0:T(8,128)(2,1)S(1)}, bf16[18,64,128]{2,1,0:T(8,128)(2,1)S(1)}, u32[]{:S(2)}, u32[]{:S(2)}) collective-permute-start(bf16[18,64,128]{2,1,0:T(8,128)(2,1)S(1)} %get-tuple-element.13), channel_id=1, source_target_pairs={{0,1},{1,0},{2,3},{3,2},{4,5},{5,4},{6,7},{7,6},{8,9},{9,8},{10,11... | collective-permute-start | bytes 884744 | tf_op jit(solution)/shard_map/ppermute | solution.py:190
  23.9 2.7 %collective-permute-done.10.refs_11_ = bf16[16,64,128]{2,1,0:T(8,128)(2,1)S(1)} collective-permute-done((bf16[16,64,128]{2,1,0:T(8,128)(2,1)S(1)}, bf16[16,64,128]{2,1,0:T(8,128)(2,1)S(1)}, u32[]{:S(2)}, u32[]{:S(2)}) %collective-permute-start.10) | collective-permute-done | bytes 262176 | tf_op jit(solution)/shard_map/ppermute | solution.py:197
  26.6 5.3 %collective-permute-start.11 = (bf16[16,64,128]{2,1,0:T(8,128)(2,1)S(1)}, bf16[16,64,128]{2,1,0:T(8,128)(2,1)S(1)}, u32[]{:S(2)}, u32[]{:S(2)}) collective-permute-start(bf16[16,64,128]{2,1,0:T(8,128)(2,1)S(1)} %collective-permute-done.1.refs_2_), channel_id=1, source_target_pairs={{0,4},{1,5},{2,6},{3,7},{4,8},{5,9},{6,10},{7,11},{8,12},{9,13},{1... | collective-permute-start | bytes 786440 | tf_op jit(solution)/shard_map/ppermute | solution.py:197
  31.9 0.6 collective-permute-done.6.refs_7_
  32.6 1.3 %collective-permute-start.7 = (bf16[16,64,128]{2,1,0:T(8,128)(2,1)S(1)}, bf16[16,64,128]{2,1,0:T(8,128)(2,1)S(1)}, u32[]{:S(2)}, u32[]{:S(2)}) collective-permute-start(bf16[16,64,128]{2,1,0:T(8,128)(2,1)S(1)} %collective-permute-done.1.refs_2_), channel_id=1, source_target_pairs={{4,0},{5,1},{6,2},{7,3},{8,4},{9,5},{10,6},{11,7},{12,8},{13,9},{1... | collective-permute-start | bytes 786440 | tf_op jit(solution)/shard_map/ppermute | solution.py:197
  33.9 0.0 collective-permute-done.9.refs_10_
  33.9 4.6 %collective-permute-start.12 = (bf16[16,64,128]{2,1,0:T(8,128)(2,1)S(1)}, bf16[16,64,128]{2,1,0:T(8,128)(2,1)S(1)}, u32[]{:S(2)}, u32[]{:S(2)}) collective-permute-start(bf16[16,64,128]{2,1,0:T(8,128)(2,1)S(1)} %collective-permute-done.2.refs_3_), channel_id=1, source_target_pairs={{0,4},{1,5},{2,6},{3,7},{4,8},{5,9},{6,10},{7,11},{8,12},{9,13},{1... | collective-permute-start | bytes 786440 | tf_op jit(solution)/shard_map/ppermute | solution.py:197
  38.4 0.0 collective-permute-done.5.refs_6_
  38.4 1.3 %collective-permute-start.8 = (bf16[16,64,128]{2,1,0:T(8,128)(2,1)S(1)}, bf16[16,64,128]{2,1,0:T(8,128)(2,1)S(1)}, u32[]{:S(2)}, u32[]{:S(2)}) collective-permute-start(bf16[16,64,128]{2,1,0:T(8,128)(2,1)S(1)} %collective-permute-done.2.refs_3_), channel_id=1, source_target_pairs={{4,0},{5,1},{6,2},{7,3},{8,4},{9,5},{10,6},{11,7},{12,8},{13,9},{1... | collective-permute-start | bytes 786440 | tf_op jit(solution)/shard_map/ppermute | solution.py:197
  39.7 0.0 collective-permute-done.refs_1_
  39.8 0.0 collective-permute-done.11.refs_12_
  39.8 3.2 %collective-permute-done.7.refs_8_ = bf16[16,64,128]{2,1,0:T(8,128)(2,1)S(1)} collective-permute-done((bf16[16,64,128]{2,1,0:T(8,128)(2,1)S(1)}, bf16[16,64,128]{2,1,0:T(8,128)(2,1)S(1)}, u32[]{:S(2)}, u32[]{:S(2)}) %collective-permute-start.7) | collective-permute-done | bytes 262176 | tf_op jit(solution)/shard_map/ppermute | solution.py:197
  43.0 1.0 %collective-permute-done.12.refs_13_ = bf16[16,64,128]{2,1,0:T(8,128)(2,1)S(1)} collective-permute-done((bf16[16,64,128]{2,1,0:T(8,128)(2,1)S(1)}, bf16[16,64,128]{2,1,0:T(8,128)(2,1)S(1)}, u32[]{:S(2)}, u32[]{:S(2)}) %collective-permute-start.12) | collective-permute-done | bytes 262176 | tf_op jit(solution)/shard_map/ppermute | solution.py:197
  44.0 4.4 %collective-permute-done.8.refs_9_ = bf16[16,64,128]{2,1,0:T(8,128)(2,1)S(1)} collective-permute-done((bf16[16,64,128]{2,1,0:T(8,128)(2,1)S(1)}, bf16[16,64,128]{2,1,0:T(8,128)(2,1)S(1)}, u32[]{:S(2)}, u32[]{:S(2)}) %collective-permute-start.8) | collective-permute-done | bytes 262176 | tf_op jit(solution)/shard_map/ppermute | solution.py:197
  48.4 0.0 copy-done.2
  48.4 0.0 copy-done.4
  48.4 4.8 %shard_map.60 = (bf16[256,1,16,128]{3,2,1,0:T(8,128)(2,1)}, f32[256,256]{1,0:T(8,128)S(1)}) custom-call(s32[1,64,128]{2,1,0:T(8,128)S(1)} %copy-done.2, f32[16]{0:T(128)S(1)} %copy-done.3, f32[16]{0:T(128)S(1)} %copy-done.4, bf16[18,64,128]{2,1,0:T(8,128)(2,1)S(1)} %get-tuple-element.12.refs_0_, bf16[18,64,128]{2,1,0:T(8,128)(2,1)S(1)} %collective-permute-done.refs_1_, ...), custom_call_target="tpu_custom_call" | custom-call | tf_op jit(solution)/shard_map/pallas_call | solution.py:163
  53.2 13.7 %all_to_all.5 = f32[16,16,256]{2,1,0:T(8,128)S(1)} all-to-all(f32[16,16,256]{2,1,0:T(8,128)S(1)} %bitcast.1), channel_id=1, replica_groups=mesh['roll'=2,'dom'=4,'blk'=4] {'dom','blk'}, dimensions={0} | all-to-all | bytes 524288 | tf_op jit(solution)/shard_map/all_to_all | solution.py:210
  66.9 0.6 reduce_sum.9
Async XLA Ops:
  0.6 1.2 %copy-start = (bf16[64,1,64,128]{3,2,1,0:T(8,128)(2,1)S(1)}, bf16[64,1,64,128]{3,2,1,0:T(8,128)(2,1)}, u32[]{:S(2)}) copy-start(bf16[64,1,64,128]{3,2,1,0:T(8,128)(2,1)} %basis_ref.1) | copy-start | bytes 3145732
  1.9 0.8 %copy-start.1 = (s32[1,64,128]{2,1,0:T(8,128)S(1)}, s32[1,64,128]{2,1,0:T(8,128)}, u32[]{:S(2)}) copy-start(s32[1,64,128]{2,1,0:T(8,128)} %zone_ref.3) | copy-start | bytes 98308
  2.6 0.7 copy-start.3
  3.3 45.1 %copy-start.2 = (s32[1,64,128]{2,1,0:T(8,128)S(1)}, s32[1,64,128]{2,1,0:T(8,128)}, u32[]{:S(2)}) copy-start(s32[1,64,128]{2,1,0:T(8,128)} %zone_ref.3) | copy-start | bytes 98308
  5.5 15.3 %collective-permute-start.1 = (bf16[16,64,128]{2,1,0:T(8,128)(2,1)S(1)}, bf16[16,64,128]{2,1,0:T(8,128)(2,1)S(1)}, u32[]{:S(2)}, u32[]{:S(2)}) collective-permute-start(bf16[16,64,128]{2,1,0:T(8,128)(2,1)S(1)} %get-tuple-element.14), channel_id=1, source_target_pairs={{0,2},{1,3},{2,0},{3,1},{4,6},{5,7},{6,4},{7,5},{8,10},{9,11},{10,... | collective-permute-start | bytes 786440 | tf_op jit(solution)/shard_map/ppermute | solution.py:190
  8.5 7.8 %collective-permute-start.3 = (bf16[2,64,128]{2,1,0:T(8,128)(2,1)S(1)}, bf16[2,64,128]{2,1,0:T(8,128)(2,1)S(1)}, u32[]{:S(2)}, u32[]{:S(2)}) collective-permute-start(bf16[2,64,128]{2,1,0:T(8,128)(2,1)S(1)} %get-tuple-element.16), channel_id=1, source_target_pairs={{0,2},{1,3},{2,0},{3,1},{4,6},{5,7},{6,4},{7,5},{8,10},{9,11},{10,... | collective-permute-start | bytes 98312 | tf_op jit(solution)/shard_map/ppermute | solution.py:190
  8.6 9.0 %collective-permute-start.4 = (bf16[2,64,128]{2,1,0:T(8,128)(2,1)S(1)}, bf16[2,64,128]{2,1,0:T(8,128)(2,1)S(1)}, u32[]{:S(2)}, u32[]{:S(2)}) collective-permute-start(bf16[2,64,128]{2,1,0:T(8,128)(2,1)S(1)} %get-tuple-element.17), channel_id=1, source_target_pairs={{0,3},{1,2},{2,1},{3,0},{4,7},{5,6},{6,5},{7,4},{8,11},{9,10},{10,... | collective-permute-start | bytes 98312 | tf_op jit(solution)/shard_map/ppermute | solution.py:190
  9.4 12.7 %collective-permute-start.2 = (bf16[16,64,128]{2,1,0:T(8,128)(2,1)S(1)}, bf16[16,64,128]{2,1,0:T(8,128)(2,1)S(1)}, u32[]{:S(2)}, u32[]{:S(2)}) collective-permute-start(bf16[16,64,128]{2,1,0:T(8,128)(2,1)S(1)} %get-tuple-element.15), channel_id=1, source_target_pairs={{0,3},{1,2},{2,1},{3,0},{4,7},{5,6},{6,5},{7,4},{8,11},{9,10},{10,... | collective-permute-start | bytes 786440 | tf_op jit(solution)/shard_map/ppermute | solution.py:190
  10.4 23.5 %collective-permute-start.9 = (bf16[17,64,128]{2,1,0:T(8,128)(2,1)S(1)}, bf16[17,64,128]{2,1,0:T(8,128)(2,1)S(1)}, u32[]{:S(2)}, u32[]{:S(2)}) collective-permute-start(bf16[17,64,128]{2,1,0:T(8,128)(2,1)S(1)} %get-tuple-element.18), channel_id=1, source_target_pairs={{0,4},{1,5},{2,6},{3,7},{4,8},{5,9},{6,10},{7,11},{8,12},{9,13},{1... | collective-permute-start | bytes 835592 | tf_op jit(solution)/shard_map/ppermute | solution.py:197
  16.4 22.1 %collective-permute-start.5 = (bf16[17,64,128]{2,1,0:T(8,128)(2,1)S(1)}, bf16[17,64,128]{2,1,0:T(8,128)(2,1)S(1)}, u32[]{:S(2)}, u32[]{:S(2)}) collective-permute-start(bf16[17,64,128]{2,1,0:T(8,128)(2,1)S(1)} %get-tuple-element.18), channel_id=1, source_target_pairs={{4,0},{5,1},{6,2},{7,3},{8,4},{9,5},{10,6},{11,7},{12,8},{13,9},{1... | collective-permute-start | bytes 835592 | tf_op jit(solution)/shard_map/ppermute | solution.py:197
  17.7 8.9 %collective-permute-start.10 = (bf16[16,64,128]{2,1,0:T(8,128)(2,1)S(1)}, bf16[16,64,128]{2,1,0:T(8,128)(2,1)S(1)}, u32[]{:S(2)}, u32[]{:S(2)}) collective-permute-start(bf16[16,64,128]{2,1,0:T(8,128)(2,1)S(1)} %get-tuple-element.19), channel_id=1, source_target_pairs={{0,5},{1,4},{2,7},{3,6},{4,9},{5,8},{6,11},{7,10},{8,13},{9,12},{1... | collective-permute-start | bytes 786440 | tf_op jit(solution)/shard_map/ppermute | solution.py:197
  20.9 11.7 %collective-permute-start.6 = (bf16[16,64,128]{2,1,0:T(8,128)(2,1)S(1)}, bf16[16,64,128]{2,1,0:T(8,128)(2,1)S(1)}, u32[]{:S(2)}, u32[]{:S(2)}) collective-permute-start(bf16[16,64,128]{2,1,0:T(8,128)(2,1)S(1)} %get-tuple-element.19), channel_id=1, source_target_pairs={{4,1},{5,0},{6,3},{7,2},{8,5},{9,4},{10,7},{11,6},{12,9},{13,8},{1... | collective-permute-start | bytes 786440 | tf_op jit(solution)/shard_map/ppermute | solution.py:197
  22.2 26.2 %copy-start.4 = (f32[16]{0:T(128)S(1)}, f32[16]{0:T(128)}, u32[]{:S(2)}) copy-start(f32[16]{0:T(128)} %heat_ref.1) | copy-start | bytes 196
  22.2 17.6 %collective-permute-start = (bf16[18,64,128]{2,1,0:T(8,128)(2,1)S(1)}, bf16[18,64,128]{2,1,0:T(8,128)(2,1)S(1)}, u32[]{:S(2)}, u32[]{:S(2)}) collective-permute-start(bf16[18,64,128]{2,1,0:T(8,128)(2,1)S(1)} %get-tuple-element.13), channel_id=1, source_target_pairs={{0,1},{1,0},{2,3},{3,2},{4,5},{5,4},{6,7},{7,6},{8,9},{9,8},{10,11... | collective-permute-start | bytes 884744 | tf_op jit(solution)/shard_map/ppermute | solution.py:190
  26.6 13.2 %collective-permute-start.11 = (bf16[16,64,128]{2,1,0:T(8,128)(2,1)S(1)}, bf16[16,64,128]{2,1,0:T(8,128)(2,1)S(1)}, u32[]{:S(2)}, u32[]{:S(2)}) collective-permute-start(bf16[16,64,128]{2,1,0:T(8,128)(2,1)S(1)} %collective-permute-done.1.refs_2_), channel_id=1, source_target_pairs={{0,4},{1,5},{2,6},{3,7},{4,8},{5,9},{6,10},{7,11},{8,12},{9,13},{1... | collective-permute-start | bytes 786440 | tf_op jit(solution)/shard_map/ppermute | solution.py:197
  32.6 10.4 %collective-permute-start.7 = (bf16[16,64,128]{2,1,0:T(8,128)(2,1)S(1)}, bf16[16,64,128]{2,1,0:T(8,128)(2,1)S(1)}, u32[]{:S(2)}, u32[]{:S(2)}) collective-permute-start(bf16[16,64,128]{2,1,0:T(8,128)(2,1)S(1)} %collective-permute-done.1.refs_2_), channel_id=1, source_target_pairs={{4,0},{5,1},{6,2},{7,3},{8,4},{9,5},{10,6},{11,7},{12,8},{13,9},{1... | collective-permute-start | bytes 786440 | tf_op jit(solution)/shard_map/ppermute | solution.py:197
  33.9 10.1 %collective-permute-start.12 = (bf16[16,64,128]{2,1,0:T(8,128)(2,1)S(1)}, bf16[16,64,128]{2,1,0:T(8,128)(2,1)S(1)}, u32[]{:S(2)}, u32[]{:S(2)}) collective-permute-start(bf16[16,64,128]{2,1,0:T(8,128)(2,1)S(1)} %collective-permute-done.2.refs_3_), channel_id=1, source_target_pairs={{0,4},{1,5},{2,6},{3,7},{4,8},{5,9},{6,10},{7,11},{8,12},{9,13},{1... | collective-permute-start | bytes 786440 | tf_op jit(solution)/shard_map/ppermute | solution.py:197
  38.4 10.0 %collective-permute-start.8 = (bf16[16,64,128]{2,1,0:T(8,128)(2,1)S(1)}, bf16[16,64,128]{2,1,0:T(8,128)(2,1)S(1)}, u32[]{:S(2)}, u32[]{:S(2)}) collective-permute-start(bf16[16,64,128]{2,1,0:T(8,128)(2,1)S(1)} %collective-permute-done.2.refs_3_), channel_id=1, source_target_pairs={{4,0},{5,1},{6,2},{7,3},{8,4},{9,5},{10,6},{11,7},{12,8},{13,9},{1... | collective-permute-start | bytes 786440 | tf_op jit(solution)/shard_map/ppermute | solution.py:197

commit v2 on v0

v2 whole, which is shorter than its diff:
```python
import functools

import jax
import jax.numpy as jnp
from jax import lax
from jax.experimental import pallas as pl
from jax.experimental.pallas import tpu as pltpu
from jax.sharding import PartitionSpec as P

ZONES = 16
CORES = 2
F32 = jnp.float32
BF16 = jnp.bfloat16
VMEM = pl.BlockSpec(memory_space=pltpu.VMEM)
SMEM = pl.BlockSpec(memory_space=pltpu.SMEM)
HBM = pl.BlockSpec(memory_space=pltpu.HBM)


def lookup(zone, table_ref):
    result = jnp.zeros(zone.shape, F32)
    for which in range(ZONES):
        result = jnp.where(zone == which, table_ref[which], result)
    return result


def cond_of(zone, table_ref):
    return lookup(zone, table_ref).astype(BF16).astype(F32)


def prepare_kernel(chips, basis_hbm, zone_hbm, cond_hbm, *refs):
    outs, (basis, zone, table, wide, turned, cond_pad, in_sems, out_sems) = refs[:chips + 1], refs[chips + 1:]
    columns, _, ny, nz = basis.shape
    rows = ny // chips
    chip = lax.axis_index("blk") // CORES
    step = 16
    chunks = columns // step
    loads = [
        pltpu.make_async_copy(basis_hbm.at[pl.ds(i * step, step)], basis.at[pl.ds(i * step, step)], in_sems.at[i])
        for i in range(chunks)
    ]
    loads.append(pltpu.make_async_copy(zone_hbm, zone, in_sems.at[chunks]))
    loads.append(pltpu.make_async_copy(cond_hbm, table, in_sems.at[chunks + 1]))
    for load in loads:
        load.start()
    turned[0] = jnp.zeros((columns, nz), BF16)
    turned[ny + 1] = jnp.zeros((columns, nz), BF16)
    for i in range(chunks):
        loads[i].wait()
        for c in range(i * step, (i + 1) * step):
            wide[c * ny:(c + 1) * ny, :] = basis[c, 0].astype(F32)
        for y in range(ny):
            block = wide[pl.ds(i * step * ny + y, step, stride=ny), :]
            turned[y + 1, i * step:(i + 1) * step, :] = block.astype(BF16)
    loads[chunks].wait()
    loads[chunks + 1].wait()
    mine = zone[0, pl.ds(pl.multiple_of(chip * rows, rows), rows), :]
    own = cond_of(mine, table)
    cond_pad[...] = jnp.concatenate([own, jnp.zeros((columns - rows, nz), F32)], 0).astype(BF16)

    stores = [
        pltpu.make_async_copy(turned.at[pl.ds((chip ^ k) * rows, rows + 2)], outs[1 + k], out_sems.at[k])
        for k in range(chips)
    ]
    stores.append(
        pltpu.make_async_copy(turned.at[pl.ds(chip * rows + 1, rows)], outs[0].at[pl.ds(0, rows)], out_sems.at[chips])
    )
    stores.append(pltpu.make_async_copy(cond_pad, outs[0].at[rows], out_sems.at[chips + 1]))
    for store in stores:
        store.start()
    for store in stores:
        store.wait()


def prepare(basis, zone, cond_table, chips):
    columns, _, ny, nz = basis.shape
    rows = ny // chips
    shapes = [jax.ShapeDtypeStruct((rows + 1, columns, nz), BF16)]
    shapes += [jax.ShapeDtypeStruct((rows + 2, columns, nz), BF16)] * chips
    results = pl.pallas_call(
        functools.partial(prepare_kernel, chips),
        out_shape=shapes,
        in_specs=[HBM, HBM, HBM],
        out_specs=[pl.BlockSpec(memory_space=pl.ANY)] * len(shapes),
        scratch_shapes=[
            pltpu.VMEM(basis.shape, BF16),
            pltpu.VMEM(zone.shape, jnp.int32),
            pltpu.SMEM((ZONES,), F32),
            pltpu.VMEM((columns * ny, nz), F32),
            pltpu.VMEM((ny + 2, columns, nz), BF16),
            pltpu.VMEM((columns, nz), BF16),
            pltpu.SemaphoreType.DMA((columns // 16 + 2,)),
            pltpu.SemaphoreType.DMA((chips + 2,)),
        ],
        compiler_params=pltpu.CompilerParams(vmem_limit_bytes=16 << 20),
    )(basis, zone, cond_table)
    return results[0], results[1], results[2:]


def image_rows(coef, center, one, two, skip, mine, theirs, flat):
    rows = coef.shape[1]
    columns, nz = center.shape[1:]
    half = rows // CORES
    core = lax.axis_index("blk") % CORES
    lane = lax.broadcasted_iota(jnp.int32, (columns, nz), 1)
    first, last = lane == 0, lane == nz - 1
    for y in range(rows):
        face = [jnp.broadcast_to(coef[k, y:y + 1, :], (columns, nz)) for k in range(7)]
        v = center[y + 1].astype(F32)
        total = face[0] * v
        total += face[1] * (v - one[y + skip].astype(F32))
        total += face[2] * (v - two[y + skip].astype(F32))
        total += face[3] * (v - center[y].astype(F32))
        total += face[4] * (v - center[y + 2].astype(F32))
        total += face[5] * (v - jnp.where(first, 0.0, pltpu.roll(v, 1, 1)))
        total += face[6] * (v - jnp.where(last, 0.0, pltpu.roll(v, nz - 1, 1)))
        flat[:, y * nz:(y + 1) * nz] = total.astype(BF16)
    for y in range(half):
        low = flat[:, y * nz:(y + 1) * nz]
        high = flat[:, (half + y) * nz:(half + y + 1) * nz]
        mine[y] = jnp.where(core == 0, low, high)
        theirs[y] = jnp.where(core == 0, high, low)


def gram_of(left, flat):
    return lax.dot_general(left[...], flat[...], (((1,), (1,)), ((), ())), preferred_element_type=F32)


def near_kernel(chips, weight, zone_ref, cond_ref, heat_ref, center, one, two, *refs):
    others, (mine, theirs, coef, left, gram, cond_pad, flat) = refs[:2 * chips - 1], refs[2 * chips - 1:]
    rows = center.shape[0] - 2
    columns, nz = center.shape[1:]
    ny = zone_ref.shape[1]
    me = lax.axis_index("blk")
    chip = me // CORES

    cond_pad[0:8, :] = jnp.zeros((8, nz), F32)
    cond_pad[8:8 + ny, :] = cond_of(zone_ref[0], cond_ref)
    cond_pad[8 + ny:16 + ny, :] = jnp.zeros((8, nz), F32)
    base = pl.multiple_of(chip * rows, 8)
    near = cond_pad[pl.ds(base, rows + 16), :]
    own = near[8:8 + rows]
    lane = lax.broadcasted_iota(jnp.int32, (rows, nz), 1)
    coef[0] = lookup(zone_ref[0, pl.ds(base, rows), :], heat_ref)
    beside = (
        one[rows].astype(F32)[:rows],
        two[rows].astype(F32)[:rows],
        near[7:7 + rows],
        near[9:9 + rows],
        jnp.where(lane == 0, 0.0, pltpu.roll(own, 1, 1)),
        jnp.where(lane == nz - 1, 0.0, pltpu.roll(own, nz - 1, 1)),
    )
    for which, other in enumerate(beside):
        coef[1 + which] = 0.5 * (own + other)

    image_rows(coef, center, one, two, 0, mine, theirs, flat)
    pieces = [(center, 0)]
    pieces += [(ref, CORES * (k + 1)) for k, ref in enumerate(others[:chips - 1])]
    pieces += [(ref, CORES * k + 1) for k, ref in enumerate(others[chips - 1:])]
    for ref, partner in pieces:
        where = pl.ds(pl.multiple_of((me ^ partner) * columns, columns), columns)
        for y in range(rows):
            left[where, y * nz:(y + 1) * nz] = ref[y + 1]
    gram[...] = weight * gram_of(left, flat)


def far_kernel(chips, weight, coef, left, near_gram, *refs):
    count = chips - 1
    centers, ones, twos, mine, theirs = (refs[i * count:(i + 1) * count] for i in range(5))
    gram, flat = refs[5 * count:]
    columns = centers[0].shape[1]
    gram[:, 0:columns] = near_gram[...]
    for k in range(count):
        image_rows(coef, centers[k], ones[k], twos[k], 1, mine[k], theirs[k], flat)
        gram[:, (k + 1) * columns:(k + 2) * columns] = weight * gram_of(left, flat)


def finish_kernel(blocks, *refs):
    images, (applied, wide) = refs[:blocks], refs[blocks:]
    rows, columns, nz = images[0].shape
    me = lax.axis_index("blk")
    for s, image in enumerate(images):
        for y in range(rows):
            wide[pl.ds(y, columns, stride=rows), :] = image[y].astype(F32)
        start = (me ^ s) * columns
        for c in range(columns):
            applied[start + c, 0] = wide[c * rows:(c + 1) * rows, :].astype(BF16)


def sum_kernel(slabs, blocks, shares, out):
    chips = blocks // CORES
    columns = shares.shape[2] // chips
    for core in range(CORES):
        sums = []
        for chip in range(chips):
            total = shares[CORES * chip + core]
            for slab in range(1, slabs):
                total += shares[slab * blocks + CORES * chip + core]
            sums.append(total)
        for target in range(chips):
            parts = [sums[chip][:, (chip ^ target) * columns:((chip ^ target) + 1) * columns] for chip in range(chips)]
            start = (CORES * target + core) * columns
            out[:, start:start + columns] = functools.reduce(jnp.add, parts)


def per_device(basis, zone, cond_table, heat_table):
    blocks = lax.axis_size("blk")
    slabs = lax.axis_size("dom")
    chips = blocks // CORES
    columns, planes, ny, nz = basis.shape
    rows = ny // chips
    half = ny // blocks
    total = columns * blocks
    weight = 1.0 / (slabs * planes * ny * nz)

    def swap(array, s):
        return lax.ppermute(array, "blk", [(i, i ^ s) for i in range(blocks)])

    def along(array):
        result = []
        for offset in (0, 1):
            partner = [((d + offset) ^ 1) - offset for d in range(slabs)]
            pairs = [(d, to) for d, to in enumerate(partner) if 0 <= to < slabs]
            result.append(lax.ppermute(array, "dom", pairs))
        return result

    sent, center, others = prepare(basis, zone, cond_table, chips)
    others = [swap(other, CORES * (k + 1)) for k, other in enumerate(others)]
    one, two = along(sent)
    theirs = [swap(center, 1)]
    far = [along(other) for other in others]
    theirs += [swap(other, 1) for other in others]

    image = jax.ShapeDtypeStruct((half, columns, nz), BF16)
    left = jax.ShapeDtypeStruct((total, rows * nz), BF16)
    flat = pltpu.VMEM((columns, rows * nz), BF16)
    params = pltpu.CompilerParams(vmem_limit_bytes=32 << 20)
    near_mine, near_theirs, coef, left, near_gram = pl.pallas_call(
        functools.partial(near_kernel, chips, weight),
        out_shape=(
            image, image, jax.ShapeDtypeStruct((7, rows, nz), F32), left, jax.ShapeDtypeStruct((total, columns), F32),
        ),
        in_specs=[VMEM, SMEM, SMEM] + [VMEM] * (2 * chips + 2),
        out_specs=[VMEM] * 5,
        scratch_shapes=[pltpu.VMEM((ny + 16, nz), F32), flat],
        compiler_params=params,
    )(zone, cond_table, heat_table, center, one, two, *others, *theirs)

    count = chips - 1
    *images, gram = pl.pallas_call(
        functools.partial(far_kernel, chips, weight),
        out_shape=[image] * (2 * count) + [jax.ShapeDtypeStruct((total, chips * columns), F32)],
        in_specs=[VMEM] * (3 + 3 * count),
        out_specs=[VMEM] * (2 * count + 1),
        scratch_shapes=[flat],
        compiler_params=params,
    )(coef, left, near_gram, *others, *(one for one, _ in far), *(two for _, two in far))

    near_theirs = swap(near_theirs, 1)
    far_theirs = [swap(array, 1) for array in images[count:]]
    pieces = [near_mine, near_theirs]
    for k in range(count):
        pieces += [images[k], far_theirs[k]]
    applied = pl.pallas_call(
        functools.partial(finish_kernel, blocks),
        out_shape=jax.ShapeDtypeStruct((total, 1, half, nz), BF16),
        in_specs=[VMEM] * blocks,
        out_specs=VMEM,
        scratch_shapes=[pltpu.VMEM((columns * half, nz), F32)],
        compiler_params=params,
    )(*pieces)

    parts = slabs * blocks
    shares = gram.reshape(parts, total // parts, chips * columns)
    shares = lax.all_to_all(shares, ("dom", "blk"), split_axis=0, concat_axis=0, tiled=True)
    reduced = pl.pallas_call(
        functools.partial(sum_kernel, slabs, blocks),
        out_shape=jax.ShapeDtypeStruct((total // parts, total), F32),
        in_specs=[VMEM],
        out_specs=VMEM,
    )(shares)
    return applied, reduced


def solution(mesh):
    placed = (P("blk", "dom", "roll", None), P("dom", "roll", None), P(), P())
    return jax.shard_map(
        per_device,
        mesh=mesh,
        in_specs=placed,
        out_specs=(P("roll", "dom", "blk", None), P(("dom", "blk"), "roll")),
        check_vma=False,
    )
```

time: 173 us -> 74.5 us (0.43)
  waiting for transfers between devices: 84.1 us -> 18.2 us
  other arithmetic: 38.8 us -> 0 us
  blocking collectives: 0 us -> 32.4 us
  local copies, waits for them, and re-layouts: 20.5 us -> 4.69 us
  between operations: 14.2 us -> 0.73 us
  Pallas kernels: 0 us -> 9.72 us
  starting transfers between devices: 14.3 us -> 8.36 us
    unnamed x2 -> x0, waiting for transfers between devices: 54.7 us -> none
    all_to_all x0 -> x1, blocking collectives: none -> 32.4 us  [per_device(): lax.all_to_all(shares, ('dom', 'blk'), split_axis=0, concat_axis=0, tiled...]
    convert_element_type x4 -> x0, other arithmetic: 24.3 us -> none  [the longest x1 10.1 us: per_device(): table_lookup(zone, cond_table).astype(jnp.bfloat16)]
    all_to_all x2 -> x0, waiting for transfers between devices: 12.1 us -> none  [the longest x1 12.1 us: per_device(): lax.all_to_all(image, 'blk', split_axis=2, concat_axis=0, tiled=True)]
    mul x2 -> x0, other arithmetic: 11.1 us -> none  [the longest x1 10.9 us: apply_operator(): total = heat * center]
    pallas_call x0 -> x5, Pallas kernels: none -> 9.72 us  [the longest x1 2.64 us: per_device(): pl.pallas_call(functools.partial(near_kernel, chips, weight), out_shape=(...]
    all_to_all x2 -> x0, starting transfers between devices: 7.77 us -> none  [the longest x1 4.25 us: per_device(): lax.all_to_all(basis, 'blk', split_axis=2, concat_axis=0, tiled=True)]
    concatenate x1 -> x0, local copies, waits for them, and re-layouts: 6.43 us -> none  [with_halo(): jnp.concatenate([lax.ppermute(tail, axis, [(i, (i + 1) % count) for i in...]
  transfers between devices with their start and end apart: 5 -> 9, of which waited for: 4 -> 2; matrix products, arithmetic and copies ran while one was open for 18% -> 0% of each run, Pallas kernels for 0% -> 6%
where the time goes in v2:
time: 74.5 us; the launch traced here: 74.1 us
  blocking collectives  32.4 us (43%)
  waiting for transfers between devices  18.2 us (24%)
  Pallas kernels  9.72 us (13%)
  starting transfers between devices  8.36 us (11%)
  local copies, waits for them, and re-layouts  4.69 us (6%)
    all_to_all x1, blocking collectives, per_device(): lax.all_to_all(shares, ('dom', 'blk'), split_axis=0, concat_axis=0, tiled...  32.4 us
    ppermute x5, waiting for transfers between devices, swap(): return lax.ppermute(array, 'blk', [(i, i ^ s) for i in range(blocks)])  11.1 us
    ppermute x4, waiting for transfers between devices, along(): result.append(lax.ppermute(array, 'dom', pairs))  7.14 us
    ppermute x4, starting transfers between devices, along(): result.append(lax.ppermute(array, 'dom', pairs))  4.78 us
    unnamed x12, local copies, waits for them, and re-layouts  4.69 us
    ppermute x5, starting transfers between devices, swap(): return lax.ppermute(array, 'blk', [(i, i ^ s) for i in range(blocks)])  3.58 us
    pallas_call x1, Pallas kernels, per_device(): pl.pallas_call(functools.partial(near_kernel, chips, weight), out_shape=(...  2.64 us
    pallas_call x1, Pallas kernels, per_device(): pl.pallas_call(functools.partial(finish_kernel, blocks), out_shape=jax.Sh...  2.05 us
  transfers between devices with their start and end apart: 9, of which 2 were waited for; matrix products, arithmetic and copies ran while one was open for 0% of the time, Pallas kernels for 6%

profile of v2, /device:TPU:0, one launch (start us, length us, event | category | flops | bytes accessed | tf_op | source)
XLA Modules:
  0.0 74.1 jit_solution(11633665784295900665)
XLA Ops:
  0.6 0.0 copy-start
  0.6 1.2 %copy-done = bf16[64,1,64,128]{3,2,1,0:T(8,128)(2,1)S(1)} copy-done((bf16[64,1,64,128]{3,2,1,0:T(8,128)(2,1)S(1)}, bf16[64,1,64,128]{3,2,1,0:T(8,128)(2,1)}, u32[]{:S(2)}) %copy-start) | copy-done | bytes 1048600
  1.9 0.0 copy-start.1
  1.9 0.8 %copy-done.1 = s32[1,64,128]{2,1,0:T(8,128)S(1)} copy-done((s32[1,64,128]{2,1,0:T(8,128)S(1)}, s32[1,64,128]{2,1,0:T(8,128)}, u32[]{:S(2)}) %copy-start.1) | copy-done | bytes 32792
  2.6 0.0 copy-start.3
  2.6 0.7 copy-done.3
  3.3 1.8 %shard_map.59 = (bf16[33,64,128]{2,1,0:T(8,128)(2,1)S(1)}, bf16[34,64,128]{2,1,0:T(8,128)(2,1)S(1)}, bf16[34,64,128]{2,1,0:T(8,128)(2,1)S(1)}) custom-call(bf16[64,1,64,128]{3,2,1,0:T(8,128)(2,1)S(1)} %copy-done, s32[1,64,128]{2,1,0:T(8,128)S(1)} %copy-done.1, f32[16]{0:T(128)S(1)} %copy-done.3), custom_call_target="tpu_custom_call" | custom-call | tf_op jit(solution)/shard_map/pallas_call | solution.py:79
  5.0 3.0 %collective-permute-start.2 = (bf16[34,64,128]{2,1,0:T(8,128)(2,1)S(1)}, bf16[34,64,128]{2,1,0:T(8,128)(2,1)S(1)}, u32[]{:S(2)}, u32[]{:S(2)}) collective-permute-start(bf16[34,64,128]{2,1,0:T(8,128)(2,1)S(1)} %get-tuple-element.15), channel_id=1, source_target_pairs={{0,2},{1,3},{2,0},{3,1},{4,6},{5,7},{6,4},{7,5},{8,10},{9,11},{10,... | collective-permute-start | bytes 1671176 | tf_op jit(solution)/shard_map/ppermute | solution.py:216
  8.0 1.6 %collective-permute-start = (bf16[33,64,128]{2,1,0:T(8,128)(2,1)S(1)}, bf16[33,64,128]{2,1,0:T(8,128)(2,1)S(1)}, u32[]{:S(2)}, u32[]{:S(2)}) collective-permute-start(bf16[33,64,128]{2,1,0:T(8,128)(2,1)S(1)} %get-tuple-element.14), channel_id=1, source_target_pairs={{0,4},{4,0},{8,12},{12,8},{1,5},{5,1},{9,13},{13,9},{2,6},{6,2},{1... | collective-permute-start | bytes 1622024 | tf_op jit(solution)/shard_map/ppermute | solution.py:223
  9.6 0.0 collective-permute-start.3
  9.6 11.0 %collective-permute-done.2.refs_0_ = bf16[34,64,128]{2,1,0:T(8,128)(2,1)S(1)} collective-permute-done((bf16[34,64,128]{2,1,0:T(8,128)(2,1)S(1)}, bf16[34,64,128]{2,1,0:T(8,128)(2,1)S(1)}, u32[]{:S(2)}, u32[]{:S(2)}) %collective-permute-start.2) | collective-permute-done | bytes 557088 | tf_op jit(solution)/shard_map/ppermute | solution.py:216
  20.7 0.0 collective-permute-start.4
  20.7 1.8 %collective-permute-start.6 = (bf16[34,64,128]{2,1,0:T(8,128)(2,1)S(1)}, bf16[34,64,128]{2,1,0:T(8,128)(2,1)S(1)}, u32[]{:S(2)}, u32[]{:S(2)}) collective-permute-start(bf16[34,64,128]{2,1,0:T(8,128)(2,1)S(1)} %collective-permute-done.2.refs_0_), channel_id=1, source_target_pairs={{0,4},{4,0},{8,12},{12,8},{1,5},{5,1},{9,13},{13,9},{2,6},{6,2},{1... | collective-permute-start | bytes 1671176 | tf_op jit(solution)/shard_map/ppermute | solution.py:223
  22.5 0.7 collective-permute-start.7
  23.2 0.0 collective-permute-done.one
  23.2 0.7 collective-permute-start.1
  23.9 0.0 collective-permute-done.1.two
  23.9 0.0 collective-permute-done.3.refs_1_
  23.9 0.0 collective-permute-done.4.refs_2_
  23.9 0.0 copy-start.2
  23.9 0.7 %copy-done.2 = s32[1,64,128]{2,1,0:T(8,128)S(1)} copy-done((s32[1,64,128]{2,1,0:T(8,128)S(1)}, s32[1,64,128]{2,1,0:T(8,128)}, u32[]{:S(2)}) %copy-start.2) | copy-done | bytes 32792
  24.7 0.0 copy-start.4
  24.7 0.7 copy-done.4
  25.4 0.0 copy-start.5
  25.4 0.7 copy-done.5
  26.0 2.6 %shard_map.60 = (bf16[16,64,128]{2,1,0:T(8,128)(2,1)S(1)}, bf16[16,64,128]{2,1,0:T(8,128)(2,1)S(1)}, f32[7,32,128]{2,1,0:T(8,128)S(1)}, bf16[256,4096]{1,0:T(8,128)(2,1)S(1)}, f32[256,64]{1,0:T(8,128)S(1)}) custom-call(s32[1,64,128]{2,1,0:T(8,128)S(1)} %copy-done.2, f32[16]{0:T(128)S(1)} %copy-done.4, f32[16]{0:T(128)S(1)} %copy-done.5, ...), custom_call_target="tpu_custom_call" | custom-call | tf_op jit(solution)/shard_map/pallas_call | solution.py:237
  28.7 7.1 %collective-permute-done.6.refs_1_ = bf16[34,64,128]{2,1,0:T(8,128)(2,1)S(1)} collective-permute-done((bf16[34,64,128]{2,1,0:T(8,128)(2,1)S(1)}, bf16[34,64,128]{2,1,0:T(8,128)(2,1)S(1)}, u32[]{:S(2)}, u32[]{:S(2)}) %collective-permute-start.6) | collective-permute-done | bytes 557088 | tf_op jit(solution)/shard_map/ppermute | solution.py:223
  35.8 0.0 collective-permute-done.7.refs_2_
  35.8 1.6 %shard_map.61 = (bf16[16,64,128]{2,1,0:T(8,128)(2,1)S(1)}, bf16[16,64,128]{2,1,0:T(8,128)(2,1)S(1)}, f32[256,128]{1,0:T(8,128)S(1)}) custom-call(f32[7,32,128]{2,1,0:T(8,128)S(1)} %get-tuple-element.18.coef, bf16[256,4096]{1,0:T(8,128)(2,1)S(1)} %get-tuple-element.19.left, f32[256,64]{1,0:T(8,128)S(1)} %get-tuple-element.20.near_gram, ...), custom_call_target="tpu_custom_call" | custom-call | tf_op jit(solution)/shard_map/pallas_call | solution.py:249
  37.4 0.1 collective-permute-start.8
  37.5 0.5 collective-permute-start.5
  38.0 32.4 %all_to_all.5.shares = f32[16,16,128]{2,1,0:T(8,128)} all-to-all(f32[16,16,128]{2,1,0:T(8,128)S(1)} %bitcast.1), channel_id=1, replica_groups=mesh['roll'=2,'dom'=4,'blk'=4] {'dom','blk'}, dimensions={0} | all-to-all | bytes 262144 | tf_op jit(solution)/shard_map/all_to_all | solution.py:274
  70.4 1.7 %shard_map.63 = f32[16,256]{1,0:T(8,128)} custom-call(f32[16,16,128]{2,1,0:T(8,128)} %all_to_all.5.shares), custom_call_target="tpu_custom_call" | custom-call | tf_op jit(solution)/shard_map/pallas_call | solution.py:275
  72.0 0.0 collective-permute-done.8.refs_3_
  72.1 0.0 collective-permute-done.5.refs_1_
  72.1 2.1 %shard_map.62 = bf16[256,1,16,128]{3,2,1,0:T(8,128)(2,1)} custom-call(bf16[16,64,128]{2,1,0:T(8,128)(2,1)S(1)} %get-tuple-element.16.refs_0_, bf16[16,64,128]{2,1,0:T(8,128)(2,1)S(1)} %collective-permute-done.5.refs_1_, bf16[16,64,128]{2,1,0:T(8,128)(2,1)S(1)} %get-tuple-element.21.refs_2_, bf16[16,64,128]{2,1,0:T(8,128)(2,1)S(1)} %collective-permute-done.8.refs_3_), custom_call_target="tpu_custom_call" | custom-call | tf_op jit(solution)/shard_map/pallas_call | solution.py:263
Async XLA Ops:
  0.6 1.2 %copy-start = (bf16[64,1,64,128]{3,2,1,0:T(8,128)(2,1)S(1)}, bf16[64,1,64,128]{3,2,1,0:T(8,128)(2,1)}, u32[]{:S(2)}) copy-start(bf16[64,1,64,128]{3,2,1,0:T(8,128)(2,1)} %basis_hbm.1) | copy-start | bytes 3145732
  1.9 0.8 %copy-start.1 = (s32[1,64,128]{2,1,0:T(8,128)S(1)}, s32[1,64,128]{2,1,0:T(8,128)}, u32[]{:S(2)}) copy-start(s32[1,64,128]{2,1,0:T(8,128)} %zone_ref.1) | copy-start | bytes 98308
  2.6 0.7 copy-start.3
  5.0 15.6 %collective-permute-start.2 = (bf16[34,64,128]{2,1,0:T(8,128)(2,1)S(1)}, bf16[34,64,128]{2,1,0:T(8,128)(2,1)S(1)}, u32[]{:S(2)}, u32[]{:S(2)}) collective-permute-start(bf16[34,64,128]{2,1,0:T(8,128)(2,1)S(1)} %get-tuple-element.15), channel_id=1, source_target_pairs={{0,2},{1,3},{2,0},{3,1},{4,6},{5,7},{6,4},{7,5},{8,10},{9,11},{10,... | collective-permute-start | bytes 1671176 | tf_op jit(solution)/shard_map/ppermute | solution.py:216
  8.0 15.2 %collective-permute-start = (bf16[33,64,128]{2,1,0:T(8,128)(2,1)S(1)}, bf16[33,64,128]{2,1,0:T(8,128)(2,1)S(1)}, u32[]{:S(2)}, u32[]{:S(2)}) collective-permute-start(bf16[33,64,128]{2,1,0:T(8,128)(2,1)S(1)} %get-tuple-element.14), channel_id=1, source_target_pairs={{0,4},{4,0},{8,12},{12,8},{1,5},{5,1},{9,13},{13,9},{2,6},{6,2},{1... | collective-permute-start | bytes 1622024 | tf_op jit(solution)/shard_map/ppermute | solution.py:223
  9.6 14.3 %collective-permute-start.3 = (bf16[34,64,128]{2,1,0:T(8,128)(2,1)S(1)}, bf16[34,64,128]{2,1,0:T(8,128)(2,1)S(1)}, u32[]{:S(2)}, u32[]{:S(2)}) collective-permute-start(bf16[34,64,128]{2,1,0:T(8,128)(2,1)S(1)} %get-tuple-element.13.center), channel_id=1, source_target_pairs={{0,1},{1,0},{2,3},{3,2},{4,5},{5,4},{6,7},{7,6},{8,9},{9,8},{10,11... | collective-permute-start | bytes 1671176 | tf_op jit(solution)/shard_map/ppermute | solution.py:216
  20.7 3.3 %collective-permute-start.4 = (bf16[34,64,128]{2,1,0:T(8,128)(2,1)S(1)}, bf16[34,64,128]{2,1,0:T(8,128)(2,1)S(1)}, u32[]{:S(2)}, u32[]{:S(2)}) collective-permute-start(bf16[34,64,128]{2,1,0:T(8,128)(2,1)S(1)} %collective-permute-done.2.refs_0_), channel_id=1, source_target_pairs={{0,1},{1,0},{2,3},{3,2},{4,5},{5,4},{6,7},{7,6},{8,9},{9,8},{10,11... | collective-permute-start | bytes 1671176 | tf_op jit(solution)/shard_map/ppermute | solution.py:216
  20.7 15.1 %collective-permute-start.6 = (bf16[34,64,128]{2,1,0:T(8,128)(2,1)S(1)}, bf16[34,64,128]{2,1,0:T(8,128)(2,1)S(1)}, u32[]{:S(2)}, u32[]{:S(2)}) collective-permute-start(bf16[34,64,128]{2,1,0:T(8,128)(2,1)S(1)} %collective-permute-done.2.refs_0_), channel_id=1, source_target_pairs={{0,4},{4,0},{8,12},{12,8},{1,5},{5,1},{9,13},{13,9},{2,6},{6,2},{1... | collective-permute-start | bytes 1671176 | tf_op jit(solution)/shard_map/ppermute | solution.py:223
  22.5 13.3 %collective-permute-start.7 = (bf16[34,64,128]{2,1,0:T(8,128)(2,1)S(1)}, bf16[34,64,128]{2,1,0:T(8,128)(2,1)S(1)}, u32[]{:S(2)}, u32[]{:S(2)}) collective-permute-start(bf16[34,64,128]{2,1,0:T(8,128)(2,1)S(1)} %collective-permute-done.2.refs_0_), channel_id=1, source_target_pairs={{4,8},{8,4},{5,9},{9,5},{6,10},{10,6},{7,11},{11,7},{20,24},{24,20... | collective-permute-start | bytes 1671176 | tf_op jit(solution)/shard_map/ppermute | solution.py:223
  23.2 0.7 collective-permute-start.1
  23.9 0.8 %copy-start.2 = (s32[1,64,128]{2,1,0:T(8,128)S(1)}, s32[1,64,128]{2,1,0:T(8,128)}, u32[]{:S(2)}) copy-start(s32[1,64,128]{2,1,0:T(8,128)} %zone_ref.1) | copy-start | bytes 98308
  24.7 0.7 copy-start.4
  25.4 0.7 copy-start.5
  37.4 34.6 %collective-permute-start.8 = (bf16[16,64,128]{2,1,0:T(8,128)(2,1)S(1)}, bf16[16,64,128]{2,1,0:T(8,128)(2,1)S(1)}, u32[]{:S(2)}, u32[]{:S(2)}) collective-permute-start(bf16[16,64,128]{2,1,0:T(8,128)(2,1)S(1)} %get-tuple-element.22), channel_id=1, source_target_pairs={{0,1},{1,0},{2,3},{3,2},{4,5},{5,4},{6,7},{7,6},{8,9},{9,8},{10,11... | collective-permute-start | bytes 786440 | tf_op jit(solution)/shard_map/ppermute | solution.py:216
  37.5 34.6 %collective-permute-start.5 = (bf16[16,64,128]{2,1,0:T(8,128)(2,1)S(1)}, bf16[16,64,128]{2,1,0:T(8,128)(2,1)S(1)}, u32[]{:S(2)}, u32[]{:S(2)}) collective-permute-start(bf16[16,64,128]{2,1,0:T(8,128)(2,1)S(1)} %get-tuple-element.17), channel_id=1, source_target_pairs={{0,1},{1,0},{2,3},{3,2},{4,5},{5,4},{6,7},{7,6},{8,9},{9,8},{10,11... | collective-permute-start | bytes 786440 | tf_op jit(solution)/shard_map/ppermute | solution.py:216

commit v3 on v2

--- a/solution.py
+++ b/solution.py
@@ -91,7 +91,7 @@
             pltpu.SemaphoreType.DMA((columns // 16 + 2,)),
             pltpu.SemaphoreType.DMA((chips + 2,)),
         ],
-        compiler_params=pltpu.CompilerParams(vmem_limit_bytes=16 << 20),
+        compiler_params=pltpu.CompilerParams(vmem_limit_bytes=60 << 20),
     )(basis, zone, cond_table)
     return results[0], results[1], results[2:]
 
@@ -215,19 +215,19 @@
     def swap(array, s):
         return lax.ppermute(array, "blk", [(i, i ^ s) for i in range(blocks)])
 
-    def along(array):
-        result = []
-        for offset in (0, 1):
-            partner = [((d + offset) ^ 1) - offset for d in range(slabs)]
-            pairs = [(d, to) for d, to in enumerate(partner) if 0 <= to < slabs]
-            result.append(lax.ppermute(array, "dom", pairs))
-        return result
+    def exchange(array, offset):
+        partner = [((d + offset) ^ 1) - offset for d in range(slabs)]
+        return lax.ppermute(array, "dom", [(d, to) for d, to in enumerate(partner) if 0 <= to < slabs])
 
     sent, center, others = prepare(basis, zone, cond_table, chips)
     others = [swap(other, CORES * (k + 1)) for k, other in enumerate(others)]
-    one, two = along(sent)
+    one, two = exchange(sent, 0), exchange(sent, 1)
     theirs = [swap(center, 1)]
-    far = [along(other) for other in others]
+    far = []
+    for other in others:
+        far.append([
+            exchange(lax.optimization_barrier((other, near))[0], offset) for offset, near in enumerate((one, two))
+        ])
     theirs += [swap(other, 1) for other in others]
 
     image = jax.ShapeDtypeStruct((half, columns, nz), BF16)

time: 74.5 us -> 57.7 us (0.77)
  blocking collectives: 32.4 us -> 17.2 us
  Pallas kernels: 9.72 us -> 11.5 us
  local copies, waits for them, and re-layouts: 4.69 us -> 3.12 us
  waiting for transfers between devices: 18.2 us -> 16.7 us
    all_to_all x1, blocking collectives: 32.4 us -> 17.2 us  [per_device(): lax.all_to_all(shares, ('dom', 'blk'), split_axis=0, concat_axis=0, tiled...]
    ppermute x5, waiting for transfers between devices: 11.1 us -> 1.26 us  [swap(): return lax.ppermute(array, 'blk', [(i, i ^ s) for i in range(blocks)])]
    ppermute x4, waiting for transfers between devices: 7.14 us -> 15.5 us  [exchange(): lax.ppermute(array, 'dom', [(d, to) for d, to in enumerate(partner) if 0...]
    pallas_call x1, Pallas kernels: 1.76 us -> 3.53 us  [prepare(): pl.pallas_call(functools.partial(prepare_kernel, chips), out_shape=shapes...]
    unnamed x12 -> x8, local copies, waits for them, and re-layouts: 4.69 us -> 3.12 us
  transfers between devices with their start and end apart: 9 -> 9, of which waited for: 2 -> 3; matrix products, arithmetic and copies ran while one was open for 0% -> 0% of each run, Pallas kernels for 6% -> 7%
where the time goes in v3:
time: 57.7 us; the launch traced here: 57.4 us
  blocking collectives  17.2 us (30%)
  waiting for transfers between devices  16.7 us (29%)
  Pallas kernels  11.5 us (20%)
  starting transfers between devices  8.17 us (14%)
  local copies, waits for them, and re-layouts  3.12 us (5%)
  between operations  0.7 us (1%)
    all_to_all x1, blocking collectives, per_device(): lax.all_to_all(shares, ('dom', 'blk'), split_axis=0, concat_axis=0, tiled...  17.2 us
    ppermute x4, waiting for transfers between devices, exchange(): lax.ppermute(array, 'dom', [(d, to) for d, to in enumerate(partner) if 0...  15.5 us
    ppermute x4, starting transfers between devices, exchange(): lax.ppermute(array, 'dom', [(d, to) for d, to in enumerate(partner) if 0...  4.52 us
    ppermute x5, starting transfers between devices, swap(): return lax.ppermute(array, 'blk', [(i, i ^ s) for i in range(blocks)])  3.64 us
    pallas_call x1, Pallas kernels, prepare(): pl.pallas_call(functools.partial(prepare_kernel, chips), out_shape=shapes...  3.53 us
    unnamed x8, local copies, waits for them, and re-layouts  3.12 us
    pallas_call x1, Pallas kernels, per_device(): pl.pallas_call(functools.partial(near_kernel, chips, weight), out_shape=(...  2.64 us
    pallas_call x1, Pallas kernels, per_device(): pl.pallas_call(functools.partial(finish_kernel, blocks), out_shape=jax.Sh...  2.05 us
  transfers between devices with their start and end apart: 9, of which 3 were waited for; matrix products, arithmetic and copies ran while one was open for 0% of the time, Pallas kernels for 7%

profile of v3, /device:TPU:0, one launch (start us, length us, event | category | flops | bytes accessed | tf_op | source)
XLA Modules:
  0.0 57.4 jit_solution(13591797948387483018)
XLA Ops:
  0.6 3.5 %shard_map.59 = (bf16[33,64,128]{2,1,0:T(8,128)(2,1)}, bf16[34,64,128]{2,1,0:T(8,128)(2,1)}, bf16[34,64,128]{2,1,0:T(8,128)(2,1)}) custom-call(bf16[64,1,64,128]{3,2,1,0:T(8,128)(2,1)} %basis_hbm.1, s32[1,64,128]{2,1,0:T(8,128)} %zone_ref.1, f32[16]{0:T(128)} %cond_ref.1), custom_call_target="tpu_custom_call" | custom-call | tf_op jit(solution)/shard_map/pallas_call | solution.py:79
  4.2 3.0 %collective-permute-start.2 = (bf16[34,64,128]{2,1,0:T(8,128)(2,1)}, bf16[34,64,128]{2,1,0:T(8,128)(2,1)S(1)}, u32[]{:S(2)}, u32[]{:S(2)}) collective-permute-start(bf16[34,64,128]{2,1,0:T(8,128)(2,1)} %get-tuple-element.17), channel_id=1, source_target_pairs={{0,2},{1,3},{2,0},{3,1},{4,6},{5,7},{6,4},{7,5},{8,10},{9,11},{10,... | collective-permute-start | bytes 1671176 | tf_op jit(solution)/shard_map/ppermute | solution.py:216
  7.2 1.6 %collective-permute-start = (bf16[33,64,128]{2,1,0:T(8,128)(2,1)}, bf16[33,64,128]{2,1,0:T(8,128)(2,1)S(1)}, u32[]{:S(2)}, u32[]{:S(2)}) collective-permute-start(bf16[33,64,128]{2,1,0:T(8,128)(2,1)} %get-tuple-element.16), channel_id=1, source_target_pairs={{0,4},{4,0},{8,12},{12,8},{1,5},{5,1},{9,13},{13,9},{2,6},{6,2},{1... | collective-permute-start | bytes 1622024 | tf_op jit(solution)/shard_map/ppermute | solution.py:220
  8.8 0.7 %collective-permute-start.1 = (bf16[33,64,128]{2,1,0:T(8,128)(2,1)}, bf16[33,64,128]{2,1,0:T(8,128)(2,1)S(1)}, u32[]{:S(2)}, u32[]{:S(2)}) collective-permute-start(bf16[33,64,128]{2,1,0:T(8,128)(2,1)} %get-tuple-element.16), channel_id=1, source_target_pairs={{4,8},{8,4},{5,9},{9,5},{6,10},{10,6},{7,11},{11,7},{20,24},{24,20... | collective-permute-start | bytes 1622024 | tf_op jit(solution)/shard_map/ppermute | solution.py:220
  9.4 0.1 collective-permute-start.3
  9.5 11.6 %collective-permute-done.one = bf16[33,64,128]{2,1,0:T(8,128)(2,1)S(1)} collective-permute-done((bf16[33,64,128]{2,1,0:T(8,128)(2,1)}, bf16[33,64,128]{2,1,0:T(8,128)(2,1)S(1)}, u32[]{:S(2)}, u32[]{:S(2)}) %collective-permute-start) | collective-permute-done | bytes 540704 | tf_op jit(solution)/shard_map/ppermute | solution.py:220
  21.1 0.0 collective-permute-done.2.refs_0_
  21.1 1.6 %collective-permute-start.6 = (bf16[34,64,128]{2,1,0:T(8,128)(2,1)S(1)}, bf16[34,64,128]{2,1,0:T(8,128)(2,1)S(1)}, u32[]{:S(2)}, u32[]{:S(2)}) collective-permute-start(bf16[34,64,128]{2,1,0:T(8,128)(2,1)S(1)} %collective-permute-done.2.refs_0_), channel_id=1, source_target_pairs={{0,4},{4,0},{8,12},{12,8},{1,5},{5,1},{9,13},{13,9},{2,6},{6,2},{1... | collective-permute-start | bytes 1671176 | tf_op jit(solution)/shard_map/ppermute | solution.py:220
  22.7 0.0 collective-permute-start.4
  22.7 0.0 collective-permute-done.1.two
  22.7 0.7 %collective-permute-start.7 = (bf16[34,64,128]{2,1,0:T(8,128)(2,1)S(1)}, bf16[34,64,128]{2,1,0:T(8,128)(2,1)S(1)}, u32[]{:S(2)}, u32[]{:S(2)}) collective-permute-start(bf16[34,64,128]{2,1,0:T(8,128)(2,1)S(1)} %collective-permute-done.2.refs_0_), channel_id=1, source_target_pairs={{4,8},{8,4},{5,9},{9,5},{6,10},{10,6},{7,11},{11,7},{20,24},{24,20... | collective-permute-start | bytes 1671176 | tf_op jit(solution)/shard_map/ppermute | solution.py:220
  23.4 0.0 collective-permute-done.3.refs_1_
  23.4 1.2 %collective-permute-done.4.refs_2_ = bf16[34,64,128]{2,1,0:T(8,128)(2,1)S(1)} collective-permute-done((bf16[34,64,128]{2,1,0:T(8,128)(2,1)S(1)}, bf16[34,64,128]{2,1,0:T(8,128)(2,1)S(1)}, u32[]{:S(2)}, u32[]{:S(2)}) %collective-permute-start.4) | collective-permute-done | bytes 557088 | tf_op jit(solution)/shard_map/ppermute | solution.py:216
  24.7 0.0 copy-start
  24.7 1.1 %copy-done = bf16[34,64,128]{2,1,0:T(8,128)(2,1)S(1)} copy-done((bf16[34,64,128]{2,1,0:T(8,128)(2,1)S(1)}, bf16[34,64,128]{2,1,0:T(8,128)(2,1)}, u32[]{:S(2)}) %copy-start) | copy-done | bytes 557080
  25.7 0.0 copy-start.1
  25.7 0.8 %copy-done.1 = s32[1,64,128]{2,1,0:T(8,128)S(1)} copy-done((s32[1,64,128]{2,1,0:T(8,128)S(1)}, s32[1,64,128]{2,1,0:T(8,128)}, u32[]{:S(2)}) %copy-start.1) | copy-done | bytes 32792
  26.5 0.0 copy-start.2
  26.5 0.7 %copy-done.2 = f32[16]{0:T(128)S(1)} copy-done((f32[16]{0:T(128)S(1)}, f32[16]{0:T(128)}, u32[]{:S(2)}) %copy-start.2) | copy-done | bytes 88
  27.1 0.0 copy-start.3
  27.1 0.7 %copy-done.3 = f32[16]{0:T(128)S(1)} copy-done((f32[16]{0:T(128)S(1)}, f32[16]{0:T(128)}, u32[]{:S(2)}) %copy-start.3) | copy-done | bytes 88
  27.8 2.6 %shard_map.60 = (bf16[16,64,128]{2,1,0:T(8,128)(2,1)S(1)}, bf16[16,64,128]{2,1,0:T(8,128)(2,1)S(1)}, f32[7,32,128]{2,1,0:T(8,128)S(1)}, bf16[256,4096]{1,0:T(8,128)(2,1)S(1)}, f32[256,64]{1,0:T(8,128)S(1)}) custom-call(s32[1,64,128]{2,1,0:T(8,128)S(1)} %copy-done.1, f32[16]{0:T(128)S(1)} %copy-done.2, f32[16]{0:T(128)S(1)} %copy-done.3, ...), custom_call_target="tpu_custom_call" | custom-call | tf_op jit(solution)/shard_map/pallas_call | solution.py:237
  30.4 3.9 %collective-permute-done.6.refs_1_ = bf16[34,64,128]{2,1,0:T(8,128)(2,1)S(1)} collective-permute-done((bf16[34,64,128]{2,1,0:T(8,128)(2,1)S(1)}, bf16[34,64,128]{2,1,0:T(8,128)(2,1)S(1)}, u32[]{:S(2)}, u32[]{:S(2)}) %collective-permute-start.6) | collective-permute-done | bytes 557088 | tf_op jit(solution)/shard_map/ppermute | solution.py:220
  34.3 0.0 collective-permute-done.7.refs_2_
  34.3 1.6 %shard_map.61 = (bf16[16,64,128]{2,1,0:T(8,128)(2,1)S(1)}, bf16[16,64,128]{2,1,0:T(8,128)(2,1)S(1)}, f32[256,128]{1,0:T(8,128)S(1)}) custom-call(f32[7,32,128]{2,1,0:T(8,128)S(1)} %get-tuple-element.20.coef, bf16[256,4096]{1,0:T(8,128)(2,1)S(1)} %get-tuple-element.21.left, f32[256,64]{1,0:T(8,128)S(1)} %get-tuple-element.22.near_gram, ...), custom_call_target="tpu_custom_call" | custom-call | tf_op jit(solution)/shard_map/pallas_call | solution.py:249
  35.9 0.1 collective-permute-start.8
  36.0 0.5 collective-permute-start.5
  36.5 17.2 %all_to_all.5.shares = f32[16,16,128]{2,1,0:T(8,128)} all-to-all(f32[16,16,128]{2,1,0:T(8,128)S(1)} %bitcast.1), channel_id=1, replica_groups=mesh['roll'=2,'dom'=4,'blk'=4] {'dom','blk'}, dimensions={0} | all-to-all | bytes 262144 | tf_op jit(solution)/shard_map/all_to_all | solution.py:274
  53.7 1.7 %shard_map.63 = f32[16,256]{1,0:T(8,128)} custom-call(f32[16,16,128]{2,1,0:T(8,128)} %all_to_all.5.shares), custom_call_target="tpu_custom_call" | custom-call | tf_op jit(solution)/shard_map/pallas_call | solution.py:275
  55.3 0.0 collective-permute-done.8.refs_3_
  55.3 0.0 collective-permute-done.5.refs_1_
  55.3 2.1 %shard_map.62 = bf16[256,1,16,128]{3,2,1,0:T(8,128)(2,1)} custom-call(bf16[16,64,128]{2,1,0:T(8,128)(2,1)S(1)} %get-tuple-element.18.refs_0_, bf16[16,64,128]{2,1,0:T(8,128)(2,1)S(1)} %collective-permute-done.5.refs_1_, bf16[16,64,128]{2,1,0:T(8,128)(2,1)S(1)} %get-tuple-element.25.refs_2_, bf16[16,64,128]{2,1,0:T(8,128)(2,1)S(1)} %collective-permute-done.8.refs_3_), custom_call_target="tpu_custom_call" | custom-call | tf_op jit(solution)/shard_map/pallas_call | solution.py:263
Async XLA Ops:
  4.2 17.0 %collective-permute-start.2 = (bf16[34,64,128]{2,1,0:T(8,128)(2,1)}, bf16[34,64,128]{2,1,0:T(8,128)(2,1)S(1)}, u32[]{:S(2)}, u32[]{:S(2)}) collective-permute-start(bf16[34,64,128]{2,1,0:T(8,128)(2,1)} %get-tuple-element.17), channel_id=1, source_target_pairs={{0,2},{1,3},{2,0},{3,1},{4,6},{5,7},{6,4},{7,5},{8,10},{9,11},{10,... | collective-permute-start | bytes 1671176 | tf_op jit(solution)/shard_map/ppermute | solution.py:216
  7.2 13.9 %collective-permute-start = (bf16[33,64,128]{2,1,0:T(8,128)(2,1)}, bf16[33,64,128]{2,1,0:T(8,128)(2,1)S(1)}, u32[]{:S(2)}, u32[]{:S(2)}) collective-permute-start(bf16[33,64,128]{2,1,0:T(8,128)(2,1)} %get-tuple-element.16), channel_id=1, source_target_pairs={{0,4},{4,0},{8,12},{12,8},{1,5},{5,1},{9,13},{13,9},{2,6},{6,2},{1... | collective-permute-start | bytes 1622024 | tf_op jit(solution)/shard_map/ppermute | solution.py:220
  8.8 14.0 %collective-permute-start.1 = (bf16[33,64,128]{2,1,0:T(8,128)(2,1)}, bf16[33,64,128]{2,1,0:T(8,128)(2,1)S(1)}, u32[]{:S(2)}, u32[]{:S(2)}) collective-permute-start(bf16[33,64,128]{2,1,0:T(8,128)(2,1)} %get-tuple-element.16), channel_id=1, source_target_pairs={{4,8},{8,4},{5,9},{9,5},{6,10},{10,6},{7,11},{11,7},{20,24},{24,20... | collective-permute-start | bytes 1622024 | tf_op jit(solution)/shard_map/ppermute | solution.py:220
  9.4 14.0 %collective-permute-start.3 = (bf16[34,64,128]{2,1,0:T(8,128)(2,1)}, bf16[34,64,128]{2,1,0:T(8,128)(2,1)S(1)}, u32[]{:S(2)}, u32[]{:S(2)}) collective-permute-start(bf16[34,64,128]{2,1,0:T(8,128)(2,1)} %get-tuple-element.15.center), channel_id=1, source_target_pairs={{0,1},{1,0},{2,3},{3,2},{4,5},{5,4},{6,7},{7,6},{8,9},{9,8},{10,11... | collective-permute-start | bytes 1671176 | tf_op jit(solution)/shard_map/ppermute | solution.py:216
  21.1 13.2 %collective-permute-start.6 = (bf16[34,64,128]{2,1,0:T(8,128)(2,1)S(1)}, bf16[34,64,128]{2,1,0:T(8,128)(2,1)S(1)}, u32[]{:S(2)}, u32[]{:S(2)}) collective-permute-start(bf16[34,64,128]{2,1,0:T(8,128)(2,1)S(1)} %collective-permute-done.2.refs_0_), channel_id=1, source_target_pairs={{0,4},{4,0},{8,12},{12,8},{1,5},{5,1},{9,13},{13,9},{2,6},{6,2},{1... | collective-permute-start | bytes 1671176 | tf_op jit(solution)/shard_map/ppermute | solution.py:220
  22.7 2.0 %collective-permute-start.4 = (bf16[34,64,128]{2,1,0:T(8,128)(2,1)S(1)}, bf16[34,64,128]{2,1,0:T(8,128)(2,1)S(1)}, u32[]{:S(2)}, u32[]{:S(2)}) collective-permute-start(bf16[34,64,128]{2,1,0:T(8,128)(2,1)S(1)} %collective-permute-done.2.refs_0_), channel_id=1, source_target_pairs={{0,1},{1,0},{2,3},{3,2},{4,5},{5,4},{6,7},{7,6},{8,9},{9,8},{10,11... | collective-permute-start | bytes 1671176 | tf_op jit(solution)/shard_map/ppermute | solution.py:216
  22.7 11.6 %collective-permute-start.7 = (bf16[34,64,128]{2,1,0:T(8,128)(2,1)S(1)}, bf16[34,64,128]{2,1,0:T(8,128)(2,1)S(1)}, u32[]{:S(2)}, u32[]{:S(2)}) collective-permute-start(bf16[34,64,128]{2,1,0:T(8,128)(2,1)S(1)} %collective-permute-done.2.refs_0_), channel_id=1, source_target_pairs={{4,8},{8,4},{5,9},{9,5},{6,10},{10,6},{7,11},{11,7},{20,24},{24,20... | collective-permute-start | bytes 1671176 | tf_op jit(solution)/shard_map/ppermute | solution.py:220
  24.7 1.1 %copy-start = (bf16[34,64,128]{2,1,0:T(8,128)(2,1)S(1)}, bf16[34,64,128]{2,1,0:T(8,128)(2,1)}, u32[]{:S(2)}) copy-start(bf16[34,64,128]{2,1,0:T(8,128)(2,1)} %get-tuple-element.15.center) | copy-start | bytes 1671172
  25.7 0.8 %copy-start.1 = (s32[1,64,128]{2,1,0:T(8,128)S(1)}, s32[1,64,128]{2,1,0:T(8,128)}, u32[]{:S(2)}) copy-start(s32[1,64,128]{2,1,0:T(8,128)} %zone_ref.1) | copy-start | bytes 98308
  26.5 0.7 %copy-start.2 = (f32[16]{0:T(128)S(1)}, f32[16]{0:T(128)}, u32[]{:S(2)}) copy-start(f32[16]{0:T(128)} %cond_ref.1) | copy-start | bytes 196
  27.1 0.7 %copy-start.3 = (f32[16]{0:T(128)S(1)}, f32[16]{0:T(128)}, u32[]{:S(2)}) copy-start(f32[16]{0:T(128)} %heat_ref.1) | copy-start | bytes 196
  35.9 19.4 %collective-permute-start.8 = (bf16[16,64,128]{2,1,0:T(8,128)(2,1)S(1)}, bf16[16,64,128]{2,1,0:T(8,128)(2,1)S(1)}, u32[]{:S(2)}, u32[]{:S(2)}) collective-permute-start(bf16[16,64,128]{2,1,0:T(8,128)(2,1)S(1)} %get-tuple-element.26), channel_id=1, source_target_pairs={{0,1},{1,0},{2,3},{3,2},{4,5},{5,4},{6,7},{7,6},{8,9},{9,8},{10,11... | collective-permute-start | bytes 786440 | tf_op jit(solution)/shard_map/ppermute | solution.py:216
  36.0 19.3 %collective-permute-start.5 = (bf16[16,64,128]{2,1,0:T(8,128)(2,1)S(1)}, bf16[16,64,128]{2,1,0:T(8,128)(2,1)S(1)}, u32[]{:S(2)}, u32[]{:S(2)}) collective-permute-start(bf16[16,64,128]{2,1,0:T(8,128)(2,1)S(1)} %get-tuple-element.19), channel_id=1, source_target_pairs={{0,1},{1,0},{2,3},{3,2},{4,5},{5,4},{6,7},{7,6},{8,9},{9,8},{10,11... | collective-permute-start | bytes 786440 | tf_op jit(solution)/shard_map/ppermute | solution.py:216

commit v4 on v2

v4 whole, which is shorter than its diff:
```python
import functools

import jax
import jax.numpy as jnp
from jax import lax
from jax.experimental import pallas as pl
from jax.experimental.pallas import tpu as pltpu
from jax.sharding import PartitionSpec as P

ZONES = 16
CORES = 2
COST = 1 << 30
F32 = jnp.float32
BF16 = jnp.bfloat16
VMEM = pl.BlockSpec(memory_space=pltpu.VMEM)
SMEM = pl.BlockSpec(memory_space=pltpu.SMEM)
HBM = pl.BlockSpec(memory_space=pltpu.HBM)


def lookup(zone, table_ref):
    result = jnp.zeros(zone.shape, F32)
    for which in range(ZONES):
        result = jnp.where(zone == which, table_ref[which], result)
    return result


def cond_of(zone, table_ref):
    return lookup(zone, table_ref).astype(BF16).astype(F32)


def prepare_kernel(chips, basis_hbm, zone_hbm, cond_hbm, *refs):
    outs, (basis, zone, table, wide, turned, cond_pad, in_sems, out_sems) = refs[:chips + 1], refs[chips + 1:]
    columns, _, ny, nz = basis.shape
    rows = ny // chips
    chip = lax.axis_index("blk") // CORES
    step = 16
    chunks = columns // step
    loads = [
        pltpu.make_async_copy(basis_hbm.at[pl.ds(i * step, step)], basis.at[pl.ds(i * step, step)], in_sems.at[i])
        for i in range(chunks)
    ]
    loads.append(pltpu.make_async_copy(zone_hbm, zone, in_sems.at[chunks]))
    loads.append(pltpu.make_async_copy(cond_hbm, table, in_sems.at[chunks + 1]))
    for load in loads:
        load.start()
    turned[0] = jnp.zeros((columns, nz), BF16)
    turned[ny + 1] = jnp.zeros((columns, nz), BF16)
    stores = []

    def store(source, target):
        copy = pltpu.make_async_copy(source, target, out_sems.at[len(stores)])
        copy.start()
        stores.append(copy)

    loads[chunks].wait()
    loads[chunks + 1].wait()
    mine = zone[0, pl.ds(pl.multiple_of(chip * rows, rows), rows), :]
    own = cond_of(mine, table)
    cond_pad[...] = jnp.concatenate([own, jnp.zeros((columns - rows, nz), F32)], 0).astype(BF16)
    store(cond_pad, outs[0].at[rows])
    for i in range(chunks):
        loads[i].wait()
        some = pl.ds(i * step, step)
        for c in range(i * step, (i + 1) * step):
            wide[c * ny:(c + 1) * ny, :] = basis[c, 0].astype(F32)
        for y in range(ny):
            turned[y + 1, some, :] = wide[pl.ds(i * step * ny + y, step, stride=ny), :].astype(BF16)
        for k in reversed(range(chips)):
            store(turned.at[pl.ds((chip ^ k) * rows, rows + 2), some], outs[1 + k].at[:, some])
        store(turned.at[pl.ds(chip * rows + 1, rows), some], outs[0].at[pl.ds(0, rows), some])
    for copy in stores:
        copy.wait()


def prepare(basis, zone, cond_table, chips):
    columns, _, ny, nz = basis.shape
    rows = ny // chips
    shapes = [jax.ShapeDtypeStruct((rows + 1, columns, nz), BF16)]
    shapes += [jax.ShapeDtypeStruct((rows + 2, columns, nz), BF16)] * chips
    results = pl.pallas_call(
        functools.partial(prepare_kernel, chips),
        out_shape=shapes,
        in_specs=[HBM, HBM, HBM],
        out_specs=[pl.BlockSpec(memory_space=pl.ANY)] * len(shapes),
        scratch_shapes=[
            pltpu.VMEM(basis.shape, BF16),
            pltpu.VMEM(zone.shape, jnp.int32),
            pltpu.SMEM((ZONES,), F32),
            pltpu.VMEM((columns * ny, nz), F32),
            pltpu.VMEM((ny + 2, columns, nz), BF16),
            pltpu.VMEM((columns, nz), BF16),
            pltpu.SemaphoreType.DMA((columns // 16 + 2,)),
            pltpu.SemaphoreType.DMA((1 + (chips + 1) * (columns // 16),)),
        ],
        compiler_params=pltpu.CompilerParams(vmem_limit_bytes=16 << 20),
    )(*[pltpu.with_memory_space_constraint(x, pltpu.HBM) for x in (basis, zone, cond_table)])
    return results[0], results[1], results[2:]


def plane_kernel(chips, zone_ref, cond_ref, heat_ref, center, coef, partial, cond_pad):
    rows = partial.shape[0]
    nz = center.shape[2]
    ny = zone_ref.shape[1]
    chip = lax.axis_index("blk") // CORES
    cond_pad[0:8, :] = jnp.zeros((8, nz), F32)
    cond_pad[8:8 + ny, :] = cond_of(zone_ref[0], cond_ref)
    cond_pad[8 + ny:16 + ny, :] = jnp.zeros((8, nz), F32)
    base = pl.multiple_of(chip * rows, 8)
    near = cond_pad[pl.ds(base, rows + 16), :]
    own = near[8:8 + rows]
    lane = lax.broadcasted_iota(jnp.int32, (rows, nz), 1)
    coef[0] = lookup(zone_ref[0, pl.ds(base, rows), :], heat_ref)
    beside = (
        near[7:7 + rows],
        near[9:9 + rows],
        jnp.where(lane == 0, 0.0, pltpu.roll(own, 1, 1)),
        jnp.where(lane == nz - 1, 0.0, pltpu.roll(own, nz - 1, 1)),
    )
    for which, other in enumerate(beside):
        coef[1 + which] = 0.5 * (own + other)
    coef[5] = own
    plane_rows(coef, center, partial)


def plane_rows(coef, center, partial):
    columns, nz = center.shape[1:]
    lane = lax.broadcasted_iota(jnp.int32, (columns, nz), 1)
    first, last = lane == 0, lane == nz - 1
    for y in range(partial.shape[0]):
        face = [jnp.broadcast_to(coef[k, y:y + 1, :], (columns, nz)) for k in range(5)]
        v = center[y + 1].astype(F32)
        total = face[0] * v
        total += face[1] * (v - center[y].astype(F32))
        total += face[2] * (v - center[y + 2].astype(F32))
        total += face[3] * (v - jnp.where(first, 0.0, pltpu.roll(v, 1, 1)))
        total += face[4] * (v - jnp.where(last, 0.0, pltpu.roll(v, nz - 1, 1)))
        partial[y] = total


def image_rows(coef, partial, center, one, two, skip, mine, theirs, flat):
    rows, columns, nz = partial.shape
    half = rows // CORES
    core = lax.axis_index("blk") % CORES
    for y in range(rows):
        face = [jnp.broadcast_to(coef[k, y:y + 1, :], (columns, nz)) for k in range(2)]
        v = center[y + 1].astype(F32)
        total = partial[y]
        total += face[0] * (v - one[y + skip].astype(F32))
        total += face[1] * (v - two[y + skip].astype(F32))
        image = total.astype(BF16)
        flat[:, y * nz:(y + 1) * nz] = image

        @pl.when(core == y // half)
        def _():
            mine[y % half] = image

        @pl.when(core != y // half)
        def _():
            theirs[y % half] = image


def gram_of(left, flat):
    return lax.dot_general(left[...], flat[...], (((1,), (1,)), ((), ())), preferred_element_type=F32)


def near_kernel(coef, partial, center, one, two, mine, theirs, faces, flat):
    rows = partial.shape[0]
    for which, ref in enumerate((one, two)):
        faces[which] = 0.5 * (coef[5] + ref[rows].astype(F32)[:rows])
    image_rows(faces, partial, center, one, two, 0, mine, theirs, flat)


def left_kernel(chips, weight, coef, flat, center, *refs):
    others, theirs, partials = refs[:chips - 1], refs[chips - 1:2 * chips - 1], refs[2 * chips - 1:3 * chips - 2]
    left, gram = refs[3 * chips - 2:]
    rows, columns, nz = partials[0].shape
    me = lax.axis_index("blk")
    for k, ref in enumerate((center, *others)):
        for core in range(CORES):
            where = pl.ds(pl.multiple_of((me ^ (CORES * k + core)) * columns, columns), columns)
            for y in range(rows):
                left[where, y * nz:(y + 1) * nz] = theirs[k][y] if core else ref[y + 1]
    gram[...] = weight * gram_of(left, flat)
    for k in range(chips - 1):
        plane_rows(coef, others[k], partials[k])


def far_kernel(chips, weight, faces, left, near_gram, *refs):
    count = chips - 1
    partials, centers, twos, ones, mine, theirs = (refs[i * count:(i + 1) * count] for i in range(6))
    gram, flat = refs[6 * count:]
    columns = centers[0].shape[1]
    gram[:, 0:columns] = near_gram[...]
    for k in range(count):
        image_rows(faces, partials[k], centers[k], ones[k], twos[k], 1, mine[k], theirs[k], flat)
        gram[:, (k + 1) * columns:(k + 2) * columns] = weight * gram_of(left, flat)


def finish_kernel(blocks, *refs):
    images, (applied, wide) = refs[:blocks], refs[blocks:]
    rows, columns, nz = images[0].shape
    me = lax.axis_index("blk")
    for s, image in enumerate(images):
        for y in range(rows):
            wide[pl.ds(y, columns, stride=rows), :] = image[y].astype(F32)
        start = (me ^ s) * columns
        for c in range(columns):
            applied[start + c, 0] = wide[c * rows:(c + 1) * rows, :].astype(BF16)


def sum_kernel(slabs, blocks, shares, out):
    chips = blocks // CORES
    columns = shares.shape[2] // chips
    for core in range(CORES):
        sums = []
        for chip in range(chips):
            total = shares[CORES * chip + core]
            for slab in range(1, slabs):
                total += shares[slab * blocks + CORES * chip + core]
            sums.append(total)
        for target in range(chips):
            parts = [sums[chip][:, (chip ^ target) * columns:((chip ^ target) + 1) * columns] for chip in range(chips)]
            start = (CORES * target + core) * columns
            out[:, start:start + columns] = functools.reduce(jnp.add, parts)


def per_device(basis, zone, cond_table, heat_table):
    blocks = lax.axis_size("blk")
    slabs = lax.axis_size("dom")
    chips = blocks // CORES
    columns, planes, ny, nz = basis.shape
    rows = ny // chips
    half = ny // blocks
    total = columns * blocks
    weight = 1.0 / (slabs * planes * ny * nz)

    def swap(array, s):
        return lax.ppermute(array, "blk", [(i, i ^ s) for i in range(blocks)])

    def exchange(array, offset):
        partner = [((d + offset) ^ 1) - offset for d in range(slabs)]
        return lax.ppermute(array, "dom", [(d, to) for d, to in enumerate(partner) if 0 <= to < slabs])

    sent, center, others = prepare(basis, zone, cond_table, chips)
    others = [swap(other, CORES * (k + 1)) for k, other in enumerate(others)]
    count = chips - 1
    image = jax.ShapeDtypeStruct((half, columns, nz), BF16)
    partial = jax.ShapeDtypeStruct((rows, columns, nz), F32)
    flat = pltpu.VMEM((columns, rows * nz), BF16)
    params = pltpu.CompilerParams(vmem_limit_bytes=32 << 20)
    two = exchange(sent, 1)
    one = exchange(sent, 0)
    coef, near_partial = pl.pallas_call(
        functools.partial(plane_kernel, chips),
        out_shape=(jax.ShapeDtypeStruct((6, rows, nz), F32), partial),
        in_specs=[VMEM, SMEM, SMEM, VMEM],
        out_specs=[VMEM] * 2,
        scratch_shapes=[pltpu.VMEM((ny + 16, nz), F32)],
        compiler_params=params,
        cost_estimate=pl.CostEstimate(flops=COST, bytes_accessed=COST // 8, transcendentals=0),
    )(zone, cond_table, heat_table, center)
    far = []
    for other in others:
        far_two = exchange(lax.optimization_barrier((other, one))[0], 1)
        far.append((exchange(lax.optimization_barrier((other, two))[0], 0), far_two))
    near_mine, near_theirs, faces, near_flat = pl.pallas_call(
        near_kernel,
        out_shape=(
            image,
            image,
            jax.ShapeDtypeStruct((2, rows, nz), F32),
            jax.ShapeDtypeStruct((columns, rows * nz), BF16),
        ),
        in_specs=[VMEM] * 5,
        out_specs=[VMEM] * 4,
        compiler_params=params,
        cost_estimate=pl.CostEstimate(flops=1, bytes_accessed=1, transcendentals=0),
    )(coef, near_partial, center, one, two)
    late = lax.optimization_barrier((center, others, faces))
    theirs = [swap(array[1:-1], 1) for array in (late[0], *late[1])]
    *far_partials, left, near_gram = pl.pallas_call(
        functools.partial(left_kernel, chips, weight),
        out_shape=[partial] * count + [
            jax.ShapeDtypeStruct((total, rows * nz), BF16),
            jax.ShapeDtypeStruct((total, columns), F32),
        ],
        in_specs=[VMEM] * (2 * chips + 2),
        out_specs=[VMEM] * (count + 2),
        compiler_params=params,
        cost_estimate=pl.CostEstimate(flops=1, bytes_accessed=1, transcendentals=0),
    )(coef, near_flat, center, *others, *theirs)

    *images, gram = pl.pallas_call(
        functools.partial(far_kernel, chips, weight),
        out_shape=[image] * (2 * count) + [jax.ShapeDtypeStruct((total, chips * columns), F32)],
        in_specs=[VMEM] * (3 + 4 * count),
        out_specs=[VMEM] * (2 * count + 1),
        scratch_shapes=[flat],
        compiler_params=params,
    )(faces, left, near_gram, *far_partials, *others, *(two for _, two in far), *(one for one, _ in far))

    near_theirs = swap(near_theirs, 1)
    far_theirs = [swap(array, 1) for array in images[count:]]
    pieces = [near_mine, near_theirs]
    for k in range(count):
        pieces += [images[k], far_theirs[k]]
    applied = pl.pallas_call(
        functools.partial(finish_kernel, blocks),
        out_shape=jax.ShapeDtypeStruct((total, 1, half, nz), BF16),
        in_specs=[VMEM] * blocks,
        out_specs=VMEM,
        scratch_shapes=[pltpu.VMEM((columns * half, nz), F32)],
        compiler_params=params,
    )(*pieces)

    parts = slabs * blocks
    shares = gram.reshape(parts, total // parts, chips * columns)
    shares = lax.all_to_all(shares, ("dom", "blk"), split_axis=0, concat_axis=0, tiled=True)
    reduced = pl.pallas_call(
        functools.partial(sum_kernel, slabs, blocks),
        out_shape=jax.ShapeDtypeStruct((total // parts, total), F32),
        in_specs=[VMEM],
        out_specs=VMEM,
    )(shares)
    return applied, reduced


def solution(mesh):
    placed = (P("blk", "dom", "roll", None), P("dom", "roll", None), P(), P())
    return jax.shard_map(
        per_device,
        mesh=mesh,
        in_specs=placed,
        out_specs=(P("roll", "dom", "blk", None), P(("dom", "blk"), "roll")),
        check_vma=False,
    )
```

time: 74.5 us -> 53.6 us (0.72)
  blocking collectives: 32.4 us -> 11.7 us
  starting transfers between devices: 8.36 us -> 11.2 us
  local copies, waits for them, and re-layouts: 4.69 us -> 2.14 us
  waiting for transfers between devices: 18.2 us -> 16.4 us
  Pallas kernels: 9.72 us -> 11.3 us
    all_to_all x1, blocking collectives: 32.4 us -> 11.7 us  [per_device(): lax.all_to_all(shares, ('dom', 'blk'), split_axis=0, concat_axis=0, tiled...]
    ppermute x5, waiting for transfers between devices: 11.1 us -> 1.97 us  [swap(): return lax.ppermute(array, 'blk', [(i, i ^ s) for i in range(blocks)])]
    ppermute x4, waiting for transfers between devices: 7.14 us -> 14.4 us  [exchange(): lax.ppermute(array, 'dom', [(d, to) for d, to in enumerate(partner) if 0...]
    unnamed x12 -> x6, local copies, waits for them, and re-layouts: 4.69 us -> 2.07 us
    ppermute x4, starting transfers between devices: 4.78 us -> 7.38 us  [exchange(): lax.ppermute(array, 'dom', [(d, to) for d, to in enumerate(partner) if 0...]
    pallas_call x1, Pallas kernels: 1.76 us -> 2.87 us  [prepare(): pl.pallas_call(functools.partial(prepare_kernel, chips), out_shape=shapes...]
    pallas_call x1 -> x3, Pallas kernels: 2.64 us -> 3.37 us  [the longest x1 1.45 us: per_device(): pl.pallas_call(functools.partial(left_kernel, chips, weight), out_shape=[...]
  transfers between devices with their start and end apart: 9 -> 9, of which waited for: 2 -> 4; matrix products, arithmetic and copies ran while one was open for 0% -> 0% of each run, Pallas kernels for 6% -> 12%
where the time goes in v4:
time: 53.6 us; the launch traced here: 53.3 us
  waiting for transfers between devices  16.4 us (31%)
  blocking collectives  11.7 us (22%)
  Pallas kernels  11.3 us (21%)
  starting transfers between devices  11.2 us (21%)
  local copies, waits for them, and re-layouts  2.14 us (4%)
  between operations  0.73 us (1%)
    ppermute x4, waiting for transfers between devices, exchange(): lax.ppermute(array, 'dom', [(d, to) for d, to in enumerate(partner) if 0...  14.4 us
    all_to_all x1, blocking collectives, per_device(): lax.all_to_all(shares, ('dom', 'blk'), split_axis=0, concat_axis=0, tiled...  11.7 us
    ppermute x4, starting transfers between devices, exchange(): lax.ppermute(array, 'dom', [(d, to) for d, to in enumerate(partner) if 0...  7.38 us
    ppermute x5, starting transfers between devices, swap(): return lax.ppermute(array, 'blk', [(i, i ^ s) for i in range(blocks)])  3.78 us
    pallas_call x1, Pallas kernels, prepare(): pl.pallas_call(functools.partial(prepare_kernel, chips), out_shape=shapes...  2.87 us
    unnamed x6, local copies, waits for them, and re-layouts  2.07 us
    pallas_call x1, Pallas kernels, per_device(): pl.pallas_call(functools.partial(finish_kernel, blocks), out_shape=jax.Sh...  2.05 us
    ppermute x5, waiting for transfers between devices, swap(): return lax.ppermute(array, 'blk', [(i, i ^ s) for i in range(blocks)])  1.97 us
  transfers between devices with their start and end apart: 9, of which 4 were waited for; matrix products, arithmetic and copies ran while one was open for 0% of the time, Pallas kernels for 12%

profile of v4, /device:TPU:0, one launch (start us, length us, event | category | flops | bytes accessed | tf_op | source)
XLA Modules:
  0.0 53.3 jit_solution(16798338983052522455)
XLA Ops:
  0.6 2.9 %shard_map.59 = (bf16[33,64,128]{2,1,0:T(8,128)(2,1)S(1)}, bf16[34,64,128]{2,1,0:T(8,128)(2,1)S(1)}, bf16[34,64,128]{2,1,0:T(8,128)(2,1)S(1)}) custom-call(bf16[64,1,64,128]{3,2,1,0:T(8,128)(2,1)} %basis_hbm.1, s32[1,64,128]{2,1,0:T(8,128)} %zone_ref.1, f32[16]{0:T(128)} %cond_ref.1), custom_call_target="tpu_custom_call" | custom-call | tf_op jit(solution)/shard_map/pallas_call | solution.py:80
  3.5 3.0 %collective-permute-start.3 = (bf16[34,64,128]{2,1,0:T(8,128)(2,1)S(1)}, bf16[34,64,128]{2,1,0:T(8,128)(2,1)S(1)}, u32[]{:S(2)}, u32[]{:S(2)}) collective-permute-start(bf16[34,64,128]{2,1,0:T(8,128)(2,1)S(1)} %get-tuple-element.29), channel_id=1, source_target_pairs={{0,2},{1,3},{2,0},{3,1},{4,6},{5,7},{6,4},{7,5},{8,10},{9,11},{10,... | collective-permute-start | bytes 1671176 | tf_op jit(solution)/shard_map/ppermute | solution.py:238
  6.5 1.6 %collective-permute-start = (bf16[33,64,128]{2,1,0:T(8,128)(2,1)S(1)}, bf16[33,64,128]{2,1,0:T(8,128)(2,1)S(1)}, u32[]{:S(2)}, u32[]{:S(2)}) collective-permute-start(bf16[33,64,128]{2,1,0:T(8,128)(2,1)S(1)} %get-tuple-element.24), channel_id=1, source_target_pairs={{0,4},{4,0},{8,12},{12,8},{1,5},{5,1},{9,13},{13,9},{2,6},{6,2},{1... | collective-permute-start | bytes 1622024 | tf_op jit(solution)/shard_map/ppermute | solution.py:242
  8.1 0.7 %collective-permute-start.1 = (bf16[33,64,128]{2,1,0:T(8,128)(2,1)S(1)}, bf16[33,64,128]{2,1,0:T(8,128)(2,1)S(1)}, u32[]{:S(2)}, u32[]{:S(2)}) collective-permute-start(bf16[33,64,128]{2,1,0:T(8,128)(2,1)S(1)} %get-tuple-element.24), channel_id=1, source_target_pairs={{4,8},{8,4},{5,9},{9,5},{6,10},{10,6},{7,11},{11,7},{20,24},{24,20... | collective-permute-start | bytes 1622024 | tf_op jit(solution)/shard_map/ppermute | solution.py:242
  8.8 11.5 %collective-permute-done.one = bf16[33,64,128]{2,1,0:T(8,128)(2,1)S(1)} collective-permute-done((bf16[33,64,128]{2,1,0:T(8,128)(2,1)S(1)}, bf16[33,64,128]{2,1,0:T(8,128)(2,1)S(1)}, u32[]{:S(2)}, u32[]{:S(2)}) %collective-permute-start) | collective-permute-done | bytes 540704 | tf_op jit(solution)/shard_map/ppermute | solution.py:242
  20.2 0.0 collective-permute-done.3.refs_0_.refs_1_
  20.2 0.7 %collective-permute-start.6 = (bf16[34,64,128]{2,1,0:T(8,128)(2,1)S(1)}, bf16[34,64,128]{2,1,0:T(8,128)(2,1)S(1)}, u32[]{:S(2)}, u32[]{:S(2)}) collective-permute-start(bf16[34,64,128]{2,1,0:T(8,128)(2,1)S(1)} %collective-permute-done.3.refs_0_.refs_1_), channel_id=1, source_target_pairs={{4,8},{8,4},{5,9},{9,5},{6,10},{10,6},{7,11},{11,7},{20,24},{24,20... | collective-permute-start | bytes 1671176 | tf_op jit(solution)/shard_map/ppermute | solution.py:242
  20.9 0.0 collective-permute-done.1.two
  21.0 4.4 %collective-permute-start.7 = (bf16[34,64,128]{2,1,0:T(8,128)(2,1)S(1)}, bf16[34,64,128]{2,1,0:T(8,128)(2,1)S(1)}, u32[]{:S(2)}, u32[]{:S(2)}) collective-permute-start(bf16[34,64,128]{2,1,0:T(8,128)(2,1)S(1)} %collective-permute-done.3.refs_0_.refs_1_), channel_id=1, source_target_pairs={{0,4},{4,0},{8,12},{12,8},{1,5},{5,1},{9,13},{13,9},{2,6},{6,2},{1... | collective-permute-start | bytes 1671176 | tf_op jit(solution)/shard_map/ppermute | solution.py:242
  25.4 0.0 copy-start
  25.4 0.8 %copy-done = s32[1,64,128]{2,1,0:T(8,128)S(1)} copy-done((s32[1,64,128]{2,1,0:T(8,128)S(1)}, s32[1,64,128]{2,1,0:T(8,128)}, u32[]{:S(2)}) %copy-start) | copy-done | bytes 32792
  26.1 0.0 copy-start.1
  26.1 0.7 %copy-done.1 = f32[16]{0:T(128)S(1)} copy-done((f32[16]{0:T(128)S(1)}, f32[16]{0:T(128)}, u32[]{:S(2)}) %copy-start.1) | copy-done | bytes 88
  26.8 0.0 copy-start.2
  26.8 0.7 %copy-done.2 = f32[16]{0:T(128)S(1)} copy-done((f32[16]{0:T(128)S(1)}, f32[16]{0:T(128)}, u32[]{:S(2)}) %copy-start.2) | copy-done | bytes 88
  27.5 1.3 %shard_map.60 = (f32[6,32,128]{2,1,0:T(8,128)S(1)}, f32[32,64,128]{2,1,0:T(8,128)S(1)}) custom-call(s32[1,64,128]{2,1,0:T(8,128)S(1)} %copy-done, f32[16]{0:T(128)S(1)} %copy-done.1, f32[16]{0:T(128)S(1)} %copy-done.2, bf16[34,64,128]{2,1,0:T(8,128)(2,1)S(1)} %get-tuple-element.30.center), custom_call_target="tpu_custom_call" | custom-call | flops 1073741824 | bytes 134217728 | tf_op jit(solution)/shard_map/pallas_call | solution.py:253
  28.8 0.6 %shard_map.61 = (bf16[16,64,128]{2,1,0:T(8,128)(2,1)S(1)}, bf16[16,64,128]{2,1,0:T(8,128)(2,1)S(1)}, f32[2,32,128]{2,1,0:T(8,128)S(1)}, bf16[64,4096]{1,0:T(8,128)(2,1)S(1)}) custom-call(f32[6,32,128]{2,1,0:T(8,128)S(1)} %get-tuple-element.22.coef, f32[32,64,128]{2,1,0:T(8,128)S(1)} %get-tuple-element.23.partial, ...), custom_call_target="tpu_custom_call" | custom-call | flops 1 | bytes 1 | tf_op jit(solution)/shard_map/pallas_call | solution.py:266
  29.4 0.1 collective-permute-start.4
  29.6 0.6 %collective-permute-start.5 = (bf16[32,64,128]{2,1,0:T(8,128)(2,1)S(1)}, bf16[32,64,128]{2,1,0:T(8,128)(2,1)S(1)}, u32[]{:S(2)}, u32[]{:S(2)}) collective-permute-start(bf16[32,64,128]{2,1,0:T(8,128)(2,1)S(1)} %slice.7), channel_id=1, source_target_pairs={{0,1},{1,0},{2,3},{3,2},{4,5},{5,4},{6,7},{7,6},{8,9},{9,8},{10,11... | collective-permute-start | bytes 1572872 | tf_op jit(solution)/shard_map/ppermute | solution.py:238
  30.1 0.1 collective-permute-start.2
  30.2 1.2 %collective-permute-done.4.refs_1_ = bf16[32,64,128]{2,1,0:T(8,128)(2,1)S(1)} collective-permute-done((bf16[32,64,128]{2,1,0:T(8,128)(2,1)S(1)}, bf16[32,64,128]{2,1,0:T(8,128)(2,1)S(1)}, u32[]{:S(2)}, u32[]{:S(2)}) %collective-permute-start.4) | collective-permute-done | bytes 524320 | tf_op jit(solution)/shard_map/ppermute | solution.py:238
  31.4 0.7 %collective-permute-done.5.refs_2_ = bf16[32,64,128]{2,1,0:T(8,128)(2,1)S(1)} collective-permute-done((bf16[32,64,128]{2,1,0:T(8,128)(2,1)S(1)}, bf16[32,64,128]{2,1,0:T(8,128)(2,1)S(1)}, u32[]{:S(2)}, u32[]{:S(2)}) %collective-permute-start.5) | collective-permute-done | bytes 524320 | tf_op jit(solution)/shard_map/ppermute | solution.py:238
  32.2 1.4 %shard_map.62 = (f32[32,64,128]{2,1,0:T(8,128)S(1)}, bf16[256,4096]{1,0:T(8,128)(2,1)S(1)}, f32[256,64]{1,0:T(8,128)S(1)}) custom-call(f32[6,32,128]{2,1,0:T(8,128)S(1)} %get-tuple-element.22.coef, bf16[64,4096]{1,0:T(8,128)(2,1)S(1)} %get-tuple-element.28.flat, bf16[34,64,128]{2,1,0:T(8,128)(2,1)S(1)} %get-tuple-element.30.center, ...), custom_call_target="tpu_custom_call" | custom-call | flops 1 | bytes 1 | tf_op jit(solution)/shard_map/pallas_call | solution.py:281
  33.6 0.0 collective-permute-done.6.refs_2_
  33.6 2.9 %collective-permute-done.7.refs_3_ = bf16[34,64,128]{2,1,0:T(8,128)(2,1)S(1)} collective-permute-done((bf16[34,64,128]{2,1,0:T(8,128)(2,1)S(1)}, bf16[34,64,128]{2,1,0:T(8,128)(2,1)S(1)}, u32[]{:S(2)}, u32[]{:S(2)}) %collective-permute-start.7) | collective-permute-done | bytes 557088 | tf_op jit(solution)/shard_map/ppermute | solution.py:242
  36.5 1.3 %shard_map.63 = (bf16[16,64,128]{2,1,0:T(8,128)(2,1)S(1)}, bf16[16,64,128]{2,1,0:T(8,128)(2,1)S(1)}, f32[256,128]{1,0:T(8,128)S(1)}) custom-call(f32[2,32,128]{2,1,0:T(8,128)S(1)} %get-tuple-element.27.faces, bf16[256,4096]{1,0:T(8,128)(2,1)S(1)} %get-tuple-element.32.left, f32[256,64]{1,0:T(8,128)S(1)} %get-tuple-element.33.near_gram, ...), custom_call_target="tpu_custom_call" | custom-call | tf_op jit(solution)/shard_map/pallas_call | solution.py:293
  37.9 0.1 collective-permute-start.8
  38.0 11.7 %all_to_all.5.shares = f32[16,16,128]{2,1,0:T(8,128)} all-to-all(f32[16,16,128]{2,1,0:T(8,128)S(1)} %bitcast.1), channel_id=1, replica_groups=mesh['roll'=2,'dom'=4,'blk'=4] {'dom','blk'}, dimensions={0} | all-to-all | bytes 262144 | tf_op jit(solution)/shard_map/all_to_all | solution.py:318
  49.6 1.7 %shard_map.65 = f32[16,256]{1,0:T(8,128)} custom-call(f32[16,16,128]{2,1,0:T(8,128)} %all_to_all.5.shares), custom_call_target="tpu_custom_call" | custom-call | tf_op jit(solution)/shard_map/pallas_call | solution.py:319
  51.3 0.0 collective-permute-done.2.refs_1_
  51.3 0.0 collective-permute-done.8.refs_3_
  51.3 2.1 %shard_map.64 = bf16[256,1,16,128]{3,2,1,0:T(8,128)(2,1)} custom-call(bf16[16,64,128]{2,1,0:T(8,128)(2,1)S(1)} %get-tuple-element.25.refs_0_, bf16[16,64,128]{2,1,0:T(8,128)(2,1)S(1)} %collective-permute-done.2.refs_1_, bf16[16,64,128]{2,1,0:T(8,128)(2,1)S(1)} %get-tuple-element.37.refs_2_, bf16[16,64,128]{2,1,0:T(8,128)(2,1)S(1)} %collective-permute-done.8.refs_3_), custom_call_target="tpu_custom_call" | custom-call | tf_op jit(solution)/shard_map/pallas_call | solution.py:307
  (2 shorter events, 0.1 us)
Async XLA Ops:
  3.5 16.7 %collective-permute-start.3 = (bf16[34,64,128]{2,1,0:T(8,128)(2,1)S(1)}, bf16[34,64,128]{2,1,0:T(8,128)(2,1)S(1)}, u32[]{:S(2)}, u32[]{:S(2)}) collective-permute-start(bf16[34,64,128]{2,1,0:T(8,128)(2,1)S(1)} %get-tuple-element.29), channel_id=1, source_target_pairs={{0,2},{1,3},{2,0},{3,1},{4,6},{5,7},{6,4},{7,5},{8,10},{9,11},{10,... | collective-permute-start | bytes 1671176 | tf_op jit(solution)/shard_map/ppermute | solution.py:238
  6.5 13.7 %collective-permute-start = (bf16[33,64,128]{2,1,0:T(8,128)(2,1)S(1)}, bf16[33,64,128]{2,1,0:T(8,128)(2,1)S(1)}, u32[]{:S(2)}, u32[]{:S(2)}) collective-permute-start(bf16[33,64,128]{2,1,0:T(8,128)(2,1)S(1)} %get-tuple-element.24), channel_id=1, source_target_pairs={{0,4},{4,0},{8,12},{12,8},{1,5},{5,1},{9,13},{13,9},{2,6},{6,2},{1... | collective-permute-start | bytes 1622024 | tf_op jit(solution)/shard_map/ppermute | solution.py:242
  8.1 12.9 %collective-permute-start.1 = (bf16[33,64,128]{2,1,0:T(8,128)(2,1)S(1)}, bf16[33,64,128]{2,1,0:T(8,128)(2,1)S(1)}, u32[]{:S(2)}, u32[]{:S(2)}) collective-permute-start(bf16[33,64,128]{2,1,0:T(8,128)(2,1)S(1)} %get-tuple-element.24), channel_id=1, source_target_pairs={{4,8},{8,4},{5,9},{9,5},{6,10},{10,6},{7,11},{11,7},{20,24},{24,20... | collective-permute-start | bytes 1622024 | tf_op jit(solution)/shard_map/ppermute | solution.py:242
  20.2 13.4 %collective-permute-start.6 = (bf16[34,64,128]{2,1,0:T(8,128)(2,1)S(1)}, bf16[34,64,128]{2,1,0:T(8,128)(2,1)S(1)}, u32[]{:S(2)}, u32[]{:S(2)}) collective-permute-start(bf16[34,64,128]{2,1,0:T(8,128)(2,1)S(1)} %collective-permute-done.3.refs_0_.refs_1_), channel_id=1, source_target_pairs={{4,8},{8,4},{5,9},{9,5},{6,10},{10,6},{7,11},{11,7},{20,24},{24,20... | collective-permute-start | bytes 1671176 | tf_op jit(solution)/shard_map/ppermute | solution.py:242
  21.0 15.6 %collective-permute-start.7 = (bf16[34,64,128]{2,1,0:T(8,128)(2,1)S(1)}, bf16[34,64,128]{2,1,0:T(8,128)(2,1)S(1)}, u32[]{:S(2)}, u32[]{:S(2)}) collective-permute-start(bf16[34,64,128]{2,1,0:T(8,128)(2,1)S(1)} %collective-permute-done.3.refs_0_.refs_1_), channel_id=1, source_target_pairs={{0,4},{4,0},{8,12},{12,8},{1,5},{5,1},{9,13},{13,9},{2,6},{6,2},{1... | collective-permute-start | bytes 1671176 | tf_op jit(solution)/shard_map/ppermute | solution.py:242
  25.4 0.8 %copy-start = (s32[1,64,128]{2,1,0:T(8,128)S(1)}, s32[1,64,128]{2,1,0:T(8,128)}, u32[]{:S(2)}) copy-start(s32[1,64,128]{2,1,0:T(8,128)} %zone_ref.1) | copy-start | bytes 98308
  26.1 0.7 %copy-start.1 = (f32[16]{0:T(128)S(1)}, f32[16]{0:T(128)}, u32[]{:S(2)}) copy-start(f32[16]{0:T(128)} %cond_ref.1) | copy-start | bytes 196
  26.8 0.7 %copy-start.2 = (f32[16]{0:T(128)S(1)}, f32[16]{0:T(128)}, u32[]{:S(2)}) copy-start(f32[16]{0:T(128)} %heat_ref.1) | copy-start | bytes 196
  29.4 2.0 %collective-permute-start.4 = (bf16[32,64,128]{2,1,0:T(8,128)(2,1)S(1)}, bf16[32,64,128]{2,1,0:T(8,128)(2,1)S(1)}, u32[]{:S(2)}, u32[]{:S(2)}) collective-permute-start(bf16[32,64,128]{2,1,0:T(8,128)(2,1)S(1)} %slice.6), channel_id=1, source_target_pairs={{0,1},{1,0},{2,3},{3,2},{4,5},{5,4},{6,7},{7,6},{8,9},{9,8},{10,11... | collective-permute-start | bytes 1572872 | tf_op jit(solution)/shard_map/ppermute | solution.py:238
  29.6 2.6 %collective-permute-start.5 = (bf16[32,64,128]{2,1,0:T(8,128)(2,1)S(1)}, bf16[32,64,128]{2,1,0:T(8,128)(2,1)S(1)}, u32[]{:S(2)}, u32[]{:S(2)}) collective-permute-start(bf16[32,64,128]{2,1,0:T(8,128)(2,1)S(1)} %slice.7), channel_id=1, source_target_pairs={{0,1},{1,0},{2,3},{3,2},{4,5},{5,4},{6,7},{7,6},{8,9},{9,8},{10,11... | collective-permute-start | bytes 1572872 | tf_op jit(solution)/shard_map/ppermute | solution.py:238
  30.1 21.2 %collective-permute-start.2 = (bf16[16,64,128]{2,1,0:T(8,128)(2,1)S(1)}, bf16[16,64,128]{2,1,0:T(8,128)(2,1)S(1)}, u32[]{:S(2)}, u32[]{:S(2)}) collective-permute-start(bf16[16,64,128]{2,1,0:T(8,128)(2,1)S(1)} %get-tuple-element.26), channel_id=1, source_target_pairs={{0,1},{1,0},{2,3},{3,2},{4,5},{5,4},{6,7},{7,6},{8,9},{9,8},{10,11... | collective-permute-start | bytes 786440 | tf_op jit(solution)/shard_map/ppermute | solution.py:238
  37.9 13.4 %collective-permute-start.8 = (bf16[16,64,128]{2,1,0:T(8,128)(2,1)S(1)}, bf16[16,64,128]{2,1,0:T(8,128)(2,1)S(1)}, u32[]{:S(2)}, u32[]{:S(2)}) collective-permute-start(bf16[16,64,128]{2,1,0:T(8,128)(2,1)S(1)} %get-tuple-element.38), channel_id=1, source_target_pairs={{0,1},{1,0},{2,3},{3,2},{4,5},{5,4},{6,7},{7,6},{8,9},{9,8},{10,11... | collective-permute-start | bytes 786440 | tf_op jit(solution)/shard_map/ppermute | solution.py:238

commit v5 on v4

--- a/solution.py
+++ b/solution.py
@@ -196,21 +196,37 @@
         gram[:, (k + 1) * columns:(k + 2) * columns] = weight * gram_of(left, flat)
 
 
-def finish_kernel(blocks, *refs):
-    images, (applied, wide) = refs[:blocks], refs[blocks:]
-    rows, columns, nz = images[0].shape
+def turn_out(image, start, applied, wide, turned, sem):
+    rows, columns, _ = image.shape
+    for y in range(rows):
+        wide[pl.ds(y, columns, stride=rows), :] = image[y].astype(F32)
+    for c in range(columns):
+        turned[c, 0] = wide[c * rows:(c + 1) * rows, :].astype(BF16)
+    copy = pltpu.make_async_copy(turned, applied.at[pl.ds(start, columns)], sem)
+    copy.start()
+    return copy
+
+
+def first_kernel(mine, theirs, applied, wide, turned, sems):
     me = lax.axis_index("blk")
-    for s, image in enumerate(images):
-        for y in range(rows):
-            wide[pl.ds(y, columns, stride=rows), :] = image[y].astype(F32)
-        start = (me ^ s) * columns
-        for c in range(columns):
-            applied[start + c, 0] = wide[c * rows:(c + 1) * rows, :].astype(BF16)
-
-
-def sum_kernel(slabs, blocks, shares, out):
+    columns = mine.shape[1]
+    copies = [
+        turn_out(image, (me ^ s) * columns, applied, wide.at[s], turned.at[s], sems.at[s])
+        for s, image in enumerate((mine, theirs))
+    ]
+    for copy in copies:
+        copy.wait()
+
+
+def last_kernel(slabs, blocks, shares, _, *refs):
+    images, (applied, reduced, wide, turned, sems) = refs[:blocks - CORES], refs[blocks - CORES:]
+    me = lax.axis_index("blk")
+    columns = images[0].shape[1]
+    copies = [
+        turn_out(image, (me ^ (s + CORES)) * columns, applied, wide.at[s], turned.at[s], sems.at[s])
+        for s, image in enumerate(images)
+    ]
     chips = blocks // CORES
-    columns = shares.shape[2] // chips
     for core in range(CORES):
         sums = []
         for chip in range(chips):
@@ -221,7 +237,9 @@
         for target in range(chips):
             parts = [sums[chip][:, (chip ^ target) * columns:((chip ^ target) + 1) * columns] for chip in range(chips)]
             start = (CORES * target + core) * columns
-            out[:, start:start + columns] = functools.reduce(jnp.add, parts)
+            reduced[:, start:start + columns] = functools.reduce(jnp.add, parts)
+    for copy in copies:
+        copy.wait()
 
 
 def per_device(basis, zone, cond_table, heat_table):
@@ -276,6 +294,15 @@
         compiler_params=params,
         cost_estimate=pl.CostEstimate(flops=1, bytes_accessed=1, transcendentals=0),
     )(coef, near_partial, center, one, two)
+    whole = jax.ShapeDtypeStruct((total, 1, half, nz), BF16)
+
+    def turning(n):
+        return [
+            pltpu.VMEM((n, columns * half, nz), F32),
+            pltpu.VMEM((n, columns, 1, half, nz), BF16),
+            pltpu.SemaphoreType.DMA((n,)),
+        ]
+
     late = lax.optimization_barrier((center, others, faces))
     theirs = [swap(array[1:-1], 1) for array in (late[0], *late[1])]
     *far_partials, left, near_gram = pl.pallas_call(
@@ -290,6 +317,17 @@
         cost_estimate=pl.CostEstimate(flops=1, bytes_accessed=1, transcendentals=0),
     )(coef, near_flat, center, *others, *theirs)
 
+    applied = pl.pallas_call(
+        first_kernel,
+        out_shape=whole,
+        in_specs=[VMEM] * 2,
+        out_specs=pl.BlockSpec(memory_space=pl.ANY),
+        scratch_shapes=turning(CORES),
+        compiler_params=params,
+        cost_estimate=pl.CostEstimate(flops=1, bytes_accessed=1, transcendentals=0),
+    )(near_mine, swap(near_theirs, 1))
+    faces, applied = lax.optimization_barrier((faces, applied))
+
     *images, gram = pl.pallas_call(
         functools.partial(far_kernel, chips, weight),
         out_shape=[image] * (2 * count) + [jax.ShapeDtypeStruct((total, chips * columns), F32)],
@@ -299,30 +337,21 @@
         compiler_params=params,
     )(faces, left, near_gram, *far_partials, *others, *(two for _, two in far), *(one for one, _ in far))
 
-    near_theirs = swap(near_theirs, 1)
-    far_theirs = [swap(array, 1) for array in images[count:]]
-    pieces = [near_mine, near_theirs]
+    pieces = []
     for k in range(count):
-        pieces += [images[k], far_theirs[k]]
-    applied = pl.pallas_call(
-        functools.partial(finish_kernel, blocks),
-        out_shape=jax.ShapeDtypeStruct((total, 1, half, nz), BF16),
-        in_specs=[VMEM] * blocks,
-        out_specs=VMEM,
-        scratch_shapes=[pltpu.VMEM((columns * half, nz), F32)],
-        compiler_params=params,
-    )(*pieces)
-
+        pieces += [images[k], swap(images[count + k], 1)]
     parts = slabs * blocks
     shares = gram.reshape(parts, total // parts, chips * columns)
     shares = lax.all_to_all(shares, ("dom", "blk"), split_axis=0, concat_axis=0, tiled=True)
-    reduced = pl.pallas_call(
-        functools.partial(sum_kernel, slabs, blocks),
-        out_shape=jax.ShapeDtypeStruct((total // parts, total), F32),
-        in_specs=[VMEM],
-        out_specs=VMEM,
-    )(shares)
-    return applied, reduced
+    return tuple(pl.pallas_call(
+        functools.partial(last_kernel, slabs, blocks),
+        out_shape=(whole, jax.ShapeDtypeStruct((total // parts, total), F32)),
+        in_specs=[VMEM, pl.BlockSpec(memory_space=pl.ANY)] + [VMEM] * len(pieces),
+        out_specs=(pl.BlockSpec(memory_space=pl.ANY), VMEM),
+        scratch_shapes=turning(len(pieces)),
+        input_output_aliases={1: 0},
+        compiler_params=params,
+    )(shares, applied, *pieces))
 
 
 def solution(mesh):

time: 53.6 us -> 51.6 us (0.963)
  waiting for transfers between devices: 16.4 us -> 15.1 us
  Pallas kernels: 11.3 us -> 10.7 us
    ppermute x4, waiting for transfers between devices: 14.4 us -> 12.7 us  [exchange(): lax.ppermute(array, 'dom', [(d, to) for d, to in enumerate(partner) if 0...]
    pallas_call x2, Pallas kernels: 3.7 us -> 3.15 us  [the longest x1 1.87 us: per_device(): pl.pallas_call(functools.partial(last_kernel, slabs, blocks), out_shape=(...]
  transfers between devices with their start and end apart: 9 -> 9, of which waited for: 4 -> 3; matrix products, arithmetic and copies ran while one was open for 0% -> 0% of each run, Pallas kernels for 12% -> 9%
where the time goes in v5:
time: 51.6 us; the launch traced here: 51.4 us
  waiting for transfers between devices  15.1 us (29%)
  blocking collectives  11.6 us (22%)
  starting transfers between devices  11.2 us (22%)
  Pallas kernels  10.7 us (21%)
  local copies, waits for them, and re-layouts  2.14 us (4%)
  between operations  0.75 us (1%)
    ppermute x4, waiting for transfers between devices, exchange(): lax.ppermute(array, 'dom', [(d, to) for d, to in enumerate(partner) if 0...  12.7 us
    all_to_all x1, blocking collectives, per_device(): lax.all_to_all(shares, ('dom', 'blk'), split_axis=0, concat_axis=0, tiled...  11.6 us
    ppermute x4, starting transfers between devices, exchange(): lax.ppermute(array, 'dom', [(d, to) for d, to in enumerate(partner) if 0...  7.38 us
    ppermute x5, starting transfers between devices, swap(): return lax.ppermute(array, 'blk', [(i, i ^ s) for i in range(blocks)])  3.78 us
    pallas_call x1, Pallas kernels, prepare(): pl.pallas_call(functools.partial(prepare_kernel, chips), out_shape=shapes...  2.85 us
    ppermute x5, waiting for transfers between devices, swap(): return lax.ppermute(array, 'blk', [(i, i ^ s) for i in range(blocks)])  2.35 us
    unnamed x6, local copies, waits for them, and re-layouts  2.07 us
    pallas_call x1, Pallas kernels, per_device(): pl.pallas_call(functools.partial(last_kernel, slabs, blocks), out_shape=(...  1.87 us
  transfers between devices with their start and end apart: 9, of which 3 were waited for; matrix products, arithmetic and copies ran while one was open for 0% of the time, Pallas kernels for 9%

profile of v5, /device:TPU:0, one launch (start us, length us, event | category | flops | bytes accessed | tf_op | source)
XLA Modules:
  0.0 51.4 jit_solution(3061930889263736285)
XLA Ops:
  0.6 2.8 %shard_map.59 = (bf16[33,64,128]{2,1,0:T(8,128)(2,1)S(1)}, bf16[34,64,128]{2,1,0:T(8,128)(2,1)S(1)}, bf16[34,64,128]{2,1,0:T(8,128)(2,1)S(1)}) custom-call(bf16[64,1,64,128]{3,2,1,0:T(8,128)(2,1)} %basis_hbm.1, s32[1,64,128]{2,1,0:T(8,128)} %zone_ref.1, f32[16]{0:T(128)} %cond_ref.1), custom_call_target="tpu_custom_call" | custom-call | tf_op jit(solution)/shard_map/pallas_call | solution.py:80
  3.5 3.0 %collective-permute-start.3 = (bf16[34,64,128]{2,1,0:T(8,128)(2,1)S(1)}, bf16[34,64,128]{2,1,0:T(8,128)(2,1)S(1)}, u32[]{:S(2)}, u32[]{:S(2)}) collective-permute-start(bf16[34,64,128]{2,1,0:T(8,128)(2,1)S(1)} %get-tuple-element.32), channel_id=1, source_target_pairs={{0,2},{1,3},{2,0},{3,1},{4,6},{5,7},{6,4},{7,5},{8,10},{9,11},{10,... | collective-permute-start | bytes 1671176 | tf_op jit(solution)/shard_map/ppermute | solution.py:256
  6.5 1.6 %collective-permute-start = (bf16[33,64,128]{2,1,0:T(8,128)(2,1)S(1)}, bf16[33,64,128]{2,1,0:T(8,128)(2,1)S(1)}, u32[]{:S(2)}, u32[]{:S(2)}) collective-permute-start(bf16[33,64,128]{2,1,0:T(8,128)(2,1)S(1)} %get-tuple-element.26), channel_id=1, source_target_pairs={{0,4},{4,0},{8,12},{12,8},{1,5},{5,1},{9,13},{13,9},{2,6},{6,2},{1... | collective-permute-start | bytes 1622024 | tf_op jit(solution)/shard_map/ppermute | solution.py:260
  8.1 0.7 %collective-permute-start.1 = (bf16[33,64,128]{2,1,0:T(8,128)(2,1)S(1)}, bf16[33,64,128]{2,1,0:T(8,128)(2,1)S(1)}, u32[]{:S(2)}, u32[]{:S(2)}) collective-permute-start(bf16[33,64,128]{2,1,0:T(8,128)(2,1)S(1)} %get-tuple-element.26), channel_id=1, source_target_pairs={{4,8},{8,4},{5,9},{9,5},{6,10},{10,6},{7,11},{11,7},{20,24},{24,20... | collective-permute-start | bytes 1622024 | tf_op jit(solution)/shard_map/ppermute | solution.py:260
  8.8 11.5 %collective-permute-done.one = bf16[33,64,128]{2,1,0:T(8,128)(2,1)S(1)} collective-permute-done((bf16[33,64,128]{2,1,0:T(8,128)(2,1)S(1)}, bf16[33,64,128]{2,1,0:T(8,128)(2,1)S(1)}, u32[]{:S(2)}, u32[]{:S(2)}) %collective-permute-start) | collective-permute-done | bytes 540704 | tf_op jit(solution)/shard_map/ppermute | solution.py:260
  20.2 0.0 collective-permute-done.3.refs_0_.refs_1_
  20.2 0.7 %collective-permute-start.6 = (bf16[34,64,128]{2,1,0:T(8,128)(2,1)S(1)}, bf16[34,64,128]{2,1,0:T(8,128)(2,1)S(1)}, u32[]{:S(2)}, u32[]{:S(2)}) collective-permute-start(bf16[34,64,128]{2,1,0:T(8,128)(2,1)S(1)} %collective-permute-done.3.refs_0_.refs_1_), channel_id=1, source_target_pairs={{4,8},{8,4},{5,9},{9,5},{6,10},{10,6},{7,11},{11,7},{20,24},{24,20... | collective-permute-start | bytes 1671176 | tf_op jit(solution)/shard_map/ppermute | solution.py:260
  20.9 0.0 collective-permute-done.1.two
  20.9 4.4 %collective-permute-start.7 = (bf16[34,64,128]{2,1,0:T(8,128)(2,1)S(1)}, bf16[34,64,128]{2,1,0:T(8,128)(2,1)S(1)}, u32[]{:S(2)}, u32[]{:S(2)}) collective-permute-start(bf16[34,64,128]{2,1,0:T(8,128)(2,1)S(1)} %collective-permute-done.3.refs_0_.refs_1_), channel_id=1, source_target_pairs={{0,4},{4,0},{8,12},{12,8},{1,5},{5,1},{9,13},{13,9},{2,6},{6,2},{1... | collective-permute-start | bytes 1671176 | tf_op jit(solution)/shard_map/ppermute | solution.py:260
  25.4 0.0 copy-start
  25.4 0.8 %copy-done = s32[1,64,128]{2,1,0:T(8,128)S(1)} copy-done((s32[1,64,128]{2,1,0:T(8,128)S(1)}, s32[1,64,128]{2,1,0:T(8,128)}, u32[]{:S(2)}) %copy-start) | copy-done | bytes 32792
  26.1 0.0 copy-start.1
  26.1 0.7 %copy-done.1 = f32[16]{0:T(128)S(1)} copy-done((f32[16]{0:T(128)S(1)}, f32[16]{0:T(128)}, u32[]{:S(2)}) %copy-start.1) | copy-done | bytes 88
  26.8 0.0 copy-start.2
  26.8 0.7 %copy-done.2 = f32[16]{0:T(128)S(1)} copy-done((f32[16]{0:T(128)S(1)}, f32[16]{0:T(128)}, u32[]{:S(2)}) %copy-start.2) | copy-done | bytes 88
  27.4 1.3 %shard_map.60 = (f32[6,32,128]{2,1,0:T(8,128)S(1)}, f32[32,64,128]{2,1,0:T(8,128)S(1)}) custom-call(s32[1,64,128]{2,1,0:T(8,128)S(1)} %copy-done, f32[16]{0:T(128)S(1)} %copy-done.1, f32[16]{0:T(128)S(1)} %copy-done.2, bf16[34,64,128]{2,1,0:T(8,128)(2,1)S(1)} %get-tuple-element.33.center), custom_call_target="tpu_custom_call" | custom-call | flops 1073741824 | bytes 134217728 | tf_op jit(solution)/shard_map/pallas_call | solution.py:271
  28.8 0.6 %shard_map.61 = (bf16[16,64,128]{2,1,0:T(8,128)(2,1)S(1)}, bf16[16,64,128]{2,1,0:T(8,128)(2,1)S(1)}, f32[2,32,128]{2,1,0:T(8,128)S(1)}, bf16[64,4096]{1,0:T(8,128)(2,1)S(1)}) custom-call(f32[6,32,128]{2,1,0:T(8,128)S(1)} %get-tuple-element.24.coef, f32[32,64,128]{2,1,0:T(8,128)S(1)} %get-tuple-element.25.partial, ...), custom_call_target="tpu_custom_call" | custom-call | flops 1 | bytes 1 | tf_op jit(solution)/shard_map/pallas_call | solution.py:284
  29.4 0.1 collective-permute-start.4
  29.5 0.6 %collective-permute-start.5 = (bf16[32,64,128]{2,1,0:T(8,128)(2,1)S(1)}, bf16[32,64,128]{2,1,0:T(8,128)(2,1)S(1)}, u32[]{:S(2)}, u32[]{:S(2)}) collective-permute-start(bf16[32,64,128]{2,1,0:T(8,128)(2,1)S(1)} %slice.7), channel_id=1, source_target_pairs={{0,1},{1,0},{2,3},{3,2},{4,5},{5,4},{6,7},{7,6},{8,9},{9,8},{10,11... | collective-permute-start | bytes 1572872 | tf_op jit(solution)/shard_map/ppermute | solution.py:256
  30.1 0.1 collective-permute-start.2
  30.2 2.3 %collective-permute-done.2.theirs = bf16[16,64,128]{2,1,0:T(8,128)(2,1)S(1)} collective-permute-done((bf16[16,64,128]{2,1,0:T(8,128)(2,1)S(1)}, bf16[16,64,128]{2,1,0:T(8,128)(2,1)S(1)}, u32[]{:S(2)}, u32[]{:S(2)}) %collective-permute-start.2) | collective-permute-done | bytes 262176 | tf_op jit(solution)/shard_map/ppermute | solution.py:256
  32.5 1.3 %shard_map.62._ = bf16[256,1,16,128]{3,2,1,0:T(8,128)(2,1)} custom-call(bf16[16,64,128]{2,1,0:T(8,128)(2,1)S(1)} %get-tuple-element.28.mine, bf16[16,64,128]{2,1,0:T(8,128)(2,1)S(1)} %collective-permute-done.2.theirs), custom_call_target="tpu_custom_call" | custom-call | flops 1 | bytes 1 | tf_op jit(solution)/shard_map/pallas_call | solution.py:320
  33.8 0.0 collective-permute-done.4.refs_1_
  33.8 0.0 collective-permute-done.5.refs_2_
  33.8 1.4 %shard_map.63 = (f32[32,64,128]{2,1,0:T(8,128)S(1)}, bf16[256,4096]{1,0:T(8,128)(2,1)S(1)}, f32[256,64]{1,0:T(8,128)S(1)}) custom-call(f32[6,32,128]{2,1,0:T(8,128)S(1)} %get-tuple-element.24.coef, bf16[64,4096]{1,0:T(8,128)(2,1)S(1)} %get-tuple-element.31.flat, bf16[34,64,128]{2,1,0:T(8,128)(2,1)S(1)} %get-tuple-element.33.center, ...), custom_call_target="tpu_custom_call" | custom-call | flops 1 | bytes 1 | tf_op jit(solution)/shard_map/pallas_call | solution.py:308
  35.3 0.0 collective-permute-done.6.refs_2_
  35.3 1.2 %collective-permute-done.7.refs_3_ = bf16[34,64,128]{2,1,0:T(8,128)(2,1)S(1)} collective-permute-done((bf16[34,64,128]{2,1,0:T(8,128)(2,1)S(1)}, bf16[34,64,128]{2,1,0:T(8,128)(2,1)S(1)}, u32[]{:S(2)}, u32[]{:S(2)}) %collective-permute-start.7) | collective-permute-done | bytes 557088 | tf_op jit(solution)/shard_map/ppermute | solution.py:260
  36.5 1.3 %shard_map.64 = (bf16[16,64,128]{2,1,0:T(8,128)(2,1)S(1)}, bf16[16,64,128]{2,1,0:T(8,128)(2,1)S(1)}, f32[256,128]{1,0:T(8,128)S(1)}) custom-call(f32[2,32,128]{2,1,0:T(8,128)S(1)} %get-tuple-element.30.faces, bf16[256,4096]{1,0:T(8,128)(2,1)S(1)} %get-tuple-element.35.left, f32[256,64]{1,0:T(8,128)S(1)} %get-tuple-element.36.near_gram, ...), custom_call_target="tpu_custom_call" | custom-call | tf_op jit(solution)/shard_map/pallas_call | solution.py:331
  37.8 0.1 collective-permute-start.8
  37.9 11.6 %all_to_all.5.shares = f32[16,16,128]{2,1,0:T(8,128)S(1)} all-to-all(f32[16,16,128]{2,1,0:T(8,128)S(1)} %bitcast.1), channel_id=1, replica_groups=mesh['roll'=2,'dom'=4,'blk'=4] {'dom','blk'}, dimensions={0} | all-to-all | bytes 262144 | tf_op jit(solution)/shard_map/all_to_all | solution.py:345
  49.5 0.0 collective-permute-done.8.refs_1_
  49.5 1.9 %shard_map.65 = (bf16[256,1,16,128]{3,2,1,0:T(8,128)(2,1)}, f32[16,256]{1,0:T(8,128)}) custom-call(f32[16,16,128]{2,1,0:T(8,128)S(1)} %all_to_all.5.shares, bf16[256,1,16,128]{3,2,1,0:T(8,128)(2,1)} %shard_map.62._, bf16[16,64,128]{2,1,0:T(8,128)(2,1)S(1)} %get-tuple-element.42.refs_0_, ...), custom_call_target="tpu_custom_call", output_to_operand_aliasing={{0}: (1, {})} | custom-call | tf_op jit(solution)/shard_map/pallas_call | solution.py:346
  (2 shorter events, 0.1 us)
Async XLA Ops:
  3.5 16.7 %collective-permute-start.3 = (bf16[34,64,128]{2,1,0:T(8,128)(2,1)S(1)}, bf16[34,64,128]{2,1,0:T(8,128)(2,1)S(1)}, u32[]{:S(2)}, u32[]{:S(2)}) collective-permute-start(bf16[34,64,128]{2,1,0:T(8,128)(2,1)S(1)} %get-tuple-element.32), channel_id=1, source_target_pairs={{0,2},{1,3},{2,0},{3,1},{4,6},{5,7},{6,4},{7,5},{8,10},{9,11},{10,... | collective-permute-start | bytes 1671176 | tf_op jit(solution)/shard_map/ppermute | solution.py:256
  6.5 13.7 %collective-permute-start = (bf16[33,64,128]{2,1,0:T(8,128)(2,1)S(1)}, bf16[33,64,128]{2,1,0:T(8,128)(2,1)S(1)}, u32[]{:S(2)}, u32[]{:S(2)}) collective-permute-start(bf16[33,64,128]{2,1,0:T(8,128)(2,1)S(1)} %get-tuple-element.26), channel_id=1, source_target_pairs={{0,4},{4,0},{8,12},{12,8},{1,5},{5,1},{9,13},{13,9},{2,6},{6,2},{1... | collective-permute-start | bytes 1622024 | tf_op jit(solution)/shard_map/ppermute | solution.py:260
  8.1 12.9 %collective-permute-start.1 = (bf16[33,64,128]{2,1,0:T(8,128)(2,1)S(1)}, bf16[33,64,128]{2,1,0:T(8,128)(2,1)S(1)}, u32[]{:S(2)}, u32[]{:S(2)}) collective-permute-start(bf16[33,64,128]{2,1,0:T(8,128)(2,1)S(1)} %get-tuple-element.26), channel_id=1, source_target_pairs={{4,8},{8,4},{5,9},{9,5},{6,10},{10,6},{7,11},{11,7},{20,24},{24,20... | collective-permute-start | bytes 1622024 | tf_op jit(solution)/shard_map/ppermute | solution.py:260
  20.2 15.0 %collective-permute-start.6 = (bf16[34,64,128]{2,1,0:T(8,128)(2,1)S(1)}, bf16[34,64,128]{2,1,0:T(8,128)(2,1)S(1)}, u32[]{:S(2)}, u32[]{:S(2)}) collective-permute-start(bf16[34,64,128]{2,1,0:T(8,128)(2,1)S(1)} %collective-permute-done.3.refs_0_.refs_1_), channel_id=1, source_target_pairs={{4,8},{8,4},{5,9},{9,5},{6,10},{10,6},{7,11},{11,7},{20,24},{24,20... | collective-permute-start | bytes 1671176 | tf_op jit(solution)/shard_map/ppermute | solution.py:260
  20.9 15.6 %collective-permute-start.7 = (bf16[34,64,128]{2,1,0:T(8,128)(2,1)S(1)}, bf16[34,64,128]{2,1,0:T(8,128)(2,1)S(1)}, u32[]{:S(2)}, u32[]{:S(2)}) collective-permute-start(bf16[34,64,128]{2,1,0:T(8,128)(2,1)S(1)} %collective-permute-done.3.refs_0_.refs_1_), channel_id=1, source_target_pairs={{0,4},{4,0},{8,12},{12,8},{1,5},{5,1},{9,13},{13,9},{2,6},{6,2},{1... | collective-permute-start | bytes 1671176 | tf_op jit(solution)/shard_map/ppermute | solution.py:260
  25.4 0.8 %copy-start = (s32[1,64,128]{2,1,0:T(8,128)S(1)}, s32[1,64,128]{2,1,0:T(8,128)}, u32[]{:S(2)}) copy-start(s32[1,64,128]{2,1,0:T(8,128)} %zone_ref.1) | copy-start | bytes 98308
  26.1 0.7 %copy-start.1 = (f32[16]{0:T(128)S(1)}, f32[16]{0:T(128)}, u32[]{:S(2)}) copy-start(f32[16]{0:T(128)} %cond_ref.1) | copy-start | bytes 196
  26.8 0.7 %copy-start.2 = (f32[16]{0:T(128)S(1)}, f32[16]{0:T(128)}, u32[]{:S(2)}) copy-start(f32[16]{0:T(128)} %heat_ref.1) | copy-start | bytes 196
  29.4 4.4 %collective-permute-start.4 = (bf16[32,64,128]{2,1,0:T(8,128)(2,1)S(1)}, bf16[32,64,128]{2,1,0:T(8,128)(2,1)S(1)}, u32[]{:S(2)}, u32[]{:S(2)}) collective-permute-start(bf16[32,64,128]{2,1,0:T(8,128)(2,1)S(1)} %slice.6), channel_id=1, source_target_pairs={{0,1},{1,0},{2,3},{3,2},{4,5},{5,4},{6,7},{7,6},{8,9},{9,8},{10,11... | collective-permute-start | bytes 1572872 | tf_op jit(solution)/shard_map/ppermute | solution.py:256
  29.5 4.3 %collective-permute-start.5 = (bf16[32,64,128]{2,1,0:T(8,128)(2,1)S(1)}, bf16[32,64,128]{2,1,0:T(8,128)(2,1)S(1)}, u32[]{:S(2)}, u32[]{:S(2)}) collective-permute-start(bf16[32,64,128]{2,1,0:T(8,128)(2,1)S(1)} %slice.7), channel_id=1, source_target_pairs={{0,1},{1,0},{2,3},{3,2},{4,5},{5,4},{6,7},{7,6},{8,9},{9,8},{10,11... | collective-permute-start | bytes 1572872 | tf_op jit(solution)/shard_map/ppermute | solution.py:256
  30.1 2.4 %collective-permute-start.2 = (bf16[16,64,128]{2,1,0:T(8,128)(2,1)S(1)}, bf16[16,64,128]{2,1,0:T(8,128)(2,1)S(1)}, u32[]{:S(2)}, u32[]{:S(2)}) collective-permute-start(bf16[16,64,128]{2,1,0:T(8,128)(2,1)S(1)} %get-tuple-element.29), channel_id=1, source_target_pairs={{0,1},{1,0},{2,3},{3,2},{4,5},{5,4},{6,7},{7,6},{8,9},{9,8},{10,11... | collective-permute-start | bytes 786440 | tf_op jit(solution)/shard_map/ppermute | solution.py:256
  37.8 11.6 %collective-permute-start.8 = (bf16[16,64,128]{2,1,0:T(8,128)(2,1)S(1)}, bf16[16,64,128]{2,1,0:T(8,128)(2,1)S(1)}, u32[]{:S(2)}, u32[]{:S(2)}) collective-permute-start(bf16[16,64,128]{2,1,0:T(8,128)(2,1)S(1)} %get-tuple-element.43), channel_id=1, source_target_pairs={{0,1},{1,0},{2,3},{3,2},{4,5},{5,4},{6,7},{7,6},{8,9},{9,8},{10,11... | collective-permute-start | bytes 786440 | tf_op jit(solution)/shard_map/ppermute | solution.py:256

commit v6 on v5

v6 whole, which is shorter than its diff:
```python
import functools

import jax
import jax.numpy as jnp
from jax import lax
from jax.experimental import pallas as pl
from jax.experimental.pallas import tpu as pltpu
from jax.sharding import PartitionSpec as P

ZONES = 16
CORES = 2
COST = 1 << 30
F32 = jnp.float32
BF16 = jnp.bfloat16
VMEM = pl.BlockSpec(memory_space=pltpu.VMEM)
SMEM = pl.BlockSpec(memory_space=pltpu.SMEM)
HBM = pl.BlockSpec(memory_space=pltpu.HBM)
ANY = pl.BlockSpec(memory_space=pl.ANY)


def lookup(zone, table_ref):
    result = jnp.zeros(zone.shape, F32)
    for which in range(ZONES):
        result = jnp.where(zone == which, table_ref[which], result)
    return result


def cond_of(zone, table_ref):
    return lookup(zone, table_ref).astype(BF16).astype(F32)


def halves():
    return lax.axis_index("dom") % 2


def prepare_kernel(chips, basis_hbm, zone_hbm, cond_hbm, *refs):
    near, center, plain, firsts, seconds = *refs[:3], refs[3:2 + chips], refs[2 + chips:2 * chips + 1]
    basis, zone, table, wide, turned, cond_pad, in_sems, out_sems = refs[2 * chips + 1:]
    columns, _, ny, nz = basis.shape
    rows = ny // chips
    part = rows // CORES // 2
    me = lax.axis_index("blk")
    chip, core, late = me // CORES, me % CORES, halves()
    step = 16
    chunks = columns // step
    loads = [
        pltpu.make_async_copy(basis_hbm.at[pl.ds(i * step, step)], basis.at[pl.ds(i * step, step)], in_sems.at[i])
        for i in range(chunks)
    ]
    loads.append(pltpu.make_async_copy(zone_hbm, zone, in_sems.at[chunks]))
    loads.append(pltpu.make_async_copy(cond_hbm, table, in_sems.at[chunks + 1]))
    for load in loads:
        load.start()
    turned[0] = jnp.zeros((columns, nz), BF16)
    turned[ny + 1] = jnp.zeros((columns, nz), BF16)
    stores = []

    def store(source, target):
        copy = pltpu.make_async_copy(source, target, out_sems.at[len(stores)])
        copy.start()
        stores.append(copy)

    loads[chunks].wait()
    loads[chunks + 1].wait()
    mine = zone[0, pl.ds(pl.multiple_of(chip * rows, rows), rows), :]
    own = cond_of(mine, table)
    cond_pad[...] = jnp.concatenate([own, jnp.zeros((columns - rows, nz), F32)], 0).astype(BF16)
    store(cond_pad, near.at[rows])
    for i in range(chunks):
        loads[i].wait()
        some = pl.ds(i * step, step)
        for c in range(i * step, (i + 1) * step):
            wide[c * ny:(c + 1) * ny, :] = basis[c, 0].astype(F32)
        for y in range(ny):
            turned[y + 1, some, :] = wide[pl.ds(i * step * ny + y, step, stride=ny), :].astype(BF16)
        store(turned.at[pl.ds(chip * rows + 1, rows), some], near.at[pl.ds(0, rows), some])
        for k in range(1, chips):
            base = (chip ^ k) * rows + 1
            for owner in range(CORES):
                start = base + (2 * owner + 1 - late) * part
                store(turned.at[pl.ds(start, part), some], firsts[k - 1].at[pl.ds(owner * part, part), some])
            for other in range(CORES):
                start = base + (2 * (core ^ other) + late) * part
                store(turned.at[pl.ds(start, part), some], seconds[k - 1].at[pl.ds(other * part, part), some])
        store(turned.at[pl.ds(chip * rows, rows + 2), some], center.at[:, some])
        store(turned.at[pl.ds(chip * rows + 1, rows), some], plain.at[:, some])
    for k in range(1, chips):
        base = (chip ^ k) * rows
        store(turned.at[pl.ds(base, 1)], firsts[k - 1].at[pl.ds(CORES * part, 1)])
        store(turned.at[pl.ds(base + rows + 1, 1)], firsts[k - 1].at[pl.ds(CORES * part + 1, 1)])
    for copy in stores:
        copy.wait()


def prepare(basis, zone, cond_table, chips):
    columns, _, ny, nz = basis.shape
    rows = ny // chips
    slabs = [rows + 1, rows + 2, rows] + [rows // 2 + 2] * (chips - 1) + [rows // 2] * (chips - 1)
    stores = 1 + (3 + 2 * CORES * (chips - 1)) * (columns // 16) + 2 * (chips - 1)
    results = pl.pallas_call(
        functools.partial(prepare_kernel, chips),
        out_shape=[jax.ShapeDtypeStruct((n, columns, nz), BF16) for n in slabs],
        in_specs=[HBM, HBM, HBM],
        out_specs=[ANY] * len(slabs),
        scratch_shapes=[
            pltpu.VMEM(basis.shape, BF16),
            pltpu.VMEM(zone.shape, jnp.int32),
            pltpu.SMEM((ZONES,), F32),
            pltpu.VMEM((columns * ny, nz), F32),
            pltpu.VMEM((ny + 2, columns, nz), BF16),
            pltpu.VMEM((columns, nz), BF16),
            pltpu.SemaphoreType.DMA((columns // 16 + 2,)),
            pltpu.SemaphoreType.DMA((stores,)),
        ],
        compiler_params=pltpu.CompilerParams(vmem_limit_bytes=16 << 20),
    )(*[pltpu.with_memory_space_constraint(x, pltpu.HBM) for x in (basis, zone, cond_table)])
    return (*results[:3], results[3:2 + chips], results[2 + chips:])


def plane_kernel(chips, zone_ref, cond_ref, heat_ref, center, coef, partial, cond_pad):
    rows = partial.shape[0]
    nz = center.shape[2]
    ny = zone_ref.shape[1]
    chip = lax.axis_index("blk") // CORES
    cond_pad[0:8, :] = jnp.zeros((8, nz), F32)
    cond_pad[8:8 + ny, :] = cond_of(zone_ref[0], cond_ref)
    cond_pad[8 + ny:16 + ny, :] = jnp.zeros((8, nz), F32)
    base = pl.multiple_of(chip * rows, 8)
    near = cond_pad[pl.ds(base, rows + 16), :]
    own = near[8:8 + rows]
    lane = lax.broadcasted_iota(jnp.int32, (rows, nz), 1)
    coef[0] = lookup(zone_ref[0, pl.ds(base, rows), :], heat_ref)
    beside = (
        near[7:7 + rows],
        near[9:9 + rows],
        jnp.where(lane == 0, 0.0, pltpu.roll(own, 1, 1)),
        jnp.where(lane == nz - 1, 0.0, pltpu.roll(own, nz - 1, 1)),
    )
    for which, other in enumerate(beside):
        coef[1 + which] = 0.5 * (own + other)
    coef[5] = own
    plane_rows(coef, center, partial)


def plane_rows(coef, center, partial, first=0):
    columns, nz = center.shape[1:]
    lane = lax.broadcasted_iota(jnp.int32, (columns, nz), 1)
    left_end, right_end = lane == 0, lane == nz - 1
    for i in range(partial.shape[0]):
        y = first + i
        face = [spread(coef, k, y, columns) for k in range(5)]
        v = center[y + 1].astype(F32)
        total = face[0] * v
        total += face[1] * (v - center[y].astype(F32))
        total += face[2] * (v - center[y + 2].astype(F32))
        total += face[3] * (v - jnp.where(left_end, 0.0, pltpu.roll(v, 1, 1)))
        total += face[4] * (v - jnp.where(right_end, 0.0, pltpu.roll(v, nz - 1, 1)))
        partial[i] = total


def spread(coef, k, y, columns):
    return jnp.broadcast_to(coef[k, pl.ds(y, 1), :], (columns, coef.shape[2]))


def with_dom(faces, y, v, partial, one, two):
    total = partial + spread(faces, 0, y, v.shape[0]) * (v - one)
    return total + spread(faces, 1, y, v.shape[0]) * (v - two)


def place(y, part, late):
    core, half = y // (2 * part), y // part % 2
    return ((half ^ late) * CORES + core) * part + y % part


def gram_of(left, right):
    return lax.dot_general(left, right, (((1,), (1,)), ((), ())), preferred_element_type=F32)


def near_kernel(coef, partial, center, one, two, mine, theirs, faces, flat):
    rows, columns, nz = partial.shape
    part = rows // CORES // 2
    core, late = lax.axis_index("blk") % CORES, halves()
    face = [0.5 * (coef[5] + ref[rows].astype(F32)[:rows]) for ref in (one, two)]
    which = lax.broadcasted_iota(jnp.int32, (rows, nz), 0) // part % 2
    for k in range(2):
        faces[k] = face[k]
        faces[3 + k] = jnp.where(which == late, face[k], 0.0)
    faces[2] = 0.5 * (face[0] + face[1])
    for y in range(rows):
        v, a, b, p = center[y + 1].astype(F32), one[y].astype(F32), two[y].astype(F32), partial[y]
        image = with_dom(faces, y, v, p, a, b).astype(BF16)
        share = 0.5 * p + spread(faces, 2, y, columns) * v
        share -= spread(faces, 3, y, columns) * a
        share -= spread(faces, 4, y, columns) * b
        flat[:, pl.ds(pl.multiple_of(place(y, part, late) * nz, nz), nz)] = share.astype(BF16)

        @pl.when(core == y // (2 * part))
        def _():
            mine[y % (2 * part)] = image

        @pl.when(core != y // (2 * part))
        def _():
            theirs[y % (2 * part)] = image


def gather(first, outer, second, core, center):
    part = second.shape[0] // CORES
    late = halves()
    for i in range(part):
        for c in range(CORES):
            center[1 + (2 * c + 1 - late) * part + i] = first[c * part + i]
            center[1 + (2 * (core ^ c) + late) * part + i] = second[c * part + i]
    center[0] = outer[0]
    center[2 * CORES * part + 1] = outer[1]


def gather_kernel(chips, coef, *refs):
    count = chips - 1
    firsts, seconds, other_firsts, outers, other_seconds = (refs[i * count:(i + 1) * count] for i in range(5))
    centers, partials, other_centers, other_partials = (refs[i * count:(i + 1) * count] for i in range(5, 9))
    core, late = lax.axis_index("blk") % CORES, halves()
    for k in range(count):
        halo = seconds[k].shape[0]
        gather(firsts[k], firsts[k].at[pl.ds(halo, 2)], seconds[k], core, centers[k])
        gather(other_firsts[k], outers[k], other_seconds[k], 1 - core, other_centers[k])
        plane_rows(coef, centers[k], partials[k])
        plane_rows(coef, other_centers[k], other_partials[k], (2 * core + 1 - late) * (halo // CORES))


def left_kernel(chips, faces, flat, *refs):
    count = chips - 1
    centers, others, partials = refs[:chips], refs[chips:2 * chips], refs[2 * chips:2 * chips + count]
    left, tall, flatter, right = refs[2 * chips + count:]
    rows, columns, nz = partials[0].shape
    part = rows // CORES // 2
    late = halves()
    for y in range(rows):
        where = pl.ds(pl.multiple_of(place(y, part, late) * nz, nz), nz)
        sides = [ref[y + 1] for ref in centers] + [others[0][y]] + [ref[y + 1] for ref in others[1:]]
        for i, side in enumerate(sides):
            left[i * columns:(i + 1) * columns, where] = side
    late_half = pl.ds(rows * nz // 2, rows * nz // 2)
    tall[:, 0:columns] = gram_of(left[...], flat[...])
    flatter[0:columns, :] = gram_of(flat[...], left[...])
    for k in range(count):
        for c in range(CORES):
            for i in range(part):
                y = (2 * c + 1 - late) * part + i
                share = 0.5 * partials[k][y] + spread(faces, 2, y, columns) * centers[k + 1][y + 1].astype(F32)
                right[:, (c * part + i) * nz:(c * part + i + 1) * nz] = share.astype(BF16)
        block = slice((k + 1) * columns, (k + 2) * columns)
        tall[:, block] = gram_of(left[:, late_half], right[...])
        flatter[block, :] = gram_of(right[...], left[:, late_half])


def gram_kernel(chips, weight, faces, left, tall, flatter, *refs):
    count = chips - 1
    partials, centers, ones, twos, mine, theirs = (refs[i * count:(i + 1) * count] for i in range(6))
    gram, right, rest = refs[6 * count:]
    rows, columns, nz = partials[0].shape
    part = rows // CORES // 2
    me = lax.axis_index("blk")
    core, late = me % CORES, halves()
    early_half = pl.ds(0, rows * nz // 2)
    rest[...] = jnp.zeros_like(rest)
    for k in range(count):
        for c in range(CORES):
            for i in range(part):
                y = (2 * c + late) * part + i
                v, p = centers[k][y + 1].astype(F32), partials[k][y]
                a, b = ones[k][c * part + i].astype(F32), twos[k][c * part + i].astype(F32)
                share = 0.5 * p + spread(faces, 2, y, columns) * v
                share -= spread(faces, 0, y, columns) * a
                share -= spread(faces, 1, y, columns) * b
                right[:, (c * part + i) * nz:(c * part + i + 1) * nz] = share.astype(BF16)
                image = with_dom(faces, y, v, p, a, b).astype(BF16)

                @pl.when(core == c)
                def _():
                    mine[k][i] = image

                @pl.when(core != c)
                def _():
                    theirs[k][i] = image
        block = slice((k + 1) * columns, (k + 2) * columns)
        rest[:, block] = gram_of(left[:, early_half], right[...])
        flatter[block, :] += gram_of(right[...], left[:, early_half])
    for i in range(chips * CORES):
        partner = CORES * (i % chips) + i // chips
        where = pl.ds(pl.multiple_of((me ^ partner) * columns, columns), columns)
        block = slice(i * columns, (i + 1) * columns)
        near = weight * (tall[block, :] + rest[block, :])
        far = jnp.zeros((columns, chips * columns), F32)
        share = jnp.concatenate([near, far], 1)
        if i < chips:
            share += weight * flatter[block, :]
        gram[where, :] = share


def turn_out(image, start, applied, wide, turned, sem):
    rows, columns, _ = image.shape
    for y in range(rows):
        wide[pl.ds(y, columns, stride=rows), :] = image[y].astype(F32)
    for c in range(columns):
        turned[c, 0] = wide[c * rows:(c + 1) * rows, :].astype(BF16)
    copy = pltpu.make_async_copy(turned, applied.at[pl.ds(start, columns)], sem)
    copy.start()
    return copy


def first_kernel(mine, theirs, applied, wide, turned, sems):
    me = lax.axis_index("blk")
    columns = mine.shape[1]
    copies = [
        turn_out(image, (me ^ s) * columns, applied, wide.at[s], turned.at[s], sems.at[s])
        for s, image in enumerate((mine, theirs))
    ]
    for copy in copies:
        copy.wait()


def last_kernel(slabs, blocks, shares, _, faces, *refs):
    chips = blocks // CORES
    count = chips - 1
    done, partials, centers = (refs[i * CORES * count:(i + 1) * CORES * count] for i in range(3))
    ones, twos = (refs[i * count:(i + 1) * count] for i in range(3 * CORES, 3 * CORES + 2))
    applied, reduced, wide, turned, sems = refs[(3 * CORES + 2) * count:]
    part, columns, _ = done[0].shape
    half = CORES * part
    me = lax.axis_index("blk")
    core, late = me % CORES, halves()
    first = (2 * core + 1 - late) * part
    copies = []
    for s in range(CORES * count):
        scratch = wide.at[s]
        for i in range(part):
            y = first + i
            p = partials[s][y] if s < count else partials[s][i]
            at = s // count * part + i
            v, a, b = (x.astype(F32) for x in (centers[s][y + 1], ones[s % count][at], twos[s % count][at]))
            image = with_dom(faces, y, v, p, a, b).astype(BF16).astype(F32)
            scratch[pl.ds((1 - late) * part + i, columns, stride=half), :] = image
            scratch[pl.ds(late * part + i, columns, stride=half), :] = done[s][i].astype(F32)
        for c in range(columns):
            turned[s, c, 0] = scratch[c * half:(c + 1) * half, :].astype(BF16)
        partner = CORES * (s % count + 1) + s // count
        copy = pltpu.make_async_copy(turned.at[s], applied.at[pl.ds((me ^ partner) * columns, columns)], sems.at[s])
        copy.start()
        copies.append(copy)
    sums = []
    for sender in range(blocks):
        total = shares[sender]
        for slab in range(1, slabs):
            total += shares[slab * blocks + sender]
        sums.append(total)
    for target in range(blocks):
        parts = []
        for sender in range(blocks):
            partner = sender ^ target
            i = partner % CORES * chips + partner // CORES
            parts.append(sums[sender][:, i * columns:(i + 1) * columns])
        reduced[:, target * columns:(target + 1) * columns] = functools.reduce(jnp.add, parts)
    for copy in copies:
        copy.wait()


def per_device(basis, zone, cond_table, heat_table):
    blocks = lax.axis_size("blk")
    slabs = lax.axis_size("dom")
    chips = blocks // CORES
    count = chips - 1
    columns, planes, ny, nz = basis.shape
    rows = ny // chips
    half = ny // blocks
    part = half // 2
    total = columns * blocks
    weight = 1.0 / (slabs * planes * ny * nz)
    image = jax.ShapeDtypeStruct((half, columns, nz), BF16)
    half_image = jax.ShapeDtypeStruct((part, columns, nz), BF16)
    center_shape = jax.ShapeDtypeStruct((rows + 2, columns, nz), BF16)
    partial = jax.ShapeDtypeStruct((rows, columns, nz), F32)
    whole = jax.ShapeDtypeStruct((total, 1, half, nz), BF16)
    params = pltpu.CompilerParams(vmem_limit_bytes=32 << 20)
    costly = pl.CostEstimate(flops=COST, bytes_accessed=COST // 8, transcendentals=0)
    cheap = pl.CostEstimate(flops=1, bytes_accessed=1, transcendentals=0)

    def call(kernel, out_shape, inputs, scratch=(), specs=None, out_specs=None, cost=cheap, aliases={}):
        return pl.pallas_call(
            kernel,
            out_shape=out_shape,
            in_specs=specs or [VMEM] * len(inputs),
            out_specs=out_specs or [VMEM] * len(out_shape),
            scratch_shapes=scratch,
            input_output_aliases=aliases,
            compiler_params=params,
            cost_estimate=cost,
        )(*inputs)

    def after(value, *others):
        return lax.optimization_barrier((value, *others))[0]

    def swap(array, s):
        return lax.ppermute(array, "blk", [(i, i ^ s) for i in range(blocks)])

    def exchange(array, offset, s=0):
        partner = [((d + offset) ^ 1) - offset for d in range(slabs)]
        pairs = [
            (d * blocks + b, to * blocks + (b ^ s))
            for d, to in enumerate(partner) if 0 <= to < slabs for b in range(blocks)
        ]
        return lax.ppermute(array, ("dom", "blk"), pairs)

    def turning(n):
        return [
            pltpu.VMEM((n, columns * half, nz), F32),
            pltpu.VMEM((n, columns, 1, half, nz), BF16),
            pltpu.SemaphoreType.DMA((n,)),
        ]

    sent, center, plain, firsts, seconds = prepare(basis, zone, cond_table, chips)
    two = exchange(sent, 1)
    one = exchange(sent, 0)
    firsts = [swap(array, CORES * (k + 1)) for k, array in enumerate(firsts)]
    seconds = [swap(array, CORES * (k + 1)) for k, array in enumerate(seconds)]
    plain = swap(plain, 1)
    coef, near_partial = call(
        functools.partial(plane_kernel, chips),
        (jax.ShapeDtypeStruct((6, rows, nz), F32), partial),
        (zone, cond_table, heat_table, after(center, plain)),
        [pltpu.VMEM((ny + 16, nz), F32)],
        [VMEM, SMEM, SMEM, VMEM],
        cost=costly,
    )
    early_two = [exchange(array, 1) for array in firsts]
    early_one = [exchange(array, 0) for array in firsts]
    other_firsts = [swap(array[:half], 1) for array in firsts]
    outers = [swap(array[half:], 1) for array in firsts]
    other_seconds = [swap(array, 1) for array in seconds]
    late = [jnp.concatenate([mine[:part], other[part:]]) for mine, other in zip(seconds, other_seconds)]
    late_two = [exchange(array, 1) for array in late]
    late_one = [exchange(array, 0) for array in late]

    near_mine, near_theirs, faces, near_flat = call(
        near_kernel,
        (
            image,
            image,
            jax.ShapeDtypeStruct((5, rows, nz), F32),
            jax.ShapeDtypeStruct((columns, rows * nz), BF16),
        ),
        (coef, near_partial, center, one, two),
    )
    results = call(
        functools.partial(gather_kernel, chips),
        [center_shape] * count + [partial] * count + [center_shape] * count
        + [jax.ShapeDtypeStruct((part, columns, nz), F32)] * count,
        (after(coef, faces), *firsts, *seconds, *other_firsts, *outers, *other_seconds),
    )
    centers, partials, other_centers, other_partials = (results[i * count:(i + 1) * count] for i in range(4))
    applied, = call(
        first_kernel, (whole,), (near_mine, swap(near_theirs, 1)), turning(CORES), out_specs=[ANY]
    )
    left, tall, flatter = call(
        functools.partial(left_kernel, chips),
        (
            jax.ShapeDtypeStruct((total, rows * nz), BF16),
            jax.ShapeDtypeStruct((total, chips * columns), F32),
            jax.ShapeDtypeStruct((chips * columns, total), F32),
        ),
        (faces, near_flat, center, *centers, plain, *other_centers, *partials),
        [pltpu.VMEM((columns, rows * nz // 2), BF16)],
    )
    *images, gram = call(
        functools.partial(gram_kernel, chips, weight),
        [half_image] * (2 * count) + [jax.ShapeDtypeStruct((total, total), F32)],
        (faces, left, tall, flatter, *partials, *centers, *early_one, *early_two),
        [pltpu.VMEM((columns, rows * nz // 2), BF16), pltpu.VMEM((total, chips * columns), F32)],
    )
    done = [*images[:count], *(swap(array, 1) for array in images[count:])]
    parts = slabs * blocks
    shares = gram.reshape(parts, total // parts, total)
    shares = lax.all_to_all(shares, ("dom", "blk"), split_axis=0, concat_axis=0, tiled=True)
    pieces = (*done, *partials, *other_partials, *centers, *other_centers, *late_one, *late_two)
    return tuple(call(
        functools.partial(last_kernel, slabs, blocks),
        (whole, jax.ShapeDtypeStruct((total // parts, total), F32)),
        (shares, applied, faces, *pieces),
        turning(CORES * count),
        [VMEM, ANY] + [VMEM] * (1 + len(pieces)),
        [ANY, VMEM],
        aliases={1: 0},
    ))


def solution(mesh):
    placed = (P("blk", "dom", "roll", None), P("dom", "roll", None), P(), P())
    return jax.shard_map(
        per_device,
        mesh=mesh,
        in_specs=placed,
        out_specs=(P("roll", "dom", "blk", None), P(("dom", "blk"), "roll")),
        check_vma=False,
    )
```

time: 51.6 us -> 61.9 us (1.20)
  starting transfers between devices: 11.2 us -> 23.7 us
  blocking collectives: 11.6 us -> 0 us
  local copies, waits for them, and re-layouts: 2.14 us -> 6.55 us
  Pallas kernels: 10.7 us -> 13.8 us
  waiting for transfers between devices: 15.1 us -> 16.6 us
    all_to_all x1 -> x0, blocking collectives: 11.6 us -> none  [per_device(): lax.all_to_all(shares, ('dom', 'blk'), split_axis=0, concat_axis=0, tiled...]
    all_to_all x0 -> x1, starting transfers between devices: none -> 9.12 us  [per_device(): lax.all_to_all(shares, ('dom', 'blk'), split_axis=0, concat_axis=0, tiled...]
    ppermute x5 -> x8, waiting for transfers between devices: 2.35 us -> 8.83 us  [swap(): return lax.ppermute(array, 'blk', [(i, i ^ s) for i in range(blocks)])]
    ppermute x4 -> x6, waiting for transfers between devices: 12.7 us -> 7.74 us  [exchange(): return lax.ppermute(array, ('dom', 'blk'), pairs)]
    unnamed x6 -> x18, local copies, waits for them, and re-layouts: 2.07 us -> 6.51 us
    ppermute x4 -> x6, starting transfers between devices: 7.38 us -> 11.3 us  [exchange(): return lax.ppermute(array, ('dom', 'blk'), pairs)]
    pallas_call x7 -> x8, Pallas kernels: 10.7 us -> 13.8 us  [the longest x7 10.6 us: call(): pl.pallas_call(kernel, out_shape=out_shape, in_specs=specs or [VMEM] * le...]
    ppermute x5 -> x8, starting transfers between devices: 3.78 us -> 3.37 us  [swap(): return lax.ppermute(array, 'blk', [(i, i ^ s) for i in range(blocks)])]
  transfers between devices with their start and end apart: 9 -> 15, of which waited for: 3 -> 4; matrix products, arithmetic and copies ran while one was open for 0% -> 0% of each run, Pallas kernels for 9% -> 11%
where the time goes in v6:
time: 61.9 us; the launch traced here: 61.5 us
  starting transfers between devices  23.7 us (38%)
  waiting for transfers between devices  16.6 us (27%)
  Pallas kernels  13.8 us (22%)
  local copies, waits for them, and re-layouts  6.55 us (11%)
  between operations  0.8 us (1%)
    ppermute x6, starting transfers between devices, exchange(): return lax.ppermute(array, ('dom', 'blk'), pairs)  11.3 us
    pallas_call x7, Pallas kernels, call(): pl.pallas_call(kernel, out_shape=out_shape, in_specs=specs or [VMEM] * le...  10.6 us
    all_to_all x1, starting transfers between devices, per_device(): lax.all_to_all(shares, ('dom', 'blk'), split_axis=0, concat_axis=0, tiled...  9.12 us
    ppermute x8, waiting for transfers between devices, swap(): return lax.ppermute(array, 'blk', [(i, i ^ s) for i in range(blocks)])  8.83 us
    ppermute x6, waiting for transfers between devices, exchange(): return lax.ppermute(array, ('dom', 'blk'), pairs)  7.74 us
    unnamed x18, local copies, waits for them, and re-layouts  6.51 us
    ppermute x8, starting transfers between devices, swap(): return lax.ppermute(array, 'blk', [(i, i ^ s) for i in range(blocks)])  3.37 us
    pallas_call x1, Pallas kernels, prepare(): pl.pallas_call(functools.partial(prepare_kernel, chips), out_shape=[jax.S...  3.18 us
  transfers between devices with their start and end apart: 15, of which 4 were waited for; matrix products, arithmetic and copies ran while one was open for 0% of the time, Pallas kernels for 11%

profile of v6, /device:TPU:0, one launch (start us, length us, event | category | flops | bytes accessed | tf_op | source)
XLA Modules:
  0.0 61.5 jit_solution(275165992974939808)
XLA Ops:
  0.6 3.2 %shard_map.59 = (bf16[33,64,128]{2,1,0:T(8,128)(2,1)S(1)}, bf16[34,64,128]{2,1,0:T(8,128)(2,1)S(1)}, bf16[32,64,128]{2,1,0:T(8,128)(2,1)S(1)}, bf16[18,64,128]{2,1,0:T(8,128)(2,1)S(1)}, bf16[16,64,128]{2,1,0:T(8,128)(2,1)S(1)}) custom-call(bf16[64,1,64,128]{3,2,1,0:T(8,128)(2,1)} %basis_hbm.1, s32[1,64,128]{2,1,0:T(8,128)} %zone_ref.1, f32[16]{0:T(128)} %cond_ref.1), custom_call_target="tpu_custom_call" | custom-call | tf_op jit(solution)/shard_map/pallas_call | solution.py:100
  3.8 3.1 %collective-permute-start.1 = (bf16[33,64,128]{2,1,0:T(8,128)(2,1)S(1)}, bf16[33,64,128]{2,1,0:T(8,128)(2,1)S(1)}, u32[]{:S(2)}, u32[]{:S(2)}) collective-permute-start(bf16[33,64,128]{2,1,0:T(8,128)(2,1)S(1)} %get-tuple-element.30), channel_id=1, source_target_pairs={{0,4},{1,5},{2,6},{3,7},{4,0},{5,1},{6,2},{7,3},{8,12},{9,13},{10,... | collective-permute-start | bytes 1622024 | tf_op jit(solution)/shard_map/ppermute | solution.py:411
  6.9 0.0 collective-permute-start
  6.9 0.7 %collective-permute-start.2 = (bf16[33,64,128]{2,1,0:T(8,128)(2,1)S(1)}, bf16[33,64,128]{2,1,0:T(8,128)(2,1)S(1)}, u32[]{:S(2)}, u32[]{:S(2)}) collective-permute-start(bf16[33,64,128]{2,1,0:T(8,128)(2,1)S(1)} %get-tuple-element.30), channel_id=1, source_target_pairs={{4,8},{5,9},{6,10},{7,11},{8,4},{9,5},{10,6},{11,7},{20,24},{21,25... | collective-permute-start | bytes 1622024 | tf_op jit(solution)/shard_map/ppermute | solution.py:411
  7.6 1.6 %collective-permute-start.3 = (bf16[18,64,128]{2,1,0:T(8,128)(2,1)S(1)}, bf16[18,64,128]{2,1,0:T(8,128)(2,1)S(1)}, u32[]{:S(2)}, u32[]{:S(2)}) collective-permute-start(bf16[18,64,128]{2,1,0:T(8,128)(2,1)S(1)} %get-tuple-element.34), channel_id=1, source_target_pairs={{0,2},{1,3},{2,0},{3,1},{4,6},{5,7},{6,4},{7,5},{8,10},{9,11},{10,... | collective-permute-start | bytes 884744 | tf_op jit(solution)/shard_map/ppermute | solution.py:403
  9.2 0.5 collective-permute-start.4
  9.7 7.8 %collective-permute-done.3.refs_0_ = bf16[18,64,128]{2,1,0:T(8,128)(2,1)S(1)} collective-permute-done((bf16[18,64,128]{2,1,0:T(8,128)(2,1)S(1)}, bf16[18,64,128]{2,1,0:T(8,128)(2,1)S(1)}, u32[]{:S(2)}, u32[]{:S(2)}) %collective-permute-start.3) | collective-permute-done | bytes 294944 | tf_op jit(solution)/shard_map/ppermute | solution.py:403
  17.5 4.4 %collective-permute-start.8 = (bf16[18,64,128]{2,1,0:T(8,128)(2,1)S(1)}, bf16[18,64,128]{2,1,0:T(8,128)(2,1)S(1)}, u32[]{:S(2)}, u32[]{:S(2)}) collective-permute-start(bf16[18,64,128]{2,1,0:T(8,128)(2,1)S(1)} %collective-permute-done.3.refs_0_), channel_id=1, source_target_pairs={{0,4},{1,5},{2,6},{3,7},{4,0},{5,1},{6,2},{7,3},{8,12},{9,13},{10,... | collective-permute-start | bytes 884744 | tf_op jit(solution)/shard_map/ppermute | solution.py:411
  21.9 0.8 %collective-permute-done.4.refs_1_ = bf16[16,64,128]{2,1,0:T(8,128)(2,1)S(1)} collective-permute-done((bf16[16,64,128]{2,1,0:T(8,128)(2,1)S(1)}, bf16[16,64,128]{2,1,0:T(8,128)(2,1)S(1)}, u32[]{:S(2)}, u32[]{:S(2)}) %collective-permute-start.4) | collective-permute-done | bytes 262176 | tf_op jit(solution)/shard_map/ppermute | solution.py:403
  22.7 0.7 %collective-permute-start.9 = (bf16[18,64,128]{2,1,0:T(8,128)(2,1)S(1)}, bf16[18,64,128]{2,1,0:T(8,128)(2,1)S(1)}, u32[]{:S(2)}, u32[]{:S(2)}) collective-permute-start(bf16[18,64,128]{2,1,0:T(8,128)(2,1)S(1)} %collective-permute-done.3.refs_0_), channel_id=1, source_target_pairs={{4,8},{5,9},{6,10},{7,11},{8,4},{9,5},{10,6},{11,7},{20,24},{21,25... | collective-permute-start | bytes 884744 | tf_op jit(solution)/shard_map/ppermute | solution.py:411
  23.4 0.0 collective-permute-done.refs_2_
  23.4 0.1 collective-permute-start.7
  23.5 0.0 collective-permute-done.1.one
  23.5 0.5 collective-permute-start.5
  24.0 0.0 collective-permute-done.2.two
  24.0 0.1 collective-permute-start.6
  24.1 0.0 copy-start.4
  24.1 0.8 %copy-done.4 = s32[1,64,128]{2,1,0:T(8,128)S(1)} copy-done((s32[1,64,128]{2,1,0:T(8,128)S(1)}, s32[1,64,128]{2,1,0:T(8,128)}, u32[]{:S(2)}) %copy-start.4) | copy-done | bytes 32792
  24.9 0.0 copy-start.5
  24.9 0.7 %copy-done.5 = f32[16]{0:T(128)S(1)} copy-done((f32[16]{0:T(128)S(1)}, f32[16]{0:T(128)}, u32[]{:S(2)}) %copy-start.5) | copy-done | bytes 88
  25.5 0.0 copy-start.8
  25.5 0.7 %copy-done.8 = f32[16]{0:T(128)S(1)} copy-done((f32[16]{0:T(128)S(1)}, f32[16]{0:T(128)}, u32[]{:S(2)}) %copy-start.8) | copy-done | bytes 88
  26.2 1.3 %shard_map.60 = (f32[6,32,128]{2,1,0:T(8,128)S(1)}, f32[32,64,128]{2,1,0:T(8,128)S(1)}) custom-call(s32[1,64,128]{2,1,0:T(8,128)S(1)} %copy-done.4, f32[16]{0:T(128)S(1)} %copy-done.5, f32[16]{0:T(128)S(1)} %copy-done.8, bf16[34,64,128]{2,1,0:T(8,128)(2,1)S(1)} %get-tuple-element.27.center.refs_0_), custom_call_target="tpu_custom_call" | custom-call | flops 1073741824 | bytes 134217728 | tf_op jit(solution)/shard_map/pallas_call | solution.py:388
  27.5 0.8 %shard_map.61 = (bf16[16,64,128]{2,1,0:T(8,128)(2,1)S(1)}, bf16[16,64,128]{2,1,0:T(8,128)(2,1)S(1)}, f32[5,32,128]{2,1,0:T(8,128)S(1)}, bf16[64,4096]{1,0:T(8,128)(2,1)S(1)}) custom-call(f32[6,32,128]{2,1,0:T(8,128)S(1)} %get-tuple-element.33.coef, f32[32,64,128]{2,1,0:T(8,128)S(1)} %get-tuple-element.29.partial, ...), custom_call_target="tpu_custom_call" | custom-call | flops 1 | bytes 1 | tf_op jit(solution)/shard_map/pallas_call | solution.py:388
  28.3 0.0 copy-start.6
  28.4 0.0 collective-permute-done.6.refs_3_
  28.4 0.0 collective-permute-done.7.refs_4_
  28.4 0.7 %copy-done.6 = bf16[16,64,128]{2,1,0:T(8,128)(2,1)} copy-done((bf16[16,64,128]{2,1,0:T(8,128)(2,1)}, bf16[16,64,128]{2,1,0:T(8,128)(2,1)S(1)}, u32[]{:S(2)}) %copy-start.6) | copy-done | bytes 262168
  29.0 0.0 collective-permute-done.5.refs_2_
  29.1 0.9 %shard_map.62 = (bf16[34,64,128]{2,1,0:T(8,128)(2,1)S(1)}, f32[32,64,128]{2,1,0:T(8,128)S(1)}, bf16[34,64,128]{2,1,0:T(8,128)(2,1)S(1)}, f32[8,64,128]{2,1,0:T(8,128)S(1)}) custom-call(f32[6,32,128]{2,1,0:T(8,128)S(1)} %get-tuple-element.33.coef, bf16[18,64,128]{2,1,0:T(8,128)(2,1)S(1)} %collective-permute-done.3.refs_0_, ...), custom_call_target="tpu_custom_call" | custom-call | flops 1 | bytes 1 | tf_op jit(solution)/shard_map/pallas_call | solution.py:388
  30.0 2.4 %shard_map.63 = (bf16[256,4096]{1,0:T(8,128)(2,1)S(1)}, f32[256,128]{1,0:T(8,128)S(1)}, f32[128,256]{1,0:T(8,128)S(1)}) custom-call(f32[5,32,128]{2,1,0:T(8,128)S(1)} %get-tuple-element.31.faces, bf16[64,4096]{1,0:T(8,128)(2,1)S(1)} %get-tuple-element.32.flat, bf16[34,64,128]{2,1,0:T(8,128)(2,1)S(1)} %get-tuple-element.27.center.refs_0_, ...), custom_call_target="tpu_custom_call" | custom-call | flops 1 | bytes 1 | tf_op jit(solution)/shard_map/pallas_call | solution.py:388
  32.4 0.0 collective-permute-done.8.refs_2_
  32.4 0.0 collective-permute-done.9.refs_3_
  32.4 1.9 %shard_map.64 = (bf16[8,64,128]{2,1,0:T(8,128)(2,1)S(1)}, bf16[8,64,128]{2,1,0:T(8,128)(2,1)S(1)}, f32[256,256]{1,0:T(8,128)}) custom-call(f32[5,32,128]{2,1,0:T(8,128)S(1)} %get-tuple-element.31.faces, bf16[256,4096]{1,0:T(8,128)(2,1)S(1)} %get-tuple-element.39.left, f32[256,128]{1,0:T(8,128)S(1)} %get-tuple-element.40.tall, ...), custom_call_target="tpu_custom_call" | custom-call | flops 1 | bytes 1 | tf_op jit(solution)/shard_map/pallas_call | solution.py:388
  34.3 0.0 copy-start
  34.3 0.6 %copy-done = bf16[8,64,128]{2,1,0:T(8,128)(2,1)} copy-done((bf16[8,64,128]{2,1,0:T(8,128)(2,1)}, bf16[8,64,128]{2,1,0:T(8,128)(2,1)S(1)}, u32[]{:S(2)}) %copy-start) | copy-done | bytes 131096
  35.0 0.0 copy-start.7
  35.0 0.7 %copy-done.7 = bf16[8,64,128]{2,1,0:T(8,128)(2,1)} copy-done((bf16[8,64,128]{2,1,0:T(8,128)(2,1)}, bf16[8,64,128]{2,1,0:T(8,128)(2,1)S(1)}, u32[]{:S(2)}) %copy-start.7) | copy-done | bytes 131096
  35.6 9.1 %all-to-all-start = ((f32[16,16,256]{2,1,0:T(8,128)}), f32[16,16,256]{2,1,0:T(8,128)S(1)}, u32[]{:S(2)}, u32[]{:S(2)}) async-start(f32[16,16,256]{2,1,0:T(8,128)} %bitcast), calls=%async_computation | async-start | bytes 524288 | tf_op jit(solution)/shard_map/all_to_all | solution.py:482
  44.8 0.5 collective-permute-start.10
  45.3 1.7 %collective-permute-start.12 = (bf16[16,64,128]{2,1,0:T(8,128)(2,1)S(1)}, bf16[16,64,128]{2,1,0:T(8,128)(2,1)S(1)}, u32[]{:S(2)}, u32[]{:S(2)}) collective-permute-start(bf16[16,64,128]{2,1,0:T(8,128)(2,1)S(1)} %pad_maximum_fusion), channel_id=1, source_target_pairs={{0,4},{1,5},{2,6},{3,7},{4,0},{5,1},{6,2},{7,3},{8,12},{9,13},{10,... | collective-permute-start | bytes 786440 | tf_op jit(solution)/shard_map/ppermute | solution.py:411
  47.0 0.7 %collective-permute-start.13 = (bf16[16,64,128]{2,1,0:T(8,128)(2,1)S(1)}, bf16[16,64,128]{2,1,0:T(8,128)(2,1)S(1)}, u32[]{:S(2)}, u32[]{:S(2)}) collective-permute-start(bf16[16,64,128]{2,1,0:T(8,128)(2,1)S(1)} %pad_maximum_fusion), channel_id=1, source_target_pairs={{4,8},{5,9},{6,10},{7,11},{8,4},{9,5},{10,6},{11,7},{20,24},{21,25... | collective-permute-start | bytes 786440 | tf_op jit(solution)/shard_map/ppermute | solution.py:411
  47.7 0.1 collective-permute-start.11
  47.8 0.0 collective-permute-done.10.theirs
  47.9 1.3 %shard_map.65._ = bf16[256,1,16,128]{3,2,1,0:T(8,128)(2,1)} custom-call(bf16[16,64,128]{2,1,0:T(8,128)(2,1)S(1)} %get-tuple-element.43.mine, bf16[16,64,128]{2,1,0:T(8,128)(2,1)S(1)} %collective-permute-done.10.theirs), custom_call_target="tpu_custom_call" | custom-call | flops 1 | bytes 1 | tf_op jit(solution)/shard_map/pallas_call | solution.py:388
  49.1 0.2 collective-permute-done.11.refs_1_
  49.3 0.0 copy-start.2
  49.3 0.7 %copy-done.2 = bf16[8,64,128]{2,1,0:T(8,128)(2,1)} copy-done((bf16[8,64,128]{2,1,0:T(8,128)(2,1)}, bf16[8,64,128]{2,1,0:T(8,128)(2,1)S(1)}, u32[]{:S(2)}) %copy-start.2) | copy-done | bytes 131096
  50.0 7.7 %collective-permute-done.12.refs_6_ = bf16[16,64,128]{2,1,0:T(8,128)(2,1)S(1)} collective-permute-done((bf16[16,64,128]{2,1,0:T(8,128)(2,1)S(1)}, bf16[16,64,128]{2,1,0:T(8,128)(2,1)S(1)}, u32[]{:S(2)}, u32[]{:S(2)}) %collective-permute-start.12) | collective-permute-done | bytes 262176 | tf_op jit(solution)/shard_map/ppermute | solution.py:411
  57.7 0.0 collective-permute-done.13.refs_7_
  57.7 0.0 all-to-all-done.shares
  57.7 0.0 copy-start.1
  57.7 0.9 %copy-done.1 = bf16[8,64,128]{2,1,0:T(8,128)(2,1)S(1)} copy-done((bf16[8,64,128]{2,1,0:T(8,128)(2,1)S(1)}, bf16[8,64,128]{2,1,0:T(8,128)(2,1)}, u32[]{:S(2)}) %copy-start.1) | copy-done | bytes 131096
  58.6 0.0 copy-start.3
  58.6 0.9 %copy-done.3 = bf16[8,64,128]{2,1,0:T(8,128)(2,1)S(1)} copy-done((bf16[8,64,128]{2,1,0:T(8,128)(2,1)S(1)}, bf16[8,64,128]{2,1,0:T(8,128)(2,1)}, u32[]{:S(2)}) %copy-start.3) | copy-done | bytes 131096
  59.5 1.9 %shard_map.66 = (bf16[256,1,16,128]{3,2,1,0:T(8,128)(2,1)}, f32[16,256]{1,0:T(8,128)}) custom-call(f32[16,16,256]{2,1,0:T(8,128)S(1)} %all-to-all-done.shares, bf16[256,1,16,128]{3,2,1,0:T(8,128)(2,1)} %shard_map.65._, f32[5,32,128]{2,1,0:T(8,128)S(1)} %get-tuple-element.31.faces, ...), custom_call_target="tpu_custom_call", output_to_operand_aliasing={{0}: (1, {})} | custom-call | flops 1 | bytes 1 | tf_op jit(solution)/shard_map/pallas_call | solution.py:388
  (5 shorter events, 0.1 us)
Async XLA Ops:
  3.8 19.7 %collective-permute-start.1 = (bf16[33,64,128]{2,1,0:T(8,128)(2,1)S(1)}, bf16[33,64,128]{2,1,0:T(8,128)(2,1)S(1)}, u32[]{:S(2)}, u32[]{:S(2)}) collective-permute-start(bf16[33,64,128]{2,1,0:T(8,128)(2,1)S(1)} %get-tuple-element.30), channel_id=1, source_target_pairs={{0,4},{1,5},{2,6},{3,7},{4,0},{5,1},{6,2},{7,3},{8,12},{9,13},{10,... | collective-permute-start | bytes 1622024 | tf_op jit(solution)/shard_map/ppermute | solution.py:411
  6.9 16.5 %collective-permute-start = (bf16[32,64,128]{2,1,0:T(8,128)(2,1)S(1)}, bf16[32,64,128]{2,1,0:T(8,128)(2,1)S(1)}, u32[]{:S(2)}, u32[]{:S(2)}) collective-permute-start(bf16[32,64,128]{2,1,0:T(8,128)(2,1)S(1)} %get-tuple-element.26), channel_id=1, source_target_pairs={{0,1},{1,0},{2,3},{3,2},{4,5},{5,4},{6,7},{7,6},{8,9},{9,8},{10,11... | collective-permute-start | bytes 1572872 | tf_op jit(solution)/shard_map/ppermute | solution.py:403
  6.9 17.1 %collective-permute-start.2 = (bf16[33,64,128]{2,1,0:T(8,128)(2,1)S(1)}, bf16[33,64,128]{2,1,0:T(8,128)(2,1)S(1)}, u32[]{:S(2)}, u32[]{:S(2)}) collective-permute-start(bf16[33,64,128]{2,1,0:T(8,128)(2,1)S(1)} %get-tuple-element.30), channel_id=1, source_target_pairs={{4,8},{5,9},{6,10},{7,11},{8,4},{9,5},{10,6},{11,7},{20,24},{21,25... | collective-permute-start | bytes 1622024 | tf_op jit(solution)/shard_map/ppermute | solution.py:411
  7.6 9.9 %collective-permute-start.3 = (bf16[18,64,128]{2,1,0:T(8,128)(2,1)S(1)}, bf16[18,64,128]{2,1,0:T(8,128)(2,1)S(1)}, u32[]{:S(2)}, u32[]{:S(2)}) collective-permute-start(bf16[18,64,128]{2,1,0:T(8,128)(2,1)S(1)} %get-tuple-element.34), channel_id=1, source_target_pairs={{0,2},{1,3},{2,0},{3,1},{4,6},{5,7},{6,4},{7,5},{8,10},{9,11},{10,... | collective-permute-start | bytes 884744 | tf_op jit(solution)/shard_map/ppermute | solution.py:403
  9.2 13.5 %collective-permute-start.4 = (bf16[16,64,128]{2,1,0:T(8,128)(2,1)S(1)}, bf16[16,64,128]{2,1,0:T(8,128)(2,1)S(1)}, u32[]{:S(2)}, u32[]{:S(2)}) collective-permute-start(bf16[16,64,128]{2,1,0:T(8,128)(2,1)S(1)} %get-tuple-element.35), channel_id=1, source_target_pairs={{0,2},{1,3},{2,0},{3,1},{4,6},{5,7},{6,4},{7,5},{8,10},{9,11},{10,... | collective-permute-start | bytes 786440 | tf_op jit(solution)/shard_map/ppermute | solution.py:403
  17.5 14.9 %collective-permute-start.8 = (bf16[18,64,128]{2,1,0:T(8,128)(2,1)S(1)}, bf16[18,64,128]{2,1,0:T(8,128)(2,1)S(1)}, u32[]{:S(2)}, u32[]{:S(2)}) collective-permute-start(bf16[18,64,128]{2,1,0:T(8,128)(2,1)S(1)} %collective-permute-done.3.refs_0_), channel_id=1, source_target_pairs={{0,4},{1,5},{2,6},{3,7},{4,0},{5,1},{6,2},{7,3},{8,12},{9,13},{10,... | collective-permute-start | bytes 884744 | tf_op jit(solution)/shard_map/ppermute | solution.py:411
  22.7 9.7 %collective-permute-start.9 = (bf16[18,64,128]{2,1,0:T(8,128)(2,1)S(1)}, bf16[18,64,128]{2,1,0:T(8,128)(2,1)S(1)}, u32[]{:S(2)}, u32[]{:S(2)}) collective-permute-start(bf16[18,64,128]{2,1,0:T(8,128)(2,1)S(1)} %collective-permute-done.3.refs_0_), channel_id=1, source_target_pairs={{4,8},{5,9},{6,10},{7,11},{8,4},{9,5},{10,6},{11,7},{20,24},{21,25... | collective-permute-start | bytes 884744 | tf_op jit(solution)/shard_map/ppermute | solution.py:411
  23.4 5.0 %collective-permute-start.7 = (bf16[16,64,128]{2,1,0:T(8,128)(2,1)S(1)}, bf16[16,64,128]{2,1,0:T(8,128)(2,1)S(1)}, u32[]{:S(2)}, u32[]{:S(2)}) collective-permute-start(bf16[16,64,128]{2,1,0:T(8,128)(2,1)S(1)} %collective-permute-done.4.refs_1_), channel_id=1, source_target_pairs={{0,1},{1,0},{2,3},{3,2},{4,5},{5,4},{6,7},{7,6},{8,9},{9,8},{10,11... | collective-permute-start | bytes 786440 | tf_op jit(solution)/shard_map/ppermute | solution.py:403
  23.5 5.5 %collective-permute-start.5 = (bf16[16,64,128]{2,1,0:T(8,128)(2,1)S(1)}, bf16[16,64,128]{2,1,0:T(8,128)(2,1)S(1)}, u32[]{:S(2)}, u32[]{:S(2)}) collective-permute-start(bf16[16,64,128]{2,1,0:T(8,128)(2,1)S(1)} %slice.16), channel_id=1, source_target_pairs={{0,1},{1,0},{2,3},{3,2},{4,5},{5,4},{6,7},{7,6},{8,9},{9,8},{10,11... | collective-permute-start | bytes 786440 | tf_op jit(solution)/shard_map/ppermute | solution.py:403
  24.0 4.4 %collective-permute-start.6 = (bf16[2,64,128]{2,1,0:T(8,128)(2,1)S(1)}, bf16[2,64,128]{2,1,0:T(8,128)(2,1)S(1)}, u32[]{:S(2)}, u32[]{:S(2)}) collective-permute-start(bf16[2,64,128]{2,1,0:T(8,128)(2,1)S(1)} %slice.17), channel_id=1, source_target_pairs={{0,1},{1,0},{2,3},{3,2},{4,5},{5,4},{6,7},{7,6},{8,9},{9,8},{10,11... | collective-permute-start | bytes 98312 | tf_op jit(solution)/shard_map/ppermute | solution.py:403
  24.1 0.8 %copy-start.4 = (s32[1,64,128]{2,1,0:T(8,128)S(1)}, s32[1,64,128]{2,1,0:T(8,128)}, u32[]{:S(2)}) copy-start(s32[1,64,128]{2,1,0:T(8,128)} %zone_ref.1) | copy-start | bytes 98308
  24.9 0.7 %copy-start.5 = (f32[16]{0:T(128)S(1)}, f32[16]{0:T(128)}, u32[]{:S(2)}) copy-start(f32[16]{0:T(128)} %cond_ref.1) | copy-start | bytes 196
  25.5 0.7 %copy-start.8 = (f32[16]{0:T(128)S(1)}, f32[16]{0:T(128)}, u32[]{:S(2)}) copy-start(f32[16]{0:T(128)} %heat_ref.1) | copy-start | bytes 196
  28.3 0.7 %copy-start.6 = (bf16[16,64,128]{2,1,0:T(8,128)(2,1)}, bf16[16,64,128]{2,1,0:T(8,128)(2,1)S(1)}, u32[]{:S(2)}) copy-start(bf16[16,64,128]{2,1,0:T(8,128)(2,1)S(1)} %get-tuple-element.44) | copy-start | bytes 786436
  34.3 0.6 %copy-start = (bf16[8,64,128]{2,1,0:T(8,128)(2,1)}, bf16[8,64,128]{2,1,0:T(8,128)(2,1)S(1)}, u32[]{:S(2)}) copy-start(bf16[8,64,128]{2,1,0:T(8,128)(2,1)S(1)} %get-tuple-element.45.refs_0_) | copy-start | bytes 393220
  35.0 0.7 %copy-start.7 = (bf16[8,64,128]{2,1,0:T(8,128)(2,1)}, bf16[8,64,128]{2,1,0:T(8,128)(2,1)S(1)}, u32[]{:S(2)}) copy-start(bf16[8,64,128]{2,1,0:T(8,128)(2,1)S(1)} %get-tuple-element.46) | copy-start | bytes 393220
  35.6 22.1 %all-to-all-start = ((f32[16,16,256]{2,1,0:T(8,128)}), f32[16,16,256]{2,1,0:T(8,128)S(1)}, u32[]{:S(2)}, u32[]{:S(2)}) async-start(f32[16,16,256]{2,1,0:T(8,128)} %bitcast), calls=%async_computation | async-start | bytes 524288 | tf_op jit(solution)/shard_map/all_to_all | solution.py:482
  44.8 3.1 %collective-permute-start.10 = (bf16[16,64,128]{2,1,0:T(8,128)(2,1)}, bf16[16,64,128]{2,1,0:T(8,128)(2,1)S(1)}, u32[]{:S(2)}, u32[]{:S(2)}) collective-permute-start(bf16[16,64,128]{2,1,0:T(8,128)(2,1)} %copy-done.6), channel_id=1, source_target_pairs={{0,1},{1,0},{2,3},{3,2},{4,5},{5,4},{6,7},{7,6},{8,9},{9,8},{10,11... | collective-permute-start | bytes 786440 | tf_op jit(solution)/shard_map/ppermute | solution.py:403
  45.3 12.4 %collective-permute-start.12 = (bf16[16,64,128]{2,1,0:T(8,128)(2,1)S(1)}, bf16[16,64,128]{2,1,0:T(8,128)(2,1)S(1)}, u32[]{:S(2)}, u32[]{:S(2)}) collective-permute-start(bf16[16,64,128]{2,1,0:T(8,128)(2,1)S(1)} %pad_maximum_fusion), channel_id=1, source_target_pairs={{0,4},{1,5},{2,6},{3,7},{4,0},{5,1},{6,2},{7,3},{8,12},{9,13},{10,... | collective-permute-start | bytes 786440 | tf_op jit(solution)/shard_map/ppermute | solution.py:411
  47.0 10.7 %collective-permute-start.13 = (bf16[16,64,128]{2,1,0:T(8,128)(2,1)S(1)}, bf16[16,64,128]{2,1,0:T(8,128)(2,1)S(1)}, u32[]{:S(2)}, u32[]{:S(2)}) collective-permute-start(bf16[16,64,128]{2,1,0:T(8,128)(2,1)S(1)} %pad_maximum_fusion), channel_id=1, source_target_pairs={{4,8},{5,9},{6,10},{7,11},{8,4},{9,5},{10,6},{11,7},{20,24},{21,25... | collective-permute-start | bytes 786440 | tf_op jit(solution)/shard_map/ppermute | solution.py:411
  47.7 1.6 %collective-permute-start.11 = (bf16[8,64,128]{2,1,0:T(8,128)(2,1)}, bf16[8,64,128]{2,1,0:T(8,128)(2,1)S(1)}, u32[]{:S(2)}, u32[]{:S(2)}) collective-permute-start(bf16[8,64,128]{2,1,0:T(8,128)(2,1)} %copy-done.7), channel_id=1, source_target_pairs={{0,1},{1,0},{2,3},{3,2},{4,5},{5,4},{6,7},{7,6},{8,9},{9,8},{10,11... | collective-permute-start | bytes 393224 | tf_op jit(solution)/shard_map/ppermute | solution.py:403
  49.3 0.7 %copy-start.2 = (bf16[8,64,128]{2,1,0:T(8,128)(2,1)}, bf16[8,64,128]{2,1,0:T(8,128)(2,1)S(1)}, u32[]{:S(2)}) copy-start(bf16[8,64,128]{2,1,0:T(8,128)(2,1)S(1)} %collective-permute-done.11.refs_1_) | copy-start | bytes 393220
  57.7 0.9 %copy-start.1 = (bf16[8,64,128]{2,1,0:T(8,128)(2,1)S(1)}, bf16[8,64,128]{2,1,0:T(8,128)(2,1)}, u32[]{:S(2)}) copy-start(bf16[8,64,128]{2,1,0:T(8,128)(2,1)} %copy-done) | copy-start | bytes 393220
  58.6 0.9 %copy-start.3 = (bf16[8,64,128]{2,1,0:T(8,128)(2,1)S(1)}, bf16[8,64,128]{2,1,0:T(8,128)(2,1)}, u32[]{:S(2)}) copy-start(bf16[8,64,128]{2,1,0:T(8,128)(2,1)} %copy-done.2) | copy-start | bytes 393220

commit v7 on v5

v7 whole, which is shorter than its diff:
```python
import functools

import jax
import jax.numpy as jnp
from jax import lax
from jax.experimental import pallas as pl
from jax.experimental.pallas import tpu as pltpu
from jax.sharding import PartitionSpec as P

ZONES = 16
CORES = 2
COST = 1 << 30
F32 = jnp.float32
BF16 = jnp.bfloat16
VMEM = pl.BlockSpec(memory_space=pltpu.VMEM)
SMEM = pl.BlockSpec(memory_space=pltpu.SMEM)
HBM = pl.BlockSpec(memory_space=pltpu.HBM)
ANY = pl.BlockSpec(memory_space=pl.ANY)


def lookup(zone, table_ref):
    result = jnp.zeros(zone.shape, F32)
    for which in range(ZONES):
        result = jnp.where(zone == which, table_ref[which], result)
    return result


def cond_of(zone, table_ref):
    return lookup(zone, table_ref).astype(BF16).astype(F32)


def prepare_kernel(chips, basis_hbm, zone_hbm, cond_hbm, *refs):
    near, center, plain, firsts, seconds = *refs[:3], refs[3:2 + chips], refs[2 + chips:2 * chips + 1]
    basis, zone, table, wide, turned, cond_pad, in_sems, out_sems = refs[2 * chips + 1:]
    columns, _, ny, nz = basis.shape
    rows = ny // chips
    chip = lax.axis_index("blk") // CORES
    step = 16
    chunks = columns // step
    loads = [
        pltpu.make_async_copy(basis_hbm.at[pl.ds(i * step, step)], basis.at[pl.ds(i * step, step)], in_sems.at[i])
        for i in range(chunks)
    ]
    loads.append(pltpu.make_async_copy(zone_hbm, zone, in_sems.at[chunks]))
    loads.append(pltpu.make_async_copy(cond_hbm, table, in_sems.at[chunks + 1]))
    for load in loads:
        load.start()
    turned[0] = jnp.zeros((columns, nz), BF16)
    turned[ny + 1] = jnp.zeros((columns, nz), BF16)
    stores = []

    def store(source, target):
        copy = pltpu.make_async_copy(source, target, out_sems.at[len(stores)])
        copy.start()
        stores.append(copy)

    loads[chunks].wait()
    loads[chunks + 1].wait()
    mine = zone[0, pl.ds(pl.multiple_of(chip * rows, rows), rows), :]
    own = cond_of(mine, table)
    cond_pad[...] = jnp.concatenate([own, jnp.zeros((columns - rows, nz), F32)], 0).astype(BF16)
    store(cond_pad, near.at[rows])
    for i in range(chunks):
        loads[i].wait()
        some = pl.ds(i * step, step)
        for c in range(i * step, (i + 1) * step):
            wide[c * ny:(c + 1) * ny, :] = basis[c, 0].astype(F32)
        for y in range(ny):
            turned[y + 1, some, :] = wide[pl.ds(i * step * ny + y, step, stride=ny), :].astype(BF16)
        store(turned.at[pl.ds(chip * rows + 1, rows), some], near.at[pl.ds(0, rows), some])
        for k in range(1, chips):
            start = (chip ^ k) * rows
            store(turned.at[pl.ds(start, rows // 2 + 1), some], firsts[k - 1].at[:, some])
            store(turned.at[pl.ds(start + rows // 2 + 1, rows // 2 + 1), some], seconds[k - 1].at[:, some])
        store(turned.at[pl.ds(chip * rows, rows + 2), some], center.at[:, some])
        store(turned.at[pl.ds(chip * rows + 1, rows), some], plain.at[:, some])
    for copy in stores:
        copy.wait()


def prepare(basis, zone, cond_table, chips):
    columns, _, ny, nz = basis.shape
    rows = ny // chips
    slabs = [rows + 1, rows + 2, rows] + [rows // 2 + 1] * (2 * chips - 2)
    shapes = [jax.ShapeDtypeStruct((n, columns, nz), BF16) for n in slabs]
    results = pl.pallas_call(
        functools.partial(prepare_kernel, chips),
        out_shape=shapes,
        in_specs=[HBM, HBM, HBM],
        out_specs=[pl.BlockSpec(memory_space=pl.ANY)] * len(shapes),
        scratch_shapes=[
            pltpu.VMEM(basis.shape, BF16),
            pltpu.VMEM(zone.shape, jnp.int32),
            pltpu.SMEM((ZONES,), F32),
            pltpu.VMEM((columns * ny, nz), F32),
            pltpu.VMEM((ny + 2, columns, nz), BF16),
            pltpu.VMEM((columns, nz), BF16),
            pltpu.SemaphoreType.DMA((columns // 16 + 2,)),
            pltpu.SemaphoreType.DMA((1 + (2 * chips + 1) * (columns // 16),)),
        ],
        compiler_params=pltpu.CompilerParams(vmem_limit_bytes=16 << 20),
    )(*[pltpu.with_memory_space_constraint(x, pltpu.HBM) for x in (basis, zone, cond_table)])
    return (*results[:3], results[3:2 + chips], results[2 + chips:])


def plane_kernel(chips, zone_ref, cond_ref, heat_ref, center, coef, partial, cond_pad):
    rows = partial.shape[0]
    nz = center.shape[2]
    ny = zone_ref.shape[1]
    chip = lax.axis_index("blk") // CORES
    cond_pad[0:8, :] = jnp.zeros((8, nz), F32)
    cond_pad[8:8 + ny, :] = cond_of(zone_ref[0], cond_ref)
    cond_pad[8 + ny:16 + ny, :] = jnp.zeros((8, nz), F32)
    base = pl.multiple_of(chip * rows, 8)
    near = cond_pad[pl.ds(base, rows + 16), :]
    own = near[8:8 + rows]
    lane = lax.broadcasted_iota(jnp.int32, (rows, nz), 1)
    coef[0] = lookup(zone_ref[0, pl.ds(base, rows), :], heat_ref)
    beside = (
        near[7:7 + rows],
        near[9:9 + rows],
        jnp.where(lane == 0, 0.0, pltpu.roll(own, 1, 1)),
        jnp.where(lane == nz - 1, 0.0, pltpu.roll(own, nz - 1, 1)),
    )
    for which, other in enumerate(beside):
        coef[1 + which] = 0.5 * (own + other)
    coef[5] = own
    plane_rows(coef, center, partial)


def plane_rows(coef, center, partial):
    columns, nz = center.shape[1:]
    lane = lax.broadcasted_iota(jnp.int32, (columns, nz), 1)
    first, last = lane == 0, lane == nz - 1
    for y in range(partial.shape[0]):
        face = [jnp.broadcast_to(coef[k, y:y + 1, :], (columns, nz)) for k in range(5)]
        v = center[y + 1].astype(F32)
        total = face[0] * v
        total += face[1] * (v - center[y].astype(F32))
        total += face[2] * (v - center[y + 2].astype(F32))
        total += face[3] * (v - jnp.where(first, 0.0, pltpu.roll(v, 1, 1)))
        total += face[4] * (v - jnp.where(last, 0.0, pltpu.roll(v, nz - 1, 1)))
        partial[y] = total


def image_row(faces, y, partial, v, one, two):
    columns, nz = v.shape
    face = [jnp.broadcast_to(faces[k, y:y + 1, :], (columns, nz)) for k in range(2)]
    v = v.astype(F32)
    total = partial + face[0] * (v - one.astype(F32))
    return (total + face[1] * (v - two.astype(F32))).astype(BF16)


def gram_of(left, right):
    return lax.dot_general(left, right, (((1,), (1,)), ((), ())), preferred_element_type=F32)


def near_kernel(coef, partial, center, one, two, mine, theirs, faces, flat):
    rows, _, nz = partial.shape
    half = rows // CORES
    core = lax.axis_index("blk") % CORES
    for which, ref in enumerate((one, two)):
        faces[which] = 0.5 * (coef[5] + ref[rows].astype(F32)[:rows])
    for y in range(rows):
        image = image_row(faces, y, partial[y], center[y + 1], one[y], two[y])
        flat[:, y * nz:(y + 1) * nz] = image

        @pl.when(core == y // half)
        def _():
            mine[y % half] = image

        @pl.when(core != y // half)
        def _():
            theirs[y % half] = image


def gather_kernel(chips, coef, *refs):
    count = chips - 1
    firsts, seconds, centers, partials = (refs[i * count:(i + 1) * count] for i in range(4))
    for first, second, center, partial in zip(firsts, seconds, centers, partials):
        half = first.shape[0]
        center[0:half] = first[...]
        center[half:2 * half] = second[...]
        plane_rows(coef, center, partial)


def first_far_kernel(chips, faces, *refs):
    count = chips - 1
    partials, centers, ones, twos, images, flats = (refs[i * count:(i + 1) * count] for i in range(6))
    nz = partials[0].shape[2]
    for k in range(count):
        for y in range(partials[k].shape[0] // 2):
            image = image_row(faces, y, partials[k][y], centers[k][y + 1], ones[k][y + 1], twos[k][y + 1])
            flats[k][:, y * nz:(y + 1) * nz] = image
            images[k][y] = image


def left_kernel(chips, weight, flat, center, plain, *refs):
    count = chips - 1
    flats, centers, other_firsts, other_seconds = (refs[i * count:(i + 1) * count] for i in range(4))
    left, gram = refs[4 * count:]
    columns, nz = center.shape[1:]
    rows = center.shape[0] - 2
    half = rows // 2
    me = lax.axis_index("blk")
    for k, ref in enumerate((center, *centers)):
        for core in range(CORES):
            where = pl.ds(pl.multiple_of((me ^ (CORES * k + core)) * columns, columns), columns)
            for y in range(rows):
                if not core:
                    side = ref[y + 1]
                elif not k:
                    side = plain[y]
                else:
                    side = other_firsts[k - 1][y] if y < half else other_seconds[k - 1][y - half]
                left[where, y * nz:(y + 1) * nz] = side
    gram[:, 0:columns] = weight * gram_of(left[...], flat[...])
    for k in range(count):
        gram[:, (k + 1) * columns:(k + 2) * columns] = weight * gram_of(left[:, 0:half * nz], flats[k][...])


def second_far_kernel(chips, weight, faces, left, first_gram, *refs):
    count = chips - 1
    partials, centers, ones, twos, images, mine, theirs = (refs[i * count:(i + 1) * count] for i in range(7))
    gram, flat = refs[7 * count:]
    rows, columns, nz = partials[0].shape
    half = rows // 2
    core = lax.axis_index("blk") % CORES
    gram[:, 0:columns] = first_gram[:, 0:columns]
    for k in range(count):
        for i in range(half):
            y = half + i
            image = image_row(faces, y, partials[k][y], centers[k][y + 1], ones[k][i], twos[k][i])
            flat[:, i * nz:(i + 1) * nz] = image
            other = images[k][i]
            mine[k][i] = jnp.where(core == 0, other, image)
            theirs[k][i] = jnp.where(core == 0, image, other)
        block = slice((k + 1) * columns, (k + 2) * columns)
        gram[:, block] = first_gram[:, block] + weight * gram_of(left[:, half * nz:], flat[...])


def turn_out(image, start, applied, wide, turned, sem):
    rows, columns, _ = image.shape
    for y in range(rows):
        wide[pl.ds(y, columns, stride=rows), :] = image[y].astype(F32)
    for c in range(columns):
        turned[c, 0] = wide[c * rows:(c + 1) * rows, :].astype(BF16)
    copy = pltpu.make_async_copy(turned, applied.at[pl.ds(start, columns)], sem)
    copy.start()
    return copy


def first_kernel(mine, theirs, applied, wide, turned, sems):
    me = lax.axis_index("blk")
    columns = mine.shape[1]
    copies = [
        turn_out(image, (me ^ s) * columns, applied, wide.at[s], turned.at[s], sems.at[s])
        for s, image in enumerate((mine, theirs))
    ]
    for copy in copies:
        copy.wait()


def last_kernel(blocks, applied_in, *refs):
    del applied_in
    images, (applied, wide, turned, sems) = refs[:blocks - CORES], refs[blocks - CORES:]
    me = lax.axis_index("blk")
    columns = images[0].shape[1]
    copies = [
        turn_out(image, (me ^ (s + CORES)) * columns, applied, wide.at[s], turned.at[s], sems.at[s])
        for s, image in enumerate(images)
    ]
    for copy in copies:
        copy.wait()


def sum_kernel(slabs, blocks, shares, reduced):
    chips = blocks // CORES
    columns = shares.shape[2] // chips
    for core in range(CORES):
        sums = []
        for chip in range(chips):
            total = shares[CORES * chip + core]
            for slab in range(1, slabs):
                total += shares[slab * blocks + CORES * chip + core]
            sums.append(total)
        for target in range(chips):
            parts = [sums[chip][:, (chip ^ target) * columns:((chip ^ target) + 1) * columns] for chip in range(chips)]
            start = (CORES * target + core) * columns
            reduced[:, start:start + columns] = functools.reduce(jnp.add, parts)


def per_device(basis, zone, cond_table, heat_table):
    blocks = lax.axis_size("blk")
    slabs = lax.axis_size("dom")
    chips = blocks // CORES
    count = chips - 1
    columns, planes, ny, nz = basis.shape
    rows = ny // chips
    half = ny // blocks
    total = columns * blocks
    weight = 1.0 / (slabs * planes * ny * nz)
    image = jax.ShapeDtypeStruct((half, columns, nz), BF16)
    center_shape = jax.ShapeDtypeStruct((rows + 2, columns, nz), BF16)
    partial = jax.ShapeDtypeStruct((rows, columns, nz), F32)
    whole = jax.ShapeDtypeStruct((total, 1, half, nz), BF16)
    params = pltpu.CompilerParams(vmem_limit_bytes=32 << 20)
    costly = pl.CostEstimate(flops=COST, bytes_accessed=COST // 8, transcendentals=0)
    cheap = pl.CostEstimate(flops=1, bytes_accessed=1, transcendentals=0)

    def call(kernel, out_shape, inputs, scratch=(), specs=None, out_specs=None, cost=cheap, aliases={}):
        return pl.pallas_call(
            kernel,
            out_shape=out_shape,
            in_specs=specs or [VMEM] * len(inputs),
            out_specs=out_specs or [VMEM] * len(out_shape),
            scratch_shapes=scratch,
            input_output_aliases=aliases,
            compiler_params=params,
            cost_estimate=cost,
        )(*inputs)

    def after(value, *others):
        return lax.optimization_barrier((value, *others))[0]

    def swap(array, s):
        return lax.ppermute(array, "blk", [(i, i ^ s) for i in range(blocks)])

    def exchange(array, offset):
        partner = [((d + offset) ^ 1) - offset for d in range(slabs)]
        return lax.ppermute(array, "dom", [(d, to) for d, to in enumerate(partner) if 0 <= to < slabs])

    def turning(n):
        return [
            pltpu.VMEM((n, columns * half, nz), F32),
            pltpu.VMEM((n, columns, 1, half, nz), BF16),
            pltpu.SemaphoreType.DMA((n,)),
        ]

    sent, center, plain, firsts, seconds = prepare(basis, zone, cond_table, chips)
    two = exchange(sent, 1)
    one = exchange(sent, 0)
    plain = swap(plain, 1)
    firsts = [swap(array, CORES * (k + 1)) for k, array in enumerate(firsts)]
    seconds = [swap(array, CORES * (k + 1)) for k, array in enumerate(seconds)]
    coef, near_partial = call(
        functools.partial(plane_kernel, chips),
        (jax.ShapeDtypeStruct((6, rows, nz), F32), partial),
        (zone, cond_table, heat_table, after(center, plain)),
        [pltpu.VMEM((ny + 16, nz), F32)],
        [VMEM, SMEM, SMEM, VMEM],
        cost=costly,
    )
    firsts = [after(array, coef) for array in firsts]
    first_two = [exchange(array, 1) for array in firsts]
    first_one = [exchange(array, 0) for array in firsts]
    second_two = [exchange(array, 1) for array in seconds]
    second_one = [exchange(array, 0) for array in seconds]
    near_mine, near_theirs, faces, near_flat = call(
        near_kernel,
        (
            image,
            image,
            jax.ShapeDtypeStruct((2, rows, nz), F32),
            jax.ShapeDtypeStruct((columns, rows * nz), BF16),
        ),
        (coef, near_partial, center, one, two),
    )
    results = call(
        functools.partial(gather_kernel, chips), [center_shape] * count + [partial] * count, (coef, *firsts, *seconds)
    )
    centers, partials = results[:count], results[count:]
    other_firsts = [swap(after(array, two)[1:], 1) for array in firsts]
    other_seconds = [swap(after(array, two)[:-1], 1) for array in seconds]
    half_flat = jax.ShapeDtypeStruct((columns, rows * nz // 2), BF16)
    results = call(
        functools.partial(first_far_kernel, chips),
        [image] * count + [half_flat] * count,
        (faces, *partials, *centers, *first_one, *first_two),
    )
    images, flats = results[:count], results[count:]
    applied, = call(
        first_kernel, (whole,), (near_mine, swap(near_theirs, 1)), turning(CORES), out_specs=[ANY]
    )
    gram_shape = jax.ShapeDtypeStruct((total, chips * columns), F32)
    left, first_gram = call(
        functools.partial(left_kernel, chips, weight),
        (jax.ShapeDtypeStruct((total, rows * nz), BF16), gram_shape),
        (near_flat, center, plain, *flats, *centers, *other_firsts, *other_seconds),
    )
    *images, gram = call(
        functools.partial(second_far_kernel, chips, weight),
        [image] * (2 * count) + [gram_shape],
        (faces, left, first_gram, *partials, *centers, *second_one, *second_two, *images),
        [pltpu.VMEM((columns, rows * nz // 2), BF16)],
    )
    parts = slabs * blocks
    shares = gram.reshape(parts, total // parts, chips * columns)
    shares = lax.all_to_all(shares, ("dom", "blk"), split_axis=0, concat_axis=0, tiled=True)
    pieces = []
    for k in range(count):
        pieces += [images[k], swap(images[count + k], 1)]
    applied, = call(
        functools.partial(last_kernel, blocks),
        (whole,),
        (applied, *pieces),
        turning(len(pieces)),
        [ANY] + [VMEM] * len(pieces),
        [ANY],
        aliases={0: 0},
    )
    reduced, = call(
        functools.partial(sum_kernel, slabs, blocks), (jax.ShapeDtypeStruct((total // parts, total), F32),), (shares,)
    )
    return applied, reduced


def solution(mesh):
    placed = (P("blk", "dom", "roll", None), P("dom", "roll", None), P(), P())
    return jax.shard_map(
        per_device,
        mesh=mesh,
        in_specs=placed,
        out_specs=(P("roll", "dom", "blk", None), P(("dom", "blk"), "roll")),
        check_vma=False,
    )
```

time: 51.6 us -> 51.2 us (level)
  blocking collectives: 11.6 us -> 0 us
  starting transfers between devices: 11.2 us -> 16.4 us
  waiting for transfers between devices: 15.1 us -> 19.8 us
  Pallas kernels: 10.7 us -> 11.8 us
    all_to_all x1 -> x0, blocking collectives: 11.6 us -> none  [per_device(): lax.all_to_all(shares, ('dom', 'blk'), split_axis=0, concat_axis=0, tiled...]
    all_to_all x0 -> x1, waiting for transfers between devices: none -> 6.61 us  [per_device(): lax.all_to_all(shares, ('dom', 'blk'), split_axis=0, concat_axis=0, tiled...]
    all_to_all x0 -> x1, starting transfers between devices: none -> 3.51 us  [per_device(): lax.all_to_all(shares, ('dom', 'blk'), split_axis=0, concat_axis=0, tiled...]
    ppermute x4 -> x6, waiting for transfers between devices: 12.7 us -> 10.1 us  [exchange(): lax.ppermute(array, 'dom', [(d, to) for d, to in enumerate(partner) if 0...]
    ppermute x4 -> x6, starting transfers between devices: 7.38 us -> 8.7 us  [exchange(): lax.ppermute(array, 'dom', [(d, to) for d, to in enumerate(partner) if 0...]
    pallas_call x6 -> x9, Pallas kernels: 7.86 us -> 8.72 us  [call(): pl.pallas_call(kernel, out_shape=out_shape, in_specs=specs or [VMEM] * le...]
    ppermute x5 -> x7, waiting for transfers between devices: 2.35 us -> 3.09 us  [swap(): return lax.ppermute(array, 'blk', [(i, i ^ s) for i in range(blocks)])]
    ppermute x5 -> x7, starting transfers between devices: 3.78 us -> 4.19 us  [swap(): return lax.ppermute(array, 'blk', [(i, i ^ s) for i in range(blocks)])]
  transfers between devices with their start and end apart: 9 -> 14, of which waited for: 3 -> 5; matrix products, arithmetic and copies ran while one was open for 0% -> 0% of each run, Pallas kernels for 9% -> 15%
where the time goes in v7:
time: 51.2 us; the launch traced here: 50.8 us
  waiting for transfers between devices  19.8 us (39%)
  starting transfers between devices  16.4 us (32%)
  Pallas kernels  11.8 us (23%)
  local copies, waits for them, and re-layouts  2.11 us (4%)
  between operations  0.76 us (1%)
    ppermute x6, waiting for transfers between devices, exchange(): lax.ppermute(array, 'dom', [(d, to) for d, to in enumerate(partner) if 0...  10.1 us
    pallas_call x9, Pallas kernels, call(): pl.pallas_call(kernel, out_shape=out_shape, in_specs=specs or [VMEM] * le...  8.72 us
    ppermute x6, starting transfers between devices, exchange(): lax.ppermute(array, 'dom', [(d, to) for d, to in enumerate(partner) if 0...  8.7 us
    all_to_all x1, waiting for transfers between devices, per_device(): lax.all_to_all(shares, ('dom', 'blk'), split_axis=0, concat_axis=0, tiled...  6.61 us
    ppermute x7, starting transfers between devices, swap(): return lax.ppermute(array, 'blk', [(i, i ^ s) for i in range(blocks)])  4.19 us
    all_to_all x1, starting transfers between devices, per_device(): lax.all_to_all(shares, ('dom', 'blk'), split_axis=0, concat_axis=0, tiled...  3.51 us
    ppermute x7, waiting for transfers between devices, swap(): return lax.ppermute(array, 'blk', [(i, i ^ s) for i in range(blocks)])  3.09 us
    pallas_call x1, Pallas kernels, prepare(): pl.pallas_call(functools.partial(prepare_kernel, chips), out_shape=shapes...  3.03 us
  transfers between devices with their start and end apart: 14, of which 5 were waited for; matrix products, arithmetic and copies ran while one was open for 0% of the time, Pallas kernels for 15%

profile of v7, /device:TPU:0, one launch (start us, length us, event | category | flops | bytes accessed | tf_op | source)
XLA Modules:
  0.0 50.8 jit_solution(17831133608632739402)
XLA Ops:
  0.6 3.0 %shard_map.59 = (bf16[33,64,128]{2,1,0:T(8,128)(2,1)S(1)}, bf16[34,64,128]{2,1,0:T(8,128)(2,1)S(1)}, bf16[32,64,128]{2,1,0:T(8,128)(2,1)S(1)}, bf16[17,64,128]{2,1,0:T(8,128)(2,1)S(1)}, bf16[17,64,128]{2,1,0:T(8,128)(2,1)S(1)}) custom-call(bf16[64,1,64,128]{3,2,1,0:T(8,128)(2,1)} %basis_hbm.1, s32[1,64,128]{2,1,0:T(8,128)} %zone_ref.1, f32[16]{0:T(128)} %cond_ref.1), custom_call_target="tpu_custom_call" | custom-call | tf_op jit(solution)/shard_map/pallas_call | solution.py:86
  3.7 0.5 %collective-permute-start = (bf16[32,64,128]{2,1,0:T(8,128)(2,1)S(1)}, bf16[32,64,128]{2,1,0:T(8,128)(2,1)S(1)}, u32[]{:S(2)}, u32[]{:S(2)}) collective-permute-start(bf16[32,64,128]{2,1,0:T(8,128)(2,1)S(1)} %get-tuple-element.27), channel_id=1, source_target_pairs={{0,1},{1,0},{2,3},{3,2},{4,5},{5,4},{6,7},{7,6},{8,9},{9,8},{10,11... | collective-permute-start | bytes 1572872 | tf_op jit(solution)/shard_map/ppermute | solution.py:327
  4.2 2.6 %collective-permute-start.4 = (bf16[17,64,128]{2,1,0:T(8,128)(2,1)S(1)}, bf16[17,64,128]{2,1,0:T(8,128)(2,1)S(1)}, u32[]{:S(2)}, u32[]{:S(2)}) collective-permute-start(bf16[17,64,128]{2,1,0:T(8,128)(2,1)S(1)} %get-tuple-element.36), channel_id=1, source_target_pairs={{0,2},{1,3},{2,0},{3,1},{4,6},{5,7},{6,4},{7,5},{8,10},{9,11},{10,... | collective-permute-start | bytes 835592 | tf_op jit(solution)/shard_map/ppermute | solution.py:327
  6.7 0.7 %collective-permute-start.2 = (bf16[33,64,128]{2,1,0:T(8,128)(2,1)S(1)}, bf16[33,64,128]{2,1,0:T(8,128)(2,1)S(1)}, u32[]{:S(2)}, u32[]{:S(2)}) collective-permute-start(bf16[33,64,128]{2,1,0:T(8,128)(2,1)S(1)} %get-tuple-element.31), channel_id=1, source_target_pairs={{4,8},{8,4},{5,9},{9,5},{6,10},{10,6},{7,11},{11,7},{20,24},{24,20... | collective-permute-start | bytes 1622024 | tf_op jit(solution)/shard_map/ppermute | solution.py:331
  7.4 4.4 %collective-permute-start.1 = (bf16[33,64,128]{2,1,0:T(8,128)(2,1)S(1)}, bf16[33,64,128]{2,1,0:T(8,128)(2,1)S(1)}, u32[]{:S(2)}, u32[]{:S(2)}) collective-permute-start(bf16[33,64,128]{2,1,0:T(8,128)(2,1)S(1)} %get-tuple-element.31), channel_id=1, source_target_pairs={{0,4},{4,0},{8,12},{12,8},{1,5},{5,1},{9,13},{13,9},{2,6},{6,2},{1... | collective-permute-start | bytes 1622024 | tf_op jit(solution)/shard_map/ppermute | solution.py:331
  11.9 0.5 %collective-permute-start.5 = (bf16[17,64,128]{2,1,0:T(8,128)(2,1)S(1)}, bf16[17,64,128]{2,1,0:T(8,128)(2,1)S(1)}, u32[]{:S(2)}, u32[]{:S(2)}) collective-permute-start(bf16[17,64,128]{2,1,0:T(8,128)(2,1)S(1)} %get-tuple-element.38), channel_id=1, source_target_pairs={{0,2},{1,3},{2,0},{3,1},{4,6},{5,7},{6,4},{7,5},{8,10},{9,11},{10,... | collective-permute-start | bytes 835592 | tf_op jit(solution)/shard_map/ppermute | solution.py:327
  12.4 0.0 collective-permute-done.plain
  12.4 0.0 copy-start
  12.4 0.8 %copy-done = s32[1,64,128]{2,1,0:T(8,128)S(1)} copy-done((s32[1,64,128]{2,1,0:T(8,128)S(1)}, s32[1,64,128]{2,1,0:T(8,128)}, u32[]{:S(2)}) %copy-start) | copy-done | bytes 32792
  13.2 0.0 copy-start.1
  13.2 0.7 %copy-done.1 = f32[16]{0:T(128)S(1)} copy-done((f32[16]{0:T(128)S(1)}, f32[16]{0:T(128)}, u32[]{:S(2)}) %copy-start.1) | copy-done | bytes 88
  13.8 0.0 copy-start.2
  13.8 0.7 %copy-done.2 = f32[16]{0:T(128)S(1)} copy-done((f32[16]{0:T(128)S(1)}, f32[16]{0:T(128)}, u32[]{:S(2)}) %copy-start.2) | copy-done | bytes 88
  14.5 1.3 %shard_map.60 = (f32[6,32,128]{2,1,0:T(8,128)S(1)}, f32[32,64,128]{2,1,0:T(8,128)S(1)}) custom-call(s32[1,64,128]{2,1,0:T(8,128)S(1)} %copy-done, f32[16]{0:T(128)S(1)} %copy-done.1, f32[16]{0:T(128)S(1)} %copy-done.2, bf16[34,64,128]{2,1,0:T(8,128)(2,1)S(1)} %get-tuple-element.28.center), custom_call_target="tpu_custom_call" | custom-call | flops 1073741824 | bytes 134217728 | tf_op jit(solution)/shard_map/pallas_call | solution.py:312
  15.8 0.0 collective-permute-done.4.refs_0_
  15.8 0.5 collective-permute-start.6
  16.3 0.7 %collective-permute-start.7 = (bf16[17,64,128]{2,1,0:T(8,128)(2,1)S(1)}, bf16[17,64,128]{2,1,0:T(8,128)(2,1)S(1)}, u32[]{:S(2)}, u32[]{:S(2)}) collective-permute-start(bf16[17,64,128]{2,1,0:T(8,128)(2,1)S(1)} %collective-permute-done.4.refs_0_), channel_id=1, source_target_pairs={{4,8},{8,4},{5,9},{9,5},{6,10},{10,6},{7,11},{11,7},{20,24},{24,20... | collective-permute-start | bytes 835592 | tf_op jit(solution)/shard_map/ppermute | solution.py:331
  17.0 3.1 %collective-permute-done.5.refs_1_ = bf16[17,64,128]{2,1,0:T(8,128)(2,1)S(1)} collective-permute-done((bf16[17,64,128]{2,1,0:T(8,128)(2,1)S(1)}, bf16[17,64,128]{2,1,0:T(8,128)(2,1)S(1)}, u32[]{:S(2)}, u32[]{:S(2)}) %collective-permute-start.5) | collective-permute-done | bytes 278560 | tf_op jit(solution)/shard_map/ppermute | solution.py:327
  20.0 1.8 %collective-permute-start.10 = (bf16[17,64,128]{2,1,0:T(8,128)(2,1)S(1)}, bf16[17,64,128]{2,1,0:T(8,128)(2,1)S(1)}, u32[]{:S(2)}, u32[]{:S(2)}) collective-permute-start(bf16[17,64,128]{2,1,0:T(8,128)(2,1)S(1)} %collective-permute-done.5.refs_1_), channel_id=1, source_target_pairs={{0,4},{4,0},{8,12},{12,8},{1,5},{5,1},{9,13},{13,9},{2,6},{6,2},{1... | collective-permute-start | bytes 835592 | tf_op jit(solution)/shard_map/ppermute | solution.py:331
  21.8 0.0 collective-permute-done.2.two
  21.8 0.7 %collective-permute-start.11 = (bf16[17,64,128]{2,1,0:T(8,128)(2,1)S(1)}, bf16[17,64,128]{2,1,0:T(8,128)(2,1)S(1)}, u32[]{:S(2)}, u32[]{:S(2)}) collective-permute-start(bf16[17,64,128]{2,1,0:T(8,128)(2,1)S(1)} %collective-permute-done.5.refs_1_), channel_id=1, source_target_pairs={{4,8},{8,4},{5,9},{9,5},{6,10},{10,6},{7,11},{11,7},{20,24},{24,20... | collective-permute-start | bytes 835592 | tf_op jit(solution)/shard_map/ppermute | solution.py:331
  22.5 2.4 %collective-permute-done.1.one = bf16[33,64,128]{2,1,0:T(8,128)(2,1)S(1)} collective-permute-done((bf16[33,64,128]{2,1,0:T(8,128)(2,1)S(1)}, bf16[33,64,128]{2,1,0:T(8,128)(2,1)S(1)}, u32[]{:S(2)}, u32[]{:S(2)}) %collective-permute-start.1) | collective-permute-done | bytes 540704 | tf_op jit(solution)/shard_map/ppermute | solution.py:331
  25.0 0.0 collective-permute-start.8
  25.0 6.0 %collective-permute-done.6.refs_2_ = bf16[17,64,128]{2,1,0:T(8,128)(2,1)S(1)} collective-permute-done((bf16[17,64,128]{2,1,0:T(8,128)(2,1)S(1)}, bf16[17,64,128]{2,1,0:T(8,128)(2,1)S(1)}, u32[]{:S(2)}, u32[]{:S(2)}) %collective-permute-start.6) | collective-permute-done | bytes 278560 | tf_op jit(solution)/shard_map/ppermute | solution.py:331
  30.9 0.0 collective-permute-start.9
  30.9 0.7 %shard_map.63 = (bf16[34,64,128]{2,1,0:T(8,128)(2,1)S(1)}, f32[32,64,128]{2,1,0:T(8,128)S(1)}) custom-call(f32[6,32,128]{2,1,0:T(8,128)S(1)} %get-tuple-element.29.coef, bf16[17,64,128]{2,1,0:T(8,128)(2,1)S(1)} %collective-permute-done.4.refs_0_, bf16[17,64,128]{2,1,0:T(8,128)(2,1)S(1)} %collective-permute-done.5.refs_1_), custom_call_target="tpu_custom_call" | custom-call | flops 1 | bytes 1 | tf_op jit(solution)/shard_map/pallas_call | solution.py:312
  31.7 0.6 %shard_map.61 = (bf16[16,64,128]{2,1,0:T(8,128)(2,1)S(1)}, bf16[16,64,128]{2,1,0:T(8,128)(2,1)S(1)}, f32[2,32,128]{2,1,0:T(8,128)S(1)}, bf16[64,4096]{1,0:T(8,128)(2,1)S(1)}) custom-call(f32[6,32,128]{2,1,0:T(8,128)S(1)} %get-tuple-element.29.coef, f32[32,64,128]{2,1,0:T(8,128)S(1)} %get-tuple-element.30.partial, ...), custom_call_target="tpu_custom_call" | custom-call | flops 1 | bytes 1 | tf_op jit(solution)/shard_map/pallas_call | solution.py:312
  32.2 0.0 collective-permute-done.7.refs_3_
  32.3 0.6 %collective-permute-start.3 = (bf16[16,64,128]{2,1,0:T(8,128)(2,1)S(1)}, bf16[16,64,128]{2,1,0:T(8,128)(2,1)S(1)}, u32[]{:S(2)}, u32[]{:S(2)}) collective-permute-start(bf16[16,64,128]{2,1,0:T(8,128)(2,1)S(1)} %get-tuple-element.33), channel_id=1, source_target_pairs={{0,1},{1,0},{2,3},{3,2},{4,5},{5,4},{6,7},{7,6},{8,9},{9,8},{10,11... | collective-permute-start | bytes 786440 | tf_op jit(solution)/shard_map/ppermute | solution.py:327
  32.8 0.2 shard_map.64
  33.0 0.0 collective-permute-done.8.refs_2_
  33.0 0.0 collective-permute-done.9.refs_3_
  33.0 1.4 %shard_map.65 = (bf16[256,4096]{1,0:T(8,128)(2,1)S(1)}, f32[256,128]{1,0:T(8,128)S(1)}) custom-call(bf16[64,4096]{1,0:T(8,128)(2,1)S(1)} %get-tuple-element.35.flat, bf16[34,64,128]{2,1,0:T(8,128)(2,1)S(1)} %get-tuple-element.28.center, bf16[32,64,128]{2,1,0:T(8,128)(2,1)S(1)} %collective-permute-done.plain, bf16[64,2048]{1,0:T(8,128)(2,1)S(1)} %get-tuple-element.41.refs_0_, ...), custom_call_target="tpu_custom_call" | custom-call | flops 1 | bytes 1 | tf_op jit(solution)/shard_map/pallas_call | solution.py:312
  34.4 1.7 %collective-permute-done.10.refs_2_ = bf16[17,64,128]{2,1,0:T(8,128)(2,1)S(1)} collective-permute-done((bf16[17,64,128]{2,1,0:T(8,128)(2,1)S(1)}, bf16[17,64,128]{2,1,0:T(8,128)(2,1)S(1)}, u32[]{:S(2)}, u32[]{:S(2)}) %collective-permute-start.10) | collective-permute-done | bytes 278560 | tf_op jit(solution)/shard_map/ppermute | solution.py:331
  36.1 0.0 collective-permute-done.11.refs_3_
  36.1 1.2 %shard_map.66 = (bf16[16,64,128]{2,1,0:T(8,128)(2,1)S(1)}, bf16[16,64,128]{2,1,0:T(8,128)(2,1)S(1)}, f32[256,128]{1,0:T(8,128)}) custom-call(f32[2,32,128]{2,1,0:T(8,128)S(1)} %get-tuple-element.34.faces, bf16[256,4096]{1,0:T(8,128)(2,1)S(1)} %get-tuple-element.44.left, f32[256,128]{1,0:T(8,128)S(1)} %get-tuple-element.45.first_gram, ...), custom_call_target="tpu_custom_call" | custom-call | flops 1 | bytes 1 | tf_op jit(solution)/shard_map/pallas_call | solution.py:312
  37.4 0.0 collective-permute-start.12
  37.4 3.5 %all-to-all-start = ((f32[16,16,128]{2,1,0:T(8,128)}), f32[16,16,128]{2,1,0:T(8,128)S(1)}, u32[]{:S(2)}, u32[]{:S(2)}) async-start(f32[16,16,128]{2,1,0:T(8,128)} %bitcast), calls=%async_computation | async-start | bytes 262144 | tf_op jit(solution)/shard_map/all_to_all | solution.py:399
  40.9 0.0 collective-permute-done.3.theirs
  40.9 1.3 %shard_map.62.applied_in = bf16[256,1,16,128]{3,2,1,0:T(8,128)(2,1)} custom-call(bf16[16,64,128]{2,1,0:T(8,128)(2,1)S(1)} %get-tuple-element.32.mine, bf16[16,64,128]{2,1,0:T(8,128)(2,1)S(1)} %collective-permute-done.3.theirs), custom_call_target="tpu_custom_call" | custom-call | flops 1 | bytes 1 | tf_op jit(solution)/shard_map/pallas_call | solution.py:312
  42.2 6.6 %all-to-all-done.shares = f32[16,16,128]{2,1,0:T(8,128)S(1)} async-done(((f32[16,16,128]{2,1,0:T(8,128)}), f32[16,16,128]{2,1,0:T(8,128)S(1)}, u32[]{:S(2)}, u32[]{:S(2)}) %all-to-all-start) | async-done | bytes 131104 | tf_op jit(solution)/shard_map/all_to_all | solution.py:399
  48.8 0.7 %shard_map.68 = f32[16,256]{1,0:T(8,128)} custom-call(f32[16,16,128]{2,1,0:T(8,128)S(1)} %all-to-all-done.shares), custom_call_target="tpu_custom_call" | custom-call | flops 1 | bytes 1 | tf_op jit(solution)/shard_map/pallas_call | solution.py:312
  49.5 0.0 collective-permute-done.12.refs_1_
  49.5 1.3 %shard_map.67 = bf16[256,1,16,128]{3,2,1,0:T(8,128)(2,1)} custom-call(bf16[256,1,16,128]{3,2,1,0:T(8,128)(2,1)} %shard_map.62.applied_in, bf16[16,64,128]{2,1,0:T(8,128)(2,1)S(1)} %get-tuple-element.47.refs_0_, bf16[16,64,128]{2,1,0:T(8,128)(2,1)S(1)} %collective-permute-done.12.refs_1_), custom_call_target="tpu_custom_call", output_to_operand_aliasing={{}: (0, {})} | custom-call | flops 1 | bytes 1 | tf_op jit(solution)/shard_map/pallas_call | solution.py:312
  (2 shorter events, 0.0 us)
Async XLA Ops:
  3.7 8.7 %collective-permute-start = (bf16[32,64,128]{2,1,0:T(8,128)(2,1)S(1)}, bf16[32,64,128]{2,1,0:T(8,128)(2,1)S(1)}, u32[]{:S(2)}, u32[]{:S(2)}) collective-permute-start(bf16[32,64,128]{2,1,0:T(8,128)(2,1)S(1)} %get-tuple-element.27), channel_id=1, source_target_pairs={{0,1},{1,0},{2,3},{3,2},{4,5},{5,4},{6,7},{7,6},{8,9},{9,8},{10,11... | collective-permute-start | bytes 1572872 | tf_op jit(solution)/shard_map/ppermute | solution.py:327
  4.2 11.6 %collective-permute-start.4 = (bf16[17,64,128]{2,1,0:T(8,128)(2,1)S(1)}, bf16[17,64,128]{2,1,0:T(8,128)(2,1)S(1)}, u32[]{:S(2)}, u32[]{:S(2)}) collective-permute-start(bf16[17,64,128]{2,1,0:T(8,128)(2,1)S(1)} %get-tuple-element.36), channel_id=1, source_target_pairs={{0,2},{1,3},{2,0},{3,1},{4,6},{5,7},{6,4},{7,5},{8,10},{9,11},{10,... | collective-permute-start | bytes 835592 | tf_op jit(solution)/shard_map/ppermute | solution.py:327
  6.7 15.1 %collective-permute-start.2 = (bf16[33,64,128]{2,1,0:T(8,128)(2,1)S(1)}, bf16[33,64,128]{2,1,0:T(8,128)(2,1)S(1)}, u32[]{:S(2)}, u32[]{:S(2)}) collective-permute-start(bf16[33,64,128]{2,1,0:T(8,128)(2,1)S(1)} %get-tuple-element.31), channel_id=1, source_target_pairs={{4,8},{8,4},{5,9},{9,5},{6,10},{10,6},{7,11},{11,7},{20,24},{24,20... | collective-permute-start | bytes 1622024 | tf_op jit(solution)/shard_map/ppermute | solution.py:331
  7.4 17.5 %collective-permute-start.1 = (bf16[33,64,128]{2,1,0:T(8,128)(2,1)S(1)}, bf16[33,64,128]{2,1,0:T(8,128)(2,1)S(1)}, u32[]{:S(2)}, u32[]{:S(2)}) collective-permute-start(bf16[33,64,128]{2,1,0:T(8,128)(2,1)S(1)} %get-tuple-element.31), channel_id=1, source_target_pairs={{0,4},{4,0},{8,12},{12,8},{1,5},{5,1},{9,13},{13,9},{2,6},{6,2},{1... | collective-permute-start | bytes 1622024 | tf_op jit(solution)/shard_map/ppermute | solution.py:331
  11.9 8.2 %collective-permute-start.5 = (bf16[17,64,128]{2,1,0:T(8,128)(2,1)S(1)}, bf16[17,64,128]{2,1,0:T(8,128)(2,1)S(1)}, u32[]{:S(2)}, u32[]{:S(2)}) collective-permute-start(bf16[17,64,128]{2,1,0:T(8,128)(2,1)S(1)} %get-tuple-element.38), channel_id=1, source_target_pairs={{0,2},{1,3},{2,0},{3,1},{4,6},{5,7},{6,4},{7,5},{8,10},{9,11},{10,... | collective-permute-start | bytes 835592 | tf_op jit(solution)/shard_map/ppermute | solution.py:327
  12.4 0.8 %copy-start = (s32[1,64,128]{2,1,0:T(8,128)S(1)}, s32[1,64,128]{2,1,0:T(8,128)}, u32[]{:S(2)}) copy-start(s32[1,64,128]{2,1,0:T(8,128)} %zone_ref.1) | copy-start | bytes 98308
  13.2 0.7 %copy-start.1 = (f32[16]{0:T(128)S(1)}, f32[16]{0:T(128)}, u32[]{:S(2)}) copy-start(f32[16]{0:T(128)} %cond_ref.1) | copy-start | bytes 196
  13.8 0.7 %copy-start.2 = (f32[16]{0:T(128)S(1)}, f32[16]{0:T(128)}, u32[]{:S(2)}) copy-start(f32[16]{0:T(128)} %heat_ref.1) | copy-start | bytes 196
  15.8 15.1 %collective-permute-start.6 = (bf16[17,64,128]{2,1,0:T(8,128)(2,1)S(1)}, bf16[17,64,128]{2,1,0:T(8,128)(2,1)S(1)}, u32[]{:S(2)}, u32[]{:S(2)}) collective-permute-start(bf16[17,64,128]{2,1,0:T(8,128)(2,1)S(1)} %collective-permute-done.4.refs_0_), channel_id=1, source_target_pairs={{0,4},{4,0},{8,12},{12,8},{1,5},{5,1},{9,13},{13,9},{2,6},{6,2},{1... | collective-permute-start | bytes 835592 | tf_op jit(solution)/shard_map/ppermute | solution.py:331
  16.3 16.0 %collective-permute-start.7 = (bf16[17,64,128]{2,1,0:T(8,128)(2,1)S(1)}, bf16[17,64,128]{2,1,0:T(8,128)(2,1)S(1)}, u32[]{:S(2)}, u32[]{:S(2)}) collective-permute-start(bf16[17,64,128]{2,1,0:T(8,128)(2,1)S(1)} %collective-permute-done.4.refs_0_), channel_id=1, source_target_pairs={{4,8},{8,4},{5,9},{9,5},{6,10},{10,6},{7,11},{11,7},{20,24},{24,20... | collective-permute-start | bytes 835592 | tf_op jit(solution)/shard_map/ppermute | solution.py:331
  20.0 16.1 %collective-permute-start.10 = (bf16[17,64,128]{2,1,0:T(8,128)(2,1)S(1)}, bf16[17,64,128]{2,1,0:T(8,128)(2,1)S(1)}, u32[]{:S(2)}, u32[]{:S(2)}) collective-permute-start(bf16[17,64,128]{2,1,0:T(8,128)(2,1)S(1)} %collective-permute-done.5.refs_1_), channel_id=1, source_target_pairs={{0,4},{4,0},{8,12},{12,8},{1,5},{5,1},{9,13},{13,9},{2,6},{6,2},{1... | collective-permute-start | bytes 835592 | tf_op jit(solution)/shard_map/ppermute | solution.py:331
  21.8 14.3 %collective-permute-start.11 = (bf16[17,64,128]{2,1,0:T(8,128)(2,1)S(1)}, bf16[17,64,128]{2,1,0:T(8,128)(2,1)S(1)}, u32[]{:S(2)}, u32[]{:S(2)}) collective-permute-start(bf16[17,64,128]{2,1,0:T(8,128)(2,1)S(1)} %collective-permute-done.5.refs_1_), channel_id=1, source_target_pairs={{4,8},{8,4},{5,9},{9,5},{6,10},{10,6},{7,11},{11,7},{20,24},{24,20... | collective-permute-start | bytes 835592 | tf_op jit(solution)/shard_map/ppermute | solution.py:331
  25.0 8.0 %collective-permute-start.8 = (bf16[16,64,128]{2,1,0:T(8,128)(2,1)S(1)}, bf16[16,64,128]{2,1,0:T(8,128)(2,1)S(1)}, u32[]{:S(2)}, u32[]{:S(2)}) collective-permute-start(bf16[16,64,128]{2,1,0:T(8,128)(2,1)S(1)} %slice.6), channel_id=1, source_target_pairs={{0,1},{1,0},{2,3},{3,2},{4,5},{5,4},{6,7},{7,6},{8,9},{9,8},{10,11... | collective-permute-start | bytes 786440 | tf_op jit(solution)/shard_map/ppermute | solution.py:327
  30.9 2.1 %collective-permute-start.9 = (bf16[16,64,128]{2,1,0:T(8,128)(2,1)S(1)}, bf16[16,64,128]{2,1,0:T(8,128)(2,1)S(1)}, u32[]{:S(2)}, u32[]{:S(2)}) collective-permute-start(bf16[16,64,128]{2,1,0:T(8,128)(2,1)S(1)} %slice.7), channel_id=1, source_target_pairs={{0,1},{1,0},{2,3},{3,2},{4,5},{5,4},{6,7},{7,6},{8,9},{9,8},{10,11... | collective-permute-start | bytes 786440 | tf_op jit(solution)/shard_map/ppermute | solution.py:327
  32.3 8.6 %collective-permute-start.3 = (bf16[16,64,128]{2,1,0:T(8,128)(2,1)S(1)}, bf16[16,64,128]{2,1,0:T(8,128)(2,1)S(1)}, u32[]{:S(2)}, u32[]{:S(2)}) collective-permute-start(bf16[16,64,128]{2,1,0:T(8,128)(2,1)S(1)} %get-tuple-element.33), channel_id=1, source_target_pairs={{0,1},{1,0},{2,3},{3,2},{4,5},{5,4},{6,7},{7,6},{8,9},{9,8},{10,11... | collective-permute-start | bytes 786440 | tf_op jit(solution)/shard_map/ppermute | solution.py:327
  37.4 12.2 %collective-permute-start.12 = (bf16[16,64,128]{2,1,0:T(8,128)(2,1)S(1)}, bf16[16,64,128]{2,1,0:T(8,128)(2,1)S(1)}, u32[]{:S(2)}, u32[]{:S(2)}) collective-permute-start(bf16[16,64,128]{2,1,0:T(8,128)(2,1)S(1)} %get-tuple-element.48), channel_id=1, source_target_pairs={{0,1},{1,0},{2,3},{3,2},{4,5},{5,4},{6,7},{7,6},{8,9},{9,8},{10,11... | collective-permute-start | bytes 786440 | tf_op jit(solution)/shard_map/ppermute | solution.py:327
  37.4 11.4 %all-to-all-start = ((f32[16,16,128]{2,1,0:T(8,128)}), f32[16,16,128]{2,1,0:T(8,128)S(1)}, u32[]{:S(2)}, u32[]{:S(2)}) async-start(f32[16,16,128]{2,1,0:T(8,128)} %bitcast), calls=%async_computation | async-start | bytes 262144 | tf_op jit(solution)/shard_map/all_to_all | solution.py:399

commit v8 on v7

--- a/solution.py
+++ b/solution.py
@@ -340,13 +340,12 @@
     sent, center, plain, firsts, seconds = prepare(basis, zone, cond_table, chips)
     two = exchange(sent, 1)
     one = exchange(sent, 0)
-    plain = swap(plain, 1)
     firsts = [swap(array, CORES * (k + 1)) for k, array in enumerate(firsts)]
     seconds = [swap(array, CORES * (k + 1)) for k, array in enumerate(seconds)]
     coef, near_partial = call(
         functools.partial(plane_kernel, chips),
         (jax.ShapeDtypeStruct((6, rows, nz), F32), partial),
-        (zone, cond_table, heat_table, after(center, plain)),
+        (zone, cond_table, heat_table, center),
         [pltpu.VMEM((ny + 16, nz), F32)],
         [VMEM, SMEM, SMEM, VMEM],
         cost=costly,
@@ -370,6 +369,7 @@
         functools.partial(gather_kernel, chips), [center_shape] * count + [partial] * count, (coef, *firsts, *seconds)
     )
     centers, partials = results[:count], results[count:]
+    plain = swap(after(plain, one, two), 1)
     other_firsts = [swap(after(array, two)[1:], 1) for array in firsts]
     other_seconds = [swap(after(array, two)[:-1], 1) for array in seconds]
     half_flat = jax.ShapeDtypeStruct((columns, rows * nz // 2), BF16)
@@ -410,7 +410,7 @@
         aliases={0: 0},
     )
     reduced, = call(
-        functools.partial(sum_kernel, slabs, blocks), (jax.ShapeDtypeStruct((total // parts, total), F32),), (shares,)
+        functools.partial(sum_kernel, slabs, blocks), (jax.ShapeDtypeStruct((total // parts, total), F32),), (after(shares, applied),)
     )
     return applied, reduced
 

time: 51.2 us -> 49.1 us (0.959)
  waiting for transfers between devices: 19.8 us -> 17.4 us
    ppermute x6, waiting for transfers between devices: 10.1 us -> 7.21 us  [exchange(): lax.ppermute(array, 'dom', [(d, to) for d, to in enumerate(partner) if 0...]
    ppermute x7, waiting for transfers between devices: 3.09 us -> 4.85 us  [swap(): return lax.ppermute(array, 'blk', [(i, i ^ s) for i in range(blocks)])]
    ppermute x7, starting transfers between devices: 4.19 us -> 2.69 us  [swap(): return lax.ppermute(array, 'blk', [(i, i ^ s) for i in range(blocks)])]
    all_to_all x1, waiting for transfers between devices: 6.61 us -> 5.35 us  [per_device(): lax.all_to_all(shares, ('dom', 'blk'), split_axis=0, concat_axis=0, tiled...]
    all_to_all x1, starting transfers between devices: 3.51 us -> 4.65 us  [per_device(): lax.all_to_all(shares, ('dom', 'blk'), split_axis=0, concat_axis=0, tiled...]
    ppermute x6, starting transfers between devices: 8.7 us -> 9.37 us  [exchange(): lax.ppermute(array, 'dom', [(d, to) for d, to in enumerate(partner) if 0...]
  transfers between devices with their start and end apart: 14 -> 14, of which waited for: 5 -> 6; matrix products, arithmetic and copies ran while one was open for 0% -> 0% of each run, Pallas kernels for 15% -> 16%
where the time goes in v8:
time: 49.1 us; the launch traced here: 48.8 us
  waiting for transfers between devices  17.4 us (35%)
  starting transfers between devices  16.7 us (34%)
  Pallas kernels  11.8 us (24%)
  local copies, waits for them, and re-layouts  2.1 us (4%)
  between operations  0.78 us (2%)
    ppermute x6, starting transfers between devices, exchange(): lax.ppermute(array, 'dom', [(d, to) for d, to in enumerate(partner) if 0...  9.37 us
    pallas_call x9, Pallas kernels, call(): pl.pallas_call(kernel, out_shape=out_shape, in_specs=specs or [VMEM] * le...  8.73 us
    ppermute x6, waiting for transfers between devices, exchange(): lax.ppermute(array, 'dom', [(d, to) for d, to in enumerate(partner) if 0...  7.21 us
    all_to_all x1, waiting for transfers between devices, per_device(): lax.all_to_all(shares, ('dom', 'blk'), split_axis=0, concat_axis=0, tiled...  5.35 us
    ppermute x7, waiting for transfers between devices, swap(): return lax.ppermute(array, 'blk', [(i, i ^ s) for i in range(blocks)])  4.85 us
    all_to_all x1, starting transfers between devices, per_device(): lax.all_to_all(shares, ('dom', 'blk'), split_axis=0, concat_axis=0, tiled...  4.65 us
    pallas_call x1, Pallas kernels, prepare(): pl.pallas_call(functools.partial(prepare_kernel, chips), out_shape=shapes...  3.03 us
    ppermute x7, starting transfers between devices, swap(): return lax.ppermute(array, 'blk', [(i, i ^ s) for i in range(blocks)])  2.69 us
  transfers between devices with their start and end apart: 14, of which 6 were waited for; matrix products, arithmetic and copies ran while one was open for 0% of the time, Pallas kernels for 16%

profile of v8, /device:TPU:0, one launch (start us, length us, event | category | flops | bytes accessed | tf_op | source)
XLA Modules:
  0.0 48.8 jit_solution(6372138826360014395)
XLA Ops:
  0.6 3.0 %shard_map.59 = (bf16[33,64,128]{2,1,0:T(8,128)(2,1)S(1)}, bf16[34,64,128]{2,1,0:T(8,128)(2,1)S(1)}, bf16[32,64,128]{2,1,0:T(8,128)(2,1)S(1)}, bf16[17,64,128]{2,1,0:T(8,128)(2,1)S(1)}, bf16[17,64,128]{2,1,0:T(8,128)(2,1)S(1)}) custom-call(bf16[64,1,64,128]{3,2,1,0:T(8,128)(2,1)} %basis_hbm.1, s32[1,64,128]{2,1,0:T(8,128)} %zone_ref.1, f32[16]{0:T(128)} %cond_ref.1), custom_call_target="tpu_custom_call" | custom-call | tf_op jit(solution)/shard_map/pallas_call | solution.py:86
  3.7 0.7 %collective-permute-start.1 = (bf16[33,64,128]{2,1,0:T(8,128)(2,1)S(1)}, bf16[33,64,128]{2,1,0:T(8,128)(2,1)S(1)}, u32[]{:S(2)}, u32[]{:S(2)}) collective-permute-start(bf16[33,64,128]{2,1,0:T(8,128)(2,1)S(1)} %get-tuple-element.30), channel_id=1, source_target_pairs={{4,8},{8,4},{5,9},{9,5},{6,10},{10,6},{7,11},{11,7},{20,24},{24,20... | collective-permute-start | bytes 1622024 | tf_op jit(solution)/shard_map/ppermute | solution.py:331
  4.4 5.9 %collective-permute-start = (bf16[33,64,128]{2,1,0:T(8,128)(2,1)S(1)}, bf16[33,64,128]{2,1,0:T(8,128)(2,1)S(1)}, u32[]{:S(2)}, u32[]{:S(2)}) collective-permute-start(bf16[33,64,128]{2,1,0:T(8,128)(2,1)S(1)} %get-tuple-element.30), channel_id=1, source_target_pairs={{0,4},{4,0},{8,12},{12,8},{1,5},{5,1},{9,13},{13,9},{2,6},{6,2},{1... | collective-permute-start | bytes 1622024 | tf_op jit(solution)/shard_map/ppermute | solution.py:331
  10.2 1.5 %collective-permute-start.4 = (bf16[17,64,128]{2,1,0:T(8,128)(2,1)S(1)}, bf16[17,64,128]{2,1,0:T(8,128)(2,1)S(1)}, u32[]{:S(2)}, u32[]{:S(2)}) collective-permute-start(bf16[17,64,128]{2,1,0:T(8,128)(2,1)S(1)} %get-tuple-element.37), channel_id=1, source_target_pairs={{0,2},{1,3},{2,0},{3,1},{4,6},{5,7},{6,4},{7,5},{8,10},{9,11},{10,... | collective-permute-start | bytes 835592 | tf_op jit(solution)/shard_map/ppermute | solution.py:327
  11.7 0.5 %collective-permute-start.5 = (bf16[17,64,128]{2,1,0:T(8,128)(2,1)S(1)}, bf16[17,64,128]{2,1,0:T(8,128)(2,1)S(1)}, u32[]{:S(2)}, u32[]{:S(2)}) collective-permute-start(bf16[17,64,128]{2,1,0:T(8,128)(2,1)S(1)} %get-tuple-element.39), channel_id=1, source_target_pairs={{0,2},{1,3},{2,0},{3,1},{4,6},{5,7},{6,4},{7,5},{8,10},{9,11},{10,... | collective-permute-start | bytes 835592 | tf_op jit(solution)/shard_map/ppermute | solution.py:327
  12.3 0.0 copy-start
  12.3 0.8 %copy-done = s32[1,64,128]{2,1,0:T(8,128)S(1)} copy-done((s32[1,64,128]{2,1,0:T(8,128)S(1)}, s32[1,64,128]{2,1,0:T(8,128)}, u32[]{:S(2)}) %copy-start) | copy-done | bytes 32792
  13.0 0.0 copy-start.1
  13.0 0.7 %copy-done.1 = f32[16]{0:T(128)S(1)} copy-done((f32[16]{0:T(128)S(1)}, f32[16]{0:T(128)}, u32[]{:S(2)}) %copy-start.1) | copy-done | bytes 88
  13.7 0.0 copy-start.2
  13.7 0.7 %copy-done.2 = f32[16]{0:T(128)S(1)} copy-done((f32[16]{0:T(128)S(1)}, f32[16]{0:T(128)}, u32[]{:S(2)}) %copy-start.2) | copy-done | bytes 88
  14.3 1.3 %shard_map.60 = (f32[6,32,128]{2,1,0:T(8,128)S(1)}, f32[32,64,128]{2,1,0:T(8,128)S(1)}) custom-call(s32[1,64,128]{2,1,0:T(8,128)S(1)} %copy-done, f32[16]{0:T(128)S(1)} %copy-done.1, f32[16]{0:T(128)S(1)} %copy-done.2, bf16[34,64,128]{2,1,0:T(8,128)(2,1)S(1)} %get-tuple-element.27.center), custom_call_target="tpu_custom_call" | custom-call | flops 1073741824 | bytes 134217728 | tf_op jit(solution)/shard_map/pallas_call | solution.py:312
  15.7 4.2 %collective-permute-done.4.refs_0_ = bf16[17,64,128]{2,1,0:T(8,128)(2,1)S(1)} collective-permute-done((bf16[17,64,128]{2,1,0:T(8,128)(2,1)S(1)}, bf16[17,64,128]{2,1,0:T(8,128)(2,1)S(1)}, u32[]{:S(2)}, u32[]{:S(2)}) %collective-permute-start.4) | collective-permute-done | bytes 278560 | tf_op jit(solution)/shard_map/ppermute | solution.py:327
  19.8 0.1 collective-permute-start.6
  19.9 0.7 %collective-permute-start.7 = (bf16[17,64,128]{2,1,0:T(8,128)(2,1)S(1)}, bf16[17,64,128]{2,1,0:T(8,128)(2,1)S(1)}, u32[]{:S(2)}, u32[]{:S(2)}) collective-permute-start(bf16[17,64,128]{2,1,0:T(8,128)(2,1)S(1)} %collective-permute-done.4.refs_0_), channel_id=1, source_target_pairs={{4,8},{8,4},{5,9},{9,5},{6,10},{10,6},{7,11},{11,7},{20,24},{24,20... | collective-permute-start | bytes 835592 | tf_op jit(solution)/shard_map/ppermute | solution.py:331
  20.6 0.0 collective-permute-done.1.two
  20.6 2.8 %collective-permute-done.one = bf16[33,64,128]{2,1,0:T(8,128)(2,1)S(1)} collective-permute-done((bf16[33,64,128]{2,1,0:T(8,128)(2,1)S(1)}, bf16[33,64,128]{2,1,0:T(8,128)(2,1)S(1)}, u32[]{:S(2)}, u32[]{:S(2)}) %collective-permute-start) | collective-permute-done | bytes 540704 | tf_op jit(solution)/shard_map/ppermute | solution.py:331
  23.4 0.0 collective-permute-start.3
  23.4 0.7 %collective-permute-done.5.refs_1_ = bf16[17,64,128]{2,1,0:T(8,128)(2,1)S(1)} collective-permute-done((bf16[17,64,128]{2,1,0:T(8,128)(2,1)S(1)}, bf16[17,64,128]{2,1,0:T(8,128)(2,1)S(1)}, u32[]{:S(2)}, u32[]{:S(2)}) %collective-permute-start.5) | collective-permute-done | bytes 278560 | tf_op jit(solution)/shard_map/ppermute | solution.py:327
  24.1 1.4 %collective-permute-start.10 = (bf16[17,64,128]{2,1,0:T(8,128)(2,1)S(1)}, bf16[17,64,128]{2,1,0:T(8,128)(2,1)S(1)}, u32[]{:S(2)}, u32[]{:S(2)}) collective-permute-start(bf16[17,64,128]{2,1,0:T(8,128)(2,1)S(1)} %collective-permute-done.5.refs_1_), channel_id=1, source_target_pairs={{0,4},{4,0},{8,12},{12,8},{1,5},{5,1},{9,13},{13,9},{2,6},{6,2},{1... | collective-permute-start | bytes 835592 | tf_op jit(solution)/shard_map/ppermute | solution.py:331
  25.5 0.7 %collective-permute-start.11 = (bf16[17,64,128]{2,1,0:T(8,128)(2,1)S(1)}, bf16[17,64,128]{2,1,0:T(8,128)(2,1)S(1)}, u32[]{:S(2)}, u32[]{:S(2)}) collective-permute-start(bf16[17,64,128]{2,1,0:T(8,128)(2,1)S(1)} %collective-permute-done.5.refs_1_), channel_id=1, source_target_pairs={{4,8},{8,4},{5,9},{9,5},{6,10},{10,6},{7,11},{11,7},{20,24},{24,20... | collective-permute-start | bytes 835592 | tf_op jit(solution)/shard_map/ppermute | solution.py:331
  26.2 3.3 %collective-permute-done.6.refs_2_ = bf16[17,64,128]{2,1,0:T(8,128)(2,1)S(1)} collective-permute-done((bf16[17,64,128]{2,1,0:T(8,128)(2,1)S(1)}, bf16[17,64,128]{2,1,0:T(8,128)(2,1)S(1)}, u32[]{:S(2)}, u32[]{:S(2)}) %collective-permute-start.6) | collective-permute-done | bytes 278560 | tf_op jit(solution)/shard_map/ppermute | solution.py:331
  29.4 0.0 collective-permute-start.8
  29.5 0.0 collective-permute-done.7.refs_3_
  29.5 0.6 %collective-permute-start.9 = (bf16[16,64,128]{2,1,0:T(8,128)(2,1)S(1)}, bf16[16,64,128]{2,1,0:T(8,128)(2,1)S(1)}, u32[]{:S(2)}, u32[]{:S(2)}) collective-permute-start(bf16[16,64,128]{2,1,0:T(8,128)(2,1)S(1)} %slice.7), channel_id=1, source_target_pairs={{0,1},{1,0},{2,3},{3,2},{4,5},{5,4},{6,7},{7,6},{8,9},{9,8},{10,11... | collective-permute-start | bytes 786440 | tf_op jit(solution)/shard_map/ppermute | solution.py:327
  30.0 0.7 %shard_map.63 = (bf16[34,64,128]{2,1,0:T(8,128)(2,1)S(1)}, f32[32,64,128]{2,1,0:T(8,128)S(1)}) custom-call(f32[6,32,128]{2,1,0:T(8,128)S(1)} %get-tuple-element.28.coef, bf16[17,64,128]{2,1,0:T(8,128)(2,1)S(1)} %collective-permute-done.4.refs_0_, bf16[17,64,128]{2,1,0:T(8,128)(2,1)S(1)} %collective-permute-done.5.refs_1_), custom_call_target="tpu_custom_call" | custom-call | flops 1 | bytes 1 | tf_op jit(solution)/shard_map/pallas_call | solution.py:312
  30.8 0.6 %shard_map.61 = (bf16[16,64,128]{2,1,0:T(8,128)(2,1)S(1)}, bf16[16,64,128]{2,1,0:T(8,128)(2,1)S(1)}, f32[2,32,128]{2,1,0:T(8,128)S(1)}, bf16[64,4096]{1,0:T(8,128)(2,1)S(1)}) custom-call(f32[6,32,128]{2,1,0:T(8,128)S(1)} %get-tuple-element.28.coef, f32[32,64,128]{2,1,0:T(8,128)S(1)} %get-tuple-element.29.partial, ...), custom_call_target="tpu_custom_call" | custom-call | flops 1 | bytes 1 | tf_op jit(solution)/shard_map/pallas_call | solution.py:312
  31.3 0.2 shard_map.64
  31.5 0.0 collective-permute-done.8.refs_2_
  31.5 0.1 collective-permute-start.2
  31.6 0.0 collective-permute-done.9.refs_3_
  31.6 0.0 collective-permute-done.3.plain
  31.6 1.4 %shard_map.65 = (bf16[256,4096]{1,0:T(8,128)(2,1)S(1)}, f32[256,128]{1,0:T(8,128)S(1)}) custom-call(bf16[64,4096]{1,0:T(8,128)(2,1)S(1)} %get-tuple-element.34.flat, bf16[34,64,128]{2,1,0:T(8,128)(2,1)S(1)} %get-tuple-element.27.center, bf16[32,64,128]{2,1,0:T(8,128)(2,1)S(1)} %collective-permute-done.3.plain, ...), custom_call_target="tpu_custom_call" | custom-call | flops 1 | bytes 1 | tf_op jit(solution)/shard_map/pallas_call | solution.py:312
  33.1 1.1 %collective-permute-done.10.refs_2_ = bf16[17,64,128]{2,1,0:T(8,128)(2,1)S(1)} collective-permute-done((bf16[17,64,128]{2,1,0:T(8,128)(2,1)S(1)}, bf16[17,64,128]{2,1,0:T(8,128)(2,1)S(1)}, u32[]{:S(2)}, u32[]{:S(2)}) %collective-permute-start.10) | collective-permute-done | bytes 278560 | tf_op jit(solution)/shard_map/ppermute | solution.py:331
  34.2 0.0 collective-permute-done.11.refs_3_
  34.2 1.2 %shard_map.66 = (bf16[16,64,128]{2,1,0:T(8,128)(2,1)S(1)}, bf16[16,64,128]{2,1,0:T(8,128)(2,1)S(1)}, f32[256,128]{1,0:T(8,128)}) custom-call(f32[2,32,128]{2,1,0:T(8,128)S(1)} %get-tuple-element.33.faces, bf16[256,4096]{1,0:T(8,128)(2,1)S(1)} %get-tuple-element.45.left, f32[256,128]{1,0:T(8,128)S(1)} %get-tuple-element.46.first_gram, ...), custom_call_target="tpu_custom_call" | custom-call | flops 1 | bytes 1 | tf_op jit(solution)/shard_map/pallas_call | solution.py:312
  35.4 0.0 collective-permute-start.12
  35.4 4.6 %all-to-all-start = ((f32[16,16,128]{2,1,0:T(8,128)}), f32[16,16,128]{2,1,0:T(8,128)S(1)}, u32[]{:S(2)}, u32[]{:S(2)}) async-start(f32[16,16,128]{2,1,0:T(8,128)} %bitcast), calls=%async_computation | async-start | bytes 262144 | tf_op jit(solution)/shard_map/all_to_all | solution.py:399
  40.1 0.0 collective-permute-done.2.theirs
  40.1 1.3 %shard_map.62.applied_in = bf16[256,1,16,128]{3,2,1,0:T(8,128)(2,1)} custom-call(bf16[16,64,128]{2,1,0:T(8,128)(2,1)S(1)} %get-tuple-element.31.mine, bf16[16,64,128]{2,1,0:T(8,128)(2,1)S(1)} %collective-permute-done.2.theirs), custom_call_target="tpu_custom_call" | custom-call | flops 1 | bytes 1 | tf_op jit(solution)/shard_map/pallas_call | solution.py:312
  41.4 0.0 collective-permute-done.12.refs_1_
  41.4 1.3 %shard_map.67 = bf16[256,1,16,128]{3,2,1,0:T(8,128)(2,1)} custom-call(bf16[256,1,16,128]{3,2,1,0:T(8,128)(2,1)} %shard_map.62.applied_in, bf16[16,64,128]{2,1,0:T(8,128)(2,1)S(1)} %get-tuple-element.48.refs_0_, bf16[16,64,128]{2,1,0:T(8,128)(2,1)S(1)} %collective-permute-done.12.refs_1_), custom_call_target="tpu_custom_call", output_to_operand_aliasing={{}: (0, {})} | custom-call | flops 1 | bytes 1 | tf_op jit(solution)/shard_map/pallas_call | solution.py:312
  42.7 5.3 %all-to-all-done.shares = f32[16,16,128]{2,1,0:T(8,128)S(1)} async-done(((f32[16,16,128]{2,1,0:T(8,128)}), f32[16,16,128]{2,1,0:T(8,128)S(1)}, u32[]{:S(2)}, u32[]{:S(2)}) %all-to-all-start) | async-done | bytes 131104 | tf_op jit(solution)/shard_map/all_to_all | solution.py:399
  48.0 0.7 %shard_map.68 = f32[16,256]{1,0:T(8,128)} custom-call(f32[16,16,128]{2,1,0:T(8,128)S(1)} %all-to-all-done.shares), custom_call_target="tpu_custom_call" | custom-call | flops 1 | bytes 1 | tf_op jit(solution)/shard_map/pallas_call | solution.py:312
  (2 shorter events, 0.0 us)
Async XLA Ops:
  3.7 16.9 %collective-permute-start.1 = (bf16[33,64,128]{2,1,0:T(8,128)(2,1)S(1)}, bf16[33,64,128]{2,1,0:T(8,128)(2,1)S(1)}, u32[]{:S(2)}, u32[]{:S(2)}) collective-permute-start(bf16[33,64,128]{2,1,0:T(8,128)(2,1)S(1)} %get-tuple-element.30), channel_id=1, source_target_pairs={{4,8},{8,4},{5,9},{9,5},{6,10},{10,6},{7,11},{11,7},{20,24},{24,20... | collective-permute-start | bytes 1622024 | tf_op jit(solution)/shard_map/ppermute | solution.py:331
  4.4 19.0 %collective-permute-start = (bf16[33,64,128]{2,1,0:T(8,128)(2,1)S(1)}, bf16[33,64,128]{2,1,0:T(8,128)(2,1)S(1)}, u32[]{:S(2)}, u32[]{:S(2)}) collective-permute-start(bf16[33,64,128]{2,1,0:T(8,128)(2,1)S(1)} %get-tuple-element.30), channel_id=1, source_target_pairs={{0,4},{4,0},{8,12},{12,8},{1,5},{5,1},{9,13},{13,9},{2,6},{6,2},{1... | collective-permute-start | bytes 1622024 | tf_op jit(solution)/shard_map/ppermute | solution.py:331
  10.2 9.6 %collective-permute-start.4 = (bf16[17,64,128]{2,1,0:T(8,128)(2,1)S(1)}, bf16[17,64,128]{2,1,0:T(8,128)(2,1)S(1)}, u32[]{:S(2)}, u32[]{:S(2)}) collective-permute-start(bf16[17,64,128]{2,1,0:T(8,128)(2,1)S(1)} %get-tuple-element.37), channel_id=1, source_target_pairs={{0,2},{1,3},{2,0},{3,1},{4,6},{5,7},{6,4},{7,5},{8,10},{9,11},{10,... | collective-permute-start | bytes 835592 | tf_op jit(solution)/shard_map/ppermute | solution.py:327
  11.7 12.3 %collective-permute-start.5 = (bf16[17,64,128]{2,1,0:T(8,128)(2,1)S(1)}, bf16[17,64,128]{2,1,0:T(8,128)(2,1)S(1)}, u32[]{:S(2)}, u32[]{:S(2)}) collective-permute-start(bf16[17,64,128]{2,1,0:T(8,128)(2,1)S(1)} %get-tuple-element.39), channel_id=1, source_target_pairs={{0,2},{1,3},{2,0},{3,1},{4,6},{5,7},{6,4},{7,5},{8,10},{9,11},{10,... | collective-permute-start | bytes 835592 | tf_op jit(solution)/shard_map/ppermute | solution.py:327
  12.3 0.8 %copy-start = (s32[1,64,128]{2,1,0:T(8,128)S(1)}, s32[1,64,128]{2,1,0:T(8,128)}, u32[]{:S(2)}) copy-start(s32[1,64,128]{2,1,0:T(8,128)} %zone_ref.1) | copy-start | bytes 98308
  13.0 0.7 %copy-start.1 = (f32[16]{0:T(128)S(1)}, f32[16]{0:T(128)}, u32[]{:S(2)}) copy-start(f32[16]{0:T(128)} %cond_ref.1) | copy-start | bytes 196
  13.7 0.7 %copy-start.2 = (f32[16]{0:T(128)S(1)}, f32[16]{0:T(128)}, u32[]{:S(2)}) copy-start(f32[16]{0:T(128)} %heat_ref.1) | copy-start | bytes 196
  19.8 9.6 %collective-permute-start.6 = (bf16[17,64,128]{2,1,0:T(8,128)(2,1)S(1)}, bf16[17,64,128]{2,1,0:T(8,128)(2,1)S(1)}, u32[]{:S(2)}, u32[]{:S(2)}) collective-permute-start(bf16[17,64,128]{2,1,0:T(8,128)(2,1)S(1)} %collective-permute-done.4.refs_0_), channel_id=1, source_target_pairs={{0,4},{4,0},{8,12},{12,8},{1,5},{5,1},{9,13},{13,9},{2,6},{6,2},{1... | collective-permute-start | bytes 835592 | tf_op jit(solution)/shard_map/ppermute | solution.py:331
  19.9 9.6 %collective-permute-start.7 = (bf16[17,64,128]{2,1,0:T(8,128)(2,1)S(1)}, bf16[17,64,128]{2,1,0:T(8,128)(2,1)S(1)}, u32[]{:S(2)}, u32[]{:S(2)}) collective-permute-start(bf16[17,64,128]{2,1,0:T(8,128)(2,1)S(1)} %collective-permute-done.4.refs_0_), channel_id=1, source_target_pairs={{4,8},{8,4},{5,9},{9,5},{6,10},{10,6},{7,11},{11,7},{20,24},{24,20... | collective-permute-start | bytes 835592 | tf_op jit(solution)/shard_map/ppermute | solution.py:331
  23.4 8.3 %collective-permute-start.3 = (bf16[32,64,128]{2,1,0:T(8,128)(2,1)S(1)}, bf16[32,64,128]{2,1,0:T(8,128)(2,1)S(1)}, u32[]{:S(2)}, u32[]{:S(2)}) collective-permute-start(bf16[32,64,128]{2,1,0:T(8,128)(2,1)S(1)} %get-tuple-element.36), channel_id=1, source_target_pairs={{0,1},{1,0},{2,3},{3,2},{4,5},{5,4},{6,7},{7,6},{8,9},{9,8},{10,11... | collective-permute-start | bytes 1572872 | tf_op jit(solution)/shard_map/ppermute | solution.py:327
  24.1 10.1 %collective-permute-start.10 = (bf16[17,64,128]{2,1,0:T(8,128)(2,1)S(1)}, bf16[17,64,128]{2,1,0:T(8,128)(2,1)S(1)}, u32[]{:S(2)}, u32[]{:S(2)}) collective-permute-start(bf16[17,64,128]{2,1,0:T(8,128)(2,1)S(1)} %collective-permute-done.5.refs_1_), channel_id=1, source_target_pairs={{0,4},{4,0},{8,12},{12,8},{1,5},{5,1},{9,13},{13,9},{2,6},{6,2},{1... | collective-permute-start | bytes 835592 | tf_op jit(solution)/shard_map/ppermute | solution.py:331
  25.5 8.7 %collective-permute-start.11 = (bf16[17,64,128]{2,1,0:T(8,128)(2,1)S(1)}, bf16[17,64,128]{2,1,0:T(8,128)(2,1)S(1)}, u32[]{:S(2)}, u32[]{:S(2)}) collective-permute-start(bf16[17,64,128]{2,1,0:T(8,128)(2,1)S(1)} %collective-permute-done.5.refs_1_), channel_id=1, source_target_pairs={{4,8},{8,4},{5,9},{9,5},{6,10},{10,6},{7,11},{11,7},{20,24},{24,20... | collective-permute-start | bytes 835592 | tf_op jit(solution)/shard_map/ppermute | solution.py:331
  29.4 2.1 %collective-permute-start.8 = (bf16[16,64,128]{2,1,0:T(8,128)(2,1)S(1)}, bf16[16,64,128]{2,1,0:T(8,128)(2,1)S(1)}, u32[]{:S(2)}, u32[]{:S(2)}) collective-permute-start(bf16[16,64,128]{2,1,0:T(8,128)(2,1)S(1)} %slice.6), channel_id=1, source_target_pairs={{0,1},{1,0},{2,3},{3,2},{4,5},{5,4},{6,7},{7,6},{8,9},{9,8},{10,11... | collective-permute-start | bytes 786440 | tf_op jit(solution)/shard_map/ppermute | solution.py:327
  29.5 2.2 %collective-permute-start.9 = (bf16[16,64,128]{2,1,0:T(8,128)(2,1)S(1)}, bf16[16,64,128]{2,1,0:T(8,128)(2,1)S(1)}, u32[]{:S(2)}, u32[]{:S(2)}) collective-permute-start(bf16[16,64,128]{2,1,0:T(8,128)(2,1)S(1)} %slice.7), channel_id=1, source_target_pairs={{0,1},{1,0},{2,3},{3,2},{4,5},{5,4},{6,7},{7,6},{8,9},{9,8},{10,11... | collective-permute-start | bytes 786440 | tf_op jit(solution)/shard_map/ppermute | solution.py:327
  31.5 8.5 %collective-permute-start.2 = (bf16[16,64,128]{2,1,0:T(8,128)(2,1)S(1)}, bf16[16,64,128]{2,1,0:T(8,128)(2,1)S(1)}, u32[]{:S(2)}, u32[]{:S(2)}) collective-permute-start(bf16[16,64,128]{2,1,0:T(8,128)(2,1)S(1)} %get-tuple-element.32), channel_id=1, source_target_pairs={{0,1},{1,0},{2,3},{3,2},{4,5},{5,4},{6,7},{7,6},{8,9},{9,8},{10,11... | collective-permute-start | bytes 786440 | tf_op jit(solution)/shard_map/ppermute | solution.py:327
  35.4 6.0 %collective-permute-start.12 = (bf16[16,64,128]{2,1,0:T(8,128)(2,1)S(1)}, bf16[16,64,128]{2,1,0:T(8,128)(2,1)S(1)}, u32[]{:S(2)}, u32[]{:S(2)}) collective-permute-start(bf16[16,64,128]{2,1,0:T(8,128)(2,1)S(1)} %get-tuple-element.49), channel_id=1, source_target_pairs={{0,1},{1,0},{2,3},{3,2},{4,5},{5,4},{6,7},{7,6},{8,9},{9,8},{10,11... | collective-permute-start | bytes 786440 | tf_op jit(solution)/shard_map/ppermute | solution.py:327
  35.4 12.6 %all-to-all-start = ((f32[16,16,128]{2,1,0:T(8,128)}), f32[16,16,128]{2,1,0:T(8,128)S(1)}, u32[]{:S(2)}, u32[]{:S(2)}) async-start(f32[16,16,128]{2,1,0:T(8,128)} %bitcast), calls=%async_computation | async-start | bytes 262144 | tf_op jit(solution)/shard_map/all_to_all | solution.py:399

commit v9 on v8

--- a/solution.py
+++ b/solution.py
@@ -186,7 +186,7 @@
 
 def first_far_kernel(chips, faces, *refs):
     count = chips - 1
-    partials, centers, ones, twos, images, flats = (refs[i * count:(i + 1) * count] for i in range(6))
+    partials, centers, twos, ones, images, flats = (refs[i * count:(i + 1) * count] for i in range(6))
     nz = partials[0].shape[2]
     for k in range(count):
         for y in range(partials[k].shape[0] // 2):
@@ -221,7 +221,7 @@
 
 def second_far_kernel(chips, weight, faces, left, first_gram, *refs):
     count = chips - 1
-    partials, centers, ones, twos, images, mine, theirs = (refs[i * count:(i + 1) * count] for i in range(7))
+    partials, centers, twos, ones, images, mine, theirs = (refs[i * count:(i + 1) * count] for i in range(7))
     gram, flat = refs[7 * count:]
     rows, columns, nz = partials[0].shape
     half = rows // 2
@@ -341,7 +341,6 @@
     two = exchange(sent, 1)
     one = exchange(sent, 0)
     firsts = [swap(array, CORES * (k + 1)) for k, array in enumerate(firsts)]
-    seconds = [swap(array, CORES * (k + 1)) for k, array in enumerate(seconds)]
     coef, near_partial = call(
         functools.partial(plane_kernel, chips),
         (jax.ShapeDtypeStruct((6, rows, nz), F32), partial),
@@ -350,6 +349,7 @@
         [VMEM, SMEM, SMEM, VMEM],
         cost=costly,
     )
+    seconds = [swap(after(array, coef), CORES * (k + 1)) for k, array in enumerate(seconds)]
     firsts = [after(array, coef) for array in firsts]
     first_two = [exchange(array, 1) for array in firsts]
     first_one = [exchange(array, 0) for array in firsts]
@@ -369,14 +369,14 @@
         functools.partial(gather_kernel, chips), [center_shape] * count + [partial] * count, (coef, *firsts, *seconds)
     )
     centers, partials = results[:count], results[count:]
-    plain = swap(after(plain, one, two), 1)
+    plain = swap(after(plain, *seconds), 1)
     other_firsts = [swap(after(array, two)[1:], 1) for array in firsts]
     other_seconds = [swap(after(array, two)[:-1], 1) for array in seconds]
     half_flat = jax.ShapeDtypeStruct((columns, rows * nz // 2), BF16)
     results = call(
         functools.partial(first_far_kernel, chips),
         [image] * count + [half_flat] * count,
-        (faces, *partials, *centers, *first_one, *first_two),
+        (faces, *partials, *centers, *first_two, *first_one),
     )
     images, flats = results[:count], results[count:]
     applied, = call(
@@ -391,7 +391,7 @@
     *images, gram = call(
         functools.partial(second_far_kernel, chips, weight),
         [image] * (2 * count) + [gram_shape],
-        (faces, left, first_gram, *partials, *centers, *second_one, *second_two, *images),
+        (faces, left, first_gram, *partials, *centers, *second_two, *second_one, *images),
         [pltpu.VMEM((columns, rows * nz // 2), BF16)],
     )
     parts = slabs * blocks

time: 49.1 us -> 49.3 us (level)
  starting transfers between devices: 16.7 us -> 20.2 us
  waiting for transfers between devices: 17.4 us -> 14.2 us
    ppermute x6, waiting for transfers between devices: 7.21 us -> 3.25 us  [exchange(): lax.ppermute(array, 'dom', [(d, to) for d, to in enumerate(partner) if 0...]
    ppermute x6, starting transfers between devices: 9.37 us -> 12.6 us  [exchange(): lax.ppermute(array, 'dom', [(d, to) for d, to in enumerate(partner) if 0...]
    ppermute x7, waiting for transfers between devices: 4.85 us -> 5.55 us  [swap(): return lax.ppermute(array, 'blk', [(i, i ^ s) for i in range(blocks)])]
  transfers between devices with their start and end apart: 14 -> 14, of which waited for: 6 -> 5; matrix products, arithmetic and copies ran while one was open for 0% -> 0% of each run, Pallas kernels for 16% -> 16%
where the time goes in v9:
time: 49.3 us; the launch traced here: 49 us
  starting transfers between devices  20.2 us (41%)
  waiting for transfers between devices  14.2 us (29%)
  Pallas kernels  11.8 us (24%)
  local copies, waits for them, and re-layouts  2.1 us (4%)
  between operations  0.79 us (2%)
    ppermute x6, starting transfers between devices, exchange(): lax.ppermute(array, 'dom', [(d, to) for d, to in enumerate(partner) if 0...  12.6 us
    pallas_call x9, Pallas kernels, call(): pl.pallas_call(kernel, out_shape=out_shape, in_specs=specs or [VMEM] * le...  8.73 us
    ppermute x7, waiting for transfers between devices, swap(): return lax.ppermute(array, 'blk', [(i, i ^ s) for i in range(blocks)])  5.55 us
    all_to_all x1, waiting for transfers between devices, per_device(): lax.all_to_all(shares, ('dom', 'blk'), split_axis=0, concat_axis=0, tiled...  5.35 us
    all_to_all x1, starting transfers between devices, per_device(): lax.all_to_all(shares, ('dom', 'blk'), split_axis=0, concat_axis=0, tiled...  4.89 us
    ppermute x6, waiting for transfers between devices, exchange(): lax.ppermute(array, 'dom', [(d, to) for d, to in enumerate(partner) if 0...  3.25 us
    pallas_call x1, Pallas kernels, prepare(): pl.pallas_call(functools.partial(prepare_kernel, chips), out_shape=shapes...  3.03 us
    ppermute x7, starting transfers between devices, swap(): return lax.ppermute(array, 'blk', [(i, i ^ s) for i in range(blocks)])  2.74 us
  transfers between devices with their start and end apart: 14, of which 5 were waited for; matrix products, arithmetic and copies ran while one was open for 0% of the time, Pallas kernels for 16%

profile of v9, /device:TPU:0, one launch (start us, length us, event | category | flops | bytes accessed | tf_op | source)
XLA Modules:
  0.0 49.0 jit_solution(12329346422872562671)
XLA Ops:
  0.6 3.0 %shard_map.59 = (bf16[33,64,128]{2,1,0:T(8,128)(2,1)S(1)}, bf16[34,64,128]{2,1,0:T(8,128)(2,1)S(1)}, bf16[32,64,128]{2,1,0:T(8,128)(2,1)S(1)}, bf16[17,64,128]{2,1,0:T(8,128)(2,1)S(1)}, bf16[17,64,128]{2,1,0:T(8,128)(2,1)S(1)}) custom-call(bf16[64,1,64,128]{3,2,1,0:T(8,128)(2,1)} %basis_hbm.1, s32[1,64,128]{2,1,0:T(8,128)} %zone_ref.1, f32[16]{0:T(128)} %cond_ref.1), custom_call_target="tpu_custom_call" | custom-call | tf_op jit(solution)/shard_map/pallas_call | solution.py:86
  3.7 0.7 %collective-permute-start.1 = (bf16[33,64,128]{2,1,0:T(8,128)(2,1)S(1)}, bf16[33,64,128]{2,1,0:T(8,128)(2,1)S(1)}, u32[]{:S(2)}, u32[]{:S(2)}) collective-permute-start(bf16[33,64,128]{2,1,0:T(8,128)(2,1)S(1)} %get-tuple-element.31), channel_id=1, source_target_pairs={{4,8},{8,4},{5,9},{9,5},{6,10},{10,6},{7,11},{11,7},{20,24},{24,20... | collective-permute-start | bytes 1622024 | tf_op jit(solution)/shard_map/ppermute | solution.py:331
  4.4 5.9 %collective-permute-start = (bf16[33,64,128]{2,1,0:T(8,128)(2,1)S(1)}, bf16[33,64,128]{2,1,0:T(8,128)(2,1)S(1)}, u32[]{:S(2)}, u32[]{:S(2)}) collective-permute-start(bf16[33,64,128]{2,1,0:T(8,128)(2,1)S(1)} %get-tuple-element.31), channel_id=1, source_target_pairs={{0,4},{4,0},{8,12},{12,8},{1,5},{5,1},{9,13},{13,9},{2,6},{6,2},{1... | collective-permute-start | bytes 1622024 | tf_op jit(solution)/shard_map/ppermute | solution.py:331
  10.2 1.5 %collective-permute-start.5 = (bf16[17,64,128]{2,1,0:T(8,128)(2,1)S(1)}, bf16[17,64,128]{2,1,0:T(8,128)(2,1)S(1)}, u32[]{:S(2)}, u32[]{:S(2)}) collective-permute-start(bf16[17,64,128]{2,1,0:T(8,128)(2,1)S(1)} %get-tuple-element.40), channel_id=1, source_target_pairs={{0,2},{1,3},{2,0},{3,1},{4,6},{5,7},{6,4},{7,5},{8,10},{9,11},{10,... | collective-permute-start | bytes 835592 | tf_op jit(solution)/shard_map/ppermute | solution.py:327
  11.7 0.0 copy-start
  11.7 0.8 %copy-done = s32[1,64,128]{2,1,0:T(8,128)S(1)} copy-done((s32[1,64,128]{2,1,0:T(8,128)S(1)}, s32[1,64,128]{2,1,0:T(8,128)}, u32[]{:S(2)}) %copy-start) | copy-done | bytes 32792
  12.5 0.0 copy-start.1
  12.5 0.7 %copy-done.1 = f32[16]{0:T(128)S(1)} copy-done((f32[16]{0:T(128)S(1)}, f32[16]{0:T(128)}, u32[]{:S(2)}) %copy-start.1) | copy-done | bytes 88
  13.2 0.0 copy-start.2
  13.2 0.7 %copy-done.2 = f32[16]{0:T(128)S(1)} copy-done((f32[16]{0:T(128)S(1)}, f32[16]{0:T(128)}, u32[]{:S(2)}) %copy-start.2) | copy-done | bytes 88
  13.8 1.3 %shard_map.60 = (f32[6,32,128]{2,1,0:T(8,128)S(1)}, f32[32,64,128]{2,1,0:T(8,128)S(1)}) custom-call(s32[1,64,128]{2,1,0:T(8,128)S(1)} %copy-done, f32[16]{0:T(128)S(1)} %copy-done.1, f32[16]{0:T(128)S(1)} %copy-done.2, bf16[34,64,128]{2,1,0:T(8,128)(2,1)S(1)} %get-tuple-element.28.center), custom_call_target="tpu_custom_call" | custom-call | flops 1073741824 | bytes 134217728 | tf_op jit(solution)/shard_map/pallas_call | solution.py:312
  15.1 0.6 %collective-permute-start.3 = (bf16[17,64,128]{2,1,0:T(8,128)(2,1)S(1)}, bf16[17,64,128]{2,1,0:T(8,128)(2,1)S(1)}, u32[]{:S(2)}, u32[]{:S(2)}) collective-permute-start(bf16[17,64,128]{2,1,0:T(8,128)(2,1)S(1)} %get-tuple-element.38), channel_id=1, source_target_pairs={{0,2},{1,3},{2,0},{3,1},{4,6},{5,7},{6,4},{7,5},{8,10},{9,11},{10,... | collective-permute-start | bytes 835592 | tf_op jit(solution)/shard_map/ppermute | solution.py:327
  15.7 3.6 %collective-permute-done.5.refs_0_ = bf16[17,64,128]{2,1,0:T(8,128)(2,1)S(1)} collective-permute-done((bf16[17,64,128]{2,1,0:T(8,128)(2,1)S(1)}, bf16[17,64,128]{2,1,0:T(8,128)(2,1)S(1)}, u32[]{:S(2)}, u32[]{:S(2)}) %collective-permute-start.5) | collective-permute-done | bytes 278560 | tf_op jit(solution)/shard_map/ppermute | solution.py:327
  19.3 0.7 %collective-permute-start.6 = (bf16[17,64,128]{2,1,0:T(8,128)(2,1)S(1)}, bf16[17,64,128]{2,1,0:T(8,128)(2,1)S(1)}, u32[]{:S(2)}, u32[]{:S(2)}) collective-permute-start(bf16[17,64,128]{2,1,0:T(8,128)(2,1)S(1)} %collective-permute-done.5.refs_0_), channel_id=1, source_target_pairs={{4,8},{8,4},{5,9},{9,5},{6,10},{10,6},{7,11},{11,7},{20,24},{24,20... | collective-permute-start | bytes 835592 | tf_op jit(solution)/shard_map/ppermute | solution.py:331
  20.0 2.1 %collective-permute-start.7 = (bf16[17,64,128]{2,1,0:T(8,128)(2,1)S(1)}, bf16[17,64,128]{2,1,0:T(8,128)(2,1)S(1)}, u32[]{:S(2)}, u32[]{:S(2)}) collective-permute-start(bf16[17,64,128]{2,1,0:T(8,128)(2,1)S(1)} %collective-permute-done.5.refs_0_), channel_id=1, source_target_pairs={{0,4},{4,0},{8,12},{12,8},{1,5},{5,1},{9,13},{13,9},{2,6},{6,2},{1... | collective-permute-start | bytes 835592 | tf_op jit(solution)/shard_map/ppermute | solution.py:331
  22.1 2.0 %collective-permute-done.3.refs_1_ = bf16[17,64,128]{2,1,0:T(8,128)(2,1)S(1)} collective-permute-done((bf16[17,64,128]{2,1,0:T(8,128)(2,1)S(1)}, bf16[17,64,128]{2,1,0:T(8,128)(2,1)S(1)}, u32[]{:S(2)}, u32[]{:S(2)}) %collective-permute-start.3) | collective-permute-done | bytes 278560 | tf_op jit(solution)/shard_map/ppermute | solution.py:327
  24.1 0.0 collective-permute-start.4
  24.1 0.0 collective-permute-done.1.two
  24.1 0.7 %collective-permute-start.10 = (bf16[17,64,128]{2,1,0:T(8,128)(2,1)S(1)}, bf16[17,64,128]{2,1,0:T(8,128)(2,1)S(1)}, u32[]{:S(2)}, u32[]{:S(2)}) collective-permute-start(bf16[17,64,128]{2,1,0:T(8,128)(2,1)S(1)} %collective-permute-done.3.refs_1_), channel_id=1, source_target_pairs={{4,8},{8,4},{5,9},{9,5},{6,10},{10,6},{7,11},{11,7},{20,24},{24,20... | collective-permute-start | bytes 835592 | tf_op jit(solution)/shard_map/ppermute | solution.py:331
  24.7 0.0 collective-permute-done.one
  24.7 2.6 %collective-permute-start.11 = (bf16[17,64,128]{2,1,0:T(8,128)(2,1)S(1)}, bf16[17,64,128]{2,1,0:T(8,128)(2,1)S(1)}, u32[]{:S(2)}, u32[]{:S(2)}) collective-permute-start(bf16[17,64,128]{2,1,0:T(8,128)(2,1)S(1)} %collective-permute-done.3.refs_1_), channel_id=1, source_target_pairs={{0,4},{4,0},{8,12},{12,8},{1,5},{5,1},{9,13},{13,9},{2,6},{6,2},{1... | collective-permute-start | bytes 835592 | tf_op jit(solution)/shard_map/ppermute | solution.py:331
  27.3 0.0 collective-permute-done.6.refs_2_
  27.3 0.1 collective-permute-start.9
  27.4 1.0 %collective-permute-done.7.refs_3_ = bf16[17,64,128]{2,1,0:T(8,128)(2,1)S(1)} collective-permute-done((bf16[17,64,128]{2,1,0:T(8,128)(2,1)S(1)}, bf16[17,64,128]{2,1,0:T(8,128)(2,1)S(1)}, u32[]{:S(2)}, u32[]{:S(2)}) %collective-permute-start.7) | collective-permute-done | bytes 278560 | tf_op jit(solution)/shard_map/ppermute | solution.py:331
  28.4 0.0 collective-permute-start.8
  28.4 0.7 %shard_map.63 = (bf16[34,64,128]{2,1,0:T(8,128)(2,1)S(1)}, f32[32,64,128]{2,1,0:T(8,128)S(1)}) custom-call(f32[6,32,128]{2,1,0:T(8,128)S(1)} %get-tuple-element.29.coef, bf16[17,64,128]{2,1,0:T(8,128)(2,1)S(1)} %collective-permute-done.5.refs_0_, bf16[17,64,128]{2,1,0:T(8,128)(2,1)S(1)} %collective-permute-done.3.refs_1_), custom_call_target="tpu_custom_call" | custom-call | flops 1 | bytes 1 | tf_op jit(solution)/shard_map/pallas_call | solution.py:312
  29.1 0.6 %shard_map.61 = (bf16[16,64,128]{2,1,0:T(8,128)(2,1)S(1)}, bf16[16,64,128]{2,1,0:T(8,128)(2,1)S(1)}, f32[2,32,128]{2,1,0:T(8,128)S(1)}, bf16[64,4096]{1,0:T(8,128)(2,1)S(1)}) custom-call(f32[6,32,128]{2,1,0:T(8,128)S(1)} %get-tuple-element.29.coef, f32[32,64,128]{2,1,0:T(8,128)S(1)} %get-tuple-element.30.partial, ...), custom_call_target="tpu_custom_call" | custom-call | flops 1 | bytes 1 | tf_op jit(solution)/shard_map/pallas_call | solution.py:312
  29.7 0.2 shard_map.64
  29.9 0.0 collective-permute-done.9.refs_3_
  29.9 0.6 %collective-permute-start.2 = (bf16[16,64,128]{2,1,0:T(8,128)(2,1)S(1)}, bf16[16,64,128]{2,1,0:T(8,128)(2,1)S(1)}, u32[]{:S(2)}, u32[]{:S(2)}) collective-permute-start(bf16[16,64,128]{2,1,0:T(8,128)(2,1)S(1)} %get-tuple-element.33), channel_id=1, source_target_pairs={{0,1},{1,0},{2,3},{3,2},{4,5},{5,4},{6,7},{7,6},{8,9},{9,8},{10,11... | collective-permute-start | bytes 786440 | tf_op jit(solution)/shard_map/ppermute | solution.py:327
  30.5 0.0 collective-permute-done.8.refs_2_
  30.5 0.0 collective-permute-done.4.plain
  30.5 1.4 %shard_map.65 = (bf16[256,4096]{1,0:T(8,128)(2,1)S(1)}, f32[256,128]{1,0:T(8,128)S(1)}) custom-call(bf16[64,4096]{1,0:T(8,128)(2,1)S(1)} %get-tuple-element.35.flat, bf16[34,64,128]{2,1,0:T(8,128)(2,1)S(1)} %get-tuple-element.28.center, bf16[32,64,128]{2,1,0:T(8,128)(2,1)S(1)} %collective-permute-done.4.plain, ...), custom_call_target="tpu_custom_call" | custom-call | flops 1 | bytes 1 | tf_op jit(solution)/shard_map/pallas_call | solution.py:312
  31.9 0.0 collective-permute-done.10.refs_2_
  31.9 2.3 %collective-permute-done.11.refs_3_ = bf16[17,64,128]{2,1,0:T(8,128)(2,1)S(1)} collective-permute-done((bf16[17,64,128]{2,1,0:T(8,128)(2,1)S(1)}, bf16[17,64,128]{2,1,0:T(8,128)(2,1)S(1)}, u32[]{:S(2)}, u32[]{:S(2)}) %collective-permute-start.11) | collective-permute-done | bytes 278560 | tf_op jit(solution)/shard_map/ppermute | solution.py:331
  34.2 1.2 %shard_map.66 = (bf16[16,64,128]{2,1,0:T(8,128)(2,1)S(1)}, bf16[16,64,128]{2,1,0:T(8,128)(2,1)S(1)}, f32[256,128]{1,0:T(8,128)}) custom-call(f32[2,32,128]{2,1,0:T(8,128)S(1)} %get-tuple-element.34.faces, bf16[256,4096]{1,0:T(8,128)(2,1)S(1)} %get-tuple-element.47.left, f32[256,128]{1,0:T(8,128)S(1)} %get-tuple-element.48.first_gram, ...), custom_call_target="tpu_custom_call" | custom-call | flops 1 | bytes 1 | tf_op jit(solution)/shard_map/pallas_call | solution.py:312
  35.4 0.0 collective-permute-start.12
  35.4 4.9 %all-to-all-start = ((f32[16,16,128]{2,1,0:T(8,128)}), f32[16,16,128]{2,1,0:T(8,128)S(1)}, u32[]{:S(2)}, u32[]{:S(2)}) async-start(f32[16,16,128]{2,1,0:T(8,128)} %bitcast), calls=%async_computation | async-start | bytes 262144 | tf_op jit(solution)/shard_map/all_to_all | solution.py:399
  40.3 0.0 collective-permute-done.2.theirs
  40.3 1.3 %shard_map.62.applied_in = bf16[256,1,16,128]{3,2,1,0:T(8,128)(2,1)} custom-call(bf16[16,64,128]{2,1,0:T(8,128)(2,1)S(1)} %get-tuple-element.32.mine, bf16[16,64,128]{2,1,0:T(8,128)(2,1)S(1)} %collective-permute-done.2.theirs), custom_call_target="tpu_custom_call" | custom-call | flops 1 | bytes 1 | tf_op jit(solution)/shard_map/pallas_call | solution.py:312
  41.6 0.0 collective-permute-done.12.refs_1_
  41.6 1.3 %shard_map.67 = bf16[256,1,16,128]{3,2,1,0:T(8,128)(2,1)} custom-call(bf16[256,1,16,128]{3,2,1,0:T(8,128)(2,1)} %shard_map.62.applied_in, bf16[16,64,128]{2,1,0:T(8,128)(2,1)S(1)} %get-tuple-element.50.refs_0_, bf16[16,64,128]{2,1,0:T(8,128)(2,1)S(1)} %collective-permute-done.12.refs_1_), custom_call_target="tpu_custom_call", output_to_operand_aliasing={{}: (0, {})} | custom-call | flops 1 | bytes 1 | tf_op jit(solution)/shard_map/pallas_call | solution.py:312
  42.9 5.3 %all-to-all-done.shares = f32[16,16,128]{2,1,0:T(8,128)S(1)} async-done(((f32[16,16,128]{2,1,0:T(8,128)}), f32[16,16,128]{2,1,0:T(8,128)S(1)}, u32[]{:S(2)}, u32[]{:S(2)}) %all-to-all-start) | async-done | bytes 131104 | tf_op jit(solution)/shard_map/all_to_all | solution.py:399
  48.2 0.7 %shard_map.68 = f32[16,256]{1,0:T(8,128)} custom-call(f32[16,16,128]{2,1,0:T(8,128)S(1)} %all-to-all-done.shares), custom_call_target="tpu_custom_call" | custom-call | flops 1 | bytes 1 | tf_op jit(solution)/shard_map/pallas_call | solution.py:312
  (2 shorter events, 0.0 us)
Async XLA Ops:
  3.7 20.4 %collective-permute-start.1 = (bf16[33,64,128]{2,1,0:T(8,128)(2,1)S(1)}, bf16[33,64,128]{2,1,0:T(8,128)(2,1)S(1)}, u32[]{:S(2)}, u32[]{:S(2)}) collective-permute-start(bf16[33,64,128]{2,1,0:T(8,128)(2,1)S(1)} %get-tuple-element.31), channel_id=1, source_target_pairs={{4,8},{8,4},{5,9},{9,5},{6,10},{10,6},{7,11},{11,7},{20,24},{24,20... | collective-permute-start | bytes 1622024 | tf_op jit(solution)/shard_map/ppermute | solution.py:331
  4.4 20.4 %collective-permute-start = (bf16[33,64,128]{2,1,0:T(8,128)(2,1)S(1)}, bf16[33,64,128]{2,1,0:T(8,128)(2,1)S(1)}, u32[]{:S(2)}, u32[]{:S(2)}) collective-permute-start(bf16[33,64,128]{2,1,0:T(8,128)(2,1)S(1)} %get-tuple-element.31), channel_id=1, source_target_pairs={{0,4},{4,0},{8,12},{12,8},{1,5},{5,1},{9,13},{13,9},{2,6},{6,2},{1... | collective-permute-start | bytes 1622024 | tf_op jit(solution)/shard_map/ppermute | solution.py:331
  10.2 9.1 %collective-permute-start.5 = (bf16[17,64,128]{2,1,0:T(8,128)(2,1)S(1)}, bf16[17,64,128]{2,1,0:T(8,128)(2,1)S(1)}, u32[]{:S(2)}, u32[]{:S(2)}) collective-permute-start(bf16[17,64,128]{2,1,0:T(8,128)(2,1)S(1)} %get-tuple-element.40), channel_id=1, source_target_pairs={{0,2},{1,3},{2,0},{3,1},{4,6},{5,7},{6,4},{7,5},{8,10},{9,11},{10,... | collective-permute-start | bytes 835592 | tf_op jit(solution)/shard_map/ppermute | solution.py:327
  11.7 0.8 %copy-start = (s32[1,64,128]{2,1,0:T(8,128)S(1)}, s32[1,64,128]{2,1,0:T(8,128)}, u32[]{:S(2)}) copy-start(s32[1,64,128]{2,1,0:T(8,128)} %zone_ref.1) | copy-start | bytes 98308
  12.5 0.7 %copy-start.1 = (f32[16]{0:T(128)S(1)}, f32[16]{0:T(128)}, u32[]{:S(2)}) copy-start(f32[16]{0:T(128)} %cond_ref.1) | copy-start | bytes 196
  13.2 0.7 %copy-start.2 = (f32[16]{0:T(128)S(1)}, f32[16]{0:T(128)}, u32[]{:S(2)}) copy-start(f32[16]{0:T(128)} %heat_ref.1) | copy-start | bytes 196
  15.1 8.9 %collective-permute-start.3 = (bf16[17,64,128]{2,1,0:T(8,128)(2,1)S(1)}, bf16[17,64,128]{2,1,0:T(8,128)(2,1)S(1)}, u32[]{:S(2)}, u32[]{:S(2)}) collective-permute-start(bf16[17,64,128]{2,1,0:T(8,128)(2,1)S(1)} %get-tuple-element.38), channel_id=1, source_target_pairs={{0,2},{1,3},{2,0},{3,1},{4,6},{5,7},{6,4},{7,5},{8,10},{9,11},{10,... | collective-permute-start | bytes 835592 | tf_op jit(solution)/shard_map/ppermute | solution.py:327
  19.3 8.0 %collective-permute-start.6 = (bf16[17,64,128]{2,1,0:T(8,128)(2,1)S(1)}, bf16[17,64,128]{2,1,0:T(8,128)(2,1)S(1)}, u32[]{:S(2)}, u32[]{:S(2)}) collective-permute-start(bf16[17,64,128]{2,1,0:T(8,128)(2,1)S(1)} %collective-permute-done.5.refs_0_), channel_id=1, source_target_pairs={{4,8},{8,4},{5,9},{9,5},{6,10},{10,6},{7,11},{11,7},{20,24},{24,20... | collective-permute-start | bytes 835592 | tf_op jit(solution)/shard_map/ppermute | solution.py:331
  20.0 8.4 %collective-permute-start.7 = (bf16[17,64,128]{2,1,0:T(8,128)(2,1)S(1)}, bf16[17,64,128]{2,1,0:T(8,128)(2,1)S(1)}, u32[]{:S(2)}, u32[]{:S(2)}) collective-permute-start(bf16[17,64,128]{2,1,0:T(8,128)(2,1)S(1)} %collective-permute-done.5.refs_0_), channel_id=1, source_target_pairs={{0,4},{4,0},{8,12},{12,8},{1,5},{5,1},{9,13},{13,9},{2,6},{6,2},{1... | collective-permute-start | bytes 835592 | tf_op jit(solution)/shard_map/ppermute | solution.py:331
  24.1 6.5 %collective-permute-start.4 = (bf16[32,64,128]{2,1,0:T(8,128)(2,1)S(1)}, bf16[32,64,128]{2,1,0:T(8,128)(2,1)S(1)}, u32[]{:S(2)}, u32[]{:S(2)}) collective-permute-start(bf16[32,64,128]{2,1,0:T(8,128)(2,1)S(1)} %get-tuple-element.39), channel_id=1, source_target_pairs={{0,1},{1,0},{2,3},{3,2},{4,5},{5,4},{6,7},{7,6},{8,9},{9,8},{10,11... | collective-permute-start | bytes 1572872 | tf_op jit(solution)/shard_map/ppermute | solution.py:327
  24.1 7.9 %collective-permute-start.10 = (bf16[17,64,128]{2,1,0:T(8,128)(2,1)S(1)}, bf16[17,64,128]{2,1,0:T(8,128)(2,1)S(1)}, u32[]{:S(2)}, u32[]{:S(2)}) collective-permute-start(bf16[17,64,128]{2,1,0:T(8,128)(2,1)S(1)} %collective-permute-done.3.refs_1_), channel_id=1, source_target_pairs={{4,8},{8,4},{5,9},{9,5},{6,10},{10,6},{7,11},{11,7},{20,24},{24,20... | collective-permute-start | bytes 835592 | tf_op jit(solution)/shard_map/ppermute | solution.py:331
  24.7 9.4 %collective-permute-start.11 = (bf16[17,64,128]{2,1,0:T(8,128)(2,1)S(1)}, bf16[17,64,128]{2,1,0:T(8,128)(2,1)S(1)}, u32[]{:S(2)}, u32[]{:S(2)}) collective-permute-start(bf16[17,64,128]{2,1,0:T(8,128)(2,1)S(1)} %collective-permute-done.3.refs_1_), channel_id=1, source_target_pairs={{0,4},{4,0},{8,12},{12,8},{1,5},{5,1},{9,13},{13,9},{2,6},{6,2},{1... | collective-permute-start | bytes 835592 | tf_op jit(solution)/shard_map/ppermute | solution.py:331
  27.3 2.6 %collective-permute-start.9 = (bf16[16,64,128]{2,1,0:T(8,128)(2,1)S(1)}, bf16[16,64,128]{2,1,0:T(8,128)(2,1)S(1)}, u32[]{:S(2)}, u32[]{:S(2)}) collective-permute-start(bf16[16,64,128]{2,1,0:T(8,128)(2,1)S(1)} %slice.7), channel_id=1, source_target_pairs={{0,1},{1,0},{2,3},{3,2},{4,5},{5,4},{6,7},{7,6},{8,9},{9,8},{10,11... | collective-permute-start | bytes 786440 | tf_op jit(solution)/shard_map/ppermute | solution.py:327
  28.4 2.1 %collective-permute-start.8 = (bf16[16,64,128]{2,1,0:T(8,128)(2,1)S(1)}, bf16[16,64,128]{2,1,0:T(8,128)(2,1)S(1)}, u32[]{:S(2)}, u32[]{:S(2)}) collective-permute-start(bf16[16,64,128]{2,1,0:T(8,128)(2,1)S(1)} %slice.6), channel_id=1, source_target_pairs={{0,1},{1,0},{2,3},{3,2},{4,5},{5,4},{6,7},{7,6},{8,9},{9,8},{10,11... | collective-permute-start | bytes 786440 | tf_op jit(solution)/shard_map/ppermute | solution.py:327
  29.9 10.4 %collective-permute-start.2 = (bf16[16,64,128]{2,1,0:T(8,128)(2,1)S(1)}, bf16[16,64,128]{2,1,0:T(8,128)(2,1)S(1)}, u32[]{:S(2)}, u32[]{:S(2)}) collective-permute-start(bf16[16,64,128]{2,1,0:T(8,128)(2,1)S(1)} %get-tuple-element.33), channel_id=1, source_target_pairs={{0,1},{1,0},{2,3},{3,2},{4,5},{5,4},{6,7},{7,6},{8,9},{9,8},{10,11... | collective-permute-start | bytes 786440 | tf_op jit(solution)/shard_map/ppermute | solution.py:327
  35.4 6.2 %collective-permute-start.12 = (bf16[16,64,128]{2,1,0:T(8,128)(2,1)S(1)}, bf16[16,64,128]{2,1,0:T(8,128)(2,1)S(1)}, u32[]{:S(2)}, u32[]{:S(2)}) collective-permute-start(bf16[16,64,128]{2,1,0:T(8,128)(2,1)S(1)} %get-tuple-element.51), channel_id=1, source_target_pairs={{0,1},{1,0},{2,3},{3,2},{4,5},{5,4},{6,7},{7,6},{8,9},{9,8},{10,11... | collective-permute-start | bytes 786440 | tf_op jit(solution)/shard_map/ppermute | solution.py:327
  35.4 12.8 %all-to-all-start = ((f32[16,16,128]{2,1,0:T(8,128)}), f32[16,16,128]{2,1,0:T(8,128)S(1)}, u32[]{:S(2)}, u32[]{:S(2)}) async-start(f32[16,16,128]{2,1,0:T(8,128)} %bitcast), calls=%async_computation | async-start | bytes 262144 | tf_op jit(solution)/shard_map/all_to_all | solution.py:399

commit v10 on v9

--- a/solution.py
+++ b/solution.py
@@ -30,8 +30,8 @@
 
 
 def prepare_kernel(chips, basis_hbm, zone_hbm, cond_hbm, *refs):
-    near, center, plain, firsts, seconds = *refs[:3], refs[3:2 + chips], refs[2 + chips:2 * chips + 1]
-    basis, zone, table, wide, turned, cond_pad, in_sems, out_sems = refs[2 * chips + 1:]
+    near, outer, firsts, seconds = *refs[:2], refs[2:1 + chips], refs[1 + chips:2 * chips]
+    basis, zone, table, wide, turned, cond_pad, in_sems, out_sems = refs[2 * chips:]
     columns, _, ny, nz = basis.shape
     rows = ny // chips
     chip = lax.axis_index("blk") // CORES
@@ -72,8 +72,8 @@
             start = (chip ^ k) * rows
             store(turned.at[pl.ds(start, rows // 2 + 1), some], firsts[k - 1].at[:, some])
             store(turned.at[pl.ds(start + rows // 2 + 1, rows // 2 + 1), some], seconds[k - 1].at[:, some])
-        store(turned.at[pl.ds(chip * rows, rows + 2), some], center.at[:, some])
-        store(turned.at[pl.ds(chip * rows + 1, rows), some], plain.at[:, some])
+    store(turned.at[pl.ds(chip * rows, 1)], outer.at[pl.ds(0, 1)])
+    store(turned.at[pl.ds((chip + 1) * rows + 1, 1)], outer.at[pl.ds(1, 1)])
     for copy in stores:
         copy.wait()
 
@@ -81,7 +81,7 @@
 def prepare(basis, zone, cond_table, chips):
     columns, _, ny, nz = basis.shape
     rows = ny // chips
-    slabs = [rows + 1, rows + 2, rows] + [rows // 2 + 1] * (2 * chips - 2)
+    slabs = [rows + 1, 2] + [rows // 2 + 1] * (2 * chips - 2)
     shapes = [jax.ShapeDtypeStruct((n, columns, nz), BF16) for n in slabs]
     results = pl.pallas_call(
         functools.partial(prepare_kernel, chips),
@@ -96,16 +96,18 @@
             pltpu.VMEM((ny + 2, columns, nz), BF16),
             pltpu.VMEM((columns, nz), BF16),
             pltpu.SemaphoreType.DMA((columns // 16 + 2,)),
-            pltpu.SemaphoreType.DMA((1 + (2 * chips + 1) * (columns // 16),)),
+            pltpu.SemaphoreType.DMA((3 + (2 * chips - 1) * (columns // 16),)),
         ],
         compiler_params=pltpu.CompilerParams(vmem_limit_bytes=16 << 20),
     )(*[pltpu.with_memory_space_constraint(x, pltpu.HBM) for x in (basis, zone, cond_table)])
-    return (*results[:3], results[3:2 + chips], results[2 + chips:])
-
-
-def plane_kernel(chips, zone_ref, cond_ref, heat_ref, center, coef, partial, cond_pad):
-    rows = partial.shape[0]
-    nz = center.shape[2]
+    return (*results[:2], results[2:1 + chips], results[1 + chips:])
+
+
+def plane_kernel(chips, zone_ref, cond_ref, heat_ref, near_rows, outer, coef, partial, cond_pad, center):
+    rows, _, nz = partial.shape
+    center[0] = outer[0]
+    center[1:rows + 1] = near_rows[0:rows]
+    center[rows + 1] = outer[1]
     ny = zone_ref.shape[1]
     chip = lax.axis_index("blk") // CORES
     cond_pad[0:8, :] = jnp.zeros((8, nz), F32)
@@ -162,7 +164,7 @@
     for which, ref in enumerate((one, two)):
         faces[which] = 0.5 * (coef[5] + ref[rows].astype(F32)[:rows])
     for y in range(rows):
-        image = image_row(faces, y, partial[y], center[y + 1], one[y], two[y])
+        image = image_row(faces, y, partial[y], center[y], one[y], two[y])
         flat[:, y * nz:(y + 1) * nz] = image
 
         @pl.when(core == y // half)
@@ -200,17 +202,17 @@
     flats, centers, other_firsts, other_seconds = (refs[i * count:(i + 1) * count] for i in range(4))
     left, gram = refs[4 * count:]
     columns, nz = center.shape[1:]
-    rows = center.shape[0] - 2
-    half = rows // 2
+    half = other_firsts[0].shape[0]
+    rows = 2 * half
     me = lax.axis_index("blk")
     for k, ref in enumerate((center, *centers)):
         for core in range(CORES):
             where = pl.ds(pl.multiple_of((me ^ (CORES * k + core)) * columns, columns), columns)
             for y in range(rows):
-                if not core:
+                if not k:
+                    side = (plain if core else center)[y]
+                elif not core:
                     side = ref[y + 1]
-                elif not k:
-                    side = plain[y]
                 else:
                     side = other_firsts[k - 1][y] if y < half else other_seconds[k - 1][y - half]
                 left[where, y * nz:(y + 1) * nz] = side
@@ -337,16 +339,16 @@
             pltpu.SemaphoreType.DMA((n,)),
         ]
 
-    sent, center, plain, firsts, seconds = prepare(basis, zone, cond_table, chips)
+    sent, outer, firsts, seconds = prepare(basis, zone, cond_table, chips)
     two = exchange(sent, 1)
     one = exchange(sent, 0)
     firsts = [swap(array, CORES * (k + 1)) for k, array in enumerate(firsts)]
     coef, near_partial = call(
         functools.partial(plane_kernel, chips),
         (jax.ShapeDtypeStruct((6, rows, nz), F32), partial),
-        (zone, cond_table, heat_table, center),
-        [pltpu.VMEM((ny + 16, nz), F32)],
-        [VMEM, SMEM, SMEM, VMEM],
+        (zone, cond_table, heat_table, sent, outer),
+        [pltpu.VMEM((ny + 16, nz), F32), pltpu.VMEM((rows + 2, columns, nz), BF16)],
+        [VMEM, SMEM, SMEM, VMEM, VMEM],
         cost=costly,
     )
     seconds = [swap(after(array, coef), CORES * (k + 1)) for k, array in enumerate(seconds)]
@@ -363,15 +365,15 @@
             jax.ShapeDtypeStruct((2, rows, nz), F32),
             jax.ShapeDtypeStruct((columns, rows * nz), BF16),
         ),
-        (coef, near_partial, center, one, two),
+        (coef, near_partial, sent, one, two),
     )
     results = call(
         functools.partial(gather_kernel, chips), [center_shape] * count + [partial] * count, (coef, *firsts, *seconds)
     )
     centers, partials = results[:count], results[count:]
-    plain = swap(after(plain, *seconds), 1)
-    other_firsts = [swap(after(array, two)[1:], 1) for array in firsts]
-    other_seconds = [swap(after(array, two)[:-1], 1) for array in seconds]
+    plain = swap(after(sent, one, two), 1)
+    other_firsts = [swap(after(array, one, two)[1:], 1) for array in firsts]
+    other_seconds = [swap(after(array, one, two)[:-1], 1) for array in seconds]
     half_flat = jax.ShapeDtypeStruct((columns, rows * nz // 2), BF16)
     results = call(
         functools.partial(first_far_kernel, chips),
@@ -386,7 +388,7 @@
     left, first_gram = call(
         functools.partial(left_kernel, chips, weight),
         (jax.ShapeDtypeStruct((total, rows * nz), BF16), gram_shape),
-        (near_flat, center, plain, *flats, *centers, *other_firsts, *other_seconds),
+        (near_flat, sent, plain, *flats, *centers, *other_firsts, *other_seconds),
     )
     *images, gram = call(
         functools.partial(second_far_kernel, chips, weight),

time: 49.3 us -> 50.3 us (1.020)
  starting transfers between devices: 20.2 us -> 22.9 us
  waiting for transfers between devices: 14.2 us -> 12.5 us
    ppermute x6, starting transfers between devices: 12.6 us -> 15.8 us  [exchange(): lax.ppermute(array, 'dom', [(d, to) for d, to in enumerate(partner) if 0...]
    ppermute x7, waiting for transfers between devices: 5.55 us -> 3.86 us  [swap(): return lax.ppermute(array, 'blk', [(i, i ^ s) for i in range(blocks)])]
    all_to_all x1, starting transfers between devices: 4.89 us -> 4.16 us  [per_device(): lax.all_to_all(shares, ('dom', 'blk'), split_axis=0, concat_axis=0, tiled...]
  transfers between devices with their start and end apart: 14 -> 14, of which waited for: 5 -> 3; matrix products, arithmetic and copies ran while one was open for 0% -> 0% of each run, Pallas kernels for 16% -> 16%
where the time goes in v10:
time: 50.3 us; the launch traced here: 49.9 us
  starting transfers between devices  22.9 us (46%)
  waiting for transfers between devices  12.5 us (25%)
  Pallas kernels  11.6 us (23%)
  local copies, waits for them, and re-layouts  2.1 us (4%)
  between operations  0.8 us (2%)
    ppermute x6, starting transfers between devices, exchange(): lax.ppermute(array, 'dom', [(d, to) for d, to in enumerate(partner) if 0...  15.8 us
    pallas_call x9, Pallas kernels, call(): pl.pallas_call(kernel, out_shape=out_shape, in_specs=specs or [VMEM] * le...  8.75 us
    all_to_all x1, waiting for transfers between devices, per_device(): lax.all_to_all(shares, ('dom', 'blk'), split_axis=0, concat_axis=0, tiled...  5.35 us
    all_to_all x1, starting transfers between devices, per_device(): lax.all_to_all(shares, ('dom', 'blk'), split_axis=0, concat_axis=0, tiled...  4.16 us
    ppermute x7, waiting for transfers between devices, swap(): return lax.ppermute(array, 'blk', [(i, i ^ s) for i in range(blocks)])  3.86 us
    ppermute x6, waiting for transfers between devices, exchange(): lax.ppermute(array, 'dom', [(d, to) for d, to in enumerate(partner) if 0...  3.34 us
    ppermute x7, starting transfers between devices, swap(): return lax.ppermute(array, 'blk', [(i, i ^ s) for i in range(blocks)])  2.88 us
    pallas_call x1, Pallas kernels, prepare(): pl.pallas_call(functools.partial(prepare_kernel, chips), out_shape=shapes...  2.86 us
  transfers between devices with their start and end apart: 14, of which 3 were waited for; matrix products, arithmetic and copies ran while one was open for 0% of the time, Pallas kernels for 16%

profile of v10, /device:TPU:0, one launch (start us, length us, event | category | flops | bytes accessed | tf_op | source)
XLA Modules:
  0.0 49.9 jit_solution(12067236223313946419)
XLA Ops:
  0.6 2.9 %shard_map.59 = (bf16[33,64,128]{2,1,0:T(8,128)(2,1)S(1)}, bf16[2,64,128]{2,1,0:T(8,128)(2,1)S(1)}, bf16[17,64,128]{2,1,0:T(8,128)(2,1)S(1)}, bf16[17,64,128]{2,1,0:T(8,128)(2,1)S(1)}) custom-call(bf16[64,1,64,128]{3,2,1,0:T(8,128)(2,1)} %basis_hbm.1, s32[1,64,128]{2,1,0:T(8,128)} %zone_ref.1, f32[16]{0:T(128)} %cond_ref.1), custom_call_target="tpu_custom_call" | custom-call | tf_op jit(solution)/shard_map/pallas_call | solution.py:86
  3.5 3.1 %collective-permute-start = (bf16[33,64,128]{2,1,0:T(8,128)(2,1)S(1)}, bf16[33,64,128]{2,1,0:T(8,128)(2,1)S(1)}, u32[]{:S(2)}, u32[]{:S(2)}) collective-permute-start(bf16[33,64,128]{2,1,0:T(8,128)(2,1)S(1)} %get-tuple-element.35.near_rows.center), channel_id=1, source_target_pairs={{0,4},{4,0},{8,12},{12,8},{1,5},{5,1},{9,13},{13,9},{2,6},{6,2},{1... | collective-permute-start | bytes 1622024 | tf_op jit(solution)/shard_map/ppermute | solution.py:333
  6.6 0.7 %collective-permute-start.1 = (bf16[33,64,128]{2,1,0:T(8,128)(2,1)S(1)}, bf16[33,64,128]{2,1,0:T(8,128)(2,1)S(1)}, u32[]{:S(2)}, u32[]{:S(2)}) collective-permute-start(bf16[33,64,128]{2,1,0:T(8,128)(2,1)S(1)} %get-tuple-element.35.near_rows.center), channel_id=1, source_target_pairs={{4,8},{8,4},{5,9},{9,5},{6,10},{10,6},{7,11},{11,7},{20,24},{24,20... | collective-permute-start | bytes 1622024 | tf_op jit(solution)/shard_map/ppermute | solution.py:333
  7.3 1.6 %collective-permute-start.4 = (bf16[17,64,128]{2,1,0:T(8,128)(2,1)S(1)}, bf16[17,64,128]{2,1,0:T(8,128)(2,1)S(1)}, u32[]{:S(2)}, u32[]{:S(2)}) collective-permute-start(bf16[17,64,128]{2,1,0:T(8,128)(2,1)S(1)} %get-tuple-element.36), channel_id=1, source_target_pairs={{0,2},{1,3},{2,0},{3,1},{4,6},{5,7},{6,4},{7,5},{8,10},{9,11},{10,... | collective-permute-start | bytes 835592 | tf_op jit(solution)/shard_map/ppermute | solution.py:329
  8.8 0.0 copy-start
  8.8 0.8 %copy-done = s32[1,64,128]{2,1,0:T(8,128)S(1)} copy-done((s32[1,64,128]{2,1,0:T(8,128)S(1)}, s32[1,64,128]{2,1,0:T(8,128)}, u32[]{:S(2)}) %copy-start) | copy-done | bytes 32792
  9.6 0.0 copy-start.1
  9.6 0.7 %copy-done.1 = f32[16]{0:T(128)S(1)} copy-done((f32[16]{0:T(128)S(1)}, f32[16]{0:T(128)}, u32[]{:S(2)}) %copy-start.1) | copy-done | bytes 88
  10.2 0.0 copy-start.2
  10.2 0.7 %copy-done.2 = f32[16]{0:T(128)S(1)} copy-done((f32[16]{0:T(128)S(1)}, f32[16]{0:T(128)}, u32[]{:S(2)}) %copy-start.2) | copy-done | bytes 88
  10.9 1.3 %shard_map.60 = (f32[6,32,128]{2,1,0:T(8,128)S(1)}, f32[32,64,128]{2,1,0:T(8,128)S(1)}) custom-call(s32[1,64,128]{2,1,0:T(8,128)S(1)} %copy-done, f32[16]{0:T(128)S(1)} %copy-done.1, f32[16]{0:T(128)S(1)} %copy-done.2, bf16[33,64,128]{2,1,0:T(8,128)(2,1)S(1)} %get-tuple-element.35.near_rows.center, bf16[2,64,128]{2,1,0:T(8,128)(2,1)S(1)} %get-tuple-element.28.outer), custom_call_target="tpu_custom_call" | custom-call | flops 1073741824 | bytes 134217728 | tf_op jit(solution)/shard_map/pallas_call | solution.py:314
  12.2 0.6 %collective-permute-start.5 = (bf16[17,64,128]{2,1,0:T(8,128)(2,1)S(1)}, bf16[17,64,128]{2,1,0:T(8,128)(2,1)S(1)}, u32[]{:S(2)}, u32[]{:S(2)}) collective-permute-start(bf16[17,64,128]{2,1,0:T(8,128)(2,1)S(1)} %get-tuple-element.39), channel_id=1, source_target_pairs={{0,2},{1,3},{2,0},{3,1},{4,6},{5,7},{6,4},{7,5},{8,10},{9,11},{10,... | collective-permute-start | bytes 835592 | tf_op jit(solution)/shard_map/ppermute | solution.py:329
  12.8 3.8 %collective-permute-done.4.refs_0_ = bf16[17,64,128]{2,1,0:T(8,128)(2,1)S(1)} collective-permute-done((bf16[17,64,128]{2,1,0:T(8,128)(2,1)S(1)}, bf16[17,64,128]{2,1,0:T(8,128)(2,1)S(1)}, u32[]{:S(2)}, u32[]{:S(2)}) %collective-permute-start.4) | collective-permute-done | bytes 278560 | tf_op jit(solution)/shard_map/ppermute | solution.py:329
  16.7 0.7 %collective-permute-start.6 = (bf16[17,64,128]{2,1,0:T(8,128)(2,1)S(1)}, bf16[17,64,128]{2,1,0:T(8,128)(2,1)S(1)}, u32[]{:S(2)}, u32[]{:S(2)}) collective-permute-start(bf16[17,64,128]{2,1,0:T(8,128)(2,1)S(1)} %collective-permute-done.4.refs_0_), channel_id=1, source_target_pairs={{4,8},{8,4},{5,9},{9,5},{6,10},{10,6},{7,11},{11,7},{20,24},{24,20... | collective-permute-start | bytes 835592 | tf_op jit(solution)/shard_map/ppermute | solution.py:333
  17.4 5.7 %collective-permute-start.7 = (bf16[17,64,128]{2,1,0:T(8,128)(2,1)S(1)}, bf16[17,64,128]{2,1,0:T(8,128)(2,1)S(1)}, u32[]{:S(2)}, u32[]{:S(2)}) collective-permute-start(bf16[17,64,128]{2,1,0:T(8,128)(2,1)S(1)} %collective-permute-done.4.refs_0_), channel_id=1, source_target_pairs={{0,4},{4,0},{8,12},{12,8},{1,5},{5,1},{9,13},{13,9},{2,6},{6,2},{1... | collective-permute-start | bytes 835592 | tf_op jit(solution)/shard_map/ppermute | solution.py:333
  23.0 0.0 collective-permute-done.one
  23.0 0.0 collective-permute-done.1.two
  23.0 0.0 collective-permute-start.3
  23.0 0.0 collective-permute-done.5.refs_1_
  23.1 0.7 %collective-permute-start.10 = (bf16[17,64,128]{2,1,0:T(8,128)(2,1)S(1)}, bf16[17,64,128]{2,1,0:T(8,128)(2,1)S(1)}, u32[]{:S(2)}, u32[]{:S(2)}) collective-permute-start(bf16[17,64,128]{2,1,0:T(8,128)(2,1)S(1)} %collective-permute-done.5.refs_1_), channel_id=1, source_target_pairs={{4,8},{8,4},{5,9},{9,5},{6,10},{10,6},{7,11},{11,7},{20,24},{24,20... | collective-permute-start | bytes 835592 | tf_op jit(solution)/shard_map/ppermute | solution.py:333
  23.7 5.1 %collective-permute-start.11 = (bf16[17,64,128]{2,1,0:T(8,128)(2,1)S(1)}, bf16[17,64,128]{2,1,0:T(8,128)(2,1)S(1)}, u32[]{:S(2)}, u32[]{:S(2)}) collective-permute-start(bf16[17,64,128]{2,1,0:T(8,128)(2,1)S(1)} %collective-permute-done.5.refs_1_), channel_id=1, source_target_pairs={{0,4},{4,0},{8,12},{12,8},{1,5},{5,1},{9,13},{13,9},{2,6},{6,2},{1... | collective-permute-start | bytes 835592 | tf_op jit(solution)/shard_map/ppermute | solution.py:333
  28.8 0.0 collective-permute-done.6.refs_2_
  28.8 0.1 collective-permute-start.8
  28.9 0.0 collective-permute-done.7.refs_3_
  28.9 0.6 %collective-permute-start.9 = (bf16[16,64,128]{2,1,0:T(8,128)(2,1)S(1)}, bf16[16,64,128]{2,1,0:T(8,128)(2,1)S(1)}, u32[]{:S(2)}, u32[]{:S(2)}) collective-permute-start(bf16[16,64,128]{2,1,0:T(8,128)(2,1)S(1)} %slice.7), channel_id=1, source_target_pairs={{0,1},{1,0},{2,3},{3,2},{4,5},{5,4},{6,7},{7,6},{8,9},{9,8},{10,11... | collective-permute-start | bytes 786440 | tf_op jit(solution)/shard_map/ppermute | solution.py:329
  29.5 0.7 %shard_map.63 = (bf16[34,64,128]{2,1,0:T(8,128)(2,1)S(1)}, f32[32,64,128]{2,1,0:T(8,128)S(1)}) custom-call(f32[6,32,128]{2,1,0:T(8,128)S(1)} %get-tuple-element.29.coef, bf16[17,64,128]{2,1,0:T(8,128)(2,1)S(1)} %collective-permute-done.4.refs_0_, bf16[17,64,128]{2,1,0:T(8,128)(2,1)S(1)} %collective-permute-done.5.refs_1_), custom_call_target="tpu_custom_call" | custom-call | flops 1 | bytes 1 | tf_op jit(solution)/shard_map/pallas_call | solution.py:314
  30.2 0.6 %shard_map.61 = (bf16[16,64,128]{2,1,0:T(8,128)(2,1)S(1)}, bf16[16,64,128]{2,1,0:T(8,128)(2,1)S(1)}, f32[2,32,128]{2,1,0:T(8,128)S(1)}, bf16[64,4096]{1,0:T(8,128)(2,1)S(1)}) custom-call(f32[6,32,128]{2,1,0:T(8,128)S(1)} %get-tuple-element.29.coef, f32[32,64,128]{2,1,0:T(8,128)S(1)} %get-tuple-element.30.partial, ...), custom_call_target="tpu_custom_call" | custom-call | flops 1 | bytes 1 | tf_op jit(solution)/shard_map/pallas_call | solution.py:314
  30.8 0.2 shard_map.64
  31.0 0.0 collective-permute-done.8.refs_2_
  31.0 0.1 collective-permute-start.2
  31.1 0.0 collective-permute-done.9.refs_3_
  31.1 0.0 collective-permute-done.3.plain
  31.1 1.4 %shard_map.65 = (bf16[256,4096]{1,0:T(8,128)(2,1)S(1)}, f32[256,128]{1,0:T(8,128)S(1)}) custom-call(bf16[64,4096]{1,0:T(8,128)(2,1)S(1)} %get-tuple-element.34.flat, bf16[33,64,128]{2,1,0:T(8,128)(2,1)S(1)} %get-tuple-element.35.near_rows.center, bf16[33,64,128]{2,1,0:T(8,128)(2,1)S(1)} %collective-permute-done.3.plain, ...), custom_call_target="tpu_custom_call" | custom-call | flops 1 | bytes 1 | tf_op jit(solution)/shard_map/pallas_call | solution.py:314
  32.5 0.0 collective-permute-done.10.refs_2_
  32.5 3.3 %collective-permute-done.11.refs_3_ = bf16[17,64,128]{2,1,0:T(8,128)(2,1)S(1)} collective-permute-done((bf16[17,64,128]{2,1,0:T(8,128)(2,1)S(1)}, bf16[17,64,128]{2,1,0:T(8,128)(2,1)S(1)}, u32[]{:S(2)}, u32[]{:S(2)}) %collective-permute-start.11) | collective-permute-done | bytes 278560 | tf_op jit(solution)/shard_map/ppermute | solution.py:333
  35.8 1.2 %shard_map.66 = (bf16[16,64,128]{2,1,0:T(8,128)(2,1)S(1)}, bf16[16,64,128]{2,1,0:T(8,128)(2,1)S(1)}, f32[256,128]{1,0:T(8,128)}) custom-call(f32[2,32,128]{2,1,0:T(8,128)S(1)} %get-tuple-element.33.faces, bf16[256,4096]{1,0:T(8,128)(2,1)S(1)} %get-tuple-element.45.left, f32[256,128]{1,0:T(8,128)S(1)} %get-tuple-element.46.first_gram, ...), custom_call_target="tpu_custom_call" | custom-call | flops 1 | bytes 1 | tf_op jit(solution)/shard_map/pallas_call | solution.py:314
  37.1 0.0 collective-permute-start.12
  37.1 4.2 %all-to-all-start = ((f32[16,16,128]{2,1,0:T(8,128)}), f32[16,16,128]{2,1,0:T(8,128)S(1)}, u32[]{:S(2)}, u32[]{:S(2)}) async-start(f32[16,16,128]{2,1,0:T(8,128)} %bitcast), calls=%async_computation | async-start | bytes 262144 | tf_op jit(solution)/shard_map/all_to_all | solution.py:401
  41.3 0.0 collective-permute-done.2.theirs
  41.3 1.3 %shard_map.62.applied_in = bf16[256,1,16,128]{3,2,1,0:T(8,128)(2,1)} custom-call(bf16[16,64,128]{2,1,0:T(8,128)(2,1)S(1)} %get-tuple-element.31.mine, bf16[16,64,128]{2,1,0:T(8,128)(2,1)S(1)} %collective-permute-done.2.theirs), custom_call_target="tpu_custom_call" | custom-call | flops 1 | bytes 1 | tf_op jit(solution)/shard_map/pallas_call | solution.py:314
  42.6 0.0 collective-permute-done.12.refs_1_
  42.6 1.3 %shard_map.67 = bf16[256,1,16,128]{3,2,1,0:T(8,128)(2,1)} custom-call(bf16[256,1,16,128]{3,2,1,0:T(8,128)(2,1)} %shard_map.62.applied_in, bf16[16,64,128]{2,1,0:T(8,128)(2,1)S(1)} %get-tuple-element.48.refs_0_, bf16[16,64,128]{2,1,0:T(8,128)(2,1)S(1)} %collective-permute-done.12.refs_1_), custom_call_target="tpu_custom_call", output_to_operand_aliasing={{}: (0, {})} | custom-call | flops 1 | bytes 1 | tf_op jit(solution)/shard_map/pallas_call | solution.py:314
  43.8 5.3 %all-to-all-done.shares = f32[16,16,128]{2,1,0:T(8,128)S(1)} async-done(((f32[16,16,128]{2,1,0:T(8,128)}), f32[16,16,128]{2,1,0:T(8,128)S(1)}, u32[]{:S(2)}, u32[]{:S(2)}) %all-to-all-start) | async-done | bytes 131104 | tf_op jit(solution)/shard_map/all_to_all | solution.py:401
  49.2 0.7 %shard_map.68 = f32[16,256]{1,0:T(8,128)} custom-call(f32[16,16,128]{2,1,0:T(8,128)S(1)} %all-to-all-done.shares), custom_call_target="tpu_custom_call" | custom-call | flops 1 | bytes 1 | tf_op jit(solution)/shard_map/pallas_call | solution.py:314
  (2 shorter events, 0.0 us)
Async XLA Ops:
  3.5 19.5 %collective-permute-start = (bf16[33,64,128]{2,1,0:T(8,128)(2,1)S(1)}, bf16[33,64,128]{2,1,0:T(8,128)(2,1)S(1)}, u32[]{:S(2)}, u32[]{:S(2)}) collective-permute-start(bf16[33,64,128]{2,1,0:T(8,128)(2,1)S(1)} %get-tuple-element.35.near_rows.center), channel_id=1, source_target_pairs={{0,4},{4,0},{8,12},{12,8},{1,5},{5,1},{9,13},{13,9},{2,6},{6,2},{1... | collective-permute-start | bytes 1622024 | tf_op jit(solution)/shard_map/ppermute | solution.py:333
  6.6 16.5 %collective-permute-start.1 = (bf16[33,64,128]{2,1,0:T(8,128)(2,1)S(1)}, bf16[33,64,128]{2,1,0:T(8,128)(2,1)S(1)}, u32[]{:S(2)}, u32[]{:S(2)}) collective-permute-start(bf16[33,64,128]{2,1,0:T(8,128)(2,1)S(1)} %get-tuple-element.35.near_rows.center), channel_id=1, source_target_pairs={{4,8},{8,4},{5,9},{9,5},{6,10},{10,6},{7,11},{11,7},{20,24},{24,20... | collective-permute-start | bytes 1622024 | tf_op jit(solution)/shard_map/ppermute | solution.py:333
  7.3 9.4 %collective-permute-start.4 = (bf16[17,64,128]{2,1,0:T(8,128)(2,1)S(1)}, bf16[17,64,128]{2,1,0:T(8,128)(2,1)S(1)}, u32[]{:S(2)}, u32[]{:S(2)}) collective-permute-start(bf16[17,64,128]{2,1,0:T(8,128)(2,1)S(1)} %get-tuple-element.36), channel_id=1, source_target_pairs={{0,2},{1,3},{2,0},{3,1},{4,6},{5,7},{6,4},{7,5},{8,10},{9,11},{10,... | collective-permute-start | bytes 835592 | tf_op jit(solution)/shard_map/ppermute | solution.py:329
  8.8 0.8 %copy-start = (s32[1,64,128]{2,1,0:T(8,128)S(1)}, s32[1,64,128]{2,1,0:T(8,128)}, u32[]{:S(2)}) copy-start(s32[1,64,128]{2,1,0:T(8,128)} %zone_ref.1) | copy-start | bytes 98308
  9.6 0.7 %copy-start.1 = (f32[16]{0:T(128)S(1)}, f32[16]{0:T(128)}, u32[]{:S(2)}) copy-start(f32[16]{0:T(128)} %cond_ref.1) | copy-start | bytes 196
  10.2 0.7 %copy-start.2 = (f32[16]{0:T(128)S(1)}, f32[16]{0:T(128)}, u32[]{:S(2)}) copy-start(f32[16]{0:T(128)} %heat_ref.1) | copy-start | bytes 196
  12.2 10.8 %collective-permute-start.5 = (bf16[17,64,128]{2,1,0:T(8,128)(2,1)S(1)}, bf16[17,64,128]{2,1,0:T(8,128)(2,1)S(1)}, u32[]{:S(2)}, u32[]{:S(2)}) collective-permute-start(bf16[17,64,128]{2,1,0:T(8,128)(2,1)S(1)} %get-tuple-element.39), channel_id=1, source_target_pairs={{0,2},{1,3},{2,0},{3,1},{4,6},{5,7},{6,4},{7,5},{8,10},{9,11},{10,... | collective-permute-start | bytes 835592 | tf_op jit(solution)/shard_map/ppermute | solution.py:329
  16.7 12.1 %collective-permute-start.6 = (bf16[17,64,128]{2,1,0:T(8,128)(2,1)S(1)}, bf16[17,64,128]{2,1,0:T(8,128)(2,1)S(1)}, u32[]{:S(2)}, u32[]{:S(2)}) collective-permute-start(bf16[17,64,128]{2,1,0:T(8,128)(2,1)S(1)} %collective-permute-done.4.refs_0_), channel_id=1, source_target_pairs={{4,8},{8,4},{5,9},{9,5},{6,10},{10,6},{7,11},{11,7},{20,24},{24,20... | collective-permute-start | bytes 835592 | tf_op jit(solution)/shard_map/ppermute | solution.py:333
  17.4 11.6 %collective-permute-start.7 = (bf16[17,64,128]{2,1,0:T(8,128)(2,1)S(1)}, bf16[17,64,128]{2,1,0:T(8,128)(2,1)S(1)}, u32[]{:S(2)}, u32[]{:S(2)}) collective-permute-start(bf16[17,64,128]{2,1,0:T(8,128)(2,1)S(1)} %collective-permute-done.4.refs_0_), channel_id=1, source_target_pairs={{0,4},{4,0},{8,12},{12,8},{1,5},{5,1},{9,13},{13,9},{2,6},{6,2},{1... | collective-permute-start | bytes 835592 | tf_op jit(solution)/shard_map/ppermute | solution.py:333
  23.0 8.1 %collective-permute-start.3 = (bf16[33,64,128]{2,1,0:T(8,128)(2,1)S(1)}, bf16[33,64,128]{2,1,0:T(8,128)(2,1)S(1)}, u32[]{:S(2)}, u32[]{:S(2)}) collective-permute-start(bf16[33,64,128]{2,1,0:T(8,128)(2,1)S(1)} %get-tuple-element.35.near_rows.center), channel_id=1, source_target_pairs={{0,1},{1,0},{2,3},{3,2},{4,5},{5,4},{6,7},{7,6},{8,9},{9,8},{10,11... | collective-permute-start | bytes 1622024 | tf_op jit(solution)/shard_map/ppermute | solution.py:329
  23.1 9.5 %collective-permute-start.10 = (bf16[17,64,128]{2,1,0:T(8,128)(2,1)S(1)}, bf16[17,64,128]{2,1,0:T(8,128)(2,1)S(1)}, u32[]{:S(2)}, u32[]{:S(2)}) collective-permute-start(bf16[17,64,128]{2,1,0:T(8,128)(2,1)S(1)} %collective-permute-done.5.refs_1_), channel_id=1, source_target_pairs={{4,8},{8,4},{5,9},{9,5},{6,10},{10,6},{7,11},{11,7},{20,24},{24,20... | collective-permute-start | bytes 835592 | tf_op jit(solution)/shard_map/ppermute | solution.py:333
  23.7 12.1 %collective-permute-start.11 = (bf16[17,64,128]{2,1,0:T(8,128)(2,1)S(1)}, bf16[17,64,128]{2,1,0:T(8,128)(2,1)S(1)}, u32[]{:S(2)}, u32[]{:S(2)}) collective-permute-start(bf16[17,64,128]{2,1,0:T(8,128)(2,1)S(1)} %collective-permute-done.5.refs_1_), channel_id=1, source_target_pairs={{0,4},{4,0},{8,12},{12,8},{1,5},{5,1},{9,13},{13,9},{2,6},{6,2},{1... | collective-permute-start | bytes 835592 | tf_op jit(solution)/shard_map/ppermute | solution.py:333
  28.8 2.2 %collective-permute-start.8 = (bf16[16,64,128]{2,1,0:T(8,128)(2,1)S(1)}, bf16[16,64,128]{2,1,0:T(8,128)(2,1)S(1)}, u32[]{:S(2)}, u32[]{:S(2)}) collective-permute-start(bf16[16,64,128]{2,1,0:T(8,128)(2,1)S(1)} %slice.6), channel_id=1, source_target_pairs={{0,1},{1,0},{2,3},{3,2},{4,5},{5,4},{6,7},{7,6},{8,9},{9,8},{10,11... | collective-permute-start | bytes 786440 | tf_op jit(solution)/shard_map/ppermute | solution.py:329
  28.9 2.2 %collective-permute-start.9 = (bf16[16,64,128]{2,1,0:T(8,128)(2,1)S(1)}, bf16[16,64,128]{2,1,0:T(8,128)(2,1)S(1)}, u32[]{:S(2)}, u32[]{:S(2)}) collective-permute-start(bf16[16,64,128]{2,1,0:T(8,128)(2,1)S(1)} %slice.7), channel_id=1, source_target_pairs={{0,1},{1,0},{2,3},{3,2},{4,5},{5,4},{6,7},{7,6},{8,9},{9,8},{10,11... | collective-permute-start | bytes 786440 | tf_op jit(solution)/shard_map/ppermute | solution.py:329
  31.0 10.3 %collective-permute-start.2 = (bf16[16,64,128]{2,1,0:T(8,128)(2,1)S(1)}, bf16[16,64,128]{2,1,0:T(8,128)(2,1)S(1)}, u32[]{:S(2)}, u32[]{:S(2)}) collective-permute-start(bf16[16,64,128]{2,1,0:T(8,128)(2,1)S(1)} %get-tuple-element.32), channel_id=1, source_target_pairs={{0,1},{1,0},{2,3},{3,2},{4,5},{5,4},{6,7},{7,6},{8,9},{9,8},{10,11... | collective-permute-start | bytes 786440 | tf_op jit(solution)/shard_map/ppermute | solution.py:329
  37.1 5.5 %collective-permute-start.12 = (bf16[16,64,128]{2,1,0:T(8,128)(2,1)S(1)}, bf16[16,64,128]{2,1,0:T(8,128)(2,1)S(1)}, u32[]{:S(2)}, u32[]{:S(2)}) collective-permute-start(bf16[16,64,128]{2,1,0:T(8,128)(2,1)S(1)} %get-tuple-element.49), channel_id=1, source_target_pairs={{0,1},{1,0},{2,3},{3,2},{4,5},{5,4},{6,7},{7,6},{8,9},{9,8},{10,11... | collective-permute-start | bytes 786440 | tf_op jit(solution)/shard_map/ppermute | solution.py:329
  37.1 12.1 %all-to-all-start = ((f32[16,16,128]{2,1,0:T(8,128)}), f32[16,16,128]{2,1,0:T(8,128)S(1)}, u32[]{:S(2)}, u32[]{:S(2)}) async-start(f32[16,16,128]{2,1,0:T(8,128)} %bitcast), calls=%async_computation | async-start | bytes 262144 | tf_op jit(solution)/shard_map/all_to_all | solution.py:401

commit v11 on v6

--- a/solution.py
+++ b/solution.py
@@ -34,8 +34,8 @@
 
 
 def prepare_kernel(chips, basis_hbm, zone_hbm, cond_hbm, *refs):
-    near, center, plain, firsts, seconds = *refs[:3], refs[3:2 + chips], refs[2 + chips:2 * chips + 1]
-    basis, zone, table, wide, turned, cond_pad, in_sems, out_sems = refs[2 * chips + 1:]
+    near, center, firsts, seconds = refs[0], refs[1], refs[2:1 + chips], refs[1 + chips:2 * chips]
+    basis, zone, table, wide, turned, cond_pad, in_sems, out_sems = refs[2 * chips:]
     columns, _, ny, nz = basis.shape
     rows = ny // chips
     part = rows // CORES // 2
@@ -65,7 +65,7 @@
     mine = zone[0, pl.ds(pl.multiple_of(chip * rows, rows), rows), :]
     own = cond_of(mine, table)
     cond_pad[...] = jnp.concatenate([own, jnp.zeros((columns - rows, nz), F32)], 0).astype(BF16)
-    store(cond_pad, near.at[rows])
+    store(cond_pad, near.at[CORES * part])
     for i in range(chunks):
         loads[i].wait()
         some = pl.ds(i * step, step)
@@ -73,17 +73,16 @@
             wide[c * ny:(c + 1) * ny, :] = basis[c, 0].astype(F32)
         for y in range(ny):
             turned[y + 1, some, :] = wide[pl.ds(i * step * ny + y, step, stride=ny), :].astype(BF16)
-        store(turned.at[pl.ds(chip * rows + 1, rows), some], near.at[pl.ds(0, rows), some])
-        for k in range(1, chips):
+        for k in reversed(range(chips)):
             base = (chip ^ k) * rows + 1
             for owner in range(CORES):
                 start = base + (2 * owner + 1 - late) * part
-                store(turned.at[pl.ds(start, part), some], firsts[k - 1].at[pl.ds(owner * part, part), some])
-            for other in range(CORES):
+                target = firsts[k - 1] if k else near
+                store(turned.at[pl.ds(start, part), some], target.at[pl.ds(owner * part, part), some])
+            for other in range(CORES if k else 0):
                 start = base + (2 * (core ^ other) + late) * part
                 store(turned.at[pl.ds(start, part), some], seconds[k - 1].at[pl.ds(other * part, part), some])
         store(turned.at[pl.ds(chip * rows, rows + 2), some], center.at[:, some])
-        store(turned.at[pl.ds(chip * rows + 1, rows), some], plain.at[:, some])
     for k in range(1, chips):
         base = (chip ^ k) * rows
         store(turned.at[pl.ds(base, 1)], firsts[k - 1].at[pl.ds(CORES * part, 1)])
@@ -95,8 +94,8 @@
 def prepare(basis, zone, cond_table, chips):
     columns, _, ny, nz = basis.shape
     rows = ny // chips
-    slabs = [rows + 1, rows + 2, rows] + [rows // 2 + 2] * (chips - 1) + [rows // 2] * (chips - 1)
-    stores = 1 + (3 + 2 * CORES * (chips - 1)) * (columns // 16) + 2 * (chips - 1)
+    slabs = [rows // 2 + 1, rows + 2] + [rows // 2 + 2] * (chips - 1) + [rows // 2] * (chips - 1)
+    stores = 1 + (1 + CORES * (2 * chips - 1)) * (columns // 16) + 2 * (chips - 1)
     results = pl.pallas_call(
         functools.partial(prepare_kernel, chips),
         out_shape=[jax.ShapeDtypeStruct((n, columns, nz), BF16) for n in slabs],
@@ -114,10 +113,10 @@
         ],
         compiler_params=pltpu.CompilerParams(vmem_limit_bytes=16 << 20),
     )(*[pltpu.with_memory_space_constraint(x, pltpu.HBM) for x in (basis, zone, cond_table)])
-    return (*results[:3], results[3:2 + chips], results[2 + chips:])
-
-
-def plane_kernel(chips, zone_ref, cond_ref, heat_ref, center, coef, partial, cond_pad):
+    return (*results[:2], results[2:1 + chips], results[1 + chips:])
+
+
+def plane_kernel(chips, zone_ref, cond_ref, heat_ref, center, other, coef, partial, other_partial, late_rows, cond_pad):
     rows = partial.shape[0]
     nz = center.shape[2]
     ny = zone_ref.shape[1]
@@ -136,10 +135,16 @@
         jnp.where(lane == 0, 0.0, pltpu.roll(own, 1, 1)),
         jnp.where(lane == nz - 1, 0.0, pltpu.roll(own, nz - 1, 1)),
     )
-    for which, other in enumerate(beside):
-        coef[1 + which] = 0.5 * (own + other)
+    for which, node in enumerate(beside):
+        coef[1 + which] = 0.5 * (own + node)
     coef[5] = own
     plane_rows(coef, center, partial)
+    core, late = lax.axis_index("blk") % CORES, halves()
+    part = rows // CORES // 2
+    plane_rows(coef, other, other_partial, (2 * core + 1 - late) * part)
+    for which, ref in enumerate((center, other)):
+        for i in range(part):
+            late_rows[which * part + i] = ref[(2 * core + late) * part + i + 1]
 
 
 def plane_rows(coef, center, partial, first=0):
@@ -176,31 +181,54 @@
     return lax.dot_general(left, right, (((1,), (1,)), ((), ())), preferred_element_type=F32)
 
 
+def early_rows(faces, partial, center, one, two, mine, theirs, store):
+    columns = center.shape[1]
+    part = partial.shape[0] // CORES // 2
+    core, late = lax.axis_index("blk") % CORES, halves()
+    for c in range(CORES):
+        for i in range(part):
+            y, at = (2 * c + late) * part + i, c * part + i
+            v, p = center[y + 1].astype(F32), partial[y]
+            a, b = one[at].astype(F32), two[at].astype(F32)
+            share = 0.5 * p + spread(faces, 2, y, columns) * v
+            share -= spread(faces, 0, y, columns) * a
+            share -= spread(faces, 1, y, columns) * b
+            store(at, share.astype(BF16))
+            image = with_dom(faces, y, v, p, a, b).astype(BF16)
+
+            @pl.when(core == c)
+            def _():
+                mine[i] = image
+
+            @pl.when(core != c)
+            def _():
+                theirs[i] = image
+
+
+def late_rows_of(faces, partial, center, store):
+    columns = center.shape[1]
+    part = partial.shape[0] // CORES // 2
+    late = halves()
+    for c in range(CORES):
+        for i in range(part):
+            y = (2 * c + 1 - late) * part + i
+            share = 0.5 * partial[y] + spread(faces, 2, y, columns) * center[y + 1].astype(F32)
+            store(c * part + i, share.astype(BF16))
+
+
 def near_kernel(coef, partial, center, one, two, mine, theirs, faces, flat):
-    rows, columns, nz = partial.shape
-    part = rows // CORES // 2
-    core, late = lax.axis_index("blk") % CORES, halves()
-    face = [0.5 * (coef[5] + ref[rows].astype(F32)[:rows]) for ref in (one, two)]
-    which = lax.broadcasted_iota(jnp.int32, (rows, nz), 0) // part % 2
-    for k in range(2):
-        faces[k] = face[k]
-        faces[3 + k] = jnp.where(which == late, face[k], 0.0)
-    faces[2] = 0.5 * (face[0] + face[1])
-    for y in range(rows):
-        v, a, b, p = center[y + 1].astype(F32), one[y].astype(F32), two[y].astype(F32), partial[y]
-        image = with_dom(faces, y, v, p, a, b).astype(BF16)
-        share = 0.5 * p + spread(faces, 2, y, columns) * v
-        share -= spread(faces, 3, y, columns) * a
-        share -= spread(faces, 4, y, columns) * b
-        flat[:, pl.ds(pl.multiple_of(place(y, part, late) * nz, nz), nz)] = share.astype(BF16)
-
-        @pl.when(core == y // (2 * part))
-        def _():
-            mine[y % (2 * part)] = image
-
-        @pl.when(core != y // (2 * part))
-        def _():
-            theirs[y % (2 * part)] = image
+    rows, _, nz = partial.shape
+    for k, ref in enumerate((one, two)):
+        faces[k] = 0.5 * (coef[5] + ref[rows // 2].astype(F32)[:rows])
+    faces[2] = 0.5 * (faces[0] + faces[1])
+
+    def store(first):
+        def put(at, share):
+            flat[:, (first + at) * nz:(first + at + 1) * nz] = share
+        return put
+
+    early_rows(faces, partial, center, one, two, mine, theirs, store(0))
+    late_rows_of(faces, partial, center, store(rows // 2))
 
 
 def gather(first, outer, second, core, center):
@@ -236,18 +264,16 @@
     late = halves()
     for y in range(rows):
         where = pl.ds(pl.multiple_of(place(y, part, late) * nz, nz), nz)
-        sides = [ref[y + 1] for ref in centers] + [others[0][y]] + [ref[y + 1] for ref in others[1:]]
-        for i, side in enumerate(sides):
-            left[i * columns:(i + 1) * columns, where] = side
+        for i, ref in enumerate((*centers, *others)):
+            left[i * columns:(i + 1) * columns, where] = ref[y + 1]
     late_half = pl.ds(rows * nz // 2, rows * nz // 2)
     tall[:, 0:columns] = gram_of(left[...], flat[...])
     flatter[0:columns, :] = gram_of(flat[...], left[...])
     for k in range(count):
-        for c in range(CORES):
-            for i in range(part):
-                y = (2 * c + 1 - late) * part + i
-                share = 0.5 * partials[k][y] + spread(faces, 2, y, columns) * centers[k + 1][y + 1].astype(F32)
-                right[:, (c * part + i) * nz:(c * part + i + 1) * nz] = share.astype(BF16)
+        def put(at, share):
+            right[:, at * nz:(at + 1) * nz] = share
+
+        late_rows_of(faces, partials[k], centers[k + 1], put)
         block = slice((k + 1) * columns, (k + 2) * columns)
         tall[:, block] = gram_of(left[:, late_half], right[...])
         flatter[block, :] = gram_of(right[...], left[:, late_half])
@@ -255,33 +281,17 @@
 
 def gram_kernel(chips, weight, faces, left, tall, flatter, *refs):
     count = chips - 1
-    partials, centers, ones, twos, mine, theirs = (refs[i * count:(i + 1) * count] for i in range(6))
+    partials, centers, twos, ones, mine, theirs = (refs[i * count:(i + 1) * count] for i in range(6))
     gram, right, rest = refs[6 * count:]
     rows, columns, nz = partials[0].shape
-    part = rows // CORES // 2
     me = lax.axis_index("blk")
-    core, late = me % CORES, halves()
     early_half = pl.ds(0, rows * nz // 2)
     rest[...] = jnp.zeros_like(rest)
     for k in range(count):
-        for c in range(CORES):
-            for i in range(part):
-                y = (2 * c + late) * part + i
-                v, p = centers[k][y + 1].astype(F32), partials[k][y]
-                a, b = ones[k][c * part + i].astype(F32), twos[k][c * part + i].astype(F32)
-                share = 0.5 * p + spread(faces, 2, y, columns) * v
-                share -= spread(faces, 0, y, columns) * a
-                share -= spread(faces, 1, y, columns) * b
-                right[:, (c * part + i) * nz:(c * part + i + 1) * nz] = share.astype(BF16)
-                image = with_dom(faces, y, v, p, a, b).astype(BF16)
-
-                @pl.when(core == c)
-                def _():
-                    mine[k][i] = image
-
-                @pl.when(core != c)
-                def _():
-                    theirs[k][i] = image
+        def put(at, share):
+            right[:, at * nz:(at + 1) * nz] = share
+
+        early_rows(faces, partials[k], centers[k], ones[k], twos[k], mine[k], theirs[k], put)
         block = slice((k + 1) * columns, (k + 2) * columns)
         rest[:, block] = gram_of(left[:, early_half], right[...])
         flatter[block, :] += gram_of(right[...], left[:, early_half])
@@ -297,56 +307,39 @@
         gram[where, :] = share
 
 
-def turn_out(image, start, applied, wide, turned, sem):
-    rows, columns, _ = image.shape
-    for y in range(rows):
-        wide[pl.ds(y, columns, stride=rows), :] = image[y].astype(F32)
-    for c in range(columns):
-        turned[c, 0] = wide[c * rows:(c + 1) * rows, :].astype(BF16)
-    copy = pltpu.make_async_copy(turned, applied.at[pl.ds(start, columns)], sem)
-    copy.start()
-    return copy
-
-
-def first_kernel(mine, theirs, applied, wide, turned, sems):
-    me = lax.axis_index("blk")
-    columns = mine.shape[1]
-    copies = [
-        turn_out(image, (me ^ s) * columns, applied, wide.at[s], turned.at[s], sems.at[s])
-        for s, image in enumerate((mine, theirs))
-    ]
-    for copy in copies:
-        copy.wait()
-
-
-def last_kernel(slabs, blocks, shares, _, faces, *refs):
-    chips = blocks // CORES
-    count = chips - 1
-    done, partials, centers = (refs[i * CORES * count:(i + 1) * CORES * count] for i in range(3))
-    ones, twos = (refs[i * count:(i + 1) * count] for i in range(3 * CORES, 3 * CORES + 2))
-    applied, reduced, wide, turned, sems = refs[(3 * CORES + 2) * count:]
+def late_kernel(chips, faces, two, one, *refs):
+    blocks = chips * CORES
+    done, partials, centers = (refs[i * blocks:(i + 1) * blocks] for i in range(3))
+    applied, wide, turned, sems = refs[3 * blocks:]
     part, columns, _ = done[0].shape
     half = CORES * part
     me = lax.axis_index("blk")
     core, late = me % CORES, halves()
     first = (2 * core + 1 - late) * part
     copies = []
-    for s in range(CORES * count):
+    for s in range(blocks):
         scratch = wide.at[s]
         for i in range(part):
             y = first + i
-            p = partials[s][y] if s < count else partials[s][i]
-            at = s // count * part + i
-            v, a, b = (x.astype(F32) for x in (centers[s][y + 1], ones[s % count][at], twos[s % count][at]))
+            at = (CORES * (s % chips) + s // chips) * part + i
+            p = partials[s][y] if s < chips else partials[s][i]
+            v, a, b = (x.astype(F32) for x in (centers[s][y + 1], one[at], two[at]))
             image = with_dom(faces, y, v, p, a, b).astype(BF16).astype(F32)
             scratch[pl.ds((1 - late) * part + i, columns, stride=half), :] = image
             scratch[pl.ds(late * part + i, columns, stride=half), :] = done[s][i].astype(F32)
         for c in range(columns):
             turned[s, c, 0] = scratch[c * half:(c + 1) * half, :].astype(BF16)
-        partner = CORES * (s % count + 1) + s // count
+        partner = CORES * (s % chips) + s // chips
         copy = pltpu.make_async_copy(turned.at[s], applied.at[pl.ds((me ^ partner) * columns, columns)], sems.at[s])
         copy.start()
         copies.append(copy)
+    for copy in copies:
+        copy.wait()
+
+
+def sum_kernel(slabs, blocks, shares, reduced):
+    chips = blocks // CORES
+    columns = shares.shape[2] // blocks
     sums = []
     for sender in range(blocks):
         total = shares[sender]
@@ -360,8 +353,6 @@
             i = partner % CORES * chips + partner // CORES
             parts.append(sums[sender][:, i * columns:(i + 1) * columns])
         reduced[:, target * columns:(target + 1) * columns] = functools.reduce(jnp.add, parts)
-    for copy in copies:
-        copy.wait()
 
 
 def per_device(basis, zone, cond_table, heat_table):
@@ -410,42 +401,43 @@
         ]
         return lax.ppermute(array, ("dom", "blk"), pairs)
 
-    def turning(n):
-        return [
-            pltpu.VMEM((n, columns * half, nz), F32),
-            pltpu.VMEM((n, columns, 1, half, nz), BF16),
-            pltpu.SemaphoreType.DMA((n,)),
-        ]
-
-    sent, center, plain, firsts, seconds = prepare(basis, zone, cond_table, chips)
-    two = exchange(sent, 1)
-    one = exchange(sent, 0)
+    near, center, firsts, seconds = prepare(basis, zone, cond_table, chips)
+    other = swap(center, 1)
     firsts = [swap(array, CORES * (k + 1)) for k, array in enumerate(firsts)]
+    two = exchange(near, 1)
+    one = exchange(near, 0)
+    coef, near_partial, other_partial, late_near = call(
+        functools.partial(plane_kernel, chips),
+        (
+            jax.ShapeDtypeStruct((6, rows, nz), F32),
+            partial,
+            jax.ShapeDtypeStruct((part, columns, nz), F32),
+            image,
+        ),
+        (zone, cond_table, heat_table, center, other),
+        [pltpu.VMEM((ny + 16, nz), F32)],
+        [VMEM, SMEM, SMEM, VMEM, VMEM],
+        cost=costly,
+    )
     seconds = [swap(array, CORES * (k + 1)) for k, array in enumerate(seconds)]
-    plain = swap(plain, 1)
-    coef, near_partial = call(
-        functools.partial(plane_kernel, chips),
-        (jax.ShapeDtypeStruct((6, rows, nz), F32), partial),
-        (zone, cond_table, heat_table, after(center, plain)),
-        [pltpu.VMEM((ny + 16, nz), F32)],
-        [VMEM, SMEM, SMEM, VMEM],
-        cost=costly,
-    )
+    firsts = [after(array, coef, one) for array in firsts]
     early_two = [exchange(array, 1) for array in firsts]
     early_one = [exchange(array, 0) for array in firsts]
-    other_firsts = [swap(array[:half], 1) for array in firsts]
-    outers = [swap(array[half:], 1) for array in firsts]
-    other_seconds = [swap(array, 1) for array in seconds]
-    late = [jnp.concatenate([mine[:part], other[part:]]) for mine, other in zip(seconds, other_seconds)]
-    late_two = [exchange(array, 1) for array in late]
-    late_one = [exchange(array, 0) for array in late]
+    other_firsts = [swap(after(array, two)[:half], 1) for array in firsts]
+    outers = [swap(after(array, two)[half:], 1) for array in firsts]
+    other_seconds = [swap(after(array, coef), 1) for array in seconds]
+    late = [late_near]
+    for mine, theirs in zip(seconds, other_seconds):
+        late += [mine[:part], theirs[part:]]
+    late = jnp.concatenate(late)
+    late_two, late_one = exchange(late, 1), exchange(late, 0)
 
     near_mine, near_theirs, faces, near_flat = call(
         near_kernel,
         (
-            image,
-            image,
-            jax.ShapeDtypeStruct((5, rows, nz), F32),
+            half_image,
+            half_image,
+            jax.ShapeDtypeStruct((3, rows, nz), F32),
             jax.ShapeDtypeStruct((columns, rows * nz), BF16),
         ),
         (coef, near_partial, center, one, two),
@@ -457,9 +449,6 @@
         (after(coef, faces), *firsts, *seconds, *other_firsts, *outers, *other_seconds),
     )
     centers, partials, other_centers, other_partials = (results[i * count:(i + 1) * count] for i in range(4))
-    applied, = call(
-        first_kernel, (whole,), (near_mine, swap(near_theirs, 1)), turning(CORES), out_specs=[ANY]
-    )
     left, tall, flatter = call(
         functools.partial(left_kernel, chips),
         (
@@ -467,29 +456,39 @@
             jax.ShapeDtypeStruct((total, chips * columns), F32),
             jax.ShapeDtypeStruct((chips * columns, total), F32),
         ),
-        (faces, near_flat, center, *centers, plain, *other_centers, *partials),
+        (faces, near_flat, center, *centers, other, *other_centers, *partials),
         [pltpu.VMEM((columns, rows * nz // 2), BF16)],
     )
     *images, gram = call(
         functools.partial(gram_kernel, chips, weight),
         [half_image] * (2 * count) + [jax.ShapeDtypeStruct((total, total), F32)],
-        (faces, left, tall, flatter, *partials, *centers, *early_one, *early_two),
+        (faces, left, tall, flatter, *partials, *centers, *early_two, *early_one),
         [pltpu.VMEM((columns, rows * nz // 2), BF16), pltpu.VMEM((total, chips * columns), F32)],
     )
-    done = [*images[:count], *(swap(array, 1) for array in images[count:])]
     parts = slabs * blocks
     shares = gram.reshape(parts, total // parts, total)
     shares = lax.all_to_all(shares, ("dom", "blk"), split_axis=0, concat_axis=0, tiled=True)
-    pieces = (*done, *partials, *other_partials, *centers, *other_centers, *late_one, *late_two)
-    return tuple(call(
-        functools.partial(last_kernel, slabs, blocks),
-        (whole, jax.ShapeDtypeStruct((total // parts, total), F32)),
-        (shares, applied, faces, *pieces),
-        turning(CORES * count),
-        [VMEM, ANY] + [VMEM] * (1 + len(pieces)),
-        [ANY, VMEM],
-        aliases={1: 0},
-    ))
+    done = [near_mine, *images[:count], *(swap(array, 1) for array in (near_theirs, *images[count:]))]
+    pieces = (
+        late_two, late_one, *done, near_partial, *partials, other_partial, *other_partials,
+        center, *centers, other, *other_centers,
+    )
+    applied, = call(
+        functools.partial(late_kernel, chips),
+        (whole,),
+        (faces, *pieces),
+        [
+            pltpu.VMEM((blocks, columns * half, nz), F32),
+            pltpu.VMEM((blocks, columns, 1, half, nz), BF16),
+            pltpu.SemaphoreType.DMA((blocks,)),
+        ],
+        out_specs=[ANY],
+    )
+    reduced, = call(
+        functools.partial(sum_kernel, slabs, blocks), (jax.ShapeDtypeStruct((total // parts, total), F32),),
+        (after(shares, applied),)
+    )
+    return applied, reduced
 
 
 def solution(mesh):

time: 61.9 us -> 53.9 us (0.87)
  waiting for transfers between devices: 16.6 us -> 8.25 us
  starting transfers between devices: 23.7 us -> 19.7 us
  local copies, waits for them, and re-layouts: 6.55 us -> 9.93 us
  other arithmetic: 0.03 us -> 0.87 us
    ppermute x6, waiting for transfers between devices: 7.74 us -> 1.67 us  [exchange(): return lax.ppermute(array, ('dom', 'blk'), pairs)]
    all_to_all x1, starting transfers between devices: 9.12 us -> 4.78 us  [per_device(): lax.all_to_all(shares, ('dom', 'blk'), split_axis=0, concat_axis=0, tiled...]
    unnamed x18 -> x36, local copies, waits for them, and re-layouts: 6.51 us -> 9.89 us
    ppermute x8, waiting for transfers between devices: 8.83 us -> 6.58 us  [swap(): return lax.ppermute(array, 'blk', [(i, i ^ s) for i in range(blocks)])]
    ppermute x8, starting transfers between devices: 3.37 us -> 4.38 us  [swap(): return lax.ppermute(array, 'blk', [(i, i ^ s) for i in range(blocks)])]
    concatenate x1, other arithmetic: 0.03 us -> 0.87 us  [per_device(): late = jnp.concatenate(late)]
    ppermute x6, starting transfers between devices: 11.3 us -> 10.5 us  [exchange(): return lax.ppermute(array, ('dom', 'blk'), pairs)]
  transfers between devices with their start and end apart: 15 -> 15, of which waited for: 4 -> 5; matrix products, arithmetic and copies ran while one was open for 0% -> 2% of each run, Pallas kernels for 11% -> 18%
where the time goes in v11:
time: 53.9 us; the launch traced here: 53.3 us
  starting transfers between devices  19.7 us (37%)
  Pallas kernels  13.7 us (25%)
  local copies, waits for them, and re-layouts  9.93 us (18%)
  waiting for transfers between devices  8.25 us (15%)
  between operations  0.88 us (2%)
  other arithmetic  0.87 us (2%)
    ppermute x6, starting transfers between devices, exchange(): return lax.ppermute(array, ('dom', 'blk'), pairs)  10.5 us
    pallas_call x7, Pallas kernels, call(): pl.pallas_call(kernel, out_shape=out_shape, in_specs=specs or [VMEM] * le...  10.5 us
    unnamed x36, local copies, waits for them, and re-layouts  9.89 us
    ppermute x8, waiting for transfers between devices, swap(): return lax.ppermute(array, 'blk', [(i, i ^ s) for i in range(blocks)])  6.58 us
    all_to_all x1, starting transfers between devices, per_device(): lax.all_to_all(shares, ('dom', 'blk'), split_axis=0, concat_axis=0, tiled...  4.78 us
    ppermute x8, starting transfers between devices, swap(): return lax.ppermute(array, 'blk', [(i, i ^ s) for i in range(blocks)])  4.38 us
    pallas_call x1, Pallas kernels, prepare(): pl.pallas_call(functools.partial(prepare_kernel, chips), out_shape=[jax.S...  3.21 us
    ppermute x6, waiting for transfers between devices, exchange(): return lax.ppermute(array, ('dom', 'blk'), pairs)  1.67 us
  transfers between devices with their start and end apart: 15, of which 5 were waited for; matrix products, arithmetic and copies ran while one was open for 2% of the time, Pallas kernels for 18%

profile of v11, /device:TPU:0, one launch (start us, length us, event | category | flops | bytes accessed | tf_op | source)
XLA Modules:
  0.0 53.3 jit_solution(17276441978086010961)
XLA Ops:
  0.6 3.2 %shard_map.59 = (bf16[17,64,128]{2,1,0:T(8,128)(2,1)S(1)}, bf16[34,64,128]{2,1,0:T(8,128)(2,1)S(1)}, bf16[18,64,128]{2,1,0:T(8,128)(2,1)S(1)}, bf16[16,64,128]{2,1,0:T(8,128)(2,1)S(1)}) custom-call(bf16[64,1,64,128]{3,2,1,0:T(8,128)(2,1)} %basis_hbm.1, s32[1,64,128]{2,1,0:T(8,128)} %zone_ref.1, f32[16]{0:T(128)} %cond_ref.1), custom_call_target="tpu_custom_call" | custom-call | tf_op jit(solution)/shard_map/pallas_call | solution.py:99
  3.8 0.5 collective-permute-start
  4.4 2.6 %collective-permute-start.3 = (bf16[16,64,128]{2,1,0:T(8,128)(2,1)S(1)}, bf16[16,64,128]{2,1,0:T(8,128)(2,1)S(1)}, u32[]{:S(2)}, u32[]{:S(2)}) collective-permute-start(bf16[16,64,128]{2,1,0:T(8,128)(2,1)S(1)} %get-tuple-element.35), channel_id=1, source_target_pairs={{0,2},{1,3},{2,0},{3,1},{4,6},{5,7},{6,4},{7,5},{8,10},{9,11},{10,... | collective-permute-start | bytes 786440 | tf_op jit(solution)/shard_map/ppermute | solution.py:394
  6.9 0.1 collective-permute-start.7
  7.0 2.0 %collective-permute-start.1 = (bf16[17,64,128]{2,1,0:T(8,128)(2,1)S(1)}, bf16[17,64,128]{2,1,0:T(8,128)(2,1)S(1)}, u32[]{:S(2)}, u32[]{:S(2)}) collective-permute-start(bf16[17,64,128]{2,1,0:T(8,128)(2,1)S(1)} %get-tuple-element.32), channel_id=1, source_target_pairs={{0,4},{1,5},{2,6},{3,7},{4,0},{5,1},{6,2},{7,3},{8,12},{9,13},{10,... | collective-permute-start | bytes 835592 | tf_op jit(solution)/shard_map/ppermute | solution.py:402
  9.0 0.7 %collective-permute-start.2 = (bf16[17,64,128]{2,1,0:T(8,128)(2,1)S(1)}, bf16[17,64,128]{2,1,0:T(8,128)(2,1)S(1)}, u32[]{:S(2)}, u32[]{:S(2)}) collective-permute-start(bf16[17,64,128]{2,1,0:T(8,128)(2,1)S(1)} %get-tuple-element.32), channel_id=1, source_target_pairs={{4,8},{5,9},{6,10},{7,11},{8,4},{9,5},{10,6},{11,7},{20,24},{21,25... | collective-permute-start | bytes 835592 | tf_op jit(solution)/shard_map/ppermute | solution.py:402
  9.7 0.0 collective-permute-done.other.refs_2_.refs_10_
  9.7 0.0 copy-start.13
  9.7 0.7 %copy-done.13 = s32[1,64,128]{2,1,0:T(8,128)S(1)} copy-done((s32[1,64,128]{2,1,0:T(8,128)S(1)}, s32[1,64,128]{2,1,0:T(8,128)}, u32[]{:S(2)}) %copy-start.13) | copy-done | bytes 32792
  10.5 0.7 %copy-done.14 = f32[16]{0:T(128)S(1)} copy-done((f32[16]{0:T(128)S(1)}, f32[16]{0:T(128)}, u32[]{:S(2)}) %copy-start.14) | copy-done | bytes 88
  11.1 0.7 %copy-done.17 = f32[16]{0:T(128)S(1)} copy-done((f32[16]{0:T(128)S(1)}, f32[16]{0:T(128)}, u32[]{:S(2)}) %copy-start.17) | copy-done | bytes 88
  11.8 1.5 %shard_map.60 = (f32[6,32,128]{2,1,0:T(8,128)S(1)}, f32[32,64,128]{2,1,0:T(8,128)S(1)}, f32[8,64,128]{2,1,0:T(8,128)S(1)}, bf16[16,64,128]{2,1,0:T(8,128)(2,1)S(1)}) custom-call(s32[1,64,128]{2,1,0:T(8,128)S(1)} %copy-done.13, f32[16]{0:T(128)S(1)} %copy-done.14, f32[16]{0:T(128)S(1)} %copy-done.17, ...), custom_call_target="tpu_custom_call" | custom-call | flops 1073741824 | bytes 134217728 | tf_op jit(solution)/shard_map/pallas_call | solution.py:379
  13.3 0.0 copy-start.4
  13.3 0.8 %collective-permute-done.3.refs_1_ = bf16[16,64,128]{2,1,0:T(8,128)(2,1)S(1)} collective-permute-done((bf16[16,64,128]{2,1,0:T(8,128)(2,1)S(1)}, bf16[16,64,128]{2,1,0:T(8,128)(2,1)S(1)}, u32[]{:S(2)}, u32[]{:S(2)}) %collective-permute-start.3) | collective-permute-done | bytes 262176 | tf_op jit(solution)/shard_map/ppermute | solution.py:394
  14.1 0.0 collective-permute-start.4
  14.1 1.7 %collective-permute-done.1.one = bf16[17,64,128]{2,1,0:T(8,128)(2,1)S(1)} collective-permute-done((bf16[17,64,128]{2,1,0:T(8,128)(2,1)S(1)}, bf16[17,64,128]{2,1,0:T(8,128)(2,1)S(1)}, u32[]{:S(2)}, u32[]{:S(2)}) %collective-permute-start.1) | collective-permute-done | bytes 278560 | tf_op jit(solution)/shard_map/ppermute | solution.py:402
  15.7 4.4 %collective-permute-done.7.refs_0_ = bf16[18,64,128]{2,1,0:T(8,128)(2,1)S(1)} collective-permute-done((bf16[18,64,128]{2,1,0:T(8,128)(2,1)S(1)}, bf16[18,64,128]{2,1,0:T(8,128)(2,1)S(1)}, u32[]{:S(2)}, u32[]{:S(2)}) %collective-permute-start.7) | collective-permute-done | bytes 294944 | tf_op jit(solution)/shard_map/ppermute | solution.py:394
  20.2 0.7 %collective-permute-start.10 = (bf16[18,64,128]{2,1,0:T(8,128)(2,1)S(1)}, bf16[18,64,128]{2,1,0:T(8,128)(2,1)S(1)}, u32[]{:S(2)}, u32[]{:S(2)}) collective-permute-start(bf16[18,64,128]{2,1,0:T(8,128)(2,1)S(1)} %collective-permute-done.7.refs_0_), channel_id=1, source_target_pairs={{4,8},{5,9},{6,10},{7,11},{8,4},{9,5},{10,6},{11,7},{20,24},{21,25... | collective-permute-start | bytes 884744 | tf_op jit(solution)/shard_map/ppermute | solution.py:402
  20.8 4.7 %collective-permute-start.11 = (bf16[18,64,128]{2,1,0:T(8,128)(2,1)S(1)}, bf16[18,64,128]{2,1,0:T(8,128)(2,1)S(1)}, u32[]{:S(2)}, u32[]{:S(2)}) collective-permute-start(bf16[18,64,128]{2,1,0:T(8,128)(2,1)S(1)} %collective-permute-done.7.refs_0_), channel_id=1, source_target_pairs={{0,4},{1,5},{2,6},{3,7},{4,0},{5,1},{6,2},{7,3},{8,12},{9,13},{10,... | collective-permute-start | bytes 884744 | tf_op jit(solution)/shard_map/ppermute | solution.py:402
  25.5 0.0 collective-permute-done.2.two
  25.6 0.1 collective-permute-start.8
  25.7 0.6 %collective-permute-start.9 = (bf16[2,64,128]{2,1,0:T(8,128)(2,1)S(1)}, bf16[2,64,128]{2,1,0:T(8,128)(2,1)S(1)}, u32[]{:S(2)}, u32[]{:S(2)}) collective-permute-start(bf16[2,64,128]{2,1,0:T(8,128)(2,1)S(1)} %slice.15), channel_id=1, source_target_pairs={{0,1},{1,0},{2,3},{3,2},{4,5},{5,4},{6,7},{7,6},{8,9},{9,8},{10,11... | collective-permute-start | bytes 98312 | tf_op jit(solution)/shard_map/ppermute | solution.py:394
  26.2 0.0 collective-permute-done.4.refs_4_
  26.2 0.9 %pad_maximum_fusion = bf16[32,64,128]{2,1,0:T(8,128)(2,1)} fusion(bf16[8,64,128]{2,1,0:T(8,128)(2,1)S(1)} %slice.17, bf16[8,64,128]{2,1,0:T(8,128)(2,1)S(1)} %slice.16, bf16[16,64,128]{2,1,0:T(8,128)(2,1)S(1)} %get-tuple-element.34), kind=kLoop, calls=%fused_computation | loop fusion | flops 524288 | bytes 1048576 | tf_op jit(solution)/shard_map/concatenate | solution.py:432
  27.1 1.5 %collective-permute-start.5 = (bf16[32,64,128]{2,1,0:T(8,128)(2,1)}, bf16[32,64,128]{2,1,0:T(8,128)(2,1)}, u32[]{:S(2)}, u32[]{:S(2)}) collective-permute-start(bf16[32,64,128]{2,1,0:T(8,128)(2,1)} %pad_maximum_fusion), channel_id=1, source_target_pairs={{4,8},{5,9},{6,10},{7,11},{8,4},{9,5},{10,6},{11,7},{20,24},{21,25... | collective-permute-start | bytes 1572872 | tf_op jit(solution)/shard_map/ppermute | solution.py:402
  28.6 0.0 collective-permute-done.9.refs_3_
  28.6 1.0 %collective-permute-start.6 = (bf16[32,64,128]{2,1,0:T(8,128)(2,1)}, bf16[32,64,128]{2,1,0:T(8,128)(2,1)}, u32[]{:S(2)}, u32[]{:S(2)}) collective-permute-start(bf16[32,64,128]{2,1,0:T(8,128)(2,1)} %pad_maximum_fusion), channel_id=1, source_target_pairs={{0,4},{1,5},{2,6},{3,7},{4,0},{5,1},{6,2},{7,3},{8,12},{9,13},{10,... | collective-permute-start | bytes 1572872 | tf_op jit(solution)/shard_map/ppermute | solution.py:402
  29.6 0.5 shard_map.61
  30.1 0.0 copy-done.4
  30.1 0.0 copy-start.9
  30.1 0.0 copy-start.15
  30.1 0.0 collective-permute-done.8.refs_2_
  30.1 0.9 %shard_map.62 = (bf16[34,64,128]{2,1,0:T(8,128)(2,1)S(1)}, f32[32,64,128]{2,1,0:T(8,128)S(1)}, bf16[34,64,128]{2,1,0:T(8,128)(2,1)S(1)}, f32[8,64,128]{2,1,0:T(8,128)S(1)}) custom-call(f32[6,32,128]{2,1,0:T(8,128)S(1)} %get-tuple-element.39.coef, bf16[18,64,128]{2,1,0:T(8,128)(2,1)S(1)} %collective-permute-done.7.refs_0_, ...), custom_call_target="tpu_custom_call" | custom-call | flops 1 | bytes 1 | tf_op jit(solution)/shard_map/pallas_call | solution.py:379
  31.1 0.0 copy-start.2
  31.1 0.0 copy-start.6
  31.1 0.0 copy-done.9
  31.1 0.0 copy-done
  31.1 2.4 %shard_map.63 = (bf16[256,4096]{1,0:T(8,128)(2,1)S(1)}, f32[256,128]{1,0:T(8,128)S(1)}, f32[128,256]{1,0:T(8,128)S(1)}) custom-call(f32[3,32,128]{2,1,0:T(8,128)S(1)} %get-tuple-element.33.faces, bf16[64,4096]{1,0:T(8,128)(2,1)S(1)} %get-tuple-element.38.flat, bf16[34,64,128]{2,1,0:T(8,128)(2,1)S(1)} %get-tuple-element.29.center.refs_0_.refs_8_, ...), custom_call_target="tpu_custom_call" | custom-call | flops 1 | bytes 1 | tf_op jit(solution)/shard_map/pallas_call | solution.py:379
  33.5 0.0 copy-done.15
  33.5 0.0 copy-done.2
  33.5 0.0 collective-permute-done.10.refs_2_
  33.5 0.0 collective-permute-done.11.refs_3_
  33.5 1.2 %shard_map.64 = (bf16[8,64,128]{2,1,0:T(8,128)(2,1)S(1)}, bf16[8,64,128]{2,1,0:T(8,128)(2,1)S(1)}, f32[256,256]{1,0:T(8,128)S(1)}) custom-call(f32[3,32,128]{2,1,0:T(8,128)S(1)} %get-tuple-element.33.faces, bf16[256,4096]{1,0:T(8,128)(2,1)S(1)} %get-tuple-element.46.left, f32[256,128]{1,0:T(8,128)S(1)} %get-tuple-element.47.tall, ...), custom_call_target="tpu_custom_call" | custom-call | flops 1 | bytes 1 | tf_op jit(solution)/shard_map/pallas_call | solution.py:379
  34.8 0.0 copy-done.6
  34.8 0.0 copy-start.8
  34.8 0.7 %copy-done.8 = f32[256,256]{1,0:T(8,128)} copy-done((f32[256,256]{1,0:T(8,128)}, f32[256,256]{1,0:T(8,128)S(1)}, u32[]{:S(2)}) %copy-start.8) | copy-done | bytes 262168
  35.5 0.6 %copy-done.11 = bf16[8,64,128]{2,1,0:T(8,128)(2,1)} copy-done((bf16[8,64,128]{2,1,0:T(8,128)(2,1)}, bf16[8,64,128]{2,1,0:T(8,128)(2,1)S(1)}, u32[]{:S(2)}) %copy-start.11) | copy-done | bytes 131096
  36.1 0.6 %copy-done.16 = bf16[8,64,128]{2,1,0:T(8,128)(2,1)} copy-done((bf16[8,64,128]{2,1,0:T(8,128)(2,1)}, bf16[8,64,128]{2,1,0:T(8,128)(2,1)S(1)}, u32[]{:S(2)}) %copy-start.16) | copy-done | bytes 131096
  36.8 4.8 %all-to-all-start = ((f32[16,16,256]{2,1,0:T(8,128)}), f32[16,16,256]{2,1,0:T(8,128)S(1)}, u32[]{:S(2)}, u32[]{:S(2)}) async-start(f32[16,16,256]{2,1,0:T(8,128)} %bitcast.1), calls=%async_computation | async-start | bytes 524288 | tf_op jit(solution)/shard_map/all_to_all | solution.py:470
  41.6 0.4 collective-permute-start.12
  42.0 0.2 collective-permute-start.13
  42.1 1.0 %collective-permute-done.12.refs_2_ = bf16[8,64,128]{2,1,0:T(8,128)(2,1)S(1)} collective-permute-done((bf16[8,64,128]{2,1,0:T(8,128)(2,1)}, bf16[8,64,128]{2,1,0:T(8,128)(2,1)S(1)}, u32[]{:S(2)}, u32[]{:S(2)}) %collective-permute-start.12) | collective-permute-done | bytes 131104 | tf_op jit(solution)/shard_map/ppermute | solution.py:394
  43.2 0.3 collective-permute-done.13.refs_3_
  43.5 0.0 collective-permute-done.5.two
  43.5 0.0 collective-permute-done.6.one
  43.5 1.1 %copy-done.1 = bf16[34,64,128]{2,1,0:T(8,128)(2,1)S(1)} copy-done((bf16[34,64,128]{2,1,0:T(8,128)(2,1)S(1)}, bf16[34,64,128]{2,1,0:T(8,128)(2,1)}, u32[]{:S(2)}) %copy-start.1) | copy-done | bytes 557080
  44.6 1.1 %copy-done.3 = bf16[34,64,128]{2,1,0:T(8,128)(2,1)S(1)} copy-done((bf16[34,64,128]{2,1,0:T(8,128)(2,1)S(1)}, bf16[34,64,128]{2,1,0:T(8,128)(2,1)}, u32[]{:S(2)}) %copy-start.3) | copy-done | bytes 557080
  45.6 0.9 %copy-done.5 = f32[8,64,128]{2,1,0:T(8,128)S(1)} copy-done((f32[8,64,128]{2,1,0:T(8,128)S(1)}, f32[8,64,128]{2,1,0:T(8,128)}, u32[]{:S(2)}) %copy-start.5) | copy-done | bytes 262168
  46.6 0.9 %copy-done.7 = f32[8,64,128]{2,1,0:T(8,128)S(1)} copy-done((f32[8,64,128]{2,1,0:T(8,128)S(1)}, f32[8,64,128]{2,1,0:T(8,128)}, u32[]{:S(2)}) %copy-start.7) | copy-done | bytes 262168
  47.5 0.9 %copy-done.10 = bf16[8,64,128]{2,1,0:T(8,128)(2,1)S(1)} copy-done((bf16[8,64,128]{2,1,0:T(8,128)(2,1)S(1)}, bf16[8,64,128]{2,1,0:T(8,128)(2,1)}, u32[]{:S(2)}) %copy-start.10) | copy-done | bytes 131096
  48.5 0.9 %copy-done.12 = bf16[8,64,128]{2,1,0:T(8,128)(2,1)S(1)} copy-done((bf16[8,64,128]{2,1,0:T(8,128)(2,1)S(1)}, bf16[8,64,128]{2,1,0:T(8,128)(2,1)}, u32[]{:S(2)}) %copy-start.12) | copy-done | bytes 131096
  49.4 3.2 %shard_map.65 = bf16[256,1,16,128]{3,2,1,0:T(8,128)(2,1)} custom-call(f32[3,32,128]{2,1,0:T(8,128)S(1)} %get-tuple-element.33.faces, bf16[32,64,128]{2,1,0:T(8,128)(2,1)} %collective-permute-done.5.two, bf16[32,64,128]{2,1,0:T(8,128)(2,1)} %collective-permute-done.6.one, bf16[8,64,128]{2,1,0:T(8,128)(2,1)S(1)} %copy-done.10, ...), custom_call_target="tpu_custom_call" | custom-call | flops 1 | bytes 1 | tf_op jit(solution)/shard_map/pallas_call | solution.py:379
  52.5 0.0 all-to-all-done.shares
  52.5 0.8 %shard_map.66 = f32[16,256]{1,0:T(8,128)} custom-call(f32[16,16,256]{2,1,0:T(8,128)S(1)} %all-to-all-done.shares), custom_call_target="tpu_custom_call" | custom-call | flops 1 | bytes 1 | tf_op jit(solution)/shard_map/pallas_call | solution.py:379
  (15 shorter events, 0.1 us)
Async XLA Ops:
  3.8 5.9 %collective-permute-start = (bf16[34,64,128]{2,1,0:T(8,128)(2,1)S(1)}, bf16[34,64,128]{2,1,0:T(8,128)(2,1)S(1)}, u32[]{:S(2)}, u32[]{:S(2)}) collective-permute-start(bf16[34,64,128]{2,1,0:T(8,128)(2,1)S(1)} %get-tuple-element.29.center.refs_0_.refs_8_), channel_id=1, source_target_pairs={{0,1},{1,0},{2,3},{3,2},{4,5},{5,4},{6,7},{7,6},{8,9},{9,8},{10,11... | collective-permute-start | bytes 1671176 | tf_op jit(solution)/shard_map/ppermute | solution.py:394
  4.4 9.7 %collective-permute-start.3 = (bf16[16,64,128]{2,1,0:T(8,128)(2,1)S(1)}, bf16[16,64,128]{2,1,0:T(8,128)(2,1)S(1)}, u32[]{:S(2)}, u32[]{:S(2)}) collective-permute-start(bf16[16,64,128]{2,1,0:T(8,128)(2,1)S(1)} %get-tuple-element.35), channel_id=1, source_target_pairs={{0,2},{1,3},{2,0},{3,1},{4,6},{5,7},{6,4},{7,5},{8,10},{9,11},{10,... | collective-permute-start | bytes 786440 | tf_op jit(solution)/shard_map/ppermute | solution.py:394
  6.9 13.2 %collective-permute-start.7 = (bf16[18,64,128]{2,1,0:T(8,128)(2,1)S(1)}, bf16[18,64,128]{2,1,0:T(8,128)(2,1)S(1)}, u32[]{:S(2)}, u32[]{:S(2)}) collective-permute-start(bf16[18,64,128]{2,1,0:T(8,128)(2,1)S(1)} %get-tuple-element.40), channel_id=1, source_target_pairs={{0,2},{1,3},{2,0},{3,1},{4,6},{5,7},{6,4},{7,5},{8,10},{9,11},{10,... | collective-permute-start | bytes 884744 | tf_op jit(solution)/shard_map/ppermute | solution.py:394
  7.0 8.7 %collective-permute-start.1 = (bf16[17,64,128]{2,1,0:T(8,128)(2,1)S(1)}, bf16[17,64,128]{2,1,0:T(8,128)(2,1)S(1)}, u32[]{:S(2)}, u32[]{:S(2)}) collective-permute-start(bf16[17,64,128]{2,1,0:T(8,128)(2,1)S(1)} %get-tuple-element.32), channel_id=1, source_target_pairs={{0,4},{1,5},{2,6},{3,7},{4,0},{5,1},{6,2},{7,3},{8,12},{9,13},{10,... | collective-permute-start | bytes 835592 | tf_op jit(solution)/shard_map/ppermute | solution.py:402
  9.0 16.5 %collective-permute-start.2 = (bf16[17,64,128]{2,1,0:T(8,128)(2,1)S(1)}, bf16[17,64,128]{2,1,0:T(8,128)(2,1)S(1)}, u32[]{:S(2)}, u32[]{:S(2)}) collective-permute-start(bf16[17,64,128]{2,1,0:T(8,128)(2,1)S(1)} %get-tuple-element.32), channel_id=1, source_target_pairs={{4,8},{5,9},{6,10},{7,11},{8,4},{9,5},{10,6},{11,7},{20,24},{21,25... | collective-permute-start | bytes 835592 | tf_op jit(solution)/shard_map/ppermute | solution.py:402
  9.7 0.8 %copy-start.13 = (s32[1,64,128]{2,1,0:T(8,128)S(1)}, s32[1,64,128]{2,1,0:T(8,128)}, u32[]{:S(2)}) copy-start(s32[1,64,128]{2,1,0:T(8,128)} %zone_ref.1) | copy-start | bytes 98308
  10.5 0.7 %copy-start.14 = (f32[16]{0:T(128)S(1)}, f32[16]{0:T(128)}, u32[]{:S(2)}) copy-start(f32[16]{0:T(128)} %cond_ref.1) | copy-start | bytes 196
  11.1 0.7 %copy-start.17 = (f32[16]{0:T(128)S(1)}, f32[16]{0:T(128)}, u32[]{:S(2)}) copy-start(f32[16]{0:T(128)} %heat_ref.1) | copy-start | bytes 196
  11.8 19.3 %copy-start = (bf16[34,64,128]{2,1,0:T(8,128)(2,1)}, bf16[34,64,128]{2,1,0:T(8,128)(2,1)S(1)}, u32[]{:S(2)}) copy-start(bf16[34,64,128]{2,1,0:T(8,128)(2,1)S(1)} %collective-permute-done.other.refs_2_.refs_10_) | copy-start | bytes 1671172
  13.3 16.8 %copy-start.4 = (f32[8,64,128]{2,1,0:T(8,128)}, f32[8,64,128]{2,1,0:T(8,128)S(1)}, u32[]{:S(2)}) copy-start(f32[8,64,128]{2,1,0:T(8,128)S(1)} %get-tuple-element.52.refs_6_) | copy-start | bytes 786436
  14.1 12.1 %collective-permute-start.4 = (bf16[16,64,128]{2,1,0:T(8,128)(2,1)S(1)}, bf16[16,64,128]{2,1,0:T(8,128)(2,1)S(1)}, u32[]{:S(2)}, u32[]{:S(2)}) collective-permute-start(bf16[16,64,128]{2,1,0:T(8,128)(2,1)S(1)} %collective-permute-done.3.refs_1_), channel_id=1, source_target_pairs={{0,1},{1,0},{2,3},{3,2},{4,5},{5,4},{6,7},{7,6},{8,9},{9,8},{10,11... | collective-permute-start | bytes 786440 | tf_op jit(solution)/shard_map/ppermute | solution.py:394
  20.2 13.4 %collective-permute-start.10 = (bf16[18,64,128]{2,1,0:T(8,128)(2,1)S(1)}, bf16[18,64,128]{2,1,0:T(8,128)(2,1)S(1)}, u32[]{:S(2)}, u32[]{:S(2)}) collective-permute-start(bf16[18,64,128]{2,1,0:T(8,128)(2,1)S(1)} %collective-permute-done.7.refs_0_), channel_id=1, source_target_pairs={{4,8},{5,9},{6,10},{7,11},{8,4},{9,5},{10,6},{11,7},{20,24},{21,25... | collective-permute-start | bytes 884744 | tf_op jit(solution)/shard_map/ppermute | solution.py:402
  20.8 12.7 %collective-permute-start.11 = (bf16[18,64,128]{2,1,0:T(8,128)(2,1)S(1)}, bf16[18,64,128]{2,1,0:T(8,128)(2,1)S(1)}, u32[]{:S(2)}, u32[]{:S(2)}) collective-permute-start(bf16[18,64,128]{2,1,0:T(8,128)(2,1)S(1)} %collective-permute-done.7.refs_0_), channel_id=1, source_target_pairs={{0,4},{1,5},{2,6},{3,7},{4,0},{5,1},{6,2},{7,3},{8,12},{9,13},{10,... | collective-permute-start | bytes 884744 | tf_op jit(solution)/shard_map/ppermute | solution.py:402
  25.6 4.6 %collective-permute-start.8 = (bf16[16,64,128]{2,1,0:T(8,128)(2,1)S(1)}, bf16[16,64,128]{2,1,0:T(8,128)(2,1)S(1)}, u32[]{:S(2)}, u32[]{:S(2)}) collective-permute-start(bf16[16,64,128]{2,1,0:T(8,128)(2,1)S(1)} %slice.14), channel_id=1, source_target_pairs={{0,1},{1,0},{2,3},{3,2},{4,5},{5,4},{6,7},{7,6},{8,9},{9,8},{10,11... | collective-permute-start | bytes 786440 | tf_op jit(solution)/shard_map/ppermute | solution.py:394
  25.7 2.9 %collective-permute-start.9 = (bf16[2,64,128]{2,1,0:T(8,128)(2,1)S(1)}, bf16[2,64,128]{2,1,0:T(8,128)(2,1)S(1)}, u32[]{:S(2)}, u32[]{:S(2)}) collective-permute-start(bf16[2,64,128]{2,1,0:T(8,128)(2,1)S(1)} %slice.15), channel_id=1, source_target_pairs={{0,1},{1,0},{2,3},{3,2},{4,5},{5,4},{6,7},{7,6},{8,9},{9,8},{10,11... | collective-permute-start | bytes 98312 | tf_op jit(solution)/shard_map/ppermute | solution.py:394
  27.1 16.4 %collective-permute-start.5 = (bf16[32,64,128]{2,1,0:T(8,128)(2,1)}, bf16[32,64,128]{2,1,0:T(8,128)(2,1)}, u32[]{:S(2)}, u32[]{:S(2)}) collective-permute-start(bf16[32,64,128]{2,1,0:T(8,128)(2,1)} %pad_maximum_fusion), channel_id=1, source_target_pairs={{4,8},{5,9},{6,10},{7,11},{8,4},{9,5},{10,6},{11,7},{20,24},{21,25... | collective-permute-start | bytes 1572872 | tf_op jit(solution)/shard_map/ppermute | solution.py:402
  28.6 14.9 %collective-permute-start.6 = (bf16[32,64,128]{2,1,0:T(8,128)(2,1)}, bf16[32,64,128]{2,1,0:T(8,128)(2,1)}, u32[]{:S(2)}, u32[]{:S(2)}) collective-permute-start(bf16[32,64,128]{2,1,0:T(8,128)(2,1)} %pad_maximum_fusion), channel_id=1, source_target_pairs={{0,4},{1,5},{2,6},{3,7},{4,0},{5,1},{6,2},{7,3},{8,12},{9,13},{10,... | collective-permute-start | bytes 1572872 | tf_op jit(solution)/shard_map/ppermute | solution.py:402
  30.1 1.0 %copy-start.9 = (bf16[8,64,128]{2,1,0:T(8,128)(2,1)}, bf16[8,64,128]{2,1,0:T(8,128)(2,1)S(1)}, u32[]{:S(2)}) copy-start(bf16[8,64,128]{2,1,0:T(8,128)(2,1)S(1)} %get-tuple-element.37.refs_0_) | copy-start | bytes 393220
  30.1 3.4 %copy-start.15 = (bf16[8,64,128]{2,1,0:T(8,128)(2,1)}, bf16[8,64,128]{2,1,0:T(8,128)(2,1)S(1)}, u32[]{:S(2)}) copy-start(bf16[8,64,128]{2,1,0:T(8,128)(2,1)S(1)} %get-tuple-element.50) | copy-start | bytes 393220
  31.1 2.4 %copy-start.2 = (bf16[34,64,128]{2,1,0:T(8,128)(2,1)}, bf16[34,64,128]{2,1,0:T(8,128)(2,1)S(1)}, u32[]{:S(2)}) copy-start(bf16[34,64,128]{2,1,0:T(8,128)(2,1)S(1)} %get-tuple-element.44.refs_3_.refs_11_) | copy-start | bytes 1671172
  31.1 3.7 %copy-start.6 = (f32[8,64,128]{2,1,0:T(8,128)}, f32[8,64,128]{2,1,0:T(8,128)S(1)}, u32[]{:S(2)}) copy-start(f32[8,64,128]{2,1,0:T(8,128)S(1)} %get-tuple-element.53.refs_7_) | copy-start | bytes 786436
  34.8 0.7 %copy-start.8 = (f32[256,256]{1,0:T(8,128)}, f32[256,256]{1,0:T(8,128)S(1)}, u32[]{:S(2)}) copy-start(f32[256,256]{1,0:T(8,128)S(1)} %get-tuple-element.54) | copy-start | bytes 786436
  35.5 0.6 %copy-start.11 = (bf16[8,64,128]{2,1,0:T(8,128)(2,1)}, bf16[8,64,128]{2,1,0:T(8,128)(2,1)S(1)}, u32[]{:S(2)}) copy-start(bf16[8,64,128]{2,1,0:T(8,128)(2,1)S(1)} %get-tuple-element.49.refs_1_) | copy-start | bytes 393220
  36.1 0.6 %copy-start.16 = (bf16[8,64,128]{2,1,0:T(8,128)(2,1)}, bf16[8,64,128]{2,1,0:T(8,128)(2,1)S(1)}, u32[]{:S(2)}) copy-start(bf16[8,64,128]{2,1,0:T(8,128)(2,1)S(1)} %get-tuple-element.51) | copy-start | bytes 393220
  36.8 15.8 %all-to-all-start = ((f32[16,16,256]{2,1,0:T(8,128)}), f32[16,16,256]{2,1,0:T(8,128)S(1)}, u32[]{:S(2)}, u32[]{:S(2)}) async-start(f32[16,16,256]{2,1,0:T(8,128)} %bitcast.1), calls=%async_computation | async-start | bytes 524288 | tf_op jit(solution)/shard_map/all_to_all | solution.py:470
  41.6 1.6 %collective-permute-start.12 = (bf16[8,64,128]{2,1,0:T(8,128)(2,1)}, bf16[8,64,128]{2,1,0:T(8,128)(2,1)S(1)}, u32[]{:S(2)}, u32[]{:S(2)}) collective-permute-start(bf16[8,64,128]{2,1,0:T(8,128)(2,1)} %copy-done.15), channel_id=1, source_target_pairs={{0,1},{1,0},{2,3},{3,2},{4,5},{5,4},{6,7},{7,6},{8,9},{9,8},{10,11... | collective-permute-start | bytes 393224 | tf_op jit(solution)/shard_map/ppermute | solution.py:394
  42.0 1.6 %collective-permute-start.13 = (bf16[8,64,128]{2,1,0:T(8,128)(2,1)}, bf16[8,64,128]{2,1,0:T(8,128)(2,1)S(1)}, u32[]{:S(2)}, u32[]{:S(2)}) collective-permute-start(bf16[8,64,128]{2,1,0:T(8,128)(2,1)} %copy-done.16), channel_id=1, source_target_pairs={{0,1},{1,0},{2,3},{3,2},{4,5},{5,4},{6,7},{7,6},{8,9},{9,8},{10,11... | collective-permute-start | bytes 393224 | tf_op jit(solution)/shard_map/ppermute | solution.py:394
  43.5 1.1 %copy-start.1 = (bf16[34,64,128]{2,1,0:T(8,128)(2,1)S(1)}, bf16[34,64,128]{2,1,0:T(8,128)(2,1)}, u32[]{:S(2)}) copy-start(bf16[34,64,128]{2,1,0:T(8,128)(2,1)} %copy-done) | copy-start | bytes 1671172
  44.6 1.1 %copy-start.3 = (bf16[34,64,128]{2,1,0:T(8,128)(2,1)S(1)}, bf16[34,64,128]{2,1,0:T(8,128)(2,1)}, u32[]{:S(2)}) copy-start(bf16[34,64,128]{2,1,0:T(8,128)(2,1)} %copy-done.2) | copy-start | bytes 1671172
  45.6 0.9 %copy-start.5 = (f32[8,64,128]{2,1,0:T(8,128)S(1)}, f32[8,64,128]{2,1,0:T(8,128)}, u32[]{:S(2)}) copy-start(f32[8,64,128]{2,1,0:T(8,128)} %copy-done.4) | copy-start | bytes 786436
  46.6 0.9 %copy-start.7 = (f32[8,64,128]{2,1,0:T(8,128)S(1)}, f32[8,64,128]{2,1,0:T(8,128)}, u32[]{:S(2)}) copy-start(f32[8,64,128]{2,1,0:T(8,128)} %copy-done.6) | copy-start | bytes 786436
  47.5 0.9 %copy-start.10 = (bf16[8,64,128]{2,1,0:T(8,128)(2,1)S(1)}, bf16[8,64,128]{2,1,0:T(8,128)(2,1)}, u32[]{:S(2)}) copy-start(bf16[8,64,128]{2,1,0:T(8,128)(2,1)} %copy-done.9) | copy-start | bytes 393220
  48.5 0.9 %copy-start.12 = (bf16[8,64,128]{2,1,0:T(8,128)(2,1)S(1)}, bf16[8,64,128]{2,1,0:T(8,128)(2,1)}, u32[]{:S(2)}) copy-start(bf16[8,64,128]{2,1,0:T(8,128)(2,1)} %copy-done.11) | copy-start | bytes 393220

commit v12 on v11

--- a/solution.py
+++ b/solution.py
@@ -116,7 +116,7 @@
     return (*results[:2], results[2:1 + chips], results[1 + chips:])
 
 
-def plane_kernel(chips, zone_ref, cond_ref, heat_ref, center, other, coef, partial, other_partial, late_rows, cond_pad):
+def plane_kernel(chips, zone_ref, cond_ref, heat_ref, center, coef, partial, late_rows, late_terms, cond_pad):
     rows = partial.shape[0]
     nz = center.shape[2]
     ny = zone_ref.shape[1]
@@ -139,12 +139,15 @@
         coef[1 + which] = 0.5 * (own + node)
     coef[5] = own
     plane_rows(coef, center, partial)
-    core, late = lax.axis_index("blk") % CORES, halves()
-    part = rows // CORES // 2
-    plane_rows(coef, other, other_partial, (2 * core + 1 - late) * part)
-    for which, ref in enumerate((center, other)):
-        for i in range(part):
-            late_rows[which * part + i] = ref[(2 * core + late) * part + i + 1]
+    keep_late(center, partial, late_rows, late_terms)
+
+
+def keep_late(center, partial, late_rows, late_terms):
+    part = late_rows.shape[0]
+    first = (2 * (lax.axis_index("blk") % CORES) + 1 - halves()) * part
+    for i in range(part):
+        late_rows[i] = center[first + i + 1]
+        late_terms[i] = partial[first + i]
 
 
 def plane_rows(coef, center, partial, first=0):
@@ -242,17 +245,39 @@
     center[2 * CORES * part + 1] = outer[1]
 
 
-def gather_kernel(chips, coef, *refs):
+def gather_kernel(chips, coef, other, *refs):
     count = chips - 1
     firsts, seconds, other_firsts, outers, other_seconds = (refs[i * count:(i + 1) * count] for i in range(5))
-    centers, partials, other_centers, other_partials = (refs[i * count:(i + 1) * count] for i in range(5, 9))
+    centers, partials, other_centers = (refs[i * count:(i + 1) * count] for i in range(5, 8))
+    refs = refs[8 * count:]
+    late_rows, late_terms = refs[:count + chips], refs[count + chips:]
+    part = late_rows[0].shape[0]
     core, late = lax.axis_index("blk") % CORES, halves()
+    first = (2 * core + 1 - late) * part
     for k in range(count):
         halo = seconds[k].shape[0]
         gather(firsts[k], firsts[k].at[pl.ds(halo, 2)], seconds[k], core, centers[k])
         gather(other_firsts[k], outers[k], other_seconds[k], 1 - core, other_centers[k])
         plane_rows(coef, centers[k], partials[k])
-        plane_rows(coef, other_centers[k], other_partials[k], (2 * core + 1 - late) * (halo // CORES))
+        keep_late(centers[k], partials[k], late_rows[k], late_terms[k])
+    for k, center in enumerate((other, *other_centers)):
+        plane_rows(coef, center, late_terms[count + k], first)
+        for i in range(part):
+            late_rows[count + k][i] = center[first + i + 1]
+
+
+def pack_kernel(chips, center, other, *refs):
+    count = chips - 1
+    seconds, other_seconds, packed = refs[:count], refs[count:2 * count], refs[2 * count]
+    part = packed.shape[0] // (CORES * chips)
+    first = (2 * (lax.axis_index("blk") % CORES) + halves()) * part
+    for i in range(part):
+        packed[i] = center[first + i + 1]
+        packed[part + i] = other[first + i + 1]
+    for k in range(count):
+        start = (k + 1) * CORES * part
+        packed[start:start + part] = seconds[k][0:part]
+        packed[start + part:start + 2 * part] = other_seconds[k][part:2 * part]
 
 
 def left_kernel(chips, faces, flat, *refs):
@@ -322,8 +347,8 @@
         for i in range(part):
             y = first + i
             at = (CORES * (s % chips) + s // chips) * part + i
-            p = partials[s][y] if s < chips else partials[s][i]
-            v, a, b = (x.astype(F32) for x in (centers[s][y + 1], one[at], two[at]))
+            p = partials[s][i]
+            v, a, b = (x.astype(F32) for x in (centers[s][i], one[at], two[at]))
             image = with_dom(faces, y, v, p, a, b).astype(BF16).astype(F32)
             scratch[pl.ds((1 - late) * part + i, columns, stride=half), :] = image
             scratch[pl.ds(late * part + i, columns, stride=half), :] = done[s][i].astype(F32)
@@ -387,6 +412,9 @@
             cost_estimate=cost,
         )(*inputs)
 
+    def hbm(array):
+        return pltpu.with_memory_space_constraint(array, pltpu.HBM)
+
     def after(value, *others):
         return lax.optimization_barrier((value, *others))[0]
 
@@ -401,22 +429,20 @@
         ]
         return lax.ppermute(array, ("dom", "blk"), pairs)
 
+    late_shape = pltpu.HBM((part, columns, nz), BF16)
+    terms_shape = pltpu.HBM((part, columns, nz), F32)
+
     near, center, firsts, seconds = prepare(basis, zone, cond_table, chips)
-    other = swap(center, 1)
-    firsts = [swap(array, CORES * (k + 1)) for k, array in enumerate(firsts)]
     two = exchange(near, 1)
     one = exchange(near, 0)
-    coef, near_partial, other_partial, late_near = call(
+    firsts = [swap(array, CORES * (k + 1)) for k, array in enumerate(firsts)]
+    other = swap(center, 1)
+    coef, near_partial, late_rows, late_terms = call(
         functools.partial(plane_kernel, chips),
-        (
-            jax.ShapeDtypeStruct((6, rows, nz), F32),
-            partial,
-            jax.ShapeDtypeStruct((part, columns, nz), F32),
-            image,
-        ),
-        (zone, cond_table, heat_table, center, other),
+        (jax.ShapeDtypeStruct((6, rows, nz), F32), partial, late_shape, terms_shape),
+        (hbm(zone), hbm(cond_table), hbm(heat_table), after(center, other)),
         [pltpu.VMEM((ny + 16, nz), F32)],
-        [VMEM, SMEM, SMEM, VMEM, VMEM],
+        [VMEM, SMEM, SMEM, VMEM],
         cost=costly,
     )
     seconds = [swap(array, CORES * (k + 1)) for k, array in enumerate(seconds)]
@@ -426,16 +452,17 @@
     other_firsts = [swap(after(array, two)[:half], 1) for array in firsts]
     outers = [swap(after(array, two)[half:], 1) for array in firsts]
     other_seconds = [swap(after(array, coef), 1) for array in seconds]
-    late = [late_near]
-    for mine, theirs in zip(seconds, other_seconds):
-        late += [mine[:part], theirs[part:]]
-    late = jnp.concatenate(late)
+    late, = call(
+        functools.partial(pack_kernel, chips),
+        (jax.ShapeDtypeStruct((CORES * chips * part, columns, nz), BF16),),
+        (center, other, *seconds, *other_seconds),
+    )
     late_two, late_one = exchange(late, 1), exchange(late, 0)
 
     near_mine, near_theirs, faces, near_flat = call(
         near_kernel,
         (
-            half_image,
+            late_shape,
             half_image,
             jax.ShapeDtypeStruct((3, rows, nz), F32),
             jax.ShapeDtypeStruct((columns, rows * nz), BF16),
@@ -445,10 +472,13 @@
     results = call(
         functools.partial(gather_kernel, chips),
         [center_shape] * count + [partial] * count + [center_shape] * count
-        + [jax.ShapeDtypeStruct((part, columns, nz), F32)] * count,
-        (after(coef, faces), *firsts, *seconds, *other_firsts, *outers, *other_seconds),
-    )
-    centers, partials, other_centers, other_partials = (results[i * count:(i + 1) * count] for i in range(4))
+        + [late_shape] * (count + chips) + [terms_shape] * (count + chips),
+        (after(coef, faces), other, *firsts, *seconds, *other_firsts, *outers, *other_seconds),
+    )
+    centers, partials, other_centers = (results[i * count:(i + 1) * count] for i in range(3))
+    results = results[3 * count:]
+    late_rows = [late_rows, *results[:count + chips]]
+    late_terms = [late_terms, *results[count + chips:]]
     left, tall, flatter = call(
         functools.partial(left_kernel, chips),
         (
@@ -461,7 +491,7 @@
     )
     *images, gram = call(
         functools.partial(gram_kernel, chips, weight),
-        [half_image] * (2 * count) + [jax.ShapeDtypeStruct((total, total), F32)],
+        [late_shape] * (2 * count) + [pltpu.HBM((total, total), F32)],
         (faces, left, tall, flatter, *partials, *centers, *early_two, *early_one),
         [pltpu.VMEM((columns, rows * nz // 2), BF16), pltpu.VMEM((total, chips * columns), F32)],
     )
@@ -469,14 +499,11 @@
     shares = gram.reshape(parts, total // parts, total)
     shares = lax.all_to_all(shares, ("dom", "blk"), split_axis=0, concat_axis=0, tiled=True)
     done = [near_mine, *images[:count], *(swap(array, 1) for array in (near_theirs, *images[count:]))]
-    pieces = (
-        late_two, late_one, *done, near_partial, *partials, other_partial, *other_partials,
-        center, *centers, other, *other_centers,
-    )
+    pieces = [hbm(x) for x in (faces, late_two, late_one, *done, *late_terms, *late_rows)]
     applied, = call(
         functools.partial(late_kernel, chips),
         (whole,),
-        (faces, *pieces),
+        pieces,
         [
             pltpu.VMEM((blocks, columns * half, nz), F32),
             pltpu.VMEM((blocks, columns, 1, half, nz), BF16),

time: 53.9 us -> 52 us (0.965)
  local copies, waits for them, and re-layouts: 9.93 us -> 0.83 us
  waiting for transfers between devices: 8.25 us -> 13.3 us
  Pallas kernels: 13.7 us -> 17.4 us
  other arithmetic: 0.87 us -> 0 us
    unnamed x36 -> x10, local copies, waits for them, and re-layouts: 9.89 us -> 0.81 us
    pallas_call x7 -> x8, Pallas kernels: 10.5 us -> 14.4 us  [call(): pl.pallas_call(kernel, out_shape=out_shape, in_specs=specs or [VMEM] * le...]
    ppermute x8, waiting for transfers between devices: 6.58 us -> 9.83 us  [swap(): return lax.ppermute(array, 'blk', [(i, i ^ s) for i in range(blocks)])]
    all_to_all x1, waiting for transfers between devices: 0.01 us -> 2.27 us  [per_device(): lax.all_to_all(shares, ('dom', 'blk'), split_axis=0, concat_axis=0, tiled...]
    concatenate x1 -> x0, other arithmetic: 0.87 us -> none  [per_device(): late = jnp.concatenate(late)]
    ppermute x6, starting transfers between devices: 10.5 us -> 9.77 us  [exchange(): return lax.ppermute(array, ('dom', 'blk'), pairs)]
  transfers between devices with their start and end apart: 15 -> 15, of which waited for: 5 -> 6; matrix products, arithmetic and copies ran while one was open for 2% -> 0% of each run, Pallas kernels for 18% -> 26%
where the time goes in v12:
time: 52 us; the launch traced here: 51.7 us
  starting transfers between devices  19.3 us (37%)
  Pallas kernels  17.4 us (33%)
  waiting for transfers between devices  13.3 us (26%)
  local copies, waits for them, and re-layouts  0.83 us (2%)
  between operations  0.76 us (1%)
    pallas_call x8, Pallas kernels, call(): pl.pallas_call(kernel, out_shape=out_shape, in_specs=specs or [VMEM] * le...  14.4 us
    ppermute x8, waiting for transfers between devices, swap(): return lax.ppermute(array, 'blk', [(i, i ^ s) for i in range(blocks)])  9.83 us
    ppermute x6, starting transfers between devices, exchange(): return lax.ppermute(array, ('dom', 'blk'), pairs)  9.77 us
    all_to_all x1, starting transfers between devices, per_device(): lax.all_to_all(shares, ('dom', 'blk'), split_axis=0, concat_axis=0, tiled...  4.78 us
    ppermute x8, starting transfers between devices, swap(): return lax.ppermute(array, 'blk', [(i, i ^ s) for i in range(blocks)])  4.75 us
    pallas_call x1, Pallas kernels, prepare(): pl.pallas_call(functools.partial(prepare_kernel, chips), out_shape=[jax.S...  3.08 us
    all_to_all x1, waiting for transfers between devices, per_device(): lax.all_to_all(shares, ('dom', 'blk'), split_axis=0, concat_axis=0, tiled...  2.27 us
    ppermute x6, waiting for transfers between devices, exchange(): return lax.ppermute(array, ('dom', 'blk'), pairs)  1.23 us
  transfers between devices with their start and end apart: 15, of which 6 were waited for; matrix products, arithmetic and copies ran while one was open for 0% of the time, Pallas kernels for 26%

profile of v12, /device:TPU:0, one launch (start us, length us, event | category | flops | bytes accessed | tf_op | source)
XLA Modules:
  0.0 51.7 jit_solution(11410995920327667612)
XLA Ops:
  0.6 3.1 %shard_map.59 = (bf16[17,64,128]{2,1,0:T(8,128)(2,1)S(1)}, bf16[34,64,128]{2,1,0:T(8,128)(2,1)S(1)}, bf16[18,64,128]{2,1,0:T(8,128)(2,1)S(1)}, bf16[16,64,128]{2,1,0:T(8,128)(2,1)S(1)}) custom-call(bf16[64,1,64,128]{3,2,1,0:T(8,128)(2,1)} %basis_hbm.1, s32[1,64,128]{2,1,0:T(8,128)} %zone_ref.1, f32[16]{0:T(128)} %cond_ref.1), custom_call_target="tpu_custom_call" | custom-call | tf_op jit(solution)/shard_map/pallas_call | solution.py:99
  3.7 0.5 %collective-permute-start = (bf16[34,64,128]{2,1,0:T(8,128)(2,1)S(1)}, bf16[34,64,128]{2,1,0:T(8,128)(2,1)S(1)}, u32[]{:S(2)}, u32[]{:S(2)}) collective-permute-start(bf16[34,64,128]{2,1,0:T(8,128)(2,1)S(1)} %get-tuple-element.36.center.refs_0_), channel_id=1, source_target_pairs={{0,1},{1,0},{2,3},{3,2},{4,5},{5,4},{6,7},{7,6},{8,9},{9,8},{10,11... | collective-permute-start | bytes 1671176 | tf_op jit(solution)/shard_map/ppermute | solution.py:422
  4.2 2.6 %collective-permute-start.7 = (bf16[18,64,128]{2,1,0:T(8,128)(2,1)S(1)}, bf16[18,64,128]{2,1,0:T(8,128)(2,1)S(1)}, u32[]{:S(2)}, u32[]{:S(2)}) collective-permute-start(bf16[18,64,128]{2,1,0:T(8,128)(2,1)S(1)} %get-tuple-element.46), channel_id=1, source_target_pairs={{0,2},{1,3},{2,0},{3,1},{4,6},{5,7},{6,4},{7,5},{8,10},{9,11},{10,... | collective-permute-start | bytes 884744 | tf_op jit(solution)/shard_map/ppermute | solution.py:422
  6.8 1.6 %collective-permute-start.1 = (bf16[17,64,128]{2,1,0:T(8,128)(2,1)S(1)}, bf16[17,64,128]{2,1,0:T(8,128)(2,1)S(1)}, u32[]{:S(2)}, u32[]{:S(2)}) collective-permute-start(bf16[17,64,128]{2,1,0:T(8,128)(2,1)S(1)} %get-tuple-element.39), channel_id=1, source_target_pairs={{0,4},{1,5},{2,6},{3,7},{4,0},{5,1},{6,2},{7,3},{8,12},{9,13},{10,... | collective-permute-start | bytes 835592 | tf_op jit(solution)/shard_map/ppermute | solution.py:430
  8.4 0.5 %collective-permute-start.3 = (bf16[16,64,128]{2,1,0:T(8,128)(2,1)S(1)}, bf16[16,64,128]{2,1,0:T(8,128)(2,1)S(1)}, u32[]{:S(2)}, u32[]{:S(2)}) collective-permute-start(bf16[16,64,128]{2,1,0:T(8,128)(2,1)S(1)} %get-tuple-element.41), channel_id=1, source_target_pairs={{0,2},{1,3},{2,0},{3,1},{4,6},{5,7},{6,4},{7,5},{8,10},{9,11},{10,... | collective-permute-start | bytes 786440 | tf_op jit(solution)/shard_map/ppermute | solution.py:422
  8.9 0.7 %collective-permute-start.2 = (bf16[17,64,128]{2,1,0:T(8,128)(2,1)S(1)}, bf16[17,64,128]{2,1,0:T(8,128)(2,1)S(1)}, u32[]{:S(2)}, u32[]{:S(2)}) collective-permute-start(bf16[17,64,128]{2,1,0:T(8,128)(2,1)S(1)} %get-tuple-element.39), channel_id=1, source_target_pairs={{4,8},{5,9},{6,10},{7,11},{8,4},{9,5},{10,6},{11,7},{20,24},{21,25... | collective-permute-start | bytes 835592 | tf_op jit(solution)/shard_map/ppermute | solution.py:430
  9.6 0.0 collective-permute-done.other.refs_2_
  9.6 2.3 %shard_map.60 = (f32[6,32,128]{2,1,0:T(8,128)S(1)}, f32[32,64,128]{2,1,0:T(8,128)S(1)}, bf16[8,64,128]{2,1,0:T(8,128)(2,1)}, f32[8,64,128]{2,1,0:T(8,128)}) custom-call(s32[1,64,128]{2,1,0:T(8,128)} %zone_ref.1, f32[16]{0:T(128)} %cond_ref.1, f32[16]{0:T(128)} %heat_ref.1, bf16[34,64,128]{2,1,0:T(8,128)(2,1)S(1)} %get-tuple-element.36.center.refs_0_), custom_call_target="tpu_custom_call" | custom-call | flops 1073741824 | bytes 134217728 | tf_op jit(solution)/shard_map/pallas_call | solution.py:404
  11.9 8.1 %collective-permute-done.3.refs_0_.refs_1_ = bf16[16,64,128]{2,1,0:T(8,128)(2,1)S(1)} collective-permute-done((bf16[16,64,128]{2,1,0:T(8,128)(2,1)S(1)}, bf16[16,64,128]{2,1,0:T(8,128)(2,1)S(1)}, u32[]{:S(2)}, u32[]{:S(2)}) %collective-permute-start.3) | collective-permute-done | bytes 262176 | tf_op jit(solution)/shard_map/ppermute | solution.py:422
  20.0 0.0 collective-permute-start.4
  20.0 0.0 collective-permute-done.1.one
  20.0 0.0 collective-permute-done.7.refs_0_
  20.0 0.7 %collective-permute-start.10 = (bf16[18,64,128]{2,1,0:T(8,128)(2,1)S(1)}, bf16[18,64,128]{2,1,0:T(8,128)(2,1)S(1)}, u32[]{:S(2)}, u32[]{:S(2)}) collective-permute-start(bf16[18,64,128]{2,1,0:T(8,128)(2,1)S(1)} %collective-permute-done.7.refs_0_), channel_id=1, source_target_pairs={{4,8},{5,9},{6,10},{7,11},{8,4},{9,5},{10,6},{11,7},{20,24},{21,25... | collective-permute-start | bytes 884744 | tf_op jit(solution)/shard_map/ppermute | solution.py:430
  20.7 4.7 %collective-permute-start.11 = (bf16[18,64,128]{2,1,0:T(8,128)(2,1)S(1)}, bf16[18,64,128]{2,1,0:T(8,128)(2,1)S(1)}, u32[]{:S(2)}, u32[]{:S(2)}) collective-permute-start(bf16[18,64,128]{2,1,0:T(8,128)(2,1)S(1)} %collective-permute-done.7.refs_0_), channel_id=1, source_target_pairs={{0,4},{1,5},{2,6},{3,7},{4,0},{5,1},{6,2},{7,3},{8,12},{9,13},{10,... | collective-permute-start | bytes 884744 | tf_op jit(solution)/shard_map/ppermute | solution.py:430
  25.4 0.0 collective-permute-done.2.two
  25.5 0.1 collective-permute-start.8
  25.6 0.5 collective-permute-start.9
  26.0 0.0 collective-permute-done.4.refs_1_.refs_4_
  26.1 0.7 %collective-permute-start.5 = (bf16[32,64,128]{2,1,0:T(8,128)(2,1)S(1)}, bf16[32,64,128]{2,1,0:T(8,128)(2,1)S(1)}, u32[]{:S(2)}, u32[]{:S(2)}) collective-permute-start(bf16[32,64,128]{2,1,0:T(8,128)(2,1)S(1)} %shard_map.62), channel_id=1, source_target_pairs={{4,8},{5,9},{6,10},{7,11},{8,4},{9,5},{10,6},{11,7},{20,24},{21,25... | collective-permute-start | bytes 1572872 | tf_op jit(solution)/shard_map/ppermute | solution.py:430
  26.8 0.3 collective-permute-done.9.refs_3_
  27.1 1.4 %collective-permute-start.6 = (bf16[32,64,128]{2,1,0:T(8,128)(2,1)S(1)}, bf16[32,64,128]{2,1,0:T(8,128)(2,1)S(1)}, u32[]{:S(2)}, u32[]{:S(2)}) collective-permute-start(bf16[32,64,128]{2,1,0:T(8,128)(2,1)S(1)} %shard_map.62), channel_id=1, source_target_pairs={{0,4},{1,5},{2,6},{3,7},{4,0},{5,1},{6,2},{7,3},{8,12},{9,13},{10,... | collective-permute-start | bytes 1572872 | tf_op jit(solution)/shard_map/ppermute | solution.py:430
  28.5 1.1 %shard_map.61 = (bf16[8,64,128]{2,1,0:T(8,128)(2,1)}, bf16[8,64,128]{2,1,0:T(8,128)(2,1)S(1)}, f32[3,32,128]{2,1,0:T(8,128)S(1)}, bf16[64,4096]{1,0:T(8,128)(2,1)S(1)}) custom-call(f32[6,32,128]{2,1,0:T(8,128)S(1)} %get-tuple-element.45.coef, f32[32,64,128]{2,1,0:T(8,128)S(1)} %get-tuple-element.38.partial, ...), custom_call_target="tpu_custom_call" | custom-call | flops 1 | bytes 1 | tf_op jit(solution)/shard_map/pallas_call | solution.py:404
  29.6 0.0 copy-start
  29.6 0.0 collective-permute-done.8.refs_2_
  29.6 2.1 %shard_map.63 = (bf16[34,64,128]{2,1,0:T(8,128)(2,1)S(1)}, f32[32,64,128]{2,1,0:T(8,128)S(1)}, bf16[34,64,128]{2,1,0:T(8,128)(2,1)S(1)}, bf16[8,64,128]{2,1,0:T(...) custom-call(f32[6,32,128]{2,1,0:T(8,128)S(1)} %get-tuple-element.45., ...), custom_call_target="tpu_custom_call" | custom-call | flops 1 | bytes 1 | tf_op jit(solution)/shard_map/pallas_call | solution.py:404
  31.7 2.4 %shard_map.64 = (bf16[256,4096]{1,0:T(8,128)(2,1)S(1)}, f32[256,128]{1,0:T(8,128)S(1)}, f32[128,256]{1,0:T(8,128)S(1)}) custom-call(f32[3,32,128]{2,1,0:T(8,128)S(1)} %get-tuple-element.40.faces, bf16[64,4096]{1,0:T(8,128)(2,1)S(1)} %get-tuple-element.44.flat, bf16[34,64,128]{2,1,0:T(8,128)(2,1)S(1)} %get-tuple-element.36.center.refs_0_, ...), custom_call_target="tpu_custom_call" | custom-call | flops 1 | bytes 1 | tf_op jit(solution)/shard_map/pallas_call | solution.py:404
  34.1 0.0 collective-permute-done.10.refs_2_
  34.1 0.0 collective-permute-done.11.refs_3_
  34.1 0.0 copy-done
  34.2 1.9 %shard_map.65 = (bf16[8,64,128]{2,1,0:T(8,128)(2,1)}, bf16[8,64,128]{2,1,0:T(8,128)(2,1)}, f32[256,256]{1,0:T(8,128)}) custom-call(f32[3,32,128]{2,1,0:T(8,128)S(1)} %get-tuple-element.40.faces, bf16[256,4096]{1,0:T(8,128)(2,1)S(1)} %get-tuple-element.52.left, f32[256,128]{1,0:T(8,128)S(1)} %get-tuple-element.53.tall, ...), custom_call_target="tpu_custom_call" | custom-call | flops 1 | bytes 1 | tf_op jit(solution)/shard_map/pallas_call | solution.py:404
  36.1 4.8 %all-to-all-start = ((f32[16,16,256]{2,1,0:T(8,128)}), f32[16,16,256]{2,1,0:T(8,128)S(1)}, u32[]{:S(2)}, u32[]{:S(2)}) async-start(f32[16,16,256]{2,1,0:T(8,128)} %bitcast.1), calls=%async_computation | async-start | bytes 524288 | tf_op jit(solution)/shard_map/all_to_all | solution.py:500
  40.9 0.4 collective-permute-start.12
  41.3 0.2 collective-permute-start.13
  41.4 0.8 %collective-permute-done.12.refs_2_ = bf16[8,64,128]{2,1,0:T(8,128)(2,1)S(1)} collective-permute-done((bf16[8,64,128]{2,1,0:T(8,128)(2,1)S(1)}, bf16[8,64,128]{2,1,0:T(8,128)(2,1)S(1)}, u32[]{:S(2)}, u32[]{:S(2)}) %collective-permute-start.12) | collective-permute-done | bytes 131104 | tf_op jit(solution)/shard_map/ppermute | solution.py:422
  42.3 0.0 copy-start.3
  42.3 0.6 %collective-permute-done.13.refs_3_ = bf16[8,64,128]{2,1,0:T(8,128)(2,1)S(1)} collective-permute-done((bf16[8,64,128]{2,1,0:T(8,128)(2,1)}, bf16[8,64,128]{2,1,0:T(8,128)(2,1)S(1)}, u32[]{:S(2)}, u32[]{:S(2)}) %collective-permute-start.13) | collective-permute-done | bytes 131104 | tf_op jit(solution)/shard_map/ppermute | solution.py:422
  42.8 0.0 copy-start.4
  42.8 0.0 collective-permute-done.5.two
  42.8 0.0 copy-start.1
  42.8 1.2 %collective-permute-done.6.one = bf16[32,64,128]{2,1,0:T(8,128)(2,1)S(1)} collective-permute-done((bf16[32,64,128]{2,1,0:T(8,128)(2,1)S(1)}, bf16[32,64,128]{2,1,0:T(8,128)(2,1)S(1)}, u32[]{:S(2)}, u32[]{:S(2)}) %collective-permute-start.6) | collective-permute-done | bytes 524320 | tf_op jit(solution)/shard_map/ppermute | solution.py:430
  44.1 0.0 copy-start.2
  44.1 0.0 copy-done.3
  44.1 0.0 copy-done.4
  44.1 0.0 copy-done.1
  44.1 0.8 %copy-done.2 = bf16[32,64,128]{2,1,0:T(8,128)(2,1)} copy-done((bf16[32,64,128]{2,1,0:T(8,128)(2,1)}, bf16[32,64,128]{2,1,0:T(8,128)(2,1)S(1)}, u32[]{:S(2)}) %copy-start.2) | copy-done | bytes 524312
  44.9 3.8 %shard_map.66 = bf16[256,1,16,128]{3,2,1,0:T(8,128)(2,1)} custom-call(f32[3,32,128]{2,1,0:T(8,128)} %copy-done, bf16[32,64,128]{2,1,0:T(8,128)(2,1)} %copy-done.1, bf16[32,64,128]{2,1,0:T(8,128)(2,1)} %copy-done.2, bf16[8,64,128]{2,1,0:T(8,128)(2,1)} %get-tuple-element.43.refs_0_, bf16[8,64,128]{2,1,0:T(8,128)(2,1)} %get-tuple-element.55.refs_1_, ...), custom_call_target="tpu_custom_call" | custom-call | flops 1 | bytes 1 | tf_op jit(solution)/shard_map/pallas_call | solution.py:404
  48.6 2.3 %all-to-all-done.shares = f32[16,16,256]{2,1,0:T(8,128)S(1)} async-done(((f32[16,16,256]{2,1,0:T(8,128)}), f32[16,16,256]{2,1,0:T(8,128)S(1)}, u32[]{:S(2)}, u32[]{:S(2)}) %all-to-all-start) | async-done | bytes 262176 | tf_op jit(solution)/shard_map/all_to_all | solution.py:500
  50.9 0.8 %shard_map.67 = f32[16,256]{1,0:T(8,128)} custom-call(f32[16,16,256]{2,1,0:T(8,128)S(1)} %all-to-all-done.shares), custom_call_target="tpu_custom_call" | custom-call | flops 1 | bytes 1 | tf_op jit(solution)/shard_map/pallas_call | solution.py:404
  (3 shorter events, 0.1 us)
Async XLA Ops:
  3.7 5.9 %collective-permute-start = (bf16[34,64,128]{2,1,0:T(8,128)(2,1)S(1)}, bf16[34,64,128]{2,1,0:T(8,128)(2,1)S(1)}, u32[]{:S(2)}, u32[]{:S(2)}) collective-permute-start(bf16[34,64,128]{2,1,0:T(8,128)(2,1)S(1)} %get-tuple-element.36.center.refs_0_), channel_id=1, source_target_pairs={{0,1},{1,0},{2,3},{3,2},{4,5},{5,4},{6,7},{7,6},{8,9},{9,8},{10,11... | collective-permute-start | bytes 1671176 | tf_op jit(solution)/shard_map/ppermute | solution.py:422
  4.2 15.8 %collective-permute-start.7 = (bf16[18,64,128]{2,1,0:T(8,128)(2,1)S(1)}, bf16[18,64,128]{2,1,0:T(8,128)(2,1)S(1)}, u32[]{:S(2)}, u32[]{:S(2)}) collective-permute-start(bf16[18,64,128]{2,1,0:T(8,128)(2,1)S(1)} %get-tuple-element.46), channel_id=1, source_target_pairs={{0,2},{1,3},{2,0},{3,1},{4,6},{5,7},{6,4},{7,5},{8,10},{9,11},{10,... | collective-permute-start | bytes 884744 | tf_op jit(solution)/shard_map/ppermute | solution.py:422
  6.8 13.2 %collective-permute-start.1 = (bf16[17,64,128]{2,1,0:T(8,128)(2,1)S(1)}, bf16[17,64,128]{2,1,0:T(8,128)(2,1)S(1)}, u32[]{:S(2)}, u32[]{:S(2)}) collective-permute-start(bf16[17,64,128]{2,1,0:T(8,128)(2,1)S(1)} %get-tuple-element.39), channel_id=1, source_target_pairs={{0,4},{1,5},{2,6},{3,7},{4,0},{5,1},{6,2},{7,3},{8,12},{9,13},{10,... | collective-permute-start | bytes 835592 | tf_op jit(solution)/shard_map/ppermute | solution.py:430
  8.4 11.6 %collective-permute-start.3 = (bf16[16,64,128]{2,1,0:T(8,128)(2,1)S(1)}, bf16[16,64,128]{2,1,0:T(8,128)(2,1)S(1)}, u32[]{:S(2)}, u32[]{:S(2)}) collective-permute-start(bf16[16,64,128]{2,1,0:T(8,128)(2,1)S(1)} %get-tuple-element.41), channel_id=1, source_target_pairs={{0,2},{1,3},{2,0},{3,1},{4,6},{5,7},{6,4},{7,5},{8,10},{9,11},{10,... | collective-permute-start | bytes 786440 | tf_op jit(solution)/shard_map/ppermute | solution.py:422
  8.9 16.5 %collective-permute-start.2 = (bf16[17,64,128]{2,1,0:T(8,128)(2,1)S(1)}, bf16[17,64,128]{2,1,0:T(8,128)(2,1)S(1)}, u32[]{:S(2)}, u32[]{:S(2)}) collective-permute-start(bf16[17,64,128]{2,1,0:T(8,128)(2,1)S(1)} %get-tuple-element.39), channel_id=1, source_target_pairs={{4,8},{5,9},{6,10},{7,11},{8,4},{9,5},{10,6},{11,7},{20,24},{21,25... | collective-permute-start | bytes 835592 | tf_op jit(solution)/shard_map/ppermute | solution.py:430
  20.0 6.0 %collective-permute-start.4 = (bf16[16,64,128]{2,1,0:T(8,128)(2,1)S(1)}, bf16[16,64,128]{2,1,0:T(8,128)(2,1)S(1)}, u32[]{:S(2)}, u32[]{:S(2)}) collective-permute-start(bf16[16,64,128]{2,1,0:T(8,128)(2,1)S(1)} %collective-permute-done.3.refs_0_.refs_1_), channel_id=1, source_target_pairs={{0,1},{1,0},{2,3},{3,2},{4,5},{5,4},{6,7},{7,6},{8,9},{9,8},{10,11... | collective-permute-start | bytes 786440 | tf_op jit(solution)/shard_map/ppermute | solution.py:422
  20.0 14.1 %collective-permute-start.10 = (bf16[18,64,128]{2,1,0:T(8,128)(2,1)S(1)}, bf16[18,64,128]{2,1,0:T(8,128)(2,1)S(1)}, u32[]{:S(2)}, u32[]{:S(2)}) collective-permute-start(bf16[18,64,128]{2,1,0:T(8,128)(2,1)S(1)} %collective-permute-done.7.refs_0_), channel_id=1, source_target_pairs={{4,8},{5,9},{6,10},{7,11},{8,4},{9,5},{10,6},{11,7},{20,24},{21,25... | collective-permute-start | bytes 884744 | tf_op jit(solution)/shard_map/ppermute | solution.py:430
  20.7 13.4 %collective-permute-start.11 = (bf16[18,64,128]{2,1,0:T(8,128)(2,1)S(1)}, bf16[18,64,128]{2,1,0:T(8,128)(2,1)S(1)}, u32[]{:S(2)}, u32[]{:S(2)}) collective-permute-start(bf16[18,64,128]{2,1,0:T(8,128)(2,1)S(1)} %collective-permute-done.7.refs_0_), channel_id=1, source_target_pairs={{0,4},{1,5},{2,6},{3,7},{4,0},{5,1},{6,2},{7,3},{8,12},{9,13},{10,... | collective-permute-start | bytes 884744 | tf_op jit(solution)/shard_map/ppermute | solution.py:430
  25.5 4.2 %collective-permute-start.8 = (bf16[16,64,128]{2,1,0:T(8,128)(2,1)S(1)}, bf16[16,64,128]{2,1,0:T(8,128)(2,1)S(1)}, u32[]{:S(2)}, u32[]{:S(2)}) collective-permute-start(bf16[16,64,128]{2,1,0:T(8,128)(2,1)S(1)} %slice.6), channel_id=1, source_target_pairs={{0,1},{1,0},{2,3},{3,2},{4,5},{5,4},{6,7},{7,6},{8,9},{9,8},{10,11... | collective-permute-start | bytes 786440 | tf_op jit(solution)/shard_map/ppermute | solution.py:422
  25.6 1.6 %collective-permute-start.9 = (bf16[2,64,128]{2,1,0:T(8,128)(2,1)S(1)}, bf16[2,64,128]{2,1,0:T(8,128)(2,1)S(1)}, u32[]{:S(2)}, u32[]{:S(2)}) collective-permute-start(bf16[2,64,128]{2,1,0:T(8,128)(2,1)S(1)} %slice.7), channel_id=1, source_target_pairs={{0,1},{1,0},{2,3},{3,2},{4,5},{5,4},{6,7},{7,6},{8,9},{9,8},{10,11... | collective-permute-start | bytes 98312 | tf_op jit(solution)/shard_map/ppermute | solution.py:422
  26.1 16.8 %collective-permute-start.5 = (bf16[32,64,128]{2,1,0:T(8,128)(2,1)S(1)}, bf16[32,64,128]{2,1,0:T(8,128)(2,1)S(1)}, u32[]{:S(2)}, u32[]{:S(2)}) collective-permute-start(bf16[32,64,128]{2,1,0:T(8,128)(2,1)S(1)} %shard_map.62), channel_id=1, source_target_pairs={{4,8},{5,9},{6,10},{7,11},{8,4},{9,5},{10,6},{11,7},{20,24},{21,25... | collective-permute-start | bytes 1572872 | tf_op jit(solution)/shard_map/ppermute | solution.py:430
  27.1 16.9 %collective-permute-start.6 = (bf16[32,64,128]{2,1,0:T(8,128)(2,1)S(1)}, bf16[32,64,128]{2,1,0:T(8,128)(2,1)S(1)}, u32[]{:S(2)}, u32[]{:S(2)}) collective-permute-start(bf16[32,64,128]{2,1,0:T(8,128)(2,1)S(1)} %shard_map.62), channel_id=1, source_target_pairs={{0,4},{1,5},{2,6},{3,7},{4,0},{5,1},{6,2},{7,3},{8,12},{9,13},{10,... | collective-permute-start | bytes 1572872 | tf_op jit(solution)/shard_map/ppermute | solution.py:430
  29.6 4.5 %copy-start = (f32[3,32,128]{2,1,0:T(8,128)}, f32[3,32,128]{2,1,0:T(8,128)S(1)}, u32[]{:S(2)}) copy-start(f32[3,32,128]{2,1,0:T(8,128)S(1)} %get-tuple-element.40.faces) | copy-start | bytes 147460
  36.1 14.8 %all-to-all-start = ((f32[16,16,256]{2,1,0:T(8,128)}), f32[16,16,256]{2,1,0:T(8,128)S(1)}, u32[]{:S(2)}, u32[]{:S(2)}) async-start(f32[16,16,256]{2,1,0:T(8,128)} %bitcast.1), calls=%async_computation | async-start | bytes 524288 | tf_op jit(solution)/shard_map/all_to_all | solution.py:500
  40.9 1.4 %collective-permute-start.12 = (bf16[8,64,128]{2,1,0:T(8,128)(2,1)S(1)}, bf16[8,64,128]{2,1,0:T(8,128)(2,1)S(1)}, u32[]{:S(2)}, u32[]{:S(2)}) collective-permute-start(bf16[8,64,128]{2,1,0:T(8,128)(2,1)S(1)} %get-tuple-element.56), channel_id=1, source_target_pairs={{0,1},{1,0},{2,3},{3,2},{4,5},{5,4},{6,7},{7,6},{8,9},{9,8},{10,11... | collective-permute-start | bytes 393224 | tf_op jit(solution)/shard_map/ppermute | solution.py:422
  41.3 1.6 %collective-permute-start.13 = (bf16[8,64,128]{2,1,0:T(8,128)(2,1)}, bf16[8,64,128]{2,1,0:T(8,128)(2,1)S(1)}, u32[]{:S(2)}, u32[]{:S(2)}) collective-permute-start(bf16[8,64,128]{2,1,0:T(8,128)(2,1)} %get-tuple-element.57), channel_id=1, source_target_pairs={{0,1},{1,0},{2,3},{3,2},{4,5},{5,4},{6,7},{7,6},{8,9},{9,8},{10,11... | collective-permute-start | bytes 393224 | tf_op jit(solution)/shard_map/ppermute | solution.py:422
  42.3 1.8 %copy-start.3 = (bf16[8,64,128]{2,1,0:T(8,128)(2,1)}, bf16[8,64,128]{2,1,0:T(8,128)(2,1)S(1)}, u32[]{:S(2)}) copy-start(bf16[8,64,128]{2,1,0:T(8,128)(2,1)S(1)} %collective-permute-done.12.refs_2_) | copy-start | bytes 393220
  42.8 1.2 %copy-start.4 = (bf16[8,64,128]{2,1,0:T(8,128)(2,1)}, bf16[8,64,128]{2,1,0:T(8,128)(2,1)S(1)}, u32[]{:S(2)}) copy-start(bf16[8,64,128]{2,1,0:T(8,128)(2,1)S(1)} %collective-permute-done.13.refs_3_) | copy-start | bytes 393220
  42.8 1.2 %copy-start.1 = (bf16[32,64,128]{2,1,0:T(8,128)(2,1)}, bf16[32,64,128]{2,1,0:T(8,128)(2,1)S(1)}, u32[]{:S(2)}) copy-start(bf16[32,64,128]{2,1,0:T(8,128)(2,1)S(1)} %collective-permute-done.5.two) | copy-start | bytes 1572868
  44.1 0.8 %copy-start.2 = (bf16[32,64,128]{2,1,0:T(8,128)(2,1)}, bf16[32,64,128]{2,1,0:T(8,128)(2,1)S(1)}, u32[]{:S(2)}) copy-start(bf16[32,64,128]{2,1,0:T(8,128)(2,1)S(1)} %collective-permute-done.6.one) | copy-start | bytes 1572868

commit v13 on v9

--- a/solution.py
+++ b/solution.py
@@ -37,6 +37,7 @@
     chip = lax.axis_index("blk") // CORES
     step = 16
     chunks = columns // step
+    pitch = wide.shape[0] // columns
     loads = [
         pltpu.make_async_copy(basis_hbm.at[pl.ds(i * step, step)], basis.at[pl.ds(i * step, step)], in_sems.at[i])
         for i in range(chunks)
@@ -54,19 +55,20 @@
         copy.start()
         stores.append(copy)
 
-    loads[chunks].wait()
-    loads[chunks + 1].wait()
-    mine = zone[0, pl.ds(pl.multiple_of(chip * rows, rows), rows), :]
-    own = cond_of(mine, table)
-    cond_pad[...] = jnp.concatenate([own, jnp.zeros((columns - rows, nz), F32)], 0).astype(BF16)
-    store(cond_pad, near.at[rows])
     for i in range(chunks):
+        if i == chunks - 1:
+            loads[chunks].wait()
+            loads[chunks + 1].wait()
+            mine = zone[0, pl.ds(pl.multiple_of(chip * rows, rows), rows), :]
+            own = cond_of(mine, table)
+            cond_pad[...] = jnp.concatenate([own, jnp.zeros((columns - rows, nz), F32)], 0).astype(BF16)
+            store(cond_pad, near.at[rows])
         loads[i].wait()
         some = pl.ds(i * step, step)
         for c in range(i * step, (i + 1) * step):
-            wide[c * ny:(c + 1) * ny, :] = basis[c, 0].astype(F32)
+            wide[c * pitch:c * pitch + ny, :] = basis[c, 0].astype(F32)
         for y in range(ny):
-            turned[y + 1, some, :] = wide[pl.ds(i * step * ny + y, step, stride=ny), :].astype(BF16)
+            turned[y + 1, some, :] = wide[pl.ds(i * step * pitch + y, step, stride=pitch), :].astype(BF16)
         store(turned.at[pl.ds(chip * rows + 1, rows), some], near.at[pl.ds(0, rows), some])
         for k in range(1, chips):
             start = (chip ^ k) * rows
@@ -92,7 +94,7 @@
             pltpu.VMEM(basis.shape, BF16),
             pltpu.VMEM(zone.shape, jnp.int32),
             pltpu.SMEM((ZONES,), F32),
-            pltpu.VMEM((columns * ny, nz), F32),
+            pltpu.VMEM((columns * (ny + 8), nz), F32),
             pltpu.VMEM((ny + 2, columns, nz), BF16),
             pltpu.VMEM((columns, nz), BF16),
             pltpu.SemaphoreType.DMA((columns // 16 + 2,)),
@@ -222,21 +224,25 @@
 def second_far_kernel(chips, weight, faces, left, first_gram, *refs):
     count = chips - 1
     partials, centers, twos, ones, images, mine, theirs = (refs[i * count:(i + 1) * count] for i in range(7))
-    gram, flat = refs[7 * count:]
+    gram = refs[7 * count]
     rows, columns, nz = partials[0].shape
     half = rows // 2
     core = lax.axis_index("blk") % CORES
     gram[:, 0:columns] = first_gram[:, 0:columns]
     for k in range(count):
-        for i in range(half):
+        total = first_gram[:, (k + 1) * columns:(k + 2) * columns]
+        for i in range(0, half, 2):
+            pair = []
+            for at in (i, i + 1):
+                y = half + at
+                image = image_row(faces, y, partials[k][y], centers[k][y + 1], ones[k][at], twos[k][at])
+                other = images[k][at]
+                mine[k][at] = jnp.where(core == 0, other, image)
+                theirs[k][at] = jnp.where(core == 0, image, other)
+                pair.append(image)
             y = half + i
-            image = image_row(faces, y, partials[k][y], centers[k][y + 1], ones[k][i], twos[k][i])
-            flat[:, i * nz:(i + 1) * nz] = image
-            other = images[k][i]
-            mine[k][i] = jnp.where(core == 0, other, image)
-            theirs[k][i] = jnp.where(core == 0, image, other)
-        block = slice((k + 1) * columns, (k + 2) * columns)
-        gram[:, block] = first_gram[:, block] + weight * gram_of(left[:, half * nz:], flat[...])
+            total += weight * gram_of(left[:, y * nz:(y + 2) * nz], jnp.concatenate(pair, 1))
+        gram[:, (k + 1) * columns:(k + 2) * columns] = total
 
 
 def turn_out(image, start, applied, wide, turned, sem):
@@ -392,7 +398,6 @@
         functools.partial(second_far_kernel, chips, weight),
         [image] * (2 * count) + [gram_shape],
         (faces, left, first_gram, *partials, *centers, *second_two, *second_one, *images),
-        [pltpu.VMEM((columns, rows * nz // 2), BF16)],
     )
     parts = slabs * blocks
     shares = gram.reshape(parts, total // parts, chips * columns)

time: 49.3 us -> 48.3 us (0.980)
  Pallas kernels: 11.8 us -> 10.7 us
    pallas_call x1, Pallas kernels: 3.03 us -> 2.06 us  [prepare(): pl.pallas_call(functools.partial(prepare_kernel, chips), out_shape=shapes...]
  transfers between devices with their start and end apart: 14 -> 14, of which waited for: 5 -> 5; matrix products, arithmetic and copies ran while one was open for 0% -> 0% of each run, Pallas kernels for 16% -> 17%
where the time goes in v13:
time: 48.3 us; the launch traced here: 48 us
  starting transfers between devices  20.2 us (42%)
  waiting for transfers between devices  14.2 us (29%)
  Pallas kernels  10.7 us (22%)
  local copies, waits for them, and re-layouts  2.1 us (4%)
  between operations  0.79 us (2%)
    ppermute x6, starting transfers between devices, exchange(): lax.ppermute(array, 'dom', [(d, to) for d, to in enumerate(partner) if 0...  12.6 us
    pallas_call x9, Pallas kernels, call(): pl.pallas_call(kernel, out_shape=out_shape, in_specs=specs or [VMEM] * le...  8.68 us
    ppermute x7, waiting for transfers between devices, swap(): return lax.ppermute(array, 'blk', [(i, i ^ s) for i in range(blocks)])  5.55 us
    all_to_all x1, waiting for transfers between devices, per_device(): lax.all_to_all(shares, ('dom', 'blk'), split_axis=0, concat_axis=0, tiled...  5.35 us
    all_to_all x1, starting transfers between devices, per_device(): lax.all_to_all(shares, ('dom', 'blk'), split_axis=0, concat_axis=0, tiled...  4.89 us
    ppermute x6, waiting for transfers between devices, exchange(): lax.ppermute(array, 'dom', [(d, to) for d, to in enumerate(partner) if 0...  3.25 us
    ppermute x7, starting transfers between devices, swap(): return lax.ppermute(array, 'blk', [(i, i ^ s) for i in range(blocks)])  2.74 us
    unnamed x6, local copies, waits for them, and re-layouts  2.07 us
  transfers between devices with their start and end apart: 14, of which 5 were waited for; matrix products, arithmetic and copies ran while one was open for 0% of the time, Pallas kernels for 17%

profile of v13, /device:TPU:0, one launch (start us, length us, event | category | flops | bytes accessed | tf_op | source)
XLA Modules:
  0.0 48.0 jit_solution(11597983814772199123)
XLA Ops:
  0.6 2.1 %shard_map.59 = (bf16[33,64,128]{2,1,0:T(8,128)(2,1)S(1)}, bf16[34,64,128]{2,1,0:T(8,128)(2,1)S(1)}, bf16[32,64,128]{2,1,0:T(8,128)(2,1)S(1)}, bf16[17,64,128]{2,1,0:T(8,128)(2,1)S(1)}, bf16[17,64,128]{2,1,0:T(8,128)(2,1)S(1)}) custom-call(bf16[64,1,64,128]{3,2,1,0:T(8,128)(2,1)} %basis_hbm.1, s32[1,64,128]{2,1,0:T(8,128)} %zone_ref.1, f32[16]{0:T(128)} %cond_ref.1), custom_call_target="tpu_custom_call" | custom-call | tf_op jit(solution)/shard_map/pallas_call | solution.py:88
  2.7 0.7 %collective-permute-start.1 = (bf16[33,64,128]{2,1,0:T(8,128)(2,1)S(1)}, bf16[33,64,128]{2,1,0:T(8,128)(2,1)S(1)}, u32[]{:S(2)}, u32[]{:S(2)}) collective-permute-start(bf16[33,64,128]{2,1,0:T(8,128)(2,1)S(1)} %get-tuple-element.31), channel_id=1, source_target_pairs={{4,8},{8,4},{5,9},{9,5},{6,10},{10,6},{7,11},{11,7},{20,24},{24,20... | collective-permute-start | bytes 1622024 | tf_op jit(solution)/shard_map/ppermute | solution.py:337
  3.4 5.9 %collective-permute-start = (bf16[33,64,128]{2,1,0:T(8,128)(2,1)S(1)}, bf16[33,64,128]{2,1,0:T(8,128)(2,1)S(1)}, u32[]{:S(2)}, u32[]{:S(2)}) collective-permute-start(bf16[33,64,128]{2,1,0:T(8,128)(2,1)S(1)} %get-tuple-element.31), channel_id=1, source_target_pairs={{0,4},{4,0},{8,12},{12,8},{1,5},{5,1},{9,13},{13,9},{2,6},{6,2},{1... | collective-permute-start | bytes 1622024 | tf_op jit(solution)/shard_map/ppermute | solution.py:337
  9.3 1.5 %collective-permute-start.5 = (bf16[17,64,128]{2,1,0:T(8,128)(2,1)S(1)}, bf16[17,64,128]{2,1,0:T(8,128)(2,1)S(1)}, u32[]{:S(2)}, u32[]{:S(2)}) collective-permute-start(bf16[17,64,128]{2,1,0:T(8,128)(2,1)S(1)} %get-tuple-element.40), channel_id=1, source_target_pairs={{0,2},{1,3},{2,0},{3,1},{4,6},{5,7},{6,4},{7,5},{8,10},{9,11},{10,... | collective-permute-start | bytes 835592 | tf_op jit(solution)/shard_map/ppermute | solution.py:333
  10.8 0.0 copy-start
  10.8 0.8 %copy-done = s32[1,64,128]{2,1,0:T(8,128)S(1)} copy-done((s32[1,64,128]{2,1,0:T(8,128)S(1)}, s32[1,64,128]{2,1,0:T(8,128)}, u32[]{:S(2)}) %copy-start) | copy-done | bytes 32792
  11.5 0.0 copy-start.1
  11.5 0.7 %copy-done.1 = f32[16]{0:T(128)S(1)} copy-done((f32[16]{0:T(128)S(1)}, f32[16]{0:T(128)}, u32[]{:S(2)}) %copy-start.1) | copy-done | bytes 88
  12.2 0.0 copy-start.2
  12.2 0.7 %copy-done.2 = f32[16]{0:T(128)S(1)} copy-done((f32[16]{0:T(128)S(1)}, f32[16]{0:T(128)}, u32[]{:S(2)}) %copy-start.2) | copy-done | bytes 88
  12.8 1.3 %shard_map.60 = (f32[6,32,128]{2,1,0:T(8,128)S(1)}, f32[32,64,128]{2,1,0:T(8,128)S(1)}) custom-call(s32[1,64,128]{2,1,0:T(8,128)S(1)} %copy-done, f32[16]{0:T(128)S(1)} %copy-done.1, f32[16]{0:T(128)S(1)} %copy-done.2, bf16[34,64,128]{2,1,0:T(8,128)(2,1)S(1)} %get-tuple-element.28.center), custom_call_target="tpu_custom_call" | custom-call | flops 1073741824 | bytes 134217728 | tf_op jit(solution)/shard_map/pallas_call | solution.py:318
  14.2 0.6 %collective-permute-start.3 = (bf16[17,64,128]{2,1,0:T(8,128)(2,1)S(1)}, bf16[17,64,128]{2,1,0:T(8,128)(2,1)S(1)}, u32[]{:S(2)}, u32[]{:S(2)}) collective-permute-start(bf16[17,64,128]{2,1,0:T(8,128)(2,1)S(1)} %get-tuple-element.38), channel_id=1, source_target_pairs={{0,2},{1,3},{2,0},{3,1},{4,6},{5,7},{6,4},{7,5},{8,10},{9,11},{10,... | collective-permute-start | bytes 835592 | tf_op jit(solution)/shard_map/ppermute | solution.py:333
  14.8 3.6 %collective-permute-done.5.refs_0_ = bf16[17,64,128]{2,1,0:T(8,128)(2,1)S(1)} collective-permute-done((bf16[17,64,128]{2,1,0:T(8,128)(2,1)S(1)}, bf16[17,64,128]{2,1,0:T(8,128)(2,1)S(1)}, u32[]{:S(2)}, u32[]{:S(2)}) %collective-permute-start.5) | collective-permute-done | bytes 278560 | tf_op jit(solution)/shard_map/ppermute | solution.py:333
  18.3 0.7 %collective-permute-start.6 = (bf16[17,64,128]{2,1,0:T(8,128)(2,1)S(1)}, bf16[17,64,128]{2,1,0:T(8,128)(2,1)S(1)}, u32[]{:S(2)}, u32[]{:S(2)}) collective-permute-start(bf16[17,64,128]{2,1,0:T(8,128)(2,1)S(1)} %collective-permute-done.5.refs_0_), channel_id=1, source_target_pairs={{4,8},{8,4},{5,9},{9,5},{6,10},{10,6},{7,11},{11,7},{20,24},{24,20... | collective-permute-start | bytes 835592 | tf_op jit(solution)/shard_map/ppermute | solution.py:337
  19.0 2.1 %collective-permute-start.7 = (bf16[17,64,128]{2,1,0:T(8,128)(2,1)S(1)}, bf16[17,64,128]{2,1,0:T(8,128)(2,1)S(1)}, u32[]{:S(2)}, u32[]{:S(2)}) collective-permute-start(bf16[17,64,128]{2,1,0:T(8,128)(2,1)S(1)} %collective-permute-done.5.refs_0_), channel_id=1, source_target_pairs={{0,4},{4,0},{8,12},{12,8},{1,5},{5,1},{9,13},{13,9},{2,6},{6,2},{1... | collective-permute-start | bytes 835592 | tf_op jit(solution)/shard_map/ppermute | solution.py:337
  21.1 2.0 %collective-permute-done.3.refs_1_ = bf16[17,64,128]{2,1,0:T(8,128)(2,1)S(1)} collective-permute-done((bf16[17,64,128]{2,1,0:T(8,128)(2,1)S(1)}, bf16[17,64,128]{2,1,0:T(8,128)(2,1)S(1)}, u32[]{:S(2)}, u32[]{:S(2)}) %collective-permute-start.3) | collective-permute-done | bytes 278560 | tf_op jit(solution)/shard_map/ppermute | solution.py:333
  23.1 0.0 collective-permute-start.4
  23.1 0.0 collective-permute-done.1.two
  23.1 0.7 %collective-permute-start.10 = (bf16[17,64,128]{2,1,0:T(8,128)(2,1)S(1)}, bf16[17,64,128]{2,1,0:T(8,128)(2,1)S(1)}, u32[]{:S(2)}, u32[]{:S(2)}) collective-permute-start(bf16[17,64,128]{2,1,0:T(8,128)(2,1)S(1)} %collective-permute-done.3.refs_1_), channel_id=1, source_target_pairs={{4,8},{8,4},{5,9},{9,5},{6,10},{10,6},{7,11},{11,7},{20,24},{24,20... | collective-permute-start | bytes 835592 | tf_op jit(solution)/shard_map/ppermute | solution.py:337
  23.8 0.0 collective-permute-done.one
  23.8 2.6 %collective-permute-start.11 = (bf16[17,64,128]{2,1,0:T(8,128)(2,1)S(1)}, bf16[17,64,128]{2,1,0:T(8,128)(2,1)S(1)}, u32[]{:S(2)}, u32[]{:S(2)}) collective-permute-start(bf16[17,64,128]{2,1,0:T(8,128)(2,1)S(1)} %collective-permute-done.3.refs_1_), channel_id=1, source_target_pairs={{0,4},{4,0},{8,12},{12,8},{1,5},{5,1},{9,13},{13,9},{2,6},{6,2},{1... | collective-permute-start | bytes 835592 | tf_op jit(solution)/shard_map/ppermute | solution.py:337
  26.3 0.0 collective-permute-done.6.refs_2_
  26.4 0.1 collective-permute-start.9
  26.5 1.0 %collective-permute-done.7.refs_3_ = bf16[17,64,128]{2,1,0:T(8,128)(2,1)S(1)} collective-permute-done((bf16[17,64,128]{2,1,0:T(8,128)(2,1)S(1)}, bf16[17,64,128]{2,1,0:T(8,128)(2,1)S(1)}, u32[]{:S(2)}, u32[]{:S(2)}) %collective-permute-start.7) | collective-permute-done | bytes 278560 | tf_op jit(solution)/shard_map/ppermute | solution.py:337
  27.5 0.0 collective-permute-start.8
  27.5 0.7 %shard_map.63 = (bf16[34,64,128]{2,1,0:T(8,128)(2,1)S(1)}, f32[32,64,128]{2,1,0:T(8,128)S(1)}) custom-call(f32[6,32,128]{2,1,0:T(8,128)S(1)} %get-tuple-element.29.coef, bf16[17,64,128]{2,1,0:T(8,128)(2,1)S(1)} %collective-permute-done.5.refs_0_, bf16[17,64,128]{2,1,0:T(8,128)(2,1)S(1)} %collective-permute-done.3.refs_1_), custom_call_target="tpu_custom_call" | custom-call | flops 1 | bytes 1 | tf_op jit(solution)/shard_map/pallas_call | solution.py:318
  28.2 0.6 %shard_map.61 = (bf16[16,64,128]{2,1,0:T(8,128)(2,1)S(1)}, bf16[16,64,128]{2,1,0:T(8,128)(2,1)S(1)}, f32[2,32,128]{2,1,0:T(8,128)S(1)}, bf16[64,4096]{1,0:T(8,128)(2,1)S(1)}) custom-call(f32[6,32,128]{2,1,0:T(8,128)S(1)} %get-tuple-element.29.coef, f32[32,64,128]{2,1,0:T(8,128)S(1)} %get-tuple-element.30.partial, ...), custom_call_target="tpu_custom_call" | custom-call | flops 1 | bytes 1 | tf_op jit(solution)/shard_map/pallas_call | solution.py:318
  28.8 0.2 shard_map.64
  28.9 0.0 collective-permute-done.9.refs_3_
  29.0 0.6 %collective-permute-start.2 = (bf16[16,64,128]{2,1,0:T(8,128)(2,1)S(1)}, bf16[16,64,128]{2,1,0:T(8,128)(2,1)S(1)}, u32[]{:S(2)}, u32[]{:S(2)}) collective-permute-start(bf16[16,64,128]{2,1,0:T(8,128)(2,1)S(1)} %get-tuple-element.33), channel_id=1, source_target_pairs={{0,1},{1,0},{2,3},{3,2},{4,5},{5,4},{6,7},{7,6},{8,9},{9,8},{10,11... | collective-permute-start | bytes 786440 | tf_op jit(solution)/shard_map/ppermute | solution.py:333
  29.5 0.0 collective-permute-done.8.refs_2_
  29.5 0.0 collective-permute-done.4.plain
  29.5 1.4 %shard_map.65 = (bf16[256,4096]{1,0:T(8,128)(2,1)S(1)}, f32[256,128]{1,0:T(8,128)S(1)}) custom-call(bf16[64,4096]{1,0:T(8,128)(2,1)S(1)} %get-tuple-element.35.flat, bf16[34,64,128]{2,1,0:T(8,128)(2,1)S(1)} %get-tuple-element.28.center, bf16[32,64,128]{2,1,0:T(8,128)(2,1)S(1)} %collective-permute-done.4.plain, ...), custom_call_target="tpu_custom_call" | custom-call | flops 1 | bytes 1 | tf_op jit(solution)/shard_map/pallas_call | solution.py:318
  30.9 0.0 collective-permute-done.10.refs_2_
  30.9 2.3 %collective-permute-done.11.refs_3_ = bf16[17,64,128]{2,1,0:T(8,128)(2,1)S(1)} collective-permute-done((bf16[17,64,128]{2,1,0:T(8,128)(2,1)S(1)}, bf16[17,64,128]{2,1,0:T(8,128)(2,1)S(1)}, u32[]{:S(2)}, u32[]{:S(2)}) %collective-permute-start.11) | collective-permute-done | bytes 278560 | tf_op jit(solution)/shard_map/ppermute | solution.py:337
  33.2 1.2 %shard_map.66 = (bf16[16,64,128]{2,1,0:T(8,128)(2,1)S(1)}, bf16[16,64,128]{2,1,0:T(8,128)(2,1)S(1)}, f32[256,128]{1,0:T(8,128)}) custom-call(f32[2,32,128]{2,1,0:T(8,128)S(1)} %get-tuple-element.34.faces, bf16[256,4096]{1,0:T(8,128)(2,1)S(1)} %get-tuple-element.47.left, f32[256,128]{1,0:T(8,128)S(1)} %get-tuple-element.48.first_gram, ...), custom_call_target="tpu_custom_call" | custom-call | flops 1 | bytes 1 | tf_op jit(solution)/shard_map/pallas_call | solution.py:318
  34.4 0.0 collective-permute-start.12
  34.4 4.9 %all-to-all-start = ((f32[16,16,128]{2,1,0:T(8,128)}), f32[16,16,128]{2,1,0:T(8,128)S(1)}, u32[]{:S(2)}, u32[]{:S(2)}) async-start(f32[16,16,128]{2,1,0:T(8,128)} %bitcast), calls=%async_computation | async-start | bytes 262144 | tf_op jit(solution)/shard_map/all_to_all | solution.py:404
  39.3 0.0 collective-permute-done.2.theirs
  39.3 1.3 %shard_map.62.applied_in = bf16[256,1,16,128]{3,2,1,0:T(8,128)(2,1)} custom-call(bf16[16,64,128]{2,1,0:T(8,128)(2,1)S(1)} %get-tuple-element.32.mine, bf16[16,64,128]{2,1,0:T(8,128)(2,1)S(1)} %collective-permute-done.2.theirs), custom_call_target="tpu_custom_call" | custom-call | flops 1 | bytes 1 | tf_op jit(solution)/shard_map/pallas_call | solution.py:318
  40.6 0.0 collective-permute-done.12.refs_1_
  40.6 1.3 %shard_map.67 = bf16[256,1,16,128]{3,2,1,0:T(8,128)(2,1)} custom-call(bf16[256,1,16,128]{3,2,1,0:T(8,128)(2,1)} %shard_map.62.applied_in, bf16[16,64,128]{2,1,0:T(8,128)(2,1)S(1)} %get-tuple-element.50.refs_0_, bf16[16,64,128]{2,1,0:T(8,128)(2,1)S(1)} %collective-permute-done.12.refs_1_), custom_call_target="tpu_custom_call", output_to_operand_aliasing={{}: (0, {})} | custom-call | flops 1 | bytes 1 | tf_op jit(solution)/shard_map/pallas_call | solution.py:318
  41.9 5.3 %all-to-all-done.shares = f32[16,16,128]{2,1,0:T(8,128)S(1)} async-done(((f32[16,16,128]{2,1,0:T(8,128)}), f32[16,16,128]{2,1,0:T(8,128)S(1)}, u32[]{:S(2)}, u32[]{:S(2)}) %all-to-all-start) | async-done | bytes 131104 | tf_op jit(solution)/shard_map/all_to_all | solution.py:404
  47.2 0.7 %shard_map.68 = f32[16,256]{1,0:T(8,128)} custom-call(f32[16,16,128]{2,1,0:T(8,128)S(1)} %all-to-all-done.shares), custom_call_target="tpu_custom_call" | custom-call | flops 1 | bytes 1 | tf_op jit(solution)/shard_map/pallas_call | solution.py:318
  (2 shorter events, 0.0 us)
Async XLA Ops:
  2.7 20.4 %collective-permute-start.1 = (bf16[33,64,128]{2,1,0:T(8,128)(2,1)S(1)}, bf16[33,64,128]{2,1,0:T(8,128)(2,1)S(1)}, u32[]{:S(2)}, u32[]{:S(2)}) collective-permute-start(bf16[33,64,128]{2,1,0:T(8,128)(2,1)S(1)} %get-tuple-element.31), channel_id=1, source_target_pairs={{4,8},{8,4},{5,9},{9,5},{6,10},{10,6},{7,11},{11,7},{20,24},{24,20... | collective-permute-start | bytes 1622024 | tf_op jit(solution)/shard_map/ppermute | solution.py:337
  3.4 20.4 %collective-permute-start = (bf16[33,64,128]{2,1,0:T(8,128)(2,1)S(1)}, bf16[33,64,128]{2,1,0:T(8,128)(2,1)S(1)}, u32[]{:S(2)}, u32[]{:S(2)}) collective-permute-start(bf16[33,64,128]{2,1,0:T(8,128)(2,1)S(1)} %get-tuple-element.31), channel_id=1, source_target_pairs={{0,4},{4,0},{8,12},{12,8},{1,5},{5,1},{9,13},{13,9},{2,6},{6,2},{1... | collective-permute-start | bytes 1622024 | tf_op jit(solution)/shard_map/ppermute | solution.py:337
  9.3 9.1 %collective-permute-start.5 = (bf16[17,64,128]{2,1,0:T(8,128)(2,1)S(1)}, bf16[17,64,128]{2,1,0:T(8,128)(2,1)S(1)}, u32[]{:S(2)}, u32[]{:S(2)}) collective-permute-start(bf16[17,64,128]{2,1,0:T(8,128)(2,1)S(1)} %get-tuple-element.40), channel_id=1, source_target_pairs={{0,2},{1,3},{2,0},{3,1},{4,6},{5,7},{6,4},{7,5},{8,10},{9,11},{10,... | collective-permute-start | bytes 835592 | tf_op jit(solution)/shard_map/ppermute | solution.py:333
  10.8 0.8 %copy-start = (s32[1,64,128]{2,1,0:T(8,128)S(1)}, s32[1,64,128]{2,1,0:T(8,128)}, u32[]{:S(2)}) copy-start(s32[1,64,128]{2,1,0:T(8,128)} %zone_ref.1) | copy-start | bytes 98308
  11.5 0.7 %copy-start.1 = (f32[16]{0:T(128)S(1)}, f32[16]{0:T(128)}, u32[]{:S(2)}) copy-start(f32[16]{0:T(128)} %cond_ref.1) | copy-start | bytes 196
  12.2 0.7 %copy-start.2 = (f32[16]{0:T(128)S(1)}, f32[16]{0:T(128)}, u32[]{:S(2)}) copy-start(f32[16]{0:T(128)} %heat_ref.1) | copy-start | bytes 196
  14.2 8.9 %collective-permute-start.3 = (bf16[17,64,128]{2,1,0:T(8,128)(2,1)S(1)}, bf16[17,64,128]{2,1,0:T(8,128)(2,1)S(1)}, u32[]{:S(2)}, u32[]{:S(2)}) collective-permute-start(bf16[17,64,128]{2,1,0:T(8,128)(2,1)S(1)} %get-tuple-element.38), channel_id=1, source_target_pairs={{0,2},{1,3},{2,0},{3,1},{4,6},{5,7},{6,4},{7,5},{8,10},{9,11},{10,... | collective-permute-start | bytes 835592 | tf_op jit(solution)/shard_map/ppermute | solution.py:333
  18.3 8.0 %collective-permute-start.6 = (bf16[17,64,128]{2,1,0:T(8,128)(2,1)S(1)}, bf16[17,64,128]{2,1,0:T(8,128)(2,1)S(1)}, u32[]{:S(2)}, u32[]{:S(2)}) collective-permute-start(bf16[17,64,128]{2,1,0:T(8,128)(2,1)S(1)} %collective-permute-done.5.refs_0_), channel_id=1, source_target_pairs={{4,8},{8,4},{5,9},{9,5},{6,10},{10,6},{7,11},{11,7},{20,24},{24,20... | collective-permute-start | bytes 835592 | tf_op jit(solution)/shard_map/ppermute | solution.py:337
  19.0 8.4 %collective-permute-start.7 = (bf16[17,64,128]{2,1,0:T(8,128)(2,1)S(1)}, bf16[17,64,128]{2,1,0:T(8,128)(2,1)S(1)}, u32[]{:S(2)}, u32[]{:S(2)}) collective-permute-start(bf16[17,64,128]{2,1,0:T(8,128)(2,1)S(1)} %collective-permute-done.5.refs_0_), channel_id=1, source_target_pairs={{0,4},{4,0},{8,12},{12,8},{1,5},{5,1},{9,13},{13,9},{2,6},{6,2},{1... | collective-permute-start | bytes 835592 | tf_op jit(solution)/shard_map/ppermute | solution.py:337
  23.1 6.5 %collective-permute-start.4 = (bf16[32,64,128]{2,1,0:T(8,128)(2,1)S(1)}, bf16[32,64,128]{2,1,0:T(8,128)(2,1)S(1)}, u32[]{:S(2)}, u32[]{:S(2)}) collective-permute-start(bf16[32,64,128]{2,1,0:T(8,128)(2,1)S(1)} %get-tuple-element.39), channel_id=1, source_target_pairs={{0,1},{1,0},{2,3},{3,2},{4,5},{5,4},{6,7},{7,6},{8,9},{9,8},{10,11... | collective-permute-start | bytes 1572872 | tf_op jit(solution)/shard_map/ppermute | solution.py:333
  23.1 7.9 %collective-permute-start.10 = (bf16[17,64,128]{2,1,0:T(8,128)(2,1)S(1)}, bf16[17,64,128]{2,1,0:T(8,128)(2,1)S(1)}, u32[]{:S(2)}, u32[]{:S(2)}) collective-permute-start(bf16[17,64,128]{2,1,0:T(8,128)(2,1)S(1)} %collective-permute-done.3.refs_1_), channel_id=1, source_target_pairs={{4,8},{8,4},{5,9},{9,5},{6,10},{10,6},{7,11},{11,7},{20,24},{24,20... | collective-permute-start | bytes 835592 | tf_op jit(solution)/shard_map/ppermute | solution.py:337
  23.8 9.4 %collective-permute-start.11 = (bf16[17,64,128]{2,1,0:T(8,128)(2,1)S(1)}, bf16[17,64,128]{2,1,0:T(8,128)(2,1)S(1)}, u32[]{:S(2)}, u32[]{:S(2)}) collective-permute-start(bf16[17,64,128]{2,1,0:T(8,128)(2,1)S(1)} %collective-permute-done.3.refs_1_), channel_id=1, source_target_pairs={{0,4},{4,0},{8,12},{12,8},{1,5},{5,1},{9,13},{13,9},{2,6},{6,2},{1... | collective-permute-start | bytes 835592 | tf_op jit(solution)/shard_map/ppermute | solution.py:337
  26.4 2.6 %collective-permute-start.9 = (bf16[16,64,128]{2,1,0:T(8,128)(2,1)S(1)}, bf16[16,64,128]{2,1,0:T(8,128)(2,1)S(1)}, u32[]{:S(2)}, u32[]{:S(2)}) collective-permute-start(bf16[16,64,128]{2,1,0:T(8,128)(2,1)S(1)} %slice.7), channel_id=1, source_target_pairs={{0,1},{1,0},{2,3},{3,2},{4,5},{5,4},{6,7},{7,6},{8,9},{9,8},{10,11... | collective-permute-start | bytes 786440 | tf_op jit(solution)/shard_map/ppermute | solution.py:333
  27.5 2.1 %collective-permute-start.8 = (bf16[16,64,128]{2,1,0:T(8,128)(2,1)S(1)}, bf16[16,64,128]{2,1,0:T(8,128)(2,1)S(1)}, u32[]{:S(2)}, u32[]{:S(2)}) collective-permute-start(bf16[16,64,128]{2,1,0:T(8,128)(2,1)S(1)} %slice.6), channel_id=1, source_target_pairs={{0,1},{1,0},{2,3},{3,2},{4,5},{5,4},{6,7},{7,6},{8,9},{9,8},{10,11... | collective-permute-start | bytes 786440 | tf_op jit(solution)/shard_map/ppermute | solution.py:333
  29.0 10.3 %collective-permute-start.2 = (bf16[16,64,128]{2,1,0:T(8,128)(2,1)S(1)}, bf16[16,64,128]{2,1,0:T(8,128)(2,1)S(1)}, u32[]{:S(2)}, u32[]{:S(2)}) collective-permute-start(bf16[16,64,128]{2,1,0:T(8,128)(2,1)S(1)} %get-tuple-element.33), channel_id=1, source_target_pairs={{0,1},{1,0},{2,3},{3,2},{4,5},{5,4},{6,7},{7,6},{8,9},{9,8},{10,11... | collective-permute-start | bytes 786440 | tf_op jit(solution)/shard_map/ppermute | solution.py:333
  34.4 6.2 %collective-permute-start.12 = (bf16[16,64,128]{2,1,0:T(8,128)(2,1)S(1)}, bf16[16,64,128]{2,1,0:T(8,128)(2,1)S(1)}, u32[]{:S(2)}, u32[]{:S(2)}) collective-permute-start(bf16[16,64,128]{2,1,0:T(8,128)(2,1)S(1)} %get-tuple-element.51), channel_id=1, source_target_pairs={{0,1},{1,0},{2,3},{3,2},{4,5},{5,4},{6,7},{7,6},{8,9},{9,8},{10,11... | collective-permute-start | bytes 786440 | tf_op jit(solution)/shard_map/ppermute | solution.py:333
  34.4 12.8 %all-to-all-start = ((f32[16,16,128]{2,1,0:T(8,128)}), f32[16,16,128]{2,1,0:T(8,128)S(1)}, u32[]{:S(2)}, u32[]{:S(2)}) async-start(f32[16,16,128]{2,1,0:T(8,128)} %bitcast), calls=%async_computation | async-start | bytes 262144 | tf_op jit(solution)/shard_map/all_to_all | solution.py:404

commit v14 on v13

--- a/solution.py
+++ b/solution.py
@@ -223,14 +223,15 @@
 
 def second_far_kernel(chips, weight, faces, left, first_gram, *refs):
     count = chips - 1
-    partials, centers, twos, ones, images, mine, theirs = (refs[i * count:(i + 1) * count] for i in range(7))
-    gram = refs[7 * count]
+    partials, centers, twos, ones, images, mine, low, high = (refs[i * count:(i + 1) * count] for i in range(8))
+    gram = refs[8 * count]
     rows, columns, nz = partials[0].shape
     half = rows // 2
     core = lax.axis_index("blk") % CORES
     gram[:, 0:columns] = first_gram[:, 0:columns]
     for k in range(count):
-        total = first_gram[:, (k + 1) * columns:(k + 2) * columns]
+        block = slice((k + 1) * columns, (k + 2) * columns)
+        total = jnp.zeros((left.shape[0], columns), F32)
         for i in range(0, half, 2):
             pair = []
             for at in (i, i + 1):
@@ -238,17 +239,19 @@
                 image = image_row(faces, y, partials[k][y], centers[k][y + 1], ones[k][at], twos[k][at])
                 other = images[k][at]
                 mine[k][at] = jnp.where(core == 0, other, image)
-                theirs[k][at] = jnp.where(core == 0, image, other)
+                theirs = low[k] if at < half // 2 else high[k]
+                theirs[at % (half // 2)] = jnp.where(core == 0, image, other)
                 pair.append(image)
             y = half + i
-            total += weight * gram_of(left[:, y * nz:(y + 2) * nz], jnp.concatenate(pair, 1))
-        gram[:, (k + 1) * columns:(k + 2) * columns] = total
+            total += gram_of(left[:, y * nz:(y + 2) * nz], jnp.concatenate(pair, 1))
+        gram[:, block] = first_gram[:, block] + weight * total
 
 
 def turn_out(image, start, applied, wide, turned, sem):
-    rows, columns, _ = image.shape
-    for y in range(rows):
-        wide[pl.ds(y, columns, stride=rows), :] = image[y].astype(F32)
+    rows = sum(part.shape[0] for part in image)
+    columns = image[0].shape[1]
+    for y, row in enumerate(part.at[y] for part in image for y in range(part.shape[0])):
+        wide[pl.ds(y, columns, stride=rows), :] = row[...].astype(F32)
     for c in range(columns):
         turned[c, 0] = wide[c * rows:(c + 1) * rows, :].astype(BF16)
     copy = pltpu.make_async_copy(turned, applied.at[pl.ds(start, columns)], sem)
@@ -261,7 +264,7 @@
     columns = mine.shape[1]
     copies = [
         turn_out(image, (me ^ s) * columns, applied, wide.at[s], turned.at[s], sems.at[s])
-        for s, image in enumerate((mine, theirs))
+        for s, image in enumerate(((mine,), (theirs,)))
     ]
     for copy in copies:
         copy.wait()
@@ -269,9 +272,12 @@
 
 def last_kernel(blocks, applied_in, *refs):
     del applied_in
-    images, (applied, wide, turned, sems) = refs[:blocks - CORES], refs[blocks - CORES:]
+    *pieces, applied, wide, turned, sems = refs
+    images = []
+    for mine, low, high in zip(pieces[0::3], pieces[1::3], pieces[2::3]):
+        images += [(mine,), (low, high)]
     me = lax.axis_index("blk")
-    columns = images[0].shape[1]
+    columns = pieces[0].shape[1]
     copies = [
         turn_out(image, (me ^ (s + CORES)) * columns, applied, wide.at[s], turned.at[s], sems.at[s])
         for s, image in enumerate(images)
@@ -396,7 +402,7 @@
     )
     *images, gram = call(
         functools.partial(second_far_kernel, chips, weight),
-        [image] * (2 * count) + [gram_shape],
+        [image] * count + [jax.ShapeDtypeStruct((half // 2, columns, nz), BF16)] * (2 * count) + [gram_shape],
         (faces, left, first_gram, *partials, *centers, *second_two, *second_one, *images),
     )
     parts = slabs * blocks
@@ -404,12 +410,12 @@
     shares = lax.all_to_all(shares, ("dom", "blk"), split_axis=0, concat_axis=0, tiled=True)
     pieces = []
     for k in range(count):
-        pieces += [images[k], swap(images[count + k], 1)]
+        pieces += [images[k], *(swap(images[i * count + k], 1) for i in (1, 2))]
     applied, = call(
         functools.partial(last_kernel, blocks),
         (whole,),
         (applied, *pieces),
-        turning(len(pieces)),
+        turning(CORES * count),
         [ANY] + [VMEM] * len(pieces),
         [ANY],
         aliases={0: 0},

time: 48.3 us -> 48.5 us (level)
  starting transfers between devices: 20.2 us -> 21.7 us
  waiting for transfers between devices: 14.2 us -> 12.8 us
    ppermute x7 -> x8, starting transfers between devices: 2.74 us -> 3.88 us  [swap(): return lax.ppermute(array, 'blk', [(i, i ^ s) for i in range(blocks)])]
    ppermute x6, waiting for transfers between devices: 3.25 us -> 2.48 us  [exchange(): lax.ppermute(array, 'dom', [(d, to) for d, to in enumerate(partner) if 0...]
    ppermute x6, starting transfers between devices: 12.6 us -> 13.2 us  [exchange(): lax.ppermute(array, 'dom', [(d, to) for d, to in enumerate(partner) if 0...]
    all_to_all x1, waiting for transfers between devices: 5.35 us -> 4.77 us  [per_device(): lax.all_to_all(shares, ('dom', 'blk'), split_axis=0, concat_axis=0, tiled...]
    ppermute x7 -> x8, waiting for transfers between devices: 5.55 us -> 5.55 us  [swap(): return lax.ppermute(array, 'blk', [(i, i ^ s) for i in range(blocks)])]
  transfers between devices with their start and end apart: 14 -> 15, of which waited for: 5 -> 4; matrix products, arithmetic and copies ran while one was open for 0% -> 0% of each run, Pallas kernels for 17% -> 16%
where the time goes in v14:
time: 48.5 us; the launch traced here: 48.2 us
  starting transfers between devices  21.7 us (45%)
  waiting for transfers between devices  12.8 us (26%)
  Pallas kernels  10.8 us (22%)
  local copies, waits for them, and re-layouts  2.1 us (4%)
  between operations  0.8 us (2%)
    ppermute x6, starting transfers between devices, exchange(): lax.ppermute(array, 'dom', [(d, to) for d, to in enumerate(partner) if 0...  13.2 us
    pallas_call x9, Pallas kernels, call(): pl.pallas_call(kernel, out_shape=out_shape, in_specs=specs or [VMEM] * le...  8.7 us
    ppermute x8, waiting for transfers between devices, swap(): return lax.ppermute(array, 'blk', [(i, i ^ s) for i in range(blocks)])  5.55 us
    all_to_all x1, waiting for transfers between devices, per_device(): lax.all_to_all(shares, ('dom', 'blk'), split_axis=0, concat_axis=0, tiled...  4.77 us
    all_to_all x1, starting transfers between devices, per_device(): lax.all_to_all(shares, ('dom', 'blk'), split_axis=0, concat_axis=0, tiled...  4.61 us
    ppermute x8, starting transfers between devices, swap(): return lax.ppermute(array, 'blk', [(i, i ^ s) for i in range(blocks)])  3.88 us
    ppermute x6, waiting for transfers between devices, exchange(): lax.ppermute(array, 'dom', [(d, to) for d, to in enumerate(partner) if 0...  2.48 us
    unnamed x6, local copies, waits for them, and re-layouts  2.07 us
  transfers between devices with their start and end apart: 15, of which 4 were waited for; matrix products, arithmetic and copies ran while one was open for 0% of the time, Pallas kernels for 16%

profile of v14, /device:TPU:0, one launch (start us, length us, event | category | flops | bytes accessed | tf_op | source)
XLA Modules:
  0.0 48.2 jit_solution(12168360584760211063)
XLA Ops:
  0.6 2.1 %shard_map.59 = (bf16[33,64,128]{2,1,0:T(8,128)(2,1)S(1)}, bf16[34,64,128]{2,1,0:T(8,128)(2,1)S(1)}, bf16[32,64,128]{2,1,0:T(8,128)(2,1)S(1)}, bf16[17,64,128]{2,1,0:T(8,128)(2,1)S(1)}, bf16[17,64,128]{2,1,0:T(8,128)(2,1)S(1)}) custom-call(bf16[64,1,64,128]{3,2,1,0:T(8,128)(2,1)} %basis_hbm.1, s32[1,64,128]{2,1,0:T(8,128)} %zone_ref.1, f32[16]{0:T(128)} %cond_ref.1), custom_call_target="tpu_custom_call" | custom-call | tf_op jit(solution)/shard_map/pallas_call | solution.py:88
  2.7 0.7 %collective-permute-start.1 = (bf16[33,64,128]{2,1,0:T(8,128)(2,1)S(1)}, bf16[33,64,128]{2,1,0:T(8,128)(2,1)S(1)}, u32[]{:S(2)}, u32[]{:S(2)}) collective-permute-start(bf16[33,64,128]{2,1,0:T(8,128)(2,1)S(1)} %get-tuple-element.32), channel_id=1, source_target_pairs={{4,8},{8,4},{5,9},{9,5},{6,10},{10,6},{7,11},{11,7},{20,24},{24,20... | collective-permute-start | bytes 1622024 | tf_op jit(solution)/shard_map/ppermute | solution.py:343
  3.4 5.9 %collective-permute-start = (bf16[33,64,128]{2,1,0:T(8,128)(2,1)S(1)}, bf16[33,64,128]{2,1,0:T(8,128)(2,1)S(1)}, u32[]{:S(2)}, u32[]{:S(2)}) collective-permute-start(bf16[33,64,128]{2,1,0:T(8,128)(2,1)S(1)} %get-tuple-element.32), channel_id=1, source_target_pairs={{0,4},{4,0},{8,12},{12,8},{1,5},{5,1},{9,13},{13,9},{2,6},{6,2},{1... | collective-permute-start | bytes 1622024 | tf_op jit(solution)/shard_map/ppermute | solution.py:343
  9.3 1.5 %collective-permute-start.5 = (bf16[17,64,128]{2,1,0:T(8,128)(2,1)S(1)}, bf16[17,64,128]{2,1,0:T(8,128)(2,1)S(1)}, u32[]{:S(2)}, u32[]{:S(2)}) collective-permute-start(bf16[17,64,128]{2,1,0:T(8,128)(2,1)S(1)} %get-tuple-element.41), channel_id=1, source_target_pairs={{0,2},{1,3},{2,0},{3,1},{4,6},{5,7},{6,4},{7,5},{8,10},{9,11},{10,... | collective-permute-start | bytes 835592 | tf_op jit(solution)/shard_map/ppermute | solution.py:339
  10.8 0.0 copy-start
  10.8 0.8 %copy-done = s32[1,64,128]{2,1,0:T(8,128)S(1)} copy-done((s32[1,64,128]{2,1,0:T(8,128)S(1)}, s32[1,64,128]{2,1,0:T(8,128)}, u32[]{:S(2)}) %copy-start) | copy-done | bytes 32792
  11.5 0.0 copy-start.1
  11.5 0.7 %copy-done.1 = f32[16]{0:T(128)S(1)} copy-done((f32[16]{0:T(128)S(1)}, f32[16]{0:T(128)}, u32[]{:S(2)}) %copy-start.1) | copy-done | bytes 88
  12.2 0.0 copy-start.2
  12.2 0.7 %copy-done.2 = f32[16]{0:T(128)S(1)} copy-done((f32[16]{0:T(128)S(1)}, f32[16]{0:T(128)}, u32[]{:S(2)}) %copy-start.2) | copy-done | bytes 88
  12.8 1.3 %shard_map.60 = (f32[6,32,128]{2,1,0:T(8,128)S(1)}, f32[32,64,128]{2,1,0:T(8,128)S(1)}) custom-call(s32[1,64,128]{2,1,0:T(8,128)S(1)} %copy-done, f32[16]{0:T(128)S(1)} %copy-done.1, f32[16]{0:T(128)S(1)} %copy-done.2, bf16[34,64,128]{2,1,0:T(8,128)(2,1)S(1)} %get-tuple-element.29.center), custom_call_target="tpu_custom_call" | custom-call | flops 1073741824 | bytes 134217728 | tf_op jit(solution)/shard_map/pallas_call | solution.py:324
  14.2 0.6 %collective-permute-start.3 = (bf16[17,64,128]{2,1,0:T(8,128)(2,1)S(1)}, bf16[17,64,128]{2,1,0:T(8,128)(2,1)S(1)}, u32[]{:S(2)}, u32[]{:S(2)}) collective-permute-start(bf16[17,64,128]{2,1,0:T(8,128)(2,1)S(1)} %get-tuple-element.39), channel_id=1, source_target_pairs={{0,2},{1,3},{2,0},{3,1},{4,6},{5,7},{6,4},{7,5},{8,10},{9,11},{10,... | collective-permute-start | bytes 835592 | tf_op jit(solution)/shard_map/ppermute | solution.py:339
  14.8 3.6 %collective-permute-done.5.refs_0_ = bf16[17,64,128]{2,1,0:T(8,128)(2,1)S(1)} collective-permute-done((bf16[17,64,128]{2,1,0:T(8,128)(2,1)S(1)}, bf16[17,64,128]{2,1,0:T(8,128)(2,1)S(1)}, u32[]{:S(2)}, u32[]{:S(2)}) %collective-permute-start.5) | collective-permute-done | bytes 278560 | tf_op jit(solution)/shard_map/ppermute | solution.py:339
  18.3 0.7 %collective-permute-start.6 = (bf16[17,64,128]{2,1,0:T(8,128)(2,1)S(1)}, bf16[17,64,128]{2,1,0:T(8,128)(2,1)S(1)}, u32[]{:S(2)}, u32[]{:S(2)}) collective-permute-start(bf16[17,64,128]{2,1,0:T(8,128)(2,1)S(1)} %collective-permute-done.5.refs_0_), channel_id=1, source_target_pairs={{4,8},{8,4},{5,9},{9,5},{6,10},{10,6},{7,11},{11,7},{20,24},{24,20... | collective-permute-start | bytes 835592 | tf_op jit(solution)/shard_map/ppermute | solution.py:343
  19.0 2.1 %collective-permute-start.7 = (bf16[17,64,128]{2,1,0:T(8,128)(2,1)S(1)}, bf16[17,64,128]{2,1,0:T(8,128)(2,1)S(1)}, u32[]{:S(2)}, u32[]{:S(2)}) collective-permute-start(bf16[17,64,128]{2,1,0:T(8,128)(2,1)S(1)} %collective-permute-done.5.refs_0_), channel_id=1, source_target_pairs={{0,4},{4,0},{8,12},{12,8},{1,5},{5,1},{9,13},{13,9},{2,6},{6,2},{1... | collective-permute-start | bytes 835592 | tf_op jit(solution)/shard_map/ppermute | solution.py:343
  21.1 2.0 %collective-permute-done.3.refs_1_ = bf16[17,64,128]{2,1,0:T(8,128)(2,1)S(1)} collective-permute-done((bf16[17,64,128]{2,1,0:T(8,128)(2,1)S(1)}, bf16[17,64,128]{2,1,0:T(8,128)(2,1)S(1)}, u32[]{:S(2)}, u32[]{:S(2)}) %collective-permute-start.3) | collective-permute-done | bytes 278560 | tf_op jit(solution)/shard_map/ppermute | solution.py:339
  23.1 0.0 collective-permute-start.4
  23.1 0.0 collective-permute-done.1.two
  23.1 0.7 %collective-permute-start.10 = (bf16[17,64,128]{2,1,0:T(8,128)(2,1)S(1)}, bf16[17,64,128]{2,1,0:T(8,128)(2,1)S(1)}, u32[]{:S(2)}, u32[]{:S(2)}) collective-permute-start(bf16[17,64,128]{2,1,0:T(8,128)(2,1)S(1)} %collective-permute-done.3.refs_1_), channel_id=1, source_target_pairs={{4,8},{8,4},{5,9},{9,5},{6,10},{10,6},{7,11},{11,7},{20,24},{24,20... | collective-permute-start | bytes 835592 | tf_op jit(solution)/shard_map/ppermute | solution.py:343
  23.8 0.0 collective-permute-done.one
  23.8 0.6 %collective-permute-start.9 = (bf16[16,64,128]{2,1,0:T(8,128)(2,1)S(1)}, bf16[16,64,128]{2,1,0:T(8,128)(2,1)S(1)}, u32[]{:S(2)}, u32[]{:S(2)}) collective-permute-start(bf16[16,64,128]{2,1,0:T(8,128)(2,1)S(1)} %slice.7), channel_id=1, source_target_pairs={{0,1},{1,0},{2,3},{3,2},{4,5},{5,4},{6,7},{7,6},{8,9},{9,8},{10,11... | collective-permute-start | bytes 786440 | tf_op jit(solution)/shard_map/ppermute | solution.py:339
  24.4 0.0 collective-permute-done.6.refs_2_
  24.4 3.2 %collective-permute-start.11 = (bf16[17,64,128]{2,1,0:T(8,128)(2,1)S(1)}, bf16[17,64,128]{2,1,0:T(8,128)(2,1)S(1)}, u32[]{:S(2)}, u32[]{:S(2)}) collective-permute-start(bf16[17,64,128]{2,1,0:T(8,128)(2,1)S(1)} %collective-permute-done.3.refs_1_), channel_id=1, source_target_pairs={{0,4},{4,0},{8,12},{12,8},{1,5},{5,1},{9,13},{13,9},{2,6},{6,2},{1... | collective-permute-start | bytes 835592 | tf_op jit(solution)/shard_map/ppermute | solution.py:343
  27.6 0.0 collective-permute-done.7.refs_3_
  27.6 0.1 collective-permute-start.8
  27.7 0.6 %shard_map.61 = (bf16[16,64,128]{2,1,0:T(8,128)(2,1)S(1)}, bf16[16,64,128]{2,1,0:T(8,128)(2,1)S(1)}, f32[2,32,128]{2,1,0:T(8,128)S(1)}, bf16[64,4096]{1,0:T(8,128)(2,1)S(1)}) custom-call(f32[6,32,128]{2,1,0:T(8,128)S(1)} %get-tuple-element.30.coef, f32[32,64,128]{2,1,0:T(8,128)S(1)} %get-tuple-element.31.partial, ...), custom_call_target="tpu_custom_call" | custom-call | flops 1 | bytes 1 | tf_op jit(solution)/shard_map/pallas_call | solution.py:324
  28.3 0.0 collective-permute-done.9.refs_3_
  28.3 0.6 %collective-permute-start.2 = (bf16[16,64,128]{2,1,0:T(8,128)(2,1)S(1)}, bf16[16,64,128]{2,1,0:T(8,128)(2,1)S(1)}, u32[]{:S(2)}, u32[]{:S(2)}) collective-permute-start(bf16[16,64,128]{2,1,0:T(8,128)(2,1)S(1)} %get-tuple-element.34), channel_id=1, source_target_pairs={{0,1},{1,0},{2,3},{3,2},{4,5},{5,4},{6,7},{7,6},{8,9},{9,8},{10,11... | collective-permute-start | bytes 786440 | tf_op jit(solution)/shard_map/ppermute | solution.py:339
  28.9 0.7 %shard_map.63 = (bf16[34,64,128]{2,1,0:T(8,128)(2,1)S(1)}, f32[32,64,128]{2,1,0:T(8,128)S(1)}) custom-call(f32[6,32,128]{2,1,0:T(8,128)S(1)} %get-tuple-element.30.coef, bf16[17,64,128]{2,1,0:T(8,128)(2,1)S(1)} %collective-permute-done.5.refs_0_, bf16[17,64,128]{2,1,0:T(8,128)(2,1)S(1)} %collective-permute-done.3.refs_1_), custom_call_target="tpu_custom_call" | custom-call | flops 1 | bytes 1 | tf_op jit(solution)/shard_map/pallas_call | solution.py:324
  29.6 0.2 shard_map.64
  29.8 0.0 collective-permute-done.8.refs_2_
  29.8 0.0 collective-permute-done.4.plain
  29.8 1.4 %shard_map.65 = (bf16[256,4096]{1,0:T(8,128)(2,1)S(1)}, f32[256,128]{1,0:T(8,128)S(1)}) custom-call(bf16[64,4096]{1,0:T(8,128)(2,1)S(1)} %get-tuple-element.36.flat, bf16[34,64,128]{2,1,0:T(8,128)(2,1)S(1)} %get-tuple-element.29.center, bf16[32,64,128]{2,1,0:T(8,128)(2,1)S(1)} %collective-permute-done.4.plain, ...), custom_call_target="tpu_custom_call" | custom-call | flops 1 | bytes 1 | tf_op jit(solution)/shard_map/pallas_call | solution.py:324
  31.2 0.0 collective-permute-done.10.refs_2_
  31.2 2.5 %collective-permute-done.11.refs_3_ = bf16[17,64,128]{2,1,0:T(8,128)(2,1)S(1)} collective-permute-done((bf16[17,64,128]{2,1,0:T(8,128)(2,1)S(1)}, bf16[17,64,128]{2,1,0:T(8,128)(2,1)S(1)}, u32[]{:S(2)}, u32[]{:S(2)}) %collective-permute-start.11) | collective-permute-done | bytes 278560 | tf_op jit(solution)/shard_map/ppermute | solution.py:343
  33.7 1.2 %shard_map.66 = (bf16[16,64,128]{2,1,0:T(8,128)(2,1)S(1)}, bf16[8,64,128]{2,1,0:T(8,128)(2,1)S(1)}, bf16[8,64,128]{2,1,0:T(8,128)(2,1)S(1)}, f32[256,128]{1,0:T(8,128)}) custom-call(f32[2,32,128]{2,1,0:T(8,128)S(1)} %get-tuple-element.35.faces, bf16[256,4096]{1,0:T(8,128)(2,1)S(1)} %get-tuple-element.48.left, f32[256,128]{1,0:T(8,128)S(1)} %get-tuple-element.49.first_gram, ...), custom_call_target="tpu_custom_call" | custom-call | flops 1 | bytes 1 | tf_op jit(solution)/shard_map/pallas_call | solution.py:324
  34.9 4.6 %all-to-all-start = ((f32[16,16,128]{2,1,0:T(8,128)}), f32[16,16,128]{2,1,0:T(8,128)S(1)}, u32[]{:S(2)}, u32[]{:S(2)}) async-start(f32[16,16,128]{2,1,0:T(8,128)} %bitcast), calls=%async_computation | async-start | bytes 262144 | tf_op jit(solution)/shard_map/all_to_all | solution.py:410
  39.5 0.4 collective-permute-start.12
  39.9 0.2 collective-permute-start.13
  40.1 0.0 collective-permute-done.2.theirs
  40.1 1.3 %shard_map.62.applied_in = bf16[256,1,16,128]{3,2,1,0:T(8,128)(2,1)} custom-call(bf16[16,64,128]{2,1,0:T(8,128)(2,1)S(1)} %get-tuple-element.33.mine, bf16[16,64,128]{2,1,0:T(8,128)(2,1)S(1)} %collective-permute-done.2.theirs), custom_call_target="tpu_custom_call" | custom-call | flops 1 | bytes 1 | tf_op jit(solution)/shard_map/pallas_call | solution.py:324
  41.3 0.0 collective-permute-done.12.refs_1_
  41.4 0.0 collective-permute-done.13.refs_2_
  41.4 1.3 %shard_map.67 = bf16[256,1,16,128]{3,2,1,0:T(8,128)(2,1)} custom-call(bf16[256,1,16,128]{3,2,1,0:T(8,128)(2,1)} %shard_map.62.applied_in, bf16[16,64,128]{2,1,0:T(8,128)(2,1)S(1)} %get-tuple-element.51.refs_0_, bf16[8,64,128]{2,1,0:T(8,128)(2,1)S(1)} %collective-permute-done.12.refs_1_, ...), custom_call_target="tpu_custom_call", output_to_operand_aliasing={{}: (0, {})} | custom-call | flops 1 | bytes 1 | tf_op jit(solution)/shard_map/pallas_call | solution.py:324
  42.7 4.8 %all-to-all-done.shares = f32[16,16,128]{2,1,0:T(8,128)S(1)} async-done(((f32[16,16,128]{2,1,0:T(8,128)}), f32[16,16,128]{2,1,0:T(8,128)S(1)}, u32[]{:S(2)}, u32[]{:S(2)}) %all-to-all-start) | async-done | bytes 131104 | tf_op jit(solution)/shard_map/all_to_all | solution.py:410
  47.4 0.7 %shard_map.68 = f32[16,256]{1,0:T(8,128)} custom-call(f32[16,16,128]{2,1,0:T(8,128)S(1)} %all-to-all-done.shares), custom_call_target="tpu_custom_call" | custom-call | flops 1 | bytes 1 | tf_op jit(solution)/shard_map/pallas_call | solution.py:324
  (2 shorter events, 0.0 us)
Async XLA Ops:
  2.7 20.4 %collective-permute-start.1 = (bf16[33,64,128]{2,1,0:T(8,128)(2,1)S(1)}, bf16[33,64,128]{2,1,0:T(8,128)(2,1)S(1)}, u32[]{:S(2)}, u32[]{:S(2)}) collective-permute-start(bf16[33,64,128]{2,1,0:T(8,128)(2,1)S(1)} %get-tuple-element.32), channel_id=1, source_target_pairs={{4,8},{8,4},{5,9},{9,5},{6,10},{10,6},{7,11},{11,7},{20,24},{24,20... | collective-permute-start | bytes 1622024 | tf_op jit(solution)/shard_map/ppermute | solution.py:343
  3.4 20.4 %collective-permute-start = (bf16[33,64,128]{2,1,0:T(8,128)(2,1)S(1)}, bf16[33,64,128]{2,1,0:T(8,128)(2,1)S(1)}, u32[]{:S(2)}, u32[]{:S(2)}) collective-permute-start(bf16[33,64,128]{2,1,0:T(8,128)(2,1)S(1)} %get-tuple-element.32), channel_id=1, source_target_pairs={{0,4},{4,0},{8,12},{12,8},{1,5},{5,1},{9,13},{13,9},{2,6},{6,2},{1... | collective-permute-start | bytes 1622024 | tf_op jit(solution)/shard_map/ppermute | solution.py:343
  9.3 9.1 %collective-permute-start.5 = (bf16[17,64,128]{2,1,0:T(8,128)(2,1)S(1)}, bf16[17,64,128]{2,1,0:T(8,128)(2,1)S(1)}, u32[]{:S(2)}, u32[]{:S(2)}) collective-permute-start(bf16[17,64,128]{2,1,0:T(8,128)(2,1)S(1)} %get-tuple-element.41), channel_id=1, source_target_pairs={{0,2},{1,3},{2,0},{3,1},{4,6},{5,7},{6,4},{7,5},{8,10},{9,11},{10,... | collective-permute-start | bytes 835592 | tf_op jit(solution)/shard_map/ppermute | solution.py:339
  10.8 0.8 %copy-start = (s32[1,64,128]{2,1,0:T(8,128)S(1)}, s32[1,64,128]{2,1,0:T(8,128)}, u32[]{:S(2)}) copy-start(s32[1,64,128]{2,1,0:T(8,128)} %zone_ref.1) | copy-start | bytes 98308
  11.5 0.7 %copy-start.1 = (f32[16]{0:T(128)S(1)}, f32[16]{0:T(128)}, u32[]{:S(2)}) copy-start(f32[16]{0:T(128)} %cond_ref.1) | copy-start | bytes 196
  12.2 0.7 %copy-start.2 = (f32[16]{0:T(128)S(1)}, f32[16]{0:T(128)}, u32[]{:S(2)}) copy-start(f32[16]{0:T(128)} %heat_ref.1) | copy-start | bytes 196
  14.2 8.9 %collective-permute-start.3 = (bf16[17,64,128]{2,1,0:T(8,128)(2,1)S(1)}, bf16[17,64,128]{2,1,0:T(8,128)(2,1)S(1)}, u32[]{:S(2)}, u32[]{:S(2)}) collective-permute-start(bf16[17,64,128]{2,1,0:T(8,128)(2,1)S(1)} %get-tuple-element.39), channel_id=1, source_target_pairs={{0,2},{1,3},{2,0},{3,1},{4,6},{5,7},{6,4},{7,5},{8,10},{9,11},{10,... | collective-permute-start | bytes 835592 | tf_op jit(solution)/shard_map/ppermute | solution.py:339
  18.3 6.0 %collective-permute-start.6 = (bf16[17,64,128]{2,1,0:T(8,128)(2,1)S(1)}, bf16[17,64,128]{2,1,0:T(8,128)(2,1)S(1)}, u32[]{:S(2)}, u32[]{:S(2)}) collective-permute-start(bf16[17,64,128]{2,1,0:T(8,128)(2,1)S(1)} %collective-permute-done.5.refs_0_), channel_id=1, source_target_pairs={{4,8},{8,4},{5,9},{9,5},{6,10},{10,6},{7,11},{11,7},{20,24},{24,20... | collective-permute-start | bytes 835592 | tf_op jit(solution)/shard_map/ppermute | solution.py:343
  19.0 8.6 %collective-permute-start.7 = (bf16[17,64,128]{2,1,0:T(8,128)(2,1)S(1)}, bf16[17,64,128]{2,1,0:T(8,128)(2,1)S(1)}, u32[]{:S(2)}, u32[]{:S(2)}) collective-permute-start(bf16[17,64,128]{2,1,0:T(8,128)(2,1)S(1)} %collective-permute-done.5.refs_0_), channel_id=1, source_target_pairs={{0,4},{4,0},{8,12},{12,8},{1,5},{5,1},{9,13},{13,9},{2,6},{6,2},{1... | collective-permute-start | bytes 835592 | tf_op jit(solution)/shard_map/ppermute | solution.py:343
  23.1 6.7 %collective-permute-start.4 = (bf16[32,64,128]{2,1,0:T(8,128)(2,1)S(1)}, bf16[32,64,128]{2,1,0:T(8,128)(2,1)S(1)}, u32[]{:S(2)}, u32[]{:S(2)}) collective-permute-start(bf16[32,64,128]{2,1,0:T(8,128)(2,1)S(1)} %get-tuple-element.40), channel_id=1, source_target_pairs={{0,1},{1,0},{2,3},{3,2},{4,5},{5,4},{6,7},{7,6},{8,9},{9,8},{10,11... | collective-permute-start | bytes 1572872 | tf_op jit(solution)/shard_map/ppermute | solution.py:339
  23.1 8.1 %collective-permute-start.10 = (bf16[17,64,128]{2,1,0:T(8,128)(2,1)S(1)}, bf16[17,64,128]{2,1,0:T(8,128)(2,1)S(1)}, u32[]{:S(2)}, u32[]{:S(2)}) collective-permute-start(bf16[17,64,128]{2,1,0:T(8,128)(2,1)S(1)} %collective-permute-done.3.refs_1_), channel_id=1, source_target_pairs={{4,8},{8,4},{5,9},{9,5},{6,10},{10,6},{7,11},{11,7},{20,24},{24,20... | collective-permute-start | bytes 835592 | tf_op jit(solution)/shard_map/ppermute | solution.py:343
  23.8 4.5 %collective-permute-start.9 = (bf16[16,64,128]{2,1,0:T(8,128)(2,1)S(1)}, bf16[16,64,128]{2,1,0:T(8,128)(2,1)S(1)}, u32[]{:S(2)}, u32[]{:S(2)}) collective-permute-start(bf16[16,64,128]{2,1,0:T(8,128)(2,1)S(1)} %slice.7), channel_id=1, source_target_pairs={{0,1},{1,0},{2,3},{3,2},{4,5},{5,4},{6,7},{7,6},{8,9},{9,8},{10,11... | collective-permute-start | bytes 786440 | tf_op jit(solution)/shard_map/ppermute | solution.py:339
  24.4 9.3 %collective-permute-start.11 = (bf16[17,64,128]{2,1,0:T(8,128)(2,1)S(1)}, bf16[17,64,128]{2,1,0:T(8,128)(2,1)S(1)}, u32[]{:S(2)}, u32[]{:S(2)}) collective-permute-start(bf16[17,64,128]{2,1,0:T(8,128)(2,1)S(1)} %collective-permute-done.3.refs_1_), channel_id=1, source_target_pairs={{0,4},{4,0},{8,12},{12,8},{1,5},{5,1},{9,13},{13,9},{2,6},{6,2},{1... | collective-permute-start | bytes 835592 | tf_op jit(solution)/shard_map/ppermute | solution.py:343
  27.6 2.2 %collective-permute-start.8 = (bf16[16,64,128]{2,1,0:T(8,128)(2,1)S(1)}, bf16[16,64,128]{2,1,0:T(8,128)(2,1)S(1)}, u32[]{:S(2)}, u32[]{:S(2)}) collective-permute-start(bf16[16,64,128]{2,1,0:T(8,128)(2,1)S(1)} %slice.6), channel_id=1, source_target_pairs={{0,1},{1,0},{2,3},{3,2},{4,5},{5,4},{6,7},{7,6},{8,9},{9,8},{10,11... | collective-permute-start | bytes 786440 | tf_op jit(solution)/shard_map/ppermute | solution.py:339
  28.3 11.8 %collective-permute-start.2 = (bf16[16,64,128]{2,1,0:T(8,128)(2,1)S(1)}, bf16[16,64,128]{2,1,0:T(8,128)(2,1)S(1)}, u32[]{:S(2)}, u32[]{:S(2)}) collective-permute-start(bf16[16,64,128]{2,1,0:T(8,128)(2,1)S(1)} %get-tuple-element.34), channel_id=1, source_target_pairs={{0,1},{1,0},{2,3},{3,2},{4,5},{5,4},{6,7},{7,6},{8,9},{9,8},{10,11... | collective-permute-start | bytes 786440 | tf_op jit(solution)/shard_map/ppermute | solution.py:339
  34.9 12.6 %all-to-all-start = ((f32[16,16,128]{2,1,0:T(8,128)}), f32[16,16,128]{2,1,0:T(8,128)S(1)}, u32[]{:S(2)}, u32[]{:S(2)}) async-start(f32[16,16,128]{2,1,0:T(8,128)} %bitcast), calls=%async_computation | async-start | bytes 262144 | tf_op jit(solution)/shard_map/all_to_all | solution.py:410
  39.5 1.9 %collective-permute-start.12 = (bf16[8,64,128]{2,1,0:T(8,128)(2,1)S(1)}, bf16[8,64,128]{2,1,0:T(8,128)(2,1)S(1)}, u32[]{:S(2)}, u32[]{:S(2)}) collective-permute-start(bf16[8,64,128]{2,1,0:T(8,128)(2,1)S(1)} %get-tuple-element.52), channel_id=1, source_target_pairs={{0,1},{1,0},{2,3},{3,2},{4,5},{5,4},{6,7},{7,6},{8,9},{9,8},{10,11... | collective-permute-start | bytes 393224 | tf_op jit(solution)/shard_map/ppermute | solution.py:339
  39.9 1.5 %collective-permute-start.13 = (bf16[8,64,128]{2,1,0:T(8,128)(2,1)S(1)}, bf16[8,64,128]{2,1,0:T(8,128)(2,1)S(1)}, u32[]{:S(2)}, u32[]{:S(2)}) collective-permute-start(bf16[8,64,128]{2,1,0:T(8,128)(2,1)S(1)} %get-tuple-element.53), channel_id=1, source_target_pairs={{0,1},{1,0},{2,3},{3,2},{4,5},{5,4},{6,7},{7,6},{8,9},{9,8},{10,11... | collective-permute-start | bytes 393224 | tf_op jit(solution)/shard_map/ppermute | solution.py:339

commit v15 on v13

--- a/solution.py
+++ b/solution.py
@@ -228,9 +228,12 @@
     rows, columns, nz = partials[0].shape
     half = rows // 2
     core = lax.axis_index("blk") % CORES
-    gram[:, 0:columns] = first_gram[:, 0:columns]
+    slabs, blocks = lax.axis_size("dom"), lax.axis_size("blk")
+    share = left.shape[0] // (slabs * blocks)
+    values = [first_gram[:, 0:columns]]
     for k in range(count):
-        total = first_gram[:, (k + 1) * columns:(k + 2) * columns]
+        block = slice((k + 1) * columns, (k + 2) * columns)
+        total = jnp.zeros((left.shape[0], columns), F32)
         for i in range(0, half, 2):
             pair = []
             for at in (i, i + 1):
@@ -241,8 +244,13 @@
                 theirs[k][at] = jnp.where(core == 0, image, other)
                 pair.append(image)
             y = half + i
-            total += weight * gram_of(left[:, y * nz:(y + 2) * nz], jnp.concatenate(pair, 1))
-        gram[:, (k + 1) * columns:(k + 2) * columns] = total
+            total += gram_of(left[:, y * nz:(y + 2) * nz], jnp.concatenate(pair, 1))
+        values.append(first_gram[:, block] + weight * total)
+    for slab in range(slabs):
+        for owner in range(blocks):
+            start, place = (slab * blocks + owner) * share, (owner * slabs + slab) * share
+            for k, value in enumerate(values):
+                gram[place:place + share, k * columns:(k + 1) * columns] = value[start:start + share]
 
 
 def turn_out(image, start, applied, wide, turned, sem):
@@ -286,9 +294,9 @@
     for core in range(CORES):
         sums = []
         for chip in range(chips):
-            total = shares[CORES * chip + core]
+            total = shares[(CORES * chip + core) * slabs]
             for slab in range(1, slabs):
-                total += shares[slab * blocks + CORES * chip + core]
+                total += shares[(CORES * chip + core) * slabs + slab]
             sums.append(total)
         for target in range(chips):
             parts = [sums[chip][:, (chip ^ target) * columns:((chip ^ target) + 1) * columns] for chip in range(chips)]
@@ -401,7 +409,7 @@
     )
     parts = slabs * blocks
     shares = gram.reshape(parts, total // parts, chips * columns)
-    shares = lax.all_to_all(shares, ("dom", "blk"), split_axis=0, concat_axis=0, tiled=True)
+    shares = lax.all_to_all(shares, ("blk", "dom"), split_axis=0, concat_axis=0, tiled=True)
     pieces = []
     for k in range(count):
         pieces += [images[k], swap(images[count + k], 1)]

time: 48.3 us -> 47.7 us (0.988)
  waiting for transfers between devices: 14.2 us -> 13.6 us
    all_to_all x1, waiting for transfers between devices: 5.35 us -> 4.76 us  [per_device(): lax.all_to_all(shares, ('blk', 'dom'), split_axis=0, concat_axis=0, tiled...]
where the time goes in v15:
time: 47.7 us; the launch traced here: 47.4 us
  starting transfers between devices  20.2 us (42%)
  waiting for transfers between devices  13.6 us (29%)
  Pallas kernels  10.7 us (22%)
  local copies, waits for them, and re-layouts  2.1 us (4%)
  between operations  0.79 us (2%)
    ppermute x6, starting transfers between devices, exchange(): lax.ppermute(array, 'dom', [(d, to) for d, to in enumerate(partner) if 0...  12.6 us
    pallas_call x9, Pallas kernels, call(): pl.pallas_call(kernel, out_shape=out_shape, in_specs=specs or [VMEM] * le...  8.68 us
    ppermute x7, waiting for transfers between devices, swap(): return lax.ppermute(array, 'blk', [(i, i ^ s) for i in range(blocks)])  5.55 us
    all_to_all x1, starting transfers between devices, per_device(): lax.all_to_all(shares, ('blk', 'dom'), split_axis=0, concat_axis=0, tiled...  4.89 us
    all_to_all x1, waiting for transfers between devices, per_device(): lax.all_to_all(shares, ('blk', 'dom'), split_axis=0, concat_axis=0, tiled...  4.76 us
    ppermute x6, waiting for transfers between devices, exchange(): lax.ppermute(array, 'dom', [(d, to) for d, to in enumerate(partner) if 0...  3.25 us
    ppermute x7, starting transfers between devices, swap(): return lax.ppermute(array, 'blk', [(i, i ^ s) for i in range(blocks)])  2.74 us
    unnamed x6, local copies, waits for them, and re-layouts  2.07 us
  transfers between devices with their start and end apart: 14, of which 5 were waited for; matrix products, arithmetic and copies ran while one was open for 0% of the time, Pallas kernels for 17%

profile of v15, /device:TPU:0, one launch (start us, length us, event | category | flops | bytes accessed | tf_op | source)
XLA Modules:
  0.0 47.4 jit_solution(5557851915960143033)
XLA Ops:
  0.6 2.1 %shard_map.59 = (bf16[33,64,128]{2,1,0:T(8,128)(2,1)S(1)}, bf16[34,64,128]{2,1,0:T(8,128)(2,1)S(1)}, bf16[32,64,128]{2,1,0:T(8,128)(2,1)S(1)}, bf16[17,64,128]{2,1,0:T(8,128)(2,1)S(1)}, bf16[17,64,128]{2,1,0:T(8,128)(2,1)S(1)}) custom-call(bf16[64,1,64,128]{3,2,1,0:T(8,128)(2,1)} %basis_hbm.1, s32[1,64,128]{2,1,0:T(8,128)} %zone_ref.1, f32[16]{0:T(128)} %cond_ref.1), custom_call_target="tpu_custom_call" | custom-call | tf_op jit(solution)/shard_map/pallas_call | solution.py:88
  2.7 0.7 %collective-permute-start.1 = (bf16[33,64,128]{2,1,0:T(8,128)(2,1)S(1)}, bf16[33,64,128]{2,1,0:T(8,128)(2,1)S(1)}, u32[]{:S(2)}, u32[]{:S(2)}) collective-permute-start(bf16[33,64,128]{2,1,0:T(8,128)(2,1)S(1)} %get-tuple-element.31), channel_id=1, source_target_pairs={{4,8},{8,4},{5,9},{9,5},{6,10},{10,6},{7,11},{11,7},{20,24},{24,20... | collective-permute-start | bytes 1622024 | tf_op jit(solution)/shard_map/ppermute | solution.py:345
  3.4 5.9 %collective-permute-start = (bf16[33,64,128]{2,1,0:T(8,128)(2,1)S(1)}, bf16[33,64,128]{2,1,0:T(8,128)(2,1)S(1)}, u32[]{:S(2)}, u32[]{:S(2)}) collective-permute-start(bf16[33,64,128]{2,1,0:T(8,128)(2,1)S(1)} %get-tuple-element.31), channel_id=1, source_target_pairs={{0,4},{4,0},{8,12},{12,8},{1,5},{5,1},{9,13},{13,9},{2,6},{6,2},{1... | collective-permute-start | bytes 1622024 | tf_op jit(solution)/shard_map/ppermute | solution.py:345
  9.3 1.5 %collective-permute-start.5 = (bf16[17,64,128]{2,1,0:T(8,128)(2,1)S(1)}, bf16[17,64,128]{2,1,0:T(8,128)(2,1)S(1)}, u32[]{:S(2)}, u32[]{:S(2)}) collective-permute-start(bf16[17,64,128]{2,1,0:T(8,128)(2,1)S(1)} %get-tuple-element.40), channel_id=1, source_target_pairs={{0,2},{1,3},{2,0},{3,1},{4,6},{5,7},{6,4},{7,5},{8,10},{9,11},{10,... | collective-permute-start | bytes 835592 | tf_op jit(solution)/shard_map/ppermute | solution.py:341
  10.8 0.0 copy-start
  10.8 0.8 %copy-done = s32[1,64,128]{2,1,0:T(8,128)S(1)} copy-done((s32[1,64,128]{2,1,0:T(8,128)S(1)}, s32[1,64,128]{2,1,0:T(8,128)}, u32[]{:S(2)}) %copy-start) | copy-done | bytes 32792
  11.5 0.0 copy-start.1
  11.5 0.7 %copy-done.1 = f32[16]{0:T(128)S(1)} copy-done((f32[16]{0:T(128)S(1)}, f32[16]{0:T(128)}, u32[]{:S(2)}) %copy-start.1) | copy-done | bytes 88
  12.2 0.0 copy-start.2
  12.2 0.7 %copy-done.2 = f32[16]{0:T(128)S(1)} copy-done((f32[16]{0:T(128)S(1)}, f32[16]{0:T(128)}, u32[]{:S(2)}) %copy-start.2) | copy-done | bytes 88
  12.8 1.3 %shard_map.60 = (f32[6,32,128]{2,1,0:T(8,128)S(1)}, f32[32,64,128]{2,1,0:T(8,128)S(1)}) custom-call(s32[1,64,128]{2,1,0:T(8,128)S(1)} %copy-done, f32[16]{0:T(128)S(1)} %copy-done.1, f32[16]{0:T(128)S(1)} %copy-done.2, bf16[34,64,128]{2,1,0:T(8,128)(2,1)S(1)} %get-tuple-element.28.center), custom_call_target="tpu_custom_call" | custom-call | flops 1073741824 | bytes 134217728 | tf_op jit(solution)/shard_map/pallas_call | solution.py:326
  14.2 0.6 %collective-permute-start.3 = (bf16[17,64,128]{2,1,0:T(8,128)(2,1)S(1)}, bf16[17,64,128]{2,1,0:T(8,128)(2,1)S(1)}, u32[]{:S(2)}, u32[]{:S(2)}) collective-permute-start(bf16[17,64,128]{2,1,0:T(8,128)(2,1)S(1)} %get-tuple-element.38), channel_id=1, source_target_pairs={{0,2},{1,3},{2,0},{3,1},{4,6},{5,7},{6,4},{7,5},{8,10},{9,11},{10,... | collective-permute-start | bytes 835592 | tf_op jit(solution)/shard_map/ppermute | solution.py:341
  14.8 3.6 %collective-permute-done.5.refs_0_ = bf16[17,64,128]{2,1,0:T(8,128)(2,1)S(1)} collective-permute-done((bf16[17,64,128]{2,1,0:T(8,128)(2,1)S(1)}, bf16[17,64,128]{2,1,0:T(8,128)(2,1)S(1)}, u32[]{:S(2)}, u32[]{:S(2)}) %collective-permute-start.5) | collective-permute-done | bytes 278560 | tf_op jit(solution)/shard_map/ppermute | solution.py:341
  18.3 0.7 %collective-permute-start.6 = (bf16[17,64,128]{2,1,0:T(8,128)(2,1)S(1)}, bf16[17,64,128]{2,1,0:T(8,128)(2,1)S(1)}, u32[]{:S(2)}, u32[]{:S(2)}) collective-permute-start(bf16[17,64,128]{2,1,0:T(8,128)(2,1)S(1)} %collective-permute-done.5.refs_0_), channel_id=1, source_target_pairs={{4,8},{8,4},{5,9},{9,5},{6,10},{10,6},{7,11},{11,7},{20,24},{24,20... | collective-permute-start | bytes 835592 | tf_op jit(solution)/shard_map/ppermute | solution.py:345
  19.0 2.1 %collective-permute-start.7 = (bf16[17,64,128]{2,1,0:T(8,128)(2,1)S(1)}, bf16[17,64,128]{2,1,0:T(8,128)(2,1)S(1)}, u32[]{:S(2)}, u32[]{:S(2)}) collective-permute-start(bf16[17,64,128]{2,1,0:T(8,128)(2,1)S(1)} %collective-permute-done.5.refs_0_), channel_id=1, source_target_pairs={{0,4},{4,0},{8,12},{12,8},{1,5},{5,1},{9,13},{13,9},{2,6},{6,2},{1... | collective-permute-start | bytes 835592 | tf_op jit(solution)/shard_map/ppermute | solution.py:345
  21.1 2.0 %collective-permute-done.3.refs_1_ = bf16[17,64,128]{2,1,0:T(8,128)(2,1)S(1)} collective-permute-done((bf16[17,64,128]{2,1,0:T(8,128)(2,1)S(1)}, bf16[17,64,128]{2,1,0:T(8,128)(2,1)S(1)}, u32[]{:S(2)}, u32[]{:S(2)}) %collective-permute-start.3) | collective-permute-done | bytes 278560 | tf_op jit(solution)/shard_map/ppermute | solution.py:341
  23.1 0.0 collective-permute-start.4
  23.1 0.0 collective-permute-done.1.two
  23.1 0.7 %collective-permute-start.10 = (bf16[17,64,128]{2,1,0:T(8,128)(2,1)S(1)}, bf16[17,64,128]{2,1,0:T(8,128)(2,1)S(1)}, u32[]{:S(2)}, u32[]{:S(2)}) collective-permute-start(bf16[17,64,128]{2,1,0:T(8,128)(2,1)S(1)} %collective-permute-done.3.refs_1_), channel_id=1, source_target_pairs={{4,8},{8,4},{5,9},{9,5},{6,10},{10,6},{7,11},{11,7},{20,24},{24,20... | collective-permute-start | bytes 835592 | tf_op jit(solution)/shard_map/ppermute | solution.py:345
  23.8 0.0 collective-permute-done.one
  23.8 2.6 %collective-permute-start.11 = (bf16[17,64,128]{2,1,0:T(8,128)(2,1)S(1)}, bf16[17,64,128]{2,1,0:T(8,128)(2,1)S(1)}, u32[]{:S(2)}, u32[]{:S(2)}) collective-permute-start(bf16[17,64,128]{2,1,0:T(8,128)(2,1)S(1)} %collective-permute-done.3.refs_1_), channel_id=1, source_target_pairs={{0,4},{4,0},{8,12},{12,8},{1,5},{5,1},{9,13},{13,9},{2,6},{6,2},{1... | collective-permute-start | bytes 835592 | tf_op jit(solution)/shard_map/ppermute | solution.py:345
  26.3 0.0 collective-permute-done.6.refs_2_
  26.4 0.1 collective-permute-start.9
  26.5 1.0 %collective-permute-done.7.refs_3_ = bf16[17,64,128]{2,1,0:T(8,128)(2,1)S(1)} collective-permute-done((bf16[17,64,128]{2,1,0:T(8,128)(2,1)S(1)}, bf16[17,64,128]{2,1,0:T(8,128)(2,1)S(1)}, u32[]{:S(2)}, u32[]{:S(2)}) %collective-permute-start.7) | collective-permute-done | bytes 278560 | tf_op jit(solution)/shard_map/ppermute | solution.py:345
  27.5 0.0 collective-permute-start.8
  27.5 0.7 %shard_map.63 = (bf16[34,64,128]{2,1,0:T(8,128)(2,1)S(1)}, f32[32,64,128]{2,1,0:T(8,128)S(1)}) custom-call(f32[6,32,128]{2,1,0:T(8,128)S(1)} %get-tuple-element.29.coef, bf16[17,64,128]{2,1,0:T(8,128)(2,1)S(1)} %collective-permute-done.5.refs_0_, bf16[17,64,128]{2,1,0:T(8,128)(2,1)S(1)} %collective-permute-done.3.refs_1_), custom_call_target="tpu_custom_call" | custom-call | flops 1 | bytes 1 | tf_op jit(solution)/shard_map/pallas_call | solution.py:326
  28.2 0.6 %shard_map.61 = (bf16[16,64,128]{2,1,0:T(8,128)(2,1)S(1)}, bf16[16,64,128]{2,1,0:T(8,128)(2,1)S(1)}, f32[2,32,128]{2,1,0:T(8,128)S(1)}, bf16[64,4096]{1,0:T(8,128)(2,1)S(1)}) custom-call(f32[6,32,128]{2,1,0:T(8,128)S(1)} %get-tuple-element.29.coef, f32[32,64,128]{2,1,0:T(8,128)S(1)} %get-tuple-element.30.partial, ...), custom_call_target="tpu_custom_call" | custom-call | flops 1 | bytes 1 | tf_op jit(solution)/shard_map/pallas_call | solution.py:326
  28.8 0.2 shard_map.64
  28.9 0.0 collective-permute-done.9.refs_3_
  29.0 0.6 %collective-permute-start.2 = (bf16[16,64,128]{2,1,0:T(8,128)(2,1)S(1)}, bf16[16,64,128]{2,1,0:T(8,128)(2,1)S(1)}, u32[]{:S(2)}, u32[]{:S(2)}) collective-permute-start(bf16[16,64,128]{2,1,0:T(8,128)(2,1)S(1)} %get-tuple-element.33), channel_id=1, source_target_pairs={{0,1},{1,0},{2,3},{3,2},{4,5},{5,4},{6,7},{7,6},{8,9},{9,8},{10,11... | collective-permute-start | bytes 786440 | tf_op jit(solution)/shard_map/ppermute | solution.py:341
  29.5 0.0 collective-permute-done.8.refs_2_
  29.5 0.0 collective-permute-done.4.plain
  29.5 1.4 %shard_map.65 = (bf16[256,4096]{1,0:T(8,128)(2,1)S(1)}, f32[256,128]{1,0:T(8,128)S(1)}) custom-call(bf16[64,4096]{1,0:T(8,128)(2,1)S(1)} %get-tuple-element.35.flat, bf16[34,64,128]{2,1,0:T(8,128)(2,1)S(1)} %get-tuple-element.28.center, bf16[32,64,128]{2,1,0:T(8,128)(2,1)S(1)} %collective-permute-done.4.plain, ...), custom_call_target="tpu_custom_call" | custom-call | flops 1 | bytes 1 | tf_op jit(solution)/shard_map/pallas_call | solution.py:326
  30.9 0.0 collective-permute-done.10.refs_2_
  30.9 2.3 %collective-permute-done.11.refs_3_ = bf16[17,64,128]{2,1,0:T(8,128)(2,1)S(1)} collective-permute-done((bf16[17,64,128]{2,1,0:T(8,128)(2,1)S(1)}, bf16[17,64,128]{2,1,0:T(8,128)(2,1)S(1)}, u32[]{:S(2)}, u32[]{:S(2)}) %collective-permute-start.11) | collective-permute-done | bytes 278560 | tf_op jit(solution)/shard_map/ppermute | solution.py:345
  33.2 1.2 %shard_map.66 = (bf16[16,64,128]{2,1,0:T(8,128)(2,1)S(1)}, bf16[16,64,128]{2,1,0:T(8,128)(2,1)S(1)}, f32[256,128]{1,0:T(8,128)}) custom-call(f32[2,32,128]{2,1,0:T(8,128)S(1)} %get-tuple-element.34.faces, bf16[256,4096]{1,0:T(8,128)(2,1)S(1)} %get-tuple-element.47.left, f32[256,128]{1,0:T(8,128)S(1)} %get-tuple-element.48.first_gram, ...), custom_call_target="tpu_custom_call" | custom-call | flops 1 | bytes 1 | tf_op jit(solution)/shard_map/pallas_call | solution.py:326
  34.4 0.0 collective-permute-start.12
  34.4 4.9 %all-to-all-start = ((f32[16,16,128]{2,1,0:T(8,128)}), f32[16,16,128]{2,1,0:T(8,128)S(1)}, u32[]{:S(2)}, u32[]{:S(2)}) async-start(f32[16,16,128]{2,1,0:T(8,128)} %bitcast), calls=%async_computation | async-start | bytes 262144 | tf_op jit(solution)/shard_map/all_to_all | solution.py:412
  39.3 0.0 collective-permute-done.2.theirs
  39.3 1.3 %shard_map.62.applied_in = bf16[256,1,16,128]{3,2,1,0:T(8,128)(2,1)} custom-call(bf16[16,64,128]{2,1,0:T(8,128)(2,1)S(1)} %get-tuple-element.32.mine, bf16[16,64,128]{2,1,0:T(8,128)(2,1)S(1)} %collective-permute-done.2.theirs), custom_call_target="tpu_custom_call" | custom-call | flops 1 | bytes 1 | tf_op jit(solution)/shard_map/pallas_call | solution.py:326
  40.6 0.0 collective-permute-done.12.refs_1_
  40.6 1.3 %shard_map.67 = bf16[256,1,16,128]{3,2,1,0:T(8,128)(2,1)} custom-call(bf16[256,1,16,128]{3,2,1,0:T(8,128)(2,1)} %shard_map.62.applied_in, bf16[16,64,128]{2,1,0:T(8,128)(2,1)S(1)} %get-tuple-element.50.refs_0_, bf16[16,64,128]{2,1,0:T(8,128)(2,1)S(1)} %collective-permute-done.12.refs_1_), custom_call_target="tpu_custom_call", output_to_operand_aliasing={{}: (0, {})} | custom-call | flops 1 | bytes 1 | tf_op jit(solution)/shard_map/pallas_call | solution.py:326
  41.9 4.8 %all-to-all-done.shares = f32[16,16,128]{2,1,0:T(8,128)S(1)} async-done(((f32[16,16,128]{2,1,0:T(8,128)}), f32[16,16,128]{2,1,0:T(8,128)S(1)}, u32[]{:S(2)}, u32[]{:S(2)}) %all-to-all-start) | async-done | bytes 131104 | tf_op jit(solution)/shard_map/all_to_all | solution.py:412
  46.6 0.7 %shard_map.68 = f32[16,256]{1,0:T(8,128)} custom-call(f32[16,16,128]{2,1,0:T(8,128)S(1)} %all-to-all-done.shares), custom_call_target="tpu_custom_call" | custom-call | flops 1 | bytes 1 | tf_op jit(solution)/shard_map/pallas_call | solution.py:326
  (2 shorter events, 0.0 us)
Async XLA Ops:
  2.7 20.4 %collective-permute-start.1 = (bf16[33,64,128]{2,1,0:T(8,128)(2,1)S(1)}, bf16[33,64,128]{2,1,0:T(8,128)(2,1)S(1)}, u32[]{:S(2)}, u32[]{:S(2)}) collective-permute-start(bf16[33,64,128]{2,1,0:T(8,128)(2,1)S(1)} %get-tuple-element.31), channel_id=1, source_target_pairs={{4,8},{8,4},{5,9},{9,5},{6,10},{10,6},{7,11},{11,7},{20,24},{24,20... | collective-permute-start | bytes 1622024 | tf_op jit(solution)/shard_map/ppermute | solution.py:345
  3.4 20.4 %collective-permute-start = (bf16[33,64,128]{2,1,0:T(8,128)(2,1)S(1)}, bf16[33,64,128]{2,1,0:T(8,128)(2,1)S(1)}, u32[]{:S(2)}, u32[]{:S(2)}) collective-permute-start(bf16[33,64,128]{2,1,0:T(8,128)(2,1)S(1)} %get-tuple-element.31), channel_id=1, source_target_pairs={{0,4},{4,0},{8,12},{12,8},{1,5},{5,1},{9,13},{13,9},{2,6},{6,2},{1... | collective-permute-start | bytes 1622024 | tf_op jit(solution)/shard_map/ppermute | solution.py:345
  9.3 9.1 %collective-permute-start.5 = (bf16[17,64,128]{2,1,0:T(8,128)(2,1)S(1)}, bf16[17,64,128]{2,1,0:T(8,128)(2,1)S(1)}, u32[]{:S(2)}, u32[]{:S(2)}) collective-permute-start(bf16[17,64,128]{2,1,0:T(8,128)(2,1)S(1)} %get-tuple-element.40), channel_id=1, source_target_pairs={{0,2},{1,3},{2,0},{3,1},{4,6},{5,7},{6,4},{7,5},{8,10},{9,11},{10,... | collective-permute-start | bytes 835592 | tf_op jit(solution)/shard_map/ppermute | solution.py:341
  10.8 0.8 %copy-start = (s32[1,64,128]{2,1,0:T(8,128)S(1)}, s32[1,64,128]{2,1,0:T(8,128)}, u32[]{:S(2)}) copy-start(s32[1,64,128]{2,1,0:T(8,128)} %zone_ref.1) | copy-start | bytes 98308
  11.5 0.7 %copy-start.1 = (f32[16]{0:T(128)S(1)}, f32[16]{0:T(128)}, u32[]{:S(2)}) copy-start(f32[16]{0:T(128)} %cond_ref.1) | copy-start | bytes 196
  12.2 0.7 %copy-start.2 = (f32[16]{0:T(128)S(1)}, f32[16]{0:T(128)}, u32[]{:S(2)}) copy-start(f32[16]{0:T(128)} %heat_ref.1) | copy-start | bytes 196
  14.2 8.9 %collective-permute-start.3 = (bf16[17,64,128]{2,1,0:T(8,128)(2,1)S(1)}, bf16[17,64,128]{2,1,0:T(8,128)(2,1)S(1)}, u32[]{:S(2)}, u32[]{:S(2)}) collective-permute-start(bf16[17,64,128]{2,1,0:T(8,128)(2,1)S(1)} %get-tuple-element.38), channel_id=1, source_target_pairs={{0,2},{1,3},{2,0},{3,1},{4,6},{5,7},{6,4},{7,5},{8,10},{9,11},{10,... | collective-permute-start | bytes 835592 | tf_op jit(solution)/shard_map/ppermute | solution.py:341
  18.3 8.0 %collective-permute-start.6 = (bf16[17,64,128]{2,1,0:T(8,128)(2,1)S(1)}, bf16[17,64,128]{2,1,0:T(8,128)(2,1)S(1)}, u32[]{:S(2)}, u32[]{:S(2)}) collective-permute-start(bf16[17,64,128]{2,1,0:T(8,128)(2,1)S(1)} %collective-permute-done.5.refs_0_), channel_id=1, source_target_pairs={{4,8},{8,4},{5,9},{9,5},{6,10},{10,6},{7,11},{11,7},{20,24},{24,20... | collective-permute-start | bytes 835592 | tf_op jit(solution)/shard_map/ppermute | solution.py:345
  19.0 8.4 %collective-permute-start.7 = (bf16[17,64,128]{2,1,0:T(8,128)(2,1)S(1)}, bf16[17,64,128]{2,1,0:T(8,128)(2,1)S(1)}, u32[]{:S(2)}, u32[]{:S(2)}) collective-permute-start(bf16[17,64,128]{2,1,0:T(8,128)(2,1)S(1)} %collective-permute-done.5.refs_0_), channel_id=1, source_target_pairs={{0,4},{4,0},{8,12},{12,8},{1,5},{5,1},{9,13},{13,9},{2,6},{6,2},{1... | collective-permute-start | bytes 835592 | tf_op jit(solution)/shard_map/ppermute | solution.py:345
  23.1 6.5 %collective-permute-start.4 = (bf16[32,64,128]{2,1,0:T(8,128)(2,1)S(1)}, bf16[32,64,128]{2,1,0:T(8,128)(2,1)S(1)}, u32[]{:S(2)}, u32[]{:S(2)}) collective-permute-start(bf16[32,64,128]{2,1,0:T(8,128)(2,1)S(1)} %get-tuple-element.39), channel_id=1, source_target_pairs={{0,1},{1,0},{2,3},{3,2},{4,5},{5,4},{6,7},{7,6},{8,9},{9,8},{10,11... | collective-permute-start | bytes 1572872 | tf_op jit(solution)/shard_map/ppermute | solution.py:341
  23.1 7.9 %collective-permute-start.10 = (bf16[17,64,128]{2,1,0:T(8,128)(2,1)S(1)}, bf16[17,64,128]{2,1,0:T(8,128)(2,1)S(1)}, u32[]{:S(2)}, u32[]{:S(2)}) collective-permute-start(bf16[17,64,128]{2,1,0:T(8,128)(2,1)S(1)} %collective-permute-done.3.refs_1_), channel_id=1, source_target_pairs={{4,8},{8,4},{5,9},{9,5},{6,10},{10,6},{7,11},{11,7},{20,24},{24,20... | collective-permute-start | bytes 835592 | tf_op jit(solution)/shard_map/ppermute | solution.py:345
  23.8 9.4 %collective-permute-start.11 = (bf16[17,64,128]{2,1,0:T(8,128)(2,1)S(1)}, bf16[17,64,128]{2,1,0:T(8,128)(2,1)S(1)}, u32[]{:S(2)}, u32[]{:S(2)}) collective-permute-start(bf16[17,64,128]{2,1,0:T(8,128)(2,1)S(1)} %collective-permute-done.3.refs_1_), channel_id=1, source_target_pairs={{0,4},{4,0},{8,12},{12,8},{1,5},{5,1},{9,13},{13,9},{2,6},{6,2},{1... | collective-permute-start | bytes 835592 | tf_op jit(solution)/shard_map/ppermute | solution.py:345
  26.4 2.6 %collective-permute-start.9 = (bf16[16,64,128]{2,1,0:T(8,128)(2,1)S(1)}, bf16[16,64,128]{2,1,0:T(8,128)(2,1)S(1)}, u32[]{:S(2)}, u32[]{:S(2)}) collective-permute-start(bf16[16,64,128]{2,1,0:T(8,128)(2,1)S(1)} %slice.7), channel_id=1, source_target_pairs={{0,1},{1,0},{2,3},{3,2},{4,5},{5,4},{6,7},{7,6},{8,9},{9,8},{10,11... | collective-permute-start | bytes 786440 | tf_op jit(solution)/shard_map/ppermute | solution.py:341
  27.5 2.1 %collective-permute-start.8 = (bf16[16,64,128]{2,1,0:T(8,128)(2,1)S(1)}, bf16[16,64,128]{2,1,0:T(8,128)(2,1)S(1)}, u32[]{:S(2)}, u32[]{:S(2)}) collective-permute-start(bf16[16,64,128]{2,1,0:T(8,128)(2,1)S(1)} %slice.6), channel_id=1, source_target_pairs={{0,1},{1,0},{2,3},{3,2},{4,5},{5,4},{6,7},{7,6},{8,9},{9,8},{10,11... | collective-permute-start | bytes 786440 | tf_op jit(solution)/shard_map/ppermute | solution.py:341
  29.0 10.3 %collective-permute-start.2 = (bf16[16,64,128]{2,1,0:T(8,128)(2,1)S(1)}, bf16[16,64,128]{2,1,0:T(8,128)(2,1)S(1)}, u32[]{:S(2)}, u32[]{:S(2)}) collective-permute-start(bf16[16,64,128]{2,1,0:T(8,128)(2,1)S(1)} %get-tuple-element.33), channel_id=1, source_target_pairs={{0,1},{1,0},{2,3},{3,2},{4,5},{5,4},{6,7},{7,6},{8,9},{9,8},{10,11... | collective-permute-start | bytes 786440 | tf_op jit(solution)/shard_map/ppermute | solution.py:341
  34.4 6.2 %collective-permute-start.12 = (bf16[16,64,128]{2,1,0:T(8,128)(2,1)S(1)}, bf16[16,64,128]{2,1,0:T(8,128)(2,1)S(1)}, u32[]{:S(2)}, u32[]{:S(2)}) collective-permute-start(bf16[16,64,128]{2,1,0:T(8,128)(2,1)S(1)} %get-tuple-element.51), channel_id=1, source_target_pairs={{0,1},{1,0},{2,3},{3,2},{4,5},{5,4},{6,7},{7,6},{8,9},{9,8},{10,11... | collective-permute-start | bytes 786440 | tf_op jit(solution)/shard_map/ppermute | solution.py:341
  34.4 12.3 %all-to-all-start = ((f32[16,16,128]{2,1,0:T(8,128)}), f32[16,16,128]{2,1,0:T(8,128)S(1)}, u32[]{:S(2)}, u32[]{:S(2)}) async-start(f32[16,16,128]{2,1,0:T(8,128)} %bitcast), calls=%async_computation | async-start | bytes 262144 | tf_op jit(solution)/shard_map/all_to_all | solution.py:412

commit v16 on v15

--- a/solution.py
+++ b/solution.py
@@ -248,7 +248,7 @@
         values.append(first_gram[:, block] + weight * total)
     for slab in range(slabs):
         for owner in range(blocks):
-            start, place = (slab * blocks + owner) * share, (owner * slabs + slab) * share
+            start, place = (slab * blocks + owner) * share, (slabs * blocks - 1 - owner * slabs - slab) * share
             for k, value in enumerate(values):
                 gram[place:place + share, k * columns:(k + 1) * columns] = value[start:start + share]
 
@@ -294,9 +294,10 @@
     for core in range(CORES):
         sums = []
         for chip in range(chips):
-            total = shares[(CORES * chip + core) * slabs]
+            last = slabs * blocks - 1 - (CORES * chip + core) * slabs
+            total = shares[last]
             for slab in range(1, slabs):
-                total += shares[(CORES * chip + core) * slabs + slab]
+                total += shares[last - slab]
             sums.append(total)
         for target in range(chips):
             parts = [sums[chip][:, (chip ^ target) * columns:((chip ^ target) + 1) * columns] for chip in range(chips)]
@@ -409,7 +410,9 @@
     )
     parts = slabs * blocks
     shares = gram.reshape(parts, total // parts, chips * columns)
-    shares = lax.all_to_all(shares, ("blk", "dom"), split_axis=0, concat_axis=0, tiled=True)
+    shares = lax.all_to_all(
+        shares, ("blk", "dom"), split_axis=0, concat_axis=0, tiled=True, axis_index_groups=[[*reversed(range(parts))]]
+    )
     pieces = []
     for k in range(count):
         pieces += [images[k], swap(images[count + k], 1)]

time: 47.7 us -> 46.6 us (0.977)
  waiting for transfers between devices: 13.6 us -> 10.7 us
  starting transfers between devices: 20.2 us -> 21.9 us
    all_to_all x1, waiting for transfers between devices: 4.76 us -> 1.89 us  [per_device(): lax.all_to_all(shares, ('blk', 'dom'), split_axis=0, concat_axis=0, tiled...]
    all_to_all x1, starting transfers between devices: 4.89 us -> 6.64 us  [per_device(): lax.all_to_all(shares, ('blk', 'dom'), split_axis=0, concat_axis=0, tiled...]
where the time goes in v16:
time: 46.6 us; the launch traced here: 46.3 us
  starting transfers between devices  21.9 us (47%)
  Pallas kernels  10.7 us (23%)
  waiting for transfers between devices  10.7 us (23%)
  local copies, waits for them, and re-layouts  2.1 us (5%)
  between operations  0.77 us (2%)
    ppermute x6, starting transfers between devices, exchange(): lax.ppermute(array, 'dom', [(d, to) for d, to in enumerate(partner) if 0...  12.6 us
    pallas_call x9, Pallas kernels, call(): pl.pallas_call(kernel, out_shape=out_shape, in_specs=specs or [VMEM] * le...  8.68 us
    all_to_all x1, starting transfers between devices, per_device(): lax.all_to_all(shares, ('blk', 'dom'), split_axis=0, concat_axis=0, tiled...  6.64 us
    ppermute x7, waiting for transfers between devices, swap(): return lax.ppermute(array, 'blk', [(i, i ^ s) for i in range(blocks)])  5.55 us
    ppermute x6, waiting for transfers between devices, exchange(): lax.ppermute(array, 'dom', [(d, to) for d, to in enumerate(partner) if 0...  3.25 us
    ppermute x7, starting transfers between devices, swap(): return lax.ppermute(array, 'blk', [(i, i ^ s) for i in range(blocks)])  2.74 us
    unnamed x6, local copies, waits for them, and re-layouts  2.07 us
    pallas_call x1, Pallas kernels, prepare(): pl.pallas_call(functools.partial(prepare_kernel, chips), out_shape=shapes...  2.06 us
  transfers between devices with their start and end apart: 14, of which 5 were waited for; matrix products, arithmetic and copies ran while one was open for 0% of the time, Pallas kernels for 17%

profile of v16, /device:TPU:0, one launch (start us, length us, event | category | flops | bytes accessed | tf_op | source)
XLA Modules:
  0.0 46.3 jit_solution(8465544164939863653)
XLA Ops:
  0.6 2.1 %shard_map.59 = (bf16[33,64,128]{2,1,0:T(8,128)(2,1)S(1)}, bf16[34,64,128]{2,1,0:T(8,128)(2,1)S(1)}, bf16[32,64,128]{2,1,0:T(8,128)(2,1)S(1)}, bf16[17,64,128]{2,1,0:T(8,128)(2,1)S(1)}, bf16[17,64,128]{2,1,0:T(8,128)(2,1)S(1)}) custom-call(bf16[64,1,64,128]{3,2,1,0:T(8,128)(2,1)} %basis_hbm.1, s32[1,64,128]{2,1,0:T(8,128)} %zone_ref.1, f32[16]{0:T(128)} %cond_ref.1), custom_call_target="tpu_custom_call" | custom-call | tf_op jit(solution)/shard_map/pallas_call | solution.py:88
  2.7 0.7 %collective-permute-start.1 = (bf16[33,64,128]{2,1,0:T(8,128)(2,1)S(1)}, bf16[33,64,128]{2,1,0:T(8,128)(2,1)S(1)}, u32[]{:S(2)}, u32[]{:S(2)}) collective-permute-start(bf16[33,64,128]{2,1,0:T(8,128)(2,1)S(1)} %get-tuple-element.31), channel_id=1, source_target_pairs={{4,8},{8,4},{5,9},{9,5},{6,10},{10,6},{7,11},{11,7},{20,24},{24,20... | collective-permute-start | bytes 1622024 | tf_op jit(solution)/shard_map/ppermute | solution.py:346
  3.4 5.9 %collective-permute-start = (bf16[33,64,128]{2,1,0:T(8,128)(2,1)S(1)}, bf16[33,64,128]{2,1,0:T(8,128)(2,1)S(1)}, u32[]{:S(2)}, u32[]{:S(2)}) collective-permute-start(bf16[33,64,128]{2,1,0:T(8,128)(2,1)S(1)} %get-tuple-element.31), channel_id=1, source_target_pairs={{0,4},{4,0},{8,12},{12,8},{1,5},{5,1},{9,13},{13,9},{2,6},{6,2},{1... | collective-permute-start | bytes 1622024 | tf_op jit(solution)/shard_map/ppermute | solution.py:346
  9.3 1.5 %collective-permute-start.5 = (bf16[17,64,128]{2,1,0:T(8,128)(2,1)S(1)}, bf16[17,64,128]{2,1,0:T(8,128)(2,1)S(1)}, u32[]{:S(2)}, u32[]{:S(2)}) collective-permute-start(bf16[17,64,128]{2,1,0:T(8,128)(2,1)S(1)} %get-tuple-element.40), channel_id=1, source_target_pairs={{0,2},{1,3},{2,0},{3,1},{4,6},{5,7},{6,4},{7,5},{8,10},{9,11},{10,... | collective-permute-start | bytes 835592 | tf_op jit(solution)/shard_map/ppermute | solution.py:342
  10.8 0.0 copy-start
  10.8 0.8 %copy-done = s32[1,64,128]{2,1,0:T(8,128)S(1)} copy-done((s32[1,64,128]{2,1,0:T(8,128)S(1)}, s32[1,64,128]{2,1,0:T(8,128)}, u32[]{:S(2)}) %copy-start) | copy-done | bytes 32792
  11.5 0.0 copy-start.1
  11.5 0.7 %copy-done.1 = f32[16]{0:T(128)S(1)} copy-done((f32[16]{0:T(128)S(1)}, f32[16]{0:T(128)}, u32[]{:S(2)}) %copy-start.1) | copy-done | bytes 88
  12.2 0.0 copy-start.2
  12.2 0.7 %copy-done.2 = f32[16]{0:T(128)S(1)} copy-done((f32[16]{0:T(128)S(1)}, f32[16]{0:T(128)}, u32[]{:S(2)}) %copy-start.2) | copy-done | bytes 88
  12.8 1.3 %shard_map.60 = (f32[6,32,128]{2,1,0:T(8,128)S(1)}, f32[32,64,128]{2,1,0:T(8,128)S(1)}) custom-call(s32[1,64,128]{2,1,0:T(8,128)S(1)} %copy-done, f32[16]{0:T(128)S(1)} %copy-done.1, f32[16]{0:T(128)S(1)} %copy-done.2, bf16[34,64,128]{2,1,0:T(8,128)(2,1)S(1)} %get-tuple-element.28.center), custom_call_target="tpu_custom_call" | custom-call | flops 1073741824 | bytes 134217728 | tf_op jit(solution)/shard_map/pallas_call | solution.py:327
  14.2 0.6 %collective-permute-start.3 = (bf16[17,64,128]{2,1,0:T(8,128)(2,1)S(1)}, bf16[17,64,128]{2,1,0:T(8,128)(2,1)S(1)}, u32[]{:S(2)}, u32[]{:S(2)}) collective-permute-start(bf16[17,64,128]{2,1,0:T(8,128)(2,1)S(1)} %get-tuple-element.38), channel_id=1, source_target_pairs={{0,2},{1,3},{2,0},{3,1},{4,6},{5,7},{6,4},{7,5},{8,10},{9,11},{10,... | collective-permute-start | bytes 835592 | tf_op jit(solution)/shard_map/ppermute | solution.py:342
  14.8 3.6 %collective-permute-done.5.refs_0_ = bf16[17,64,128]{2,1,0:T(8,128)(2,1)S(1)} collective-permute-done((bf16[17,64,128]{2,1,0:T(8,128)(2,1)S(1)}, bf16[17,64,128]{2,1,0:T(8,128)(2,1)S(1)}, u32[]{:S(2)}, u32[]{:S(2)}) %collective-permute-start.5) | collective-permute-done | bytes 278560 | tf_op jit(solution)/shard_map/ppermute | solution.py:342
  18.3 0.7 %collective-permute-start.6 = (bf16[17,64,128]{2,1,0:T(8,128)(2,1)S(1)}, bf16[17,64,128]{2,1,0:T(8,128)(2,1)S(1)}, u32[]{:S(2)}, u32[]{:S(2)}) collective-permute-start(bf16[17,64,128]{2,1,0:T(8,128)(2,1)S(1)} %collective-permute-done.5.refs_0_), channel_id=1, source_target_pairs={{4,8},{8,4},{5,9},{9,5},{6,10},{10,6},{7,11},{11,7},{20,24},{24,20... | collective-permute-start | bytes 835592 | tf_op jit(solution)/shard_map/ppermute | solution.py:346
  19.0 2.1 %collective-permute-start.7 = (bf16[17,64,128]{2,1,0:T(8,128)(2,1)S(1)}, bf16[17,64,128]{2,1,0:T(8,128)(2,1)S(1)}, u32[]{:S(2)}, u32[]{:S(2)}) collective-permute-start(bf16[17,64,128]{2,1,0:T(8,128)(2,1)S(1)} %collective-permute-done.5.refs_0_), channel_id=1, source_target_pairs={{0,4},{4,0},{8,12},{12,8},{1,5},{5,1},{9,13},{13,9},{2,6},{6,2},{1... | collective-permute-start | bytes 835592 | tf_op jit(solution)/shard_map/ppermute | solution.py:346
  21.1 2.0 %collective-permute-done.3.refs_1_ = bf16[17,64,128]{2,1,0:T(8,128)(2,1)S(1)} collective-permute-done((bf16[17,64,128]{2,1,0:T(8,128)(2,1)S(1)}, bf16[17,64,128]{2,1,0:T(8,128)(2,1)S(1)}, u32[]{:S(2)}, u32[]{:S(2)}) %collective-permute-start.3) | collective-permute-done | bytes 278560 | tf_op jit(solution)/shard_map/ppermute | solution.py:342
  23.1 0.0 collective-permute-start.4
  23.1 0.0 collective-permute-done.1.two
  23.1 0.7 %collective-permute-start.10 = (bf16[17,64,128]{2,1,0:T(8,128)(2,1)S(1)}, bf16[17,64,128]{2,1,0:T(8,128)(2,1)S(1)}, u32[]{:S(2)}, u32[]{:S(2)}) collective-permute-start(bf16[17,64,128]{2,1,0:T(8,128)(2,1)S(1)} %collective-permute-done.3.refs_1_), channel_id=1, source_target_pairs={{4,8},{8,4},{5,9},{9,5},{6,10},{10,6},{7,11},{11,7},{20,24},{24,20... | collective-permute-start | bytes 835592 | tf_op jit(solution)/shard_map/ppermute | solution.py:346
  23.8 0.0 collective-permute-done.one
  23.8 2.6 %collective-permute-start.11 = (bf16[17,64,128]{2,1,0:T(8,128)(2,1)S(1)}, bf16[17,64,128]{2,1,0:T(8,128)(2,1)S(1)}, u32[]{:S(2)}, u32[]{:S(2)}) collective-permute-start(bf16[17,64,128]{2,1,0:T(8,128)(2,1)S(1)} %collective-permute-done.3.refs_1_), channel_id=1, source_target_pairs={{0,4},{4,0},{8,12},{12,8},{1,5},{5,1},{9,13},{13,9},{2,6},{6,2},{1... | collective-permute-start | bytes 835592 | tf_op jit(solution)/shard_map/ppermute | solution.py:346
  26.3 0.0 collective-permute-done.6.refs_2_
  26.4 0.1 collective-permute-start.9
  26.5 1.0 %collective-permute-done.7.refs_3_ = bf16[17,64,128]{2,1,0:T(8,128)(2,1)S(1)} collective-permute-done((bf16[17,64,128]{2,1,0:T(8,128)(2,1)S(1)}, bf16[17,64,128]{2,1,0:T(8,128)(2,1)S(1)}, u32[]{:S(2)}, u32[]{:S(2)}) %collective-permute-start.7) | collective-permute-done | bytes 278560 | tf_op jit(solution)/shard_map/ppermute | solution.py:346
  27.5 0.0 collective-permute-start.8
  27.5 0.7 %shard_map.63 = (bf16[34,64,128]{2,1,0:T(8,128)(2,1)S(1)}, f32[32,64,128]{2,1,0:T(8,128)S(1)}) custom-call(f32[6,32,128]{2,1,0:T(8,128)S(1)} %get-tuple-element.29.coef, bf16[17,64,128]{2,1,0:T(8,128)(2,1)S(1)} %collective-permute-done.5.refs_0_, bf16[17,64,128]{2,1,0:T(8,128)(2,1)S(1)} %collective-permute-done.3.refs_1_), custom_call_target="tpu_custom_call" | custom-call | flops 1 | bytes 1 | tf_op jit(solution)/shard_map/pallas_call | solution.py:327
  28.2 0.6 %shard_map.61 = (bf16[16,64,128]{2,1,0:T(8,128)(2,1)S(1)}, bf16[16,64,128]{2,1,0:T(8,128)(2,1)S(1)}, f32[2,32,128]{2,1,0:T(8,128)S(1)}, bf16[64,4096]{1,0:T(8,128)(2,1)S(1)}) custom-call(f32[6,32,128]{2,1,0:T(8,128)S(1)} %get-tuple-element.29.coef, f32[32,64,128]{2,1,0:T(8,128)S(1)} %get-tuple-element.30.partial, ...), custom_call_target="tpu_custom_call" | custom-call | flops 1 | bytes 1 | tf_op jit(solution)/shard_map/pallas_call | solution.py:327
  28.8 0.2 shard_map.64
  28.9 0.0 collective-permute-done.9.refs_3_
  29.0 0.6 %collective-permute-start.2 = (bf16[16,64,128]{2,1,0:T(8,128)(2,1)S(1)}, bf16[16,64,128]{2,1,0:T(8,128)(2,1)S(1)}, u32[]{:S(2)}, u32[]{:S(2)}) collective-permute-start(bf16[16,64,128]{2,1,0:T(8,128)(2,1)S(1)} %get-tuple-element.33), channel_id=1, source_target_pairs={{0,1},{1,0},{2,3},{3,2},{4,5},{5,4},{6,7},{7,6},{8,9},{9,8},{10,11... | collective-permute-start | bytes 786440 | tf_op jit(solution)/shard_map/ppermute | solution.py:342
  29.5 0.0 collective-permute-done.8.refs_2_
  29.5 0.0 collective-permute-done.4.plain
  29.5 1.4 %shard_map.65 = (bf16[256,4096]{1,0:T(8,128)(2,1)S(1)}, f32[256,128]{1,0:T(8,128)S(1)}) custom-call(bf16[64,4096]{1,0:T(8,128)(2,1)S(1)} %get-tuple-element.35.flat, bf16[34,64,128]{2,1,0:T(8,128)(2,1)S(1)} %get-tuple-element.28.center, bf16[32,64,128]{2,1,0:T(8,128)(2,1)S(1)} %collective-permute-done.4.plain, ...), custom_call_target="tpu_custom_call" | custom-call | flops 1 | bytes 1 | tf_op jit(solution)/shard_map/pallas_call | solution.py:327
  30.9 0.0 collective-permute-done.10.refs_2_
  30.9 2.3 %collective-permute-done.11.refs_3_ = bf16[17,64,128]{2,1,0:T(8,128)(2,1)S(1)} collective-permute-done((bf16[17,64,128]{2,1,0:T(8,128)(2,1)S(1)}, bf16[17,64,128]{2,1,0:T(8,128)(2,1)S(1)}, u32[]{:S(2)}, u32[]{:S(2)}) %collective-permute-start.11) | collective-permute-done | bytes 278560 | tf_op jit(solution)/shard_map/ppermute | solution.py:346
  33.2 1.2 %shard_map.66 = (bf16[16,64,128]{2,1,0:T(8,128)(2,1)S(1)}, bf16[16,64,128]{2,1,0:T(8,128)(2,1)S(1)}, f32[256,128]{1,0:T(8,128)}) custom-call(f32[2,32,128]{2,1,0:T(8,128)S(1)} %get-tuple-element.34.faces, bf16[256,4096]{1,0:T(8,128)(2,1)S(1)} %get-tuple-element.47.left, f32[256,128]{1,0:T(8,128)S(1)} %get-tuple-element.48.first_gram, ...), custom_call_target="tpu_custom_call" | custom-call | flops 1 | bytes 1 | tf_op jit(solution)/shard_map/pallas_call | solution.py:327
  34.4 0.0 collective-permute-start.12
  34.4 6.6 %all-to-all-start = ((f32[16,16,128]{2,1,0:T(8,128)}), f32[16,16,128]{2,1,0:T(8,128)S(1)}, u32[]{:S(2)}, u32[]{:S(2)}) async-start(f32[16,16,128]{2,1,0:T(8,128)} %bitcast), calls=%async_computation | async-start | bytes 262144 | tf_op jit(solution)/shard_map/all_to_all | solution.py:413
  41.0 0.0 collective-permute-done.2.theirs
  41.0 1.3 %shard_map.62.applied_in = bf16[256,1,16,128]{3,2,1,0:T(8,128)(2,1)} custom-call(bf16[16,64,128]{2,1,0:T(8,128)(2,1)S(1)} %get-tuple-element.32.mine, bf16[16,64,128]{2,1,0:T(8,128)(2,1)S(1)} %collective-permute-done.2.theirs), custom_call_target="tpu_custom_call" | custom-call | flops 1 | bytes 1 | tf_op jit(solution)/shard_map/pallas_call | solution.py:327
  42.3 0.0 collective-permute-done.12.refs_1_
  42.3 1.3 %shard_map.67 = bf16[256,1,16,128]{3,2,1,0:T(8,128)(2,1)} custom-call(bf16[256,1,16,128]{3,2,1,0:T(8,128)(2,1)} %shard_map.62.applied_in, bf16[16,64,128]{2,1,0:T(8,128)(2,1)S(1)} %get-tuple-element.50.refs_0_, bf16[16,64,128]{2,1,0:T(8,128)(2,1)S(1)} %collective-permute-done.12.refs_1_), custom_call_target="tpu_custom_call", output_to_operand_aliasing={{}: (0, {})} | custom-call | flops 1 | bytes 1 | tf_op jit(solution)/shard_map/pallas_call | solution.py:327
  43.6 1.9 %all-to-all-done.shares = f32[16,16,128]{2,1,0:T(8,128)S(1)} async-done(((f32[16,16,128]{2,1,0:T(8,128)}), f32[16,16,128]{2,1,0:T(8,128)S(1)}, u32[]{:S(2)}, u32[]{:S(2)}) %all-to-all-start) | async-done | bytes 131104 | tf_op jit(solution)/shard_map/all_to_all | solution.py:413
  45.5 0.7 %shard_map.68 = f32[16,256]{1,0:T(8,128)} custom-call(f32[16,16,128]{2,1,0:T(8,128)S(1)} %all-to-all-done.shares), custom_call_target="tpu_custom_call" | custom-call | flops 1 | bytes 1 | tf_op jit(solution)/shard_map/pallas_call | solution.py:327
  (2 shorter events, 0.0 us)
Async XLA Ops:
  2.7 20.4 %collective-permute-start.1 = (bf16[33,64,128]{2,1,0:T(8,128)(2,1)S(1)}, bf16[33,64,128]{2,1,0:T(8,128)(2,1)S(1)}, u32[]{:S(2)}, u32[]{:S(2)}) collective-permute-start(bf16[33,64,128]{2,1,0:T(8,128)(2,1)S(1)} %get-tuple-element.31), channel_id=1, source_target_pairs={{4,8},{8,4},{5,9},{9,5},{6,10},{10,6},{7,11},{11,7},{20,24},{24,20... | collective-permute-start | bytes 1622024 | tf_op jit(solution)/shard_map/ppermute | solution.py:346
  3.4 20.4 %collective-permute-start = (bf16[33,64,128]{2,1,0:T(8,128)(2,1)S(1)}, bf16[33,64,128]{2,1,0:T(8,128)(2,1)S(1)}, u32[]{:S(2)}, u32[]{:S(2)}) collective-permute-start(bf16[33,64,128]{2,1,0:T(8,128)(2,1)S(1)} %get-tuple-element.31), channel_id=1, source_target_pairs={{0,4},{4,0},{8,12},{12,8},{1,5},{5,1},{9,13},{13,9},{2,6},{6,2},{1... | collective-permute-start | bytes 1622024 | tf_op jit(solution)/shard_map/ppermute | solution.py:346
  9.3 9.1 %collective-permute-start.5 = (bf16[17,64,128]{2,1,0:T(8,128)(2,1)S(1)}, bf16[17,64,128]{2,1,0:T(8,128)(2,1)S(1)}, u32[]{:S(2)}, u32[]{:S(2)}) collective-permute-start(bf16[17,64,128]{2,1,0:T(8,128)(2,1)S(1)} %get-tuple-element.40), channel_id=1, source_target_pairs={{0,2},{1,3},{2,0},{3,1},{4,6},{5,7},{6,4},{7,5},{8,10},{9,11},{10,... | collective-permute-start | bytes 835592 | tf_op jit(solution)/shard_map/ppermute | solution.py:342
  10.8 0.8 %copy-start = (s32[1,64,128]{2,1,0:T(8,128)S(1)}, s32[1,64,128]{2,1,0:T(8,128)}, u32[]{:S(2)}) copy-start(s32[1,64,128]{2,1,0:T(8,128)} %zone_ref.1) | copy-start | bytes 98308
  11.5 0.7 %copy-start.1 = (f32[16]{0:T(128)S(1)}, f32[16]{0:T(128)}, u32[]{:S(2)}) copy-start(f32[16]{0:T(128)} %cond_ref.1) | copy-start | bytes 196
  12.2 0.7 %copy-start.2 = (f32[16]{0:T(128)S(1)}, f32[16]{0:T(128)}, u32[]{:S(2)}) copy-start(f32[16]{0:T(128)} %heat_ref.1) | copy-start | bytes 196
  14.2 8.9 %collective-permute-start.3 = (bf16[17,64,128]{2,1,0:T(8,128)(2,1)S(1)}, bf16[17,64,128]{2,1,0:T(8,128)(2,1)S(1)}, u32[]{:S(2)}, u32[]{:S(2)}) collective-permute-start(bf16[17,64,128]{2,1,0:T(8,128)(2,1)S(1)} %get-tuple-element.38), channel_id=1, source_target_pairs={{0,2},{1,3},{2,0},{3,1},{4,6},{5,7},{6,4},{7,5},{8,10},{9,11},{10,... | collective-permute-start | bytes 835592 | tf_op jit(solution)/shard_map/ppermute | solution.py:342
  18.3 8.0 %collective-permute-start.6 = (bf16[17,64,128]{2,1,0:T(8,128)(2,1)S(1)}, bf16[17,64,128]{2,1,0:T(8,128)(2,1)S(1)}, u32[]{:S(2)}, u32[]{:S(2)}) collective-permute-start(bf16[17,64,128]{2,1,0:T(8,128)(2,1)S(1)} %collective-permute-done.5.refs_0_), channel_id=1, source_target_pairs={{4,8},{8,4},{5,9},{9,5},{6,10},{10,6},{7,11},{11,7},{20,24},{24,20... | collective-permute-start | bytes 835592 | tf_op jit(solution)/shard_map/ppermute | solution.py:346
  19.0 8.4 %collective-permute-start.7 = (bf16[17,64,128]{2,1,0:T(8,128)(2,1)S(1)}, bf16[17,64,128]{2,1,0:T(8,128)(2,1)S(1)}, u32[]{:S(2)}, u32[]{:S(2)}) collective-permute-start(bf16[17,64,128]{2,1,0:T(8,128)(2,1)S(1)} %collective-permute-done.5.refs_0_), channel_id=1, source_target_pairs={{0,4},{4,0},{8,12},{12,8},{1,5},{5,1},{9,13},{13,9},{2,6},{6,2},{1... | collective-permute-start | bytes 835592 | tf_op jit(solution)/shard_map/ppermute | solution.py:346
  23.1 6.5 %collective-permute-start.4 = (bf16[32,64,128]{2,1,0:T(8,128)(2,1)S(1)}, bf16[32,64,128]{2,1,0:T(8,128)(2,1)S(1)}, u32[]{:S(2)}, u32[]{:S(2)}) collective-permute-start(bf16[32,64,128]{2,1,0:T(8,128)(2,1)S(1)} %get-tuple-element.39), channel_id=1, source_target_pairs={{0,1},{1,0},{2,3},{3,2},{4,5},{5,4},{6,7},{7,6},{8,9},{9,8},{10,11... | collective-permute-start | bytes 1572872 | tf_op jit(solution)/shard_map/ppermute | solution.py:342
  23.1 7.9 %collective-permute-start.10 = (bf16[17,64,128]{2,1,0:T(8,128)(2,1)S(1)}, bf16[17,64,128]{2,1,0:T(8,128)(2,1)S(1)}, u32[]{:S(2)}, u32[]{:S(2)}) collective-permute-start(bf16[17,64,128]{2,1,0:T(8,128)(2,1)S(1)} %collective-permute-done.3.refs_1_), channel_id=1, source_target_pairs={{4,8},{8,4},{5,9},{9,5},{6,10},{10,6},{7,11},{11,7},{20,24},{24,20... | collective-permute-start | bytes 835592 | tf_op jit(solution)/shard_map/ppermute | solution.py:346
  23.8 9.4 %collective-permute-start.11 = (bf16[17,64,128]{2,1,0:T(8,128)(2,1)S(1)}, bf16[17,64,128]{2,1,0:T(8,128)(2,1)S(1)}, u32[]{:S(2)}, u32[]{:S(2)}) collective-permute-start(bf16[17,64,128]{2,1,0:T(8,128)(2,1)S(1)} %collective-permute-done.3.refs_1_), channel_id=1, source_target_pairs={{0,4},{4,0},{8,12},{12,8},{1,5},{5,1},{9,13},{13,9},{2,6},{6,2},{1... | collective-permute-start | bytes 835592 | tf_op jit(solution)/shard_map/ppermute | solution.py:346
  26.4 2.6 %collective-permute-start.9 = (bf16[16,64,128]{2,1,0:T(8,128)(2,1)S(1)}, bf16[16,64,128]{2,1,0:T(8,128)(2,1)S(1)}, u32[]{:S(2)}, u32[]{:S(2)}) collective-permute-start(bf16[16,64,128]{2,1,0:T(8,128)(2,1)S(1)} %slice.7), channel_id=1, source_target_pairs={{0,1},{1,0},{2,3},{3,2},{4,5},{5,4},{6,7},{7,6},{8,9},{9,8},{10,11... | collective-permute-start | bytes 786440 | tf_op jit(solution)/shard_map/ppermute | solution.py:342
  27.5 2.1 %collective-permute-start.8 = (bf16[16,64,128]{2,1,0:T(8,128)(2,1)S(1)}, bf16[16,64,128]{2,1,0:T(8,128)(2,1)S(1)}, u32[]{:S(2)}, u32[]{:S(2)}) collective-permute-start(bf16[16,64,128]{2,1,0:T(8,128)(2,1)S(1)} %slice.6), channel_id=1, source_target_pairs={{0,1},{1,0},{2,3},{3,2},{4,5},{5,4},{6,7},{7,6},{8,9},{9,8},{10,11... | collective-permute-start | bytes 786440 | tf_op jit(solution)/shard_map/ppermute | solution.py:342
  29.0 12.1 %collective-permute-start.2 = (bf16[16,64,128]{2,1,0:T(8,128)(2,1)S(1)}, bf16[16,64,128]{2,1,0:T(8,128)(2,1)S(1)}, u32[]{:S(2)}, u32[]{:S(2)}) collective-permute-start(bf16[16,64,128]{2,1,0:T(8,128)(2,1)S(1)} %get-tuple-element.33), channel_id=1, source_target_pairs={{0,1},{1,0},{2,3},{3,2},{4,5},{5,4},{6,7},{7,6},{8,9},{9,8},{10,11... | collective-permute-start | bytes 786440 | tf_op jit(solution)/shard_map/ppermute | solution.py:342
  34.4 7.9 %collective-permute-start.12 = (bf16[16,64,128]{2,1,0:T(8,128)(2,1)S(1)}, bf16[16,64,128]{2,1,0:T(8,128)(2,1)S(1)}, u32[]{:S(2)}, u32[]{:S(2)}) collective-permute-start(bf16[16,64,128]{2,1,0:T(8,128)(2,1)S(1)} %get-tuple-element.51), channel_id=1, source_target_pairs={{0,1},{1,0},{2,3},{3,2},{4,5},{5,4},{6,7},{7,6},{8,9},{9,8},{10,11... | collective-permute-start | bytes 786440 | tf_op jit(solution)/shard_map/ppermute | solution.py:342
  34.4 11.1 %all-to-all-start = ((f32[16,16,128]{2,1,0:T(8,128)}), f32[16,16,128]{2,1,0:T(8,128)S(1)}, u32[]{:S(2)}, u32[]{:S(2)}) async-start(f32[16,16,128]{2,1,0:T(8,128)} %bitcast), calls=%async_computation | async-start | bytes 262144 | tf_op jit(solution)/shard_map/all_to_all | solution.py:413

commit v17 on v16

--- a/solution.py
+++ b/solution.py
@@ -248,7 +248,7 @@
         values.append(first_gram[:, block] + weight * total)
     for slab in range(slabs):
         for owner in range(blocks):
-            start, place = (slab * blocks + owner) * share, (slabs * blocks - 1 - owner * slabs - slab) * share
+            start, place = (slab * blocks + owner) * share, (slabs * blocks - 1 - slab * blocks - owner) * share
             for k, value in enumerate(values):
                 gram[place:place + share, k * columns:(k + 1) * columns] = value[start:start + share]
 
@@ -294,10 +294,10 @@
     for core in range(CORES):
         sums = []
         for chip in range(chips):
-            last = slabs * blocks - 1 - (CORES * chip + core) * slabs
+            last = slabs * blocks - 1 - (CORES * chip + core)
             total = shares[last]
             for slab in range(1, slabs):
-                total += shares[last - slab]
+                total += shares[last - slab * blocks]
             sums.append(total)
         for target in range(chips):
             parts = [sums[chip][:, (chip ^ target) * columns:((chip ^ target) + 1) * columns] for chip in range(chips)]
@@ -411,7 +411,7 @@
     parts = slabs * blocks
     shares = gram.reshape(parts, total // parts, chips * columns)
     shares = lax.all_to_all(
-        shares, ("blk", "dom"), split_axis=0, concat_axis=0, tiled=True, axis_index_groups=[[*reversed(range(parts))]]
+        shares, ("dom", "blk"), split_axis=0, concat_axis=0, tiled=True, axis_index_groups=[[*reversed(range(parts))]]
     )
     pieces = []
     for k in range(count):

time: 46.6 us -> 46.3 us (level)
  no operation moved by 1% of the time
where the time goes in v17:
time: 46.3 us; the launch traced here: 45.9 us
  starting transfers between devices  22 us (48%)
  Pallas kernels  10.7 us (23%)
  waiting for transfers between devices  10.4 us (22%)
  local copies, waits for them, and re-layouts  2.1 us (5%)
  between operations  0.77 us (2%)
    ppermute x6, starting transfers between devices, exchange(): lax.ppermute(array, 'dom', [(d, to) for d, to in enumerate(partner) if 0...  12.6 us
    pallas_call x9, Pallas kernels, call(): pl.pallas_call(kernel, out_shape=out_shape, in_specs=specs or [VMEM] * le...  8.68 us
    all_to_all x1, starting transfers between devices, per_device(): lax.all_to_all(shares, ('dom', 'blk'), split_axis=0, concat_axis=0, tiled...  6.65 us
    ppermute x7, waiting for transfers between devices, swap(): return lax.ppermute(array, 'blk', [(i, i ^ s) for i in range(blocks)])  5.55 us
    ppermute x6, waiting for transfers between devices, exchange(): lax.ppermute(array, 'dom', [(d, to) for d, to in enumerate(partner) if 0...  3.25 us
    ppermute x7, starting transfers between devices, swap(): return lax.ppermute(array, 'blk', [(i, i ^ s) for i in range(blocks)])  2.74 us
    unnamed x6, local copies, waits for them, and re-layouts  2.07 us
    pallas_call x1, Pallas kernels, prepare(): pl.pallas_call(functools.partial(prepare_kernel, chips), out_shape=shapes...  2.06 us
  transfers between devices with their start and end apart: 14, of which 5 were waited for; matrix products, arithmetic and copies ran while one was open for 0% of the time, Pallas kernels for 17%

profile of v17, /device:TPU:0, one launch (start us, length us, event | category | flops | bytes accessed | tf_op | source)
XLA Modules:
  0.0 45.9 jit_solution(16906511330838100685)
XLA Ops:
  0.6 2.1 %shard_map.59 = (bf16[33,64,128]{2,1,0:T(8,128)(2,1)S(1)}, bf16[34,64,128]{2,1,0:T(8,128)(2,1)S(1)}, bf16[32,64,128]{2,1,0:T(8,128)(2,1)S(1)}, bf16[17,64,128]{2,1,0:T(8,128)(2,1)S(1)}, bf16[17,64,128]{2,1,0:T(8,128)(2,1)S(1)}) custom-call(bf16[64,1,64,128]{3,2,1,0:T(8,128)(2,1)} %basis_hbm.1, s32[1,64,128]{2,1,0:T(8,128)} %zone_ref.1, f32[16]{0:T(128)} %cond_ref.1), custom_call_target="tpu_custom_call" | custom-call | tf_op jit(solution)/shard_map/pallas_call | solution.py:88
  2.7 0.7 %collective-permute-start.1 = (bf16[33,64,128]{2,1,0:T(8,128)(2,1)S(1)}, bf16[33,64,128]{2,1,0:T(8,128)(2,1)S(1)}, u32[]{:S(2)}, u32[]{:S(2)}) collective-permute-start(bf16[33,64,128]{2,1,0:T(8,128)(2,1)S(1)} %get-tuple-element.31), channel_id=1, source_target_pairs={{4,8},{8,4},{5,9},{9,5},{6,10},{10,6},{7,11},{11,7},{20,24},{24,20... | collective-permute-start | bytes 1622024 | tf_op jit(solution)/shard_map/ppermute | solution.py:346
  3.4 5.9 %collective-permute-start = (bf16[33,64,128]{2,1,0:T(8,128)(2,1)S(1)}, bf16[33,64,128]{2,1,0:T(8,128)(2,1)S(1)}, u32[]{:S(2)}, u32[]{:S(2)}) collective-permute-start(bf16[33,64,128]{2,1,0:T(8,128)(2,1)S(1)} %get-tuple-element.31), channel_id=1, source_target_pairs={{0,4},{4,0},{8,12},{12,8},{1,5},{5,1},{9,13},{13,9},{2,6},{6,2},{1... | collective-permute-start | bytes 1622024 | tf_op jit(solution)/shard_map/ppermute | solution.py:346
  9.3 1.5 %collective-permute-start.5 = (bf16[17,64,128]{2,1,0:T(8,128)(2,1)S(1)}, bf16[17,64,128]{2,1,0:T(8,128)(2,1)S(1)}, u32[]{:S(2)}, u32[]{:S(2)}) collective-permute-start(bf16[17,64,128]{2,1,0:T(8,128)(2,1)S(1)} %get-tuple-element.40), channel_id=1, source_target_pairs={{0,2},{1,3},{2,0},{3,1},{4,6},{5,7},{6,4},{7,5},{8,10},{9,11},{10,... | collective-permute-start | bytes 835592 | tf_op jit(solution)/shard_map/ppermute | solution.py:342
  10.8 0.0 copy-start
  10.8 0.8 %copy-done = s32[1,64,128]{2,1,0:T(8,128)S(1)} copy-done((s32[1,64,128]{2,1,0:T(8,128)S(1)}, s32[1,64,128]{2,1,0:T(8,128)}, u32[]{:S(2)}) %copy-start) | copy-done | bytes 32792
  11.5 0.0 copy-start.1
  11.5 0.7 %copy-done.1 = f32[16]{0:T(128)S(1)} copy-done((f32[16]{0:T(128)S(1)}, f32[16]{0:T(128)}, u32[]{:S(2)}) %copy-start.1) | copy-done | bytes 88
  12.2 0.0 copy-start.2
  12.2 0.7 %copy-done.2 = f32[16]{0:T(128)S(1)} copy-done((f32[16]{0:T(128)S(1)}, f32[16]{0:T(128)}, u32[]{:S(2)}) %copy-start.2) | copy-done | bytes 88
  12.8 1.3 %shard_map.60 = (f32[6,32,128]{2,1,0:T(8,128)S(1)}, f32[32,64,128]{2,1,0:T(8,128)S(1)}) custom-call(s32[1,64,128]{2,1,0:T(8,128)S(1)} %copy-done, f32[16]{0:T(128)S(1)} %copy-done.1, f32[16]{0:T(128)S(1)} %copy-done.2, bf16[34,64,128]{2,1,0:T(8,128)(2,1)S(1)} %get-tuple-element.28.center), custom_call_target="tpu_custom_call" | custom-call | flops 1073741824 | bytes 134217728 | tf_op jit(solution)/shard_map/pallas_call | solution.py:327
  14.2 0.6 %collective-permute-start.3 = (bf16[17,64,128]{2,1,0:T(8,128)(2,1)S(1)}, bf16[17,64,128]{2,1,0:T(8,128)(2,1)S(1)}, u32[]{:S(2)}, u32[]{:S(2)}) collective-permute-start(bf16[17,64,128]{2,1,0:T(8,128)(2,1)S(1)} %get-tuple-element.38), channel_id=1, source_target_pairs={{0,2},{1,3},{2,0},{3,1},{4,6},{5,7},{6,4},{7,5},{8,10},{9,11},{10,... | collective-permute-start | bytes 835592 | tf_op jit(solution)/shard_map/ppermute | solution.py:342
  14.8 3.6 %collective-permute-done.5.refs_0_ = bf16[17,64,128]{2,1,0:T(8,128)(2,1)S(1)} collective-permute-done((bf16[17,64,128]{2,1,0:T(8,128)(2,1)S(1)}, bf16[17,64,128]{2,1,0:T(8,128)(2,1)S(1)}, u32[]{:S(2)}, u32[]{:S(2)}) %collective-permute-start.5) | collective-permute-done | bytes 278560 | tf_op jit(solution)/shard_map/ppermute | solution.py:342
  18.3 0.7 %collective-permute-start.6 = (bf16[17,64,128]{2,1,0:T(8,128)(2,1)S(1)}, bf16[17,64,128]{2,1,0:T(8,128)(2,1)S(1)}, u32[]{:S(2)}, u32[]{:S(2)}) collective-permute-start(bf16[17,64,128]{2,1,0:T(8,128)(2,1)S(1)} %collective-permute-done.5.refs_0_), channel_id=1, source_target_pairs={{4,8},{8,4},{5,9},{9,5},{6,10},{10,6},{7,11},{11,7},{20,24},{24,20... | collective-permute-start | bytes 835592 | tf_op jit(solution)/shard_map/ppermute | solution.py:346
  19.0 2.1 %collective-permute-start.7 = (bf16[17,64,128]{2,1,0:T(8,128)(2,1)S(1)}, bf16[17,64,128]{2,1,0:T(8,128)(2,1)S(1)}, u32[]{:S(2)}, u32[]{:S(2)}) collective-permute-start(bf16[17,64,128]{2,1,0:T(8,128)(2,1)S(1)} %collective-permute-done.5.refs_0_), channel_id=1, source_target_pairs={{0,4},{4,0},{8,12},{12,8},{1,5},{5,1},{9,13},{13,9},{2,6},{6,2},{1... | collective-permute-start | bytes 835592 | tf_op jit(solution)/shard_map/ppermute | solution.py:346
  21.1 2.0 %collective-permute-done.3.refs_1_ = bf16[17,64,128]{2,1,0:T(8,128)(2,1)S(1)} collective-permute-done((bf16[17,64,128]{2,1,0:T(8,128)(2,1)S(1)}, bf16[17,64,128]{2,1,0:T(8,128)(2,1)S(1)}, u32[]{:S(2)}, u32[]{:S(2)}) %collective-permute-start.3) | collective-permute-done | bytes 278560 | tf_op jit(solution)/shard_map/ppermute | solution.py:342
  23.1 0.0 collective-permute-start.4
  23.1 0.0 collective-permute-done.1.two
  23.1 0.7 %collective-permute-start.10 = (bf16[17,64,128]{2,1,0:T(8,128)(2,1)S(1)}, bf16[17,64,128]{2,1,0:T(8,128)(2,1)S(1)}, u32[]{:S(2)}, u32[]{:S(2)}) collective-permute-start(bf16[17,64,128]{2,1,0:T(8,128)(2,1)S(1)} %collective-permute-done.3.refs_1_), channel_id=1, source_target_pairs={{4,8},{8,4},{5,9},{9,5},{6,10},{10,6},{7,11},{11,7},{20,24},{24,20... | collective-permute-start | bytes 835592 | tf_op jit(solution)/shard_map/ppermute | solution.py:346
  23.8 0.0 collective-permute-done.one
  23.8 2.6 %collective-permute-start.11 = (bf16[17,64,128]{2,1,0:T(8,128)(2,1)S(1)}, bf16[17,64,128]{2,1,0:T(8,128)(2,1)S(1)}, u32[]{:S(2)}, u32[]{:S(2)}) collective-permute-start(bf16[17,64,128]{2,1,0:T(8,128)(2,1)S(1)} %collective-permute-done.3.refs_1_), channel_id=1, source_target_pairs={{0,4},{4,0},{8,12},{12,8},{1,5},{5,1},{9,13},{13,9},{2,6},{6,2},{1... | collective-permute-start | bytes 835592 | tf_op jit(solution)/shard_map/ppermute | solution.py:346
  26.3 0.0 collective-permute-done.6.refs_2_
  26.4 0.1 collective-permute-start.9
  26.5 1.0 %collective-permute-done.7.refs_3_ = bf16[17,64,128]{2,1,0:T(8,128)(2,1)S(1)} collective-permute-done((bf16[17,64,128]{2,1,0:T(8,128)(2,1)S(1)}, bf16[17,64,128]{2,1,0:T(8,128)(2,1)S(1)}, u32[]{:S(2)}, u32[]{:S(2)}) %collective-permute-start.7) | collective-permute-done | bytes 278560 | tf_op jit(solution)/shard_map/ppermute | solution.py:346
  27.5 0.0 collective-permute-start.8
  27.5 0.7 %shard_map.63 = (bf16[34,64,128]{2,1,0:T(8,128)(2,1)S(1)}, f32[32,64,128]{2,1,0:T(8,128)S(1)}) custom-call(f32[6,32,128]{2,1,0:T(8,128)S(1)} %get-tuple-element.29.coef, bf16[17,64,128]{2,1,0:T(8,128)(2,1)S(1)} %collective-permute-done.5.refs_0_, bf16[17,64,128]{2,1,0:T(8,128)(2,1)S(1)} %collective-permute-done.3.refs_1_), custom_call_target="tpu_custom_call" | custom-call | flops 1 | bytes 1 | tf_op jit(solution)/shard_map/pallas_call | solution.py:327
  28.2 0.6 %shard_map.61 = (bf16[16,64,128]{2,1,0:T(8,128)(2,1)S(1)}, bf16[16,64,128]{2,1,0:T(8,128)(2,1)S(1)}, f32[2,32,128]{2,1,0:T(8,128)S(1)}, bf16[64,4096]{1,0:T(8,128)(2,1)S(1)}) custom-call(f32[6,32,128]{2,1,0:T(8,128)S(1)} %get-tuple-element.29.coef, f32[32,64,128]{2,1,0:T(8,128)S(1)} %get-tuple-element.30.partial, ...), custom_call_target="tpu_custom_call" | custom-call | flops 1 | bytes 1 | tf_op jit(solution)/shard_map/pallas_call | solution.py:327
  28.8 0.2 shard_map.64
  28.9 0.0 collective-permute-done.9.refs_3_
  29.0 0.6 %collective-permute-start.2 = (bf16[16,64,128]{2,1,0:T(8,128)(2,1)S(1)}, bf16[16,64,128]{2,1,0:T(8,128)(2,1)S(1)}, u32[]{:S(2)}, u32[]{:S(2)}) collective-permute-start(bf16[16,64,128]{2,1,0:T(8,128)(2,1)S(1)} %get-tuple-element.33), channel_id=1, source_target_pairs={{0,1},{1,0},{2,3},{3,2},{4,5},{5,4},{6,7},{7,6},{8,9},{9,8},{10,11... | collective-permute-start | bytes 786440 | tf_op jit(solution)/shard_map/ppermute | solution.py:342
  29.5 0.0 collective-permute-done.8.refs_2_
  29.5 0.0 collective-permute-done.4.plain
  29.5 1.4 %shard_map.65 = (bf16[256,4096]{1,0:T(8,128)(2,1)S(1)}, f32[256,128]{1,0:T(8,128)S(1)}) custom-call(bf16[64,4096]{1,0:T(8,128)(2,1)S(1)} %get-tuple-element.35.flat, bf16[34,64,128]{2,1,0:T(8,128)(2,1)S(1)} %get-tuple-element.28.center, bf16[32,64,128]{2,1,0:T(8,128)(2,1)S(1)} %collective-permute-done.4.plain, ...), custom_call_target="tpu_custom_call" | custom-call | flops 1 | bytes 1 | tf_op jit(solution)/shard_map/pallas_call | solution.py:327
  30.9 0.0 collective-permute-done.10.refs_2_
  30.9 2.3 %collective-permute-done.11.refs_3_ = bf16[17,64,128]{2,1,0:T(8,128)(2,1)S(1)} collective-permute-done((bf16[17,64,128]{2,1,0:T(8,128)(2,1)S(1)}, bf16[17,64,128]{2,1,0:T(8,128)(2,1)S(1)}, u32[]{:S(2)}, u32[]{:S(2)}) %collective-permute-start.11) | collective-permute-done | bytes 278560 | tf_op jit(solution)/shard_map/ppermute | solution.py:346
  33.2 1.2 %shard_map.66 = (bf16[16,64,128]{2,1,0:T(8,128)(2,1)S(1)}, bf16[16,64,128]{2,1,0:T(8,128)(2,1)S(1)}, f32[256,128]{1,0:T(8,128)}) custom-call(f32[2,32,128]{2,1,0:T(8,128)S(1)} %get-tuple-element.34.faces, bf16[256,4096]{1,0:T(8,128)(2,1)S(1)} %get-tuple-element.47.left, f32[256,128]{1,0:T(8,128)S(1)} %get-tuple-element.48.first_gram, ...), custom_call_target="tpu_custom_call" | custom-call | flops 1 | bytes 1 | tf_op jit(solution)/shard_map/pallas_call | solution.py:327
  34.4 0.0 collective-permute-start.12
  34.4 6.7 %all-to-all-start = ((f32[16,16,128]{2,1,0:T(8,128)}), f32[16,16,128]{2,1,0:T(8,128)S(1)}, u32[]{:S(2)}, u32[]{:S(2)}) async-start(f32[16,16,128]{2,1,0:T(8,128)} %bitcast), calls=%async_computation | async-start | bytes 262144 | tf_op jit(solution)/shard_map/all_to_all | solution.py:413
  41.0 0.0 collective-permute-done.2.theirs
  41.0 1.3 %shard_map.62.applied_in = bf16[256,1,16,128]{3,2,1,0:T(8,128)(2,1)} custom-call(bf16[16,64,128]{2,1,0:T(8,128)(2,1)S(1)} %get-tuple-element.32.mine, bf16[16,64,128]{2,1,0:T(8,128)(2,1)S(1)} %collective-permute-done.2.theirs), custom_call_target="tpu_custom_call" | custom-call | flops 1 | bytes 1 | tf_op jit(solution)/shard_map/pallas_call | solution.py:327
  42.3 0.0 collective-permute-done.12.refs_1_
  42.3 1.3 %shard_map.67 = bf16[256,1,16,128]{3,2,1,0:T(8,128)(2,1)} custom-call(bf16[256,1,16,128]{3,2,1,0:T(8,128)(2,1)} %shard_map.62.applied_in, bf16[16,64,128]{2,1,0:T(8,128)(2,1)S(1)} %get-tuple-element.50.refs_0_, bf16[16,64,128]{2,1,0:T(8,128)(2,1)S(1)} %collective-permute-done.12.refs_1_), custom_call_target="tpu_custom_call", output_to_operand_aliasing={{}: (0, {})} | custom-call | flops 1 | bytes 1 | tf_op jit(solution)/shard_map/pallas_call | solution.py:327
  43.6 1.6 %all-to-all-done.shares = f32[16,16,128]{2,1,0:T(8,128)S(1)} async-done(((f32[16,16,128]{2,1,0:T(8,128)}), f32[16,16,128]{2,1,0:T(8,128)S(1)}, u32[]{:S(2)}, u32[]{:S(2)}) %all-to-all-start) | async-done | bytes 131104 | tf_op jit(solution)/shard_map/all_to_all | solution.py:413
  45.2 0.7 %shard_map.68 = f32[16,256]{1,0:T(8,128)} custom-call(f32[16,16,128]{2,1,0:T(8,128)S(1)} %all-to-all-done.shares), custom_call_target="tpu_custom_call" | custom-call | flops 1 | bytes 1 | tf_op jit(solution)/shard_map/pallas_call | solution.py:327
  (2 shorter events, 0.0 us)
Async XLA Ops:
  2.7 20.4 %collective-permute-start.1 = (bf16[33,64,128]{2,1,0:T(8,128)(2,1)S(1)}, bf16[33,64,128]{2,1,0:T(8,128)(2,1)S(1)}, u32[]{:S(2)}, u32[]{:S(2)}) collective-permute-start(bf16[33,64,128]{2,1,0:T(8,128)(2,1)S(1)} %get-tuple-element.31), channel_id=1, source_target_pairs={{4,8},{8,4},{5,9},{9,5},{6,10},{10,6},{7,11},{11,7},{20,24},{24,20... | collective-permute-start | bytes 1622024 | tf_op jit(solution)/shard_map/ppermute | solution.py:346
  3.4 20.4 %collective-permute-start = (bf16[33,64,128]{2,1,0:T(8,128)(2,1)S(1)}, bf16[33,64,128]{2,1,0:T(8,128)(2,1)S(1)}, u32[]{:S(2)}, u32[]{:S(2)}) collective-permute-start(bf16[33,64,128]{2,1,0:T(8,128)(2,1)S(1)} %get-tuple-element.31), channel_id=1, source_target_pairs={{0,4},{4,0},{8,12},{12,8},{1,5},{5,1},{9,13},{13,9},{2,6},{6,2},{1... | collective-permute-start | bytes 1622024 | tf_op jit(solution)/shard_map/ppermute | solution.py:346
  9.3 9.1 %collective-permute-start.5 = (bf16[17,64,128]{2,1,0:T(8,128)(2,1)S(1)}, bf16[17,64,128]{2,1,0:T(8,128)(2,1)S(1)}, u32[]{:S(2)}, u32[]{:S(2)}) collective-permute-start(bf16[17,64,128]{2,1,0:T(8,128)(2,1)S(1)} %get-tuple-element.40), channel_id=1, source_target_pairs={{0,2},{1,3},{2,0},{3,1},{4,6},{5,7},{6,4},{7,5},{8,10},{9,11},{10,... | collective-permute-start | bytes 835592 | tf_op jit(solution)/shard_map/ppermute | solution.py:342
  10.8 0.8 %copy-start = (s32[1,64,128]{2,1,0:T(8,128)S(1)}, s32[1,64,128]{2,1,0:T(8,128)}, u32[]{:S(2)}) copy-start(s32[1,64,128]{2,1,0:T(8,128)} %zone_ref.1) | copy-start | bytes 98308
  11.5 0.7 %copy-start.1 = (f32[16]{0:T(128)S(1)}, f32[16]{0:T(128)}, u32[]{:S(2)}) copy-start(f32[16]{0:T(128)} %cond_ref.1) | copy-start | bytes 196
  12.2 0.7 %copy-start.2 = (f32[16]{0:T(128)S(1)}, f32[16]{0:T(128)}, u32[]{:S(2)}) copy-start(f32[16]{0:T(128)} %heat_ref.1) | copy-start | bytes 196
  14.2 8.9 %collective-permute-start.3 = (bf16[17,64,128]{2,1,0:T(8,128)(2,1)S(1)}, bf16[17,64,128]{2,1,0:T(8,128)(2,1)S(1)}, u32[]{:S(2)}, u32[]{:S(2)}) collective-permute-start(bf16[17,64,128]{2,1,0:T(8,128)(2,1)S(1)} %get-tuple-element.38), channel_id=1, source_target_pairs={{0,2},{1,3},{2,0},{3,1},{4,6},{5,7},{6,4},{7,5},{8,10},{9,11},{10,... | collective-permute-start | bytes 835592 | tf_op jit(solution)/shard_map/ppermute | solution.py:342
  18.3 8.0 %collective-permute-start.6 = (bf16[17,64,128]{2,1,0:T(8,128)(2,1)S(1)}, bf16[17,64,128]{2,1,0:T(8,128)(2,1)S(1)}, u32[]{:S(2)}, u32[]{:S(2)}) collective-permute-start(bf16[17,64,128]{2,1,0:T(8,128)(2,1)S(1)} %collective-permute-done.5.refs_0_), channel_id=1, source_target_pairs={{4,8},{8,4},{5,9},{9,5},{6,10},{10,6},{7,11},{11,7},{20,24},{24,20... | collective-permute-start | bytes 835592 | tf_op jit(solution)/shard_map/ppermute | solution.py:346
  19.0 8.4 %collective-permute-start.7 = (bf16[17,64,128]{2,1,0:T(8,128)(2,1)S(1)}, bf16[17,64,128]{2,1,0:T(8,128)(2,1)S(1)}, u32[]{:S(2)}, u32[]{:S(2)}) collective-permute-start(bf16[17,64,128]{2,1,0:T(8,128)(2,1)S(1)} %collective-permute-done.5.refs_0_), channel_id=1, source_target_pairs={{0,4},{4,0},{8,12},{12,8},{1,5},{5,1},{9,13},{13,9},{2,6},{6,2},{1... | collective-permute-start | bytes 835592 | tf_op jit(solution)/shard_map/ppermute | solution.py:346
  23.1 6.5 %collective-permute-start.4 = (bf16[32,64,128]{2,1,0:T(8,128)(2,1)S(1)}, bf16[32,64,128]{2,1,0:T(8,128)(2,1)S(1)}, u32[]{:S(2)}, u32[]{:S(2)}) collective-permute-start(bf16[32,64,128]{2,1,0:T(8,128)(2,1)S(1)} %get-tuple-element.39), channel_id=1, source_target_pairs={{0,1},{1,0},{2,3},{3,2},{4,5},{5,4},{6,7},{7,6},{8,9},{9,8},{10,11... | collective-permute-start | bytes 1572872 | tf_op jit(solution)/shard_map/ppermute | solution.py:342
  23.1 7.9 %collective-permute-start.10 = (bf16[17,64,128]{2,1,0:T(8,128)(2,1)S(1)}, bf16[17,64,128]{2,1,0:T(8,128)(2,1)S(1)}, u32[]{:S(2)}, u32[]{:S(2)}) collective-permute-start(bf16[17,64,128]{2,1,0:T(8,128)(2,1)S(1)} %collective-permute-done.3.refs_1_), channel_id=1, source_target_pairs={{4,8},{8,4},{5,9},{9,5},{6,10},{10,6},{7,11},{11,7},{20,24},{24,20... | collective-permute-start | bytes 835592 | tf_op jit(solution)/shard_map/ppermute | solution.py:346
  23.8 9.4 %collective-permute-start.11 = (bf16[17,64,128]{2,1,0:T(8,128)(2,1)S(1)}, bf16[17,64,128]{2,1,0:T(8,128)(2,1)S(1)}, u32[]{:S(2)}, u32[]{:S(2)}) collective-permute-start(bf16[17,64,128]{2,1,0:T(8,128)(2,1)S(1)} %collective-permute-done.3.refs_1_), channel_id=1, source_target_pairs={{0,4},{4,0},{8,12},{12,8},{1,5},{5,1},{9,13},{13,9},{2,6},{6,2},{1... | collective-permute-start | bytes 835592 | tf_op jit(solution)/shard_map/ppermute | solution.py:346
  26.4 2.6 %collective-permute-start.9 = (bf16[16,64,128]{2,1,0:T(8,128)(2,1)S(1)}, bf16[16,64,128]{2,1,0:T(8,128)(2,1)S(1)}, u32[]{:S(2)}, u32[]{:S(2)}) collective-permute-start(bf16[16,64,128]{2,1,0:T(8,128)(2,1)S(1)} %slice.7), channel_id=1, source_target_pairs={{0,1},{1,0},{2,3},{3,2},{4,5},{5,4},{6,7},{7,6},{8,9},{9,8},{10,11... | collective-permute-start | bytes 786440 | tf_op jit(solution)/shard_map/ppermute | solution.py:342
  27.5 2.1 %collective-permute-start.8 = (bf16[16,64,128]{2,1,0:T(8,128)(2,1)S(1)}, bf16[16,64,128]{2,1,0:T(8,128)(2,1)S(1)}, u32[]{:S(2)}, u32[]{:S(2)}) collective-permute-start(bf16[16,64,128]{2,1,0:T(8,128)(2,1)S(1)} %slice.6), channel_id=1, source_target_pairs={{0,1},{1,0},{2,3},{3,2},{4,5},{5,4},{6,7},{7,6},{8,9},{9,8},{10,11... | collective-permute-start | bytes 786440 | tf_op jit(solution)/shard_map/ppermute | solution.py:342
  29.0 12.1 %collective-permute-start.2 = (bf16[16,64,128]{2,1,0:T(8,128)(2,1)S(1)}, bf16[16,64,128]{2,1,0:T(8,128)(2,1)S(1)}, u32[]{:S(2)}, u32[]{:S(2)}) collective-permute-start(bf16[16,64,128]{2,1,0:T(8,128)(2,1)S(1)} %get-tuple-element.33), channel_id=1, source_target_pairs={{0,1},{1,0},{2,3},{3,2},{4,5},{5,4},{6,7},{7,6},{8,9},{9,8},{10,11... | collective-permute-start | bytes 786440 | tf_op jit(solution)/shard_map/ppermute | solution.py:342
  34.4 7.9 %collective-permute-start.12 = (bf16[16,64,128]{2,1,0:T(8,128)(2,1)S(1)}, bf16[16,64,128]{2,1,0:T(8,128)(2,1)S(1)}, u32[]{:S(2)}, u32[]{:S(2)}) collective-permute-start(bf16[16,64,128]{2,1,0:T(8,128)(2,1)S(1)} %get-tuple-element.51), channel_id=1, source_target_pairs={{0,1},{1,0},{2,3},{3,2},{4,5},{5,4},{6,7},{7,6},{8,9},{9,8},{10,11... | collective-permute-start | bytes 786440 | tf_op jit(solution)/shard_map/ppermute | solution.py:342
  34.4 10.8 %all-to-all-start = ((f32[16,16,128]{2,1,0:T(8,128)}), f32[16,16,128]{2,1,0:T(8,128)S(1)}, u32[]{:S(2)}, u32[]{:S(2)}) async-start(f32[16,16,128]{2,1,0:T(8,128)} %bitcast), calls=%async_computation | async-start | bytes 262144 | tf_op jit(solution)/shard_map/all_to_all | solution.py:413

commit v18 on v17

--- a/solution.py
+++ b/solution.py
@@ -188,7 +188,7 @@
 
 def first_far_kernel(chips, faces, *refs):
     count = chips - 1
-    partials, centers, twos, ones, images, flats = (refs[i * count:(i + 1) * count] for i in range(6))
+    partials, centers, ones, twos, images, flats = (refs[i * count:(i + 1) * count] for i in range(6))
     nz = partials[0].shape[2]
     for k in range(count):
         for y in range(partials[k].shape[0] // 2):
@@ -391,7 +391,7 @@
     results = call(
         functools.partial(first_far_kernel, chips),
         [image] * count + [half_flat] * count,
-        (faces, *partials, *centers, *first_two, *first_one),
+        (faces, *partials, *centers, *first_one, *first_two),
     )
     images, flats = results[:count], results[count:]
     applied, = call(

time: 46.3 us -> 46.5 us (level)
  waiting for transfers between devices: 10.4 us -> 12.2 us
  starting transfers between devices: 22 us -> 20.4 us
    ppermute x7, waiting for transfers between devices: 5.55 us -> 7.3 us  [swap(): return lax.ppermute(array, 'blk', [(i, i ^ s) for i in range(blocks)])]
    ppermute x6, starting transfers between devices: 12.6 us -> 10.9 us  [exchange(): lax.ppermute(array, 'dom', [(d, to) for d, to in enumerate(partner) if 0...]
where the time goes in v18:
time: 46.5 us; the launch traced here: 46.2 us
  starting transfers between devices  20.4 us (44%)
  waiting for transfers between devices  12.2 us (26%)
  Pallas kernels  10.7 us (23%)
  local copies, waits for them, and re-layouts  2.1 us (5%)
  between operations  0.77 us (2%)
    ppermute x6, starting transfers between devices, exchange(): lax.ppermute(array, 'dom', [(d, to) for d, to in enumerate(partner) if 0...  10.9 us
    pallas_call x9, Pallas kernels, call(): pl.pallas_call(kernel, out_shape=out_shape, in_specs=specs or [VMEM] * le...  8.68 us
    ppermute x7, waiting for transfers between devices, swap(): return lax.ppermute(array, 'blk', [(i, i ^ s) for i in range(blocks)])  7.3 us
    all_to_all x1, starting transfers between devices, per_device(): lax.all_to_all(shares, ('dom', 'blk'), split_axis=0, concat_axis=0, tiled...  6.72 us
    ppermute x6, waiting for transfers between devices, exchange(): lax.ppermute(array, 'dom', [(d, to) for d, to in enumerate(partner) if 0...  3.38 us
    ppermute x7, starting transfers between devices, swap(): return lax.ppermute(array, 'blk', [(i, i ^ s) for i in range(blocks)])  2.75 us
    unnamed x6, local copies, waits for them, and re-layouts  2.07 us
    pallas_call x1, Pallas kernels, prepare(): pl.pallas_call(functools.partial(prepare_kernel, chips), out_shape=shapes...  2.06 us
  transfers between devices with their start and end apart: 14, of which 5 were waited for; matrix products, arithmetic and copies ran while one was open for 0% of the time, Pallas kernels for 17%

profile of v18, /device:TPU:0, one launch (start us, length us, event | category | flops | bytes accessed | tf_op | source)
XLA Modules:
  0.0 46.2 jit_solution(7234858664595111340)
XLA Ops:
  0.6 2.1 %shard_map.59 = (bf16[33,64,128]{2,1,0:T(8,128)(2,1)S(1)}, bf16[34,64,128]{2,1,0:T(8,128)(2,1)S(1)}, bf16[32,64,128]{2,1,0:T(8,128)(2,1)S(1)}, bf16[17,64,128]{2,1,0:T(8,128)(2,1)S(1)}, bf16[17,64,128]{2,1,0:T(8,128)(2,1)S(1)}) custom-call(bf16[64,1,64,128]{3,2,1,0:T(8,128)(2,1)} %basis_hbm.1, s32[1,64,128]{2,1,0:T(8,128)} %zone_ref.1, f32[16]{0:T(128)} %cond_ref.1), custom_call_target="tpu_custom_call" | custom-call | tf_op jit(solution)/shard_map/pallas_call | solution.py:88
  2.7 0.7 %collective-permute-start.1 = (bf16[33,64,128]{2,1,0:T(8,128)(2,1)S(1)}, bf16[33,64,128]{2,1,0:T(8,128)(2,1)S(1)}, u32[]{:S(2)}, u32[]{:S(2)}) collective-permute-start(bf16[33,64,128]{2,1,0:T(8,128)(2,1)S(1)} %get-tuple-element.31), channel_id=1, source_target_pairs={{4,8},{8,4},{5,9},{9,5},{6,10},{10,6},{7,11},{11,7},{20,24},{24,20... | collective-permute-start | bytes 1622024 | tf_op jit(solution)/shard_map/ppermute | solution.py:346
  3.4 5.9 %collective-permute-start = (bf16[33,64,128]{2,1,0:T(8,128)(2,1)S(1)}, bf16[33,64,128]{2,1,0:T(8,128)(2,1)S(1)}, u32[]{:S(2)}, u32[]{:S(2)}) collective-permute-start(bf16[33,64,128]{2,1,0:T(8,128)(2,1)S(1)} %get-tuple-element.31), channel_id=1, source_target_pairs={{0,4},{4,0},{8,12},{12,8},{1,5},{5,1},{9,13},{13,9},{2,6},{6,2},{1... | collective-permute-start | bytes 1622024 | tf_op jit(solution)/shard_map/ppermute | solution.py:346
  9.3 1.5 %collective-permute-start.5 = (bf16[17,64,128]{2,1,0:T(8,128)(2,1)S(1)}, bf16[17,64,128]{2,1,0:T(8,128)(2,1)S(1)}, u32[]{:S(2)}, u32[]{:S(2)}) collective-permute-start(bf16[17,64,128]{2,1,0:T(8,128)(2,1)S(1)} %get-tuple-element.40), channel_id=1, source_target_pairs={{0,2},{1,3},{2,0},{3,1},{4,6},{5,7},{6,4},{7,5},{8,10},{9,11},{10,... | collective-permute-start | bytes 835592 | tf_op jit(solution)/shard_map/ppermute | solution.py:342
  10.8 0.0 copy-start
  10.8 0.8 %copy-done = s32[1,64,128]{2,1,0:T(8,128)S(1)} copy-done((s32[1,64,128]{2,1,0:T(8,128)S(1)}, s32[1,64,128]{2,1,0:T(8,128)}, u32[]{:S(2)}) %copy-start) | copy-done | bytes 32792
  11.5 0.0 copy-start.1
  11.5 0.7 %copy-done.1 = f32[16]{0:T(128)S(1)} copy-done((f32[16]{0:T(128)S(1)}, f32[16]{0:T(128)}, u32[]{:S(2)}) %copy-start.1) | copy-done | bytes 88
  12.2 0.0 copy-start.2
  12.2 0.7 %copy-done.2 = f32[16]{0:T(128)S(1)} copy-done((f32[16]{0:T(128)S(1)}, f32[16]{0:T(128)}, u32[]{:S(2)}) %copy-start.2) | copy-done | bytes 88
  12.8 1.3 %shard_map.60 = (f32[6,32,128]{2,1,0:T(8,128)S(1)}, f32[32,64,128]{2,1,0:T(8,128)S(1)}) custom-call(s32[1,64,128]{2,1,0:T(8,128)S(1)} %copy-done, f32[16]{0:T(128)S(1)} %copy-done.1, f32[16]{0:T(128)S(1)} %copy-done.2, bf16[34,64,128]{2,1,0:T(8,128)(2,1)S(1)} %get-tuple-element.28.center), custom_call_target="tpu_custom_call" | custom-call | flops 1073741824 | bytes 134217728 | tf_op jit(solution)/shard_map/pallas_call | solution.py:327
  14.2 0.6 %collective-permute-start.3 = (bf16[17,64,128]{2,1,0:T(8,128)(2,1)S(1)}, bf16[17,64,128]{2,1,0:T(8,128)(2,1)S(1)}, u32[]{:S(2)}, u32[]{:S(2)}) collective-permute-start(bf16[17,64,128]{2,1,0:T(8,128)(2,1)S(1)} %get-tuple-element.38), channel_id=1, source_target_pairs={{0,2},{1,3},{2,0},{3,1},{4,6},{5,7},{6,4},{7,5},{8,10},{9,11},{10,... | collective-permute-start | bytes 835592 | tf_op jit(solution)/shard_map/ppermute | solution.py:342
  14.8 3.6 %collective-permute-done.5.refs_0_ = bf16[17,64,128]{2,1,0:T(8,128)(2,1)S(1)} collective-permute-done((bf16[17,64,128]{2,1,0:T(8,128)(2,1)S(1)}, bf16[17,64,128]{2,1,0:T(8,128)(2,1)S(1)}, u32[]{:S(2)}, u32[]{:S(2)}) %collective-permute-start.5) | collective-permute-done | bytes 278560 | tf_op jit(solution)/shard_map/ppermute | solution.py:342
  18.3 0.4 collective-permute-start.6
  18.7 0.7 %collective-permute-start.7 = (bf16[17,64,128]{2,1,0:T(8,128)(2,1)S(1)}, bf16[17,64,128]{2,1,0:T(8,128)(2,1)S(1)}, u32[]{:S(2)}, u32[]{:S(2)}) collective-permute-start(bf16[17,64,128]{2,1,0:T(8,128)(2,1)S(1)} %collective-permute-done.5.refs_0_), channel_id=1, source_target_pairs={{4,8},{8,4},{5,9},{9,5},{6,10},{10,6},{7,11},{11,7},{20,24},{24,20... | collective-permute-start | bytes 835592 | tf_op jit(solution)/shard_map/ppermute | solution.py:346
  19.4 3.7 %collective-permute-done.3.refs_1_ = bf16[17,64,128]{2,1,0:T(8,128)(2,1)S(1)} collective-permute-done((bf16[17,64,128]{2,1,0:T(8,128)(2,1)S(1)}, bf16[17,64,128]{2,1,0:T(8,128)(2,1)S(1)}, u32[]{:S(2)}, u32[]{:S(2)}) %collective-permute-start.3) | collective-permute-done | bytes 278560 | tf_op jit(solution)/shard_map/ppermute | solution.py:342
  23.1 0.0 collective-permute-start.4
  23.1 0.0 collective-permute-done.1.two
  23.1 0.7 %collective-permute-start.10 = (bf16[17,64,128]{2,1,0:T(8,128)(2,1)S(1)}, bf16[17,64,128]{2,1,0:T(8,128)(2,1)S(1)}, u32[]{:S(2)}, u32[]{:S(2)}) collective-permute-start(bf16[17,64,128]{2,1,0:T(8,128)(2,1)S(1)} %collective-permute-done.3.refs_1_), channel_id=1, source_target_pairs={{4,8},{8,4},{5,9},{9,5},{6,10},{10,6},{7,11},{11,7},{20,24},{24,20... | collective-permute-start | bytes 835592 | tf_op jit(solution)/shard_map/ppermute | solution.py:346
  23.8 0.0 collective-permute-done.one
  23.8 2.6 %collective-permute-start.11 = (bf16[17,64,128]{2,1,0:T(8,128)(2,1)S(1)}, bf16[17,64,128]{2,1,0:T(8,128)(2,1)S(1)}, u32[]{:S(2)}, u32[]{:S(2)}) collective-permute-start(bf16[17,64,128]{2,1,0:T(8,128)(2,1)S(1)} %collective-permute-done.3.refs_1_), channel_id=1, source_target_pairs={{0,4},{4,0},{8,12},{12,8},{1,5},{5,1},{9,13},{13,9},{2,6},{6,2},{1... | collective-permute-start | bytes 835592 | tf_op jit(solution)/shard_map/ppermute | solution.py:346
  26.4 0.8 %collective-permute-done.6.refs_2_ = bf16[17,64,128]{2,1,0:T(8,128)(2,1)S(1)} collective-permute-done((bf16[17,64,128]{2,1,0:T(8,128)(2,1)S(1)}, bf16[17,64,128]{2,1,0:T(8,128)(2,1)S(1)}, u32[]{:S(2)}, u32[]{:S(2)}) %collective-permute-start.6) | collective-permute-done | bytes 278560 | tf_op jit(solution)/shard_map/ppermute | solution.py:346
  27.2 0.0 collective-permute-start.9
  27.3 0.0 collective-permute-done.7.refs_3_
  27.3 0.6 %collective-permute-start.8 = (bf16[16,64,128]{2,1,0:T(8,128)(2,1)S(1)}, bf16[16,64,128]{2,1,0:T(8,128)(2,1)S(1)}, u32[]{:S(2)}, u32[]{:S(2)}) collective-permute-start(bf16[16,64,128]{2,1,0:T(8,128)(2,1)S(1)} %slice.6), channel_id=1, source_target_pairs={{0,1},{1,0},{2,3},{3,2},{4,5},{5,4},{6,7},{7,6},{8,9},{9,8},{10,11... | collective-permute-start | bytes 786440 | tf_op jit(solution)/shard_map/ppermute | solution.py:342
  27.8 0.7 %shard_map.63 = (bf16[34,64,128]{2,1,0:T(8,128)(2,1)S(1)}, f32[32,64,128]{2,1,0:T(8,128)S(1)}) custom-call(f32[6,32,128]{2,1,0:T(8,128)S(1)} %get-tuple-element.29.coef, bf16[17,64,128]{2,1,0:T(8,128)(2,1)S(1)} %collective-permute-done.5.refs_0_, bf16[17,64,128]{2,1,0:T(8,128)(2,1)S(1)} %collective-permute-done.3.refs_1_), custom_call_target="tpu_custom_call" | custom-call | flops 1 | bytes 1 | tf_op jit(solution)/shard_map/pallas_call | solution.py:327
  28.6 0.6 %shard_map.61 = (bf16[16,64,128]{2,1,0:T(8,128)(2,1)S(1)}, bf16[16,64,128]{2,1,0:T(8,128)(2,1)S(1)}, f32[2,32,128]{2,1,0:T(8,128)S(1)}, bf16[64,4096]{1,0:T(8,128)(2,1)S(1)}) custom-call(f32[6,32,128]{2,1,0:T(8,128)S(1)} %get-tuple-element.29.coef, f32[32,64,128]{2,1,0:T(8,128)S(1)} %get-tuple-element.30.partial, ...), custom_call_target="tpu_custom_call" | custom-call | flops 1 | bytes 1 | tf_op jit(solution)/shard_map/pallas_call | solution.py:327
  29.1 0.2 shard_map.64
  29.3 0.0 collective-permute-done.9.refs_3_
  29.3 0.1 collective-permute-start.2
  29.4 0.0 collective-permute-done.8.refs_2_
  29.4 0.0 collective-permute-done.4.plain
  29.4 1.4 %shard_map.65 = (bf16[256,4096]{1,0:T(8,128)(2,1)S(1)}, f32[256,128]{1,0:T(8,128)S(1)}) custom-call(bf16[64,4096]{1,0:T(8,128)(2,1)S(1)} %get-tuple-element.35.flat, bf16[34,64,128]{2,1,0:T(8,128)(2,1)S(1)} %get-tuple-element.28.center, bf16[32,64,128]{2,1,0:T(8,128)(2,1)S(1)} %collective-permute-done.4.plain, ...), custom_call_target="tpu_custom_call" | custom-call | flops 1 | bytes 1 | tf_op jit(solution)/shard_map/pallas_call | solution.py:327
  30.9 0.0 collective-permute-done.10.refs_2_
  30.9 2.5 %collective-permute-done.11.refs_3_ = bf16[17,64,128]{2,1,0:T(8,128)(2,1)S(1)} collective-permute-done((bf16[17,64,128]{2,1,0:T(8,128)(2,1)S(1)}, bf16[17,64,128]{2,1,0:T(8,128)(2,1)S(1)}, u32[]{:S(2)}, u32[]{:S(2)}) %collective-permute-start.11) | collective-permute-done | bytes 278560 | tf_op jit(solution)/shard_map/ppermute | solution.py:346
  33.4 1.2 %shard_map.66 = (bf16[16,64,128]{2,1,0:T(8,128)(2,1)S(1)}, bf16[16,64,128]{2,1,0:T(8,128)(2,1)S(1)}, f32[256,128]{1,0:T(8,128)}) custom-call(f32[2,32,128]{2,1,0:T(8,128)S(1)} %get-tuple-element.34.faces, bf16[256,4096]{1,0:T(8,128)(2,1)S(1)} %get-tuple-element.47.left, f32[256,128]{1,0:T(8,128)S(1)} %get-tuple-element.48.first_gram, ...), custom_call_target="tpu_custom_call" | custom-call | flops 1 | bytes 1 | tf_op jit(solution)/shard_map/pallas_call | solution.py:327
  34.6 0.0 collective-permute-start.12
  34.6 6.7 %all-to-all-start = ((f32[16,16,128]{2,1,0:T(8,128)}), f32[16,16,128]{2,1,0:T(8,128)S(1)}, u32[]{:S(2)}, u32[]{:S(2)}) async-start(f32[16,16,128]{2,1,0:T(8,128)} %bitcast), calls=%async_computation | async-start | bytes 262144 | tf_op jit(solution)/shard_map/all_to_all | solution.py:413
  41.3 0.0 collective-permute-done.2.theirs
  41.3 1.3 %shard_map.62.applied_in = bf16[256,1,16,128]{3,2,1,0:T(8,128)(2,1)} custom-call(bf16[16,64,128]{2,1,0:T(8,128)(2,1)S(1)} %get-tuple-element.32.mine, bf16[16,64,128]{2,1,0:T(8,128)(2,1)S(1)} %collective-permute-done.2.theirs), custom_call_target="tpu_custom_call" | custom-call | flops 1 | bytes 1 | tf_op jit(solution)/shard_map/pallas_call | solution.py:327
  42.6 0.0 collective-permute-done.12.refs_1_
  42.6 1.3 %shard_map.67 = bf16[256,1,16,128]{3,2,1,0:T(8,128)(2,1)} custom-call(bf16[256,1,16,128]{3,2,1,0:T(8,128)(2,1)} %shard_map.62.applied_in, bf16[16,64,128]{2,1,0:T(8,128)(2,1)S(1)} %get-tuple-element.50.refs_0_, bf16[16,64,128]{2,1,0:T(8,128)(2,1)S(1)} %collective-permute-done.12.refs_1_), custom_call_target="tpu_custom_call", output_to_operand_aliasing={{}: (0, {})} | custom-call | flops 1 | bytes 1 | tf_op jit(solution)/shard_map/pallas_call | solution.py:327
  43.9 1.5 %all-to-all-done.shares = f32[16,16,128]{2,1,0:T(8,128)S(1)} async-done(((f32[16,16,128]{2,1,0:T(8,128)}), f32[16,16,128]{2,1,0:T(8,128)S(1)}, u32[]{:S(2)}, u32[]{:S(2)}) %all-to-all-start) | async-done | bytes 131104 | tf_op jit(solution)/shard_map/all_to_all | solution.py:413
  45.4 0.7 %shard_map.68 = f32[16,256]{1,0:T(8,128)} custom-call(f32[16,16,128]{2,1,0:T(8,128)S(1)} %all-to-all-done.shares), custom_call_target="tpu_custom_call" | custom-call | flops 1 | bytes 1 | tf_op jit(solution)/shard_map/pallas_call | solution.py:327
  (2 shorter events, 0.0 us)
Async XLA Ops:
  2.7 20.4 %collective-permute-start.1 = (bf16[33,64,128]{2,1,0:T(8,128)(2,1)S(1)}, bf16[33,64,128]{2,1,0:T(8,128)(2,1)S(1)}, u32[]{:S(2)}, u32[]{:S(2)}) collective-permute-start(bf16[33,64,128]{2,1,0:T(8,128)(2,1)S(1)} %get-tuple-element.31), channel_id=1, source_target_pairs={{4,8},{8,4},{5,9},{9,5},{6,10},{10,6},{7,11},{11,7},{20,24},{24,20... | collective-permute-start | bytes 1622024 | tf_op jit(solution)/shard_map/ppermute | solution.py:346
  3.4 20.4 %collective-permute-start = (bf16[33,64,128]{2,1,0:T(8,128)(2,1)S(1)}, bf16[33,64,128]{2,1,0:T(8,128)(2,1)S(1)}, u32[]{:S(2)}, u32[]{:S(2)}) collective-permute-start(bf16[33,64,128]{2,1,0:T(8,128)(2,1)S(1)} %get-tuple-element.31), channel_id=1, source_target_pairs={{0,4},{4,0},{8,12},{12,8},{1,5},{5,1},{9,13},{13,9},{2,6},{6,2},{1... | collective-permute-start | bytes 1622024 | tf_op jit(solution)/shard_map/ppermute | solution.py:346
  9.3 9.1 %collective-permute-start.5 = (bf16[17,64,128]{2,1,0:T(8,128)(2,1)S(1)}, bf16[17,64,128]{2,1,0:T(8,128)(2,1)S(1)}, u32[]{:S(2)}, u32[]{:S(2)}) collective-permute-start(bf16[17,64,128]{2,1,0:T(8,128)(2,1)S(1)} %get-tuple-element.40), channel_id=1, source_target_pairs={{0,2},{1,3},{2,0},{3,1},{4,6},{5,7},{6,4},{7,5},{8,10},{9,11},{10,... | collective-permute-start | bytes 835592 | tf_op jit(solution)/shard_map/ppermute | solution.py:342
  10.8 0.8 %copy-start = (s32[1,64,128]{2,1,0:T(8,128)S(1)}, s32[1,64,128]{2,1,0:T(8,128)}, u32[]{:S(2)}) copy-start(s32[1,64,128]{2,1,0:T(8,128)} %zone_ref.1) | copy-start | bytes 98308
  11.5 0.7 %copy-start.1 = (f32[16]{0:T(128)S(1)}, f32[16]{0:T(128)}, u32[]{:S(2)}) copy-start(f32[16]{0:T(128)} %cond_ref.1) | copy-start | bytes 196
  12.2 0.7 %copy-start.2 = (f32[16]{0:T(128)S(1)}, f32[16]{0:T(128)}, u32[]{:S(2)}) copy-start(f32[16]{0:T(128)} %heat_ref.1) | copy-start | bytes 196
  14.2 8.9 %collective-permute-start.3 = (bf16[17,64,128]{2,1,0:T(8,128)(2,1)S(1)}, bf16[17,64,128]{2,1,0:T(8,128)(2,1)S(1)}, u32[]{:S(2)}, u32[]{:S(2)}) collective-permute-start(bf16[17,64,128]{2,1,0:T(8,128)(2,1)S(1)} %get-tuple-element.38), channel_id=1, source_target_pairs={{0,2},{1,3},{2,0},{3,1},{4,6},{5,7},{6,4},{7,5},{8,10},{9,11},{10,... | collective-permute-start | bytes 835592 | tf_op jit(solution)/shard_map/ppermute | solution.py:342
  18.3 8.9 %collective-permute-start.6 = (bf16[17,64,128]{2,1,0:T(8,128)(2,1)S(1)}, bf16[17,64,128]{2,1,0:T(8,128)(2,1)S(1)}, u32[]{:S(2)}, u32[]{:S(2)}) collective-permute-start(bf16[17,64,128]{2,1,0:T(8,128)(2,1)S(1)} %collective-permute-done.5.refs_0_), channel_id=1, source_target_pairs={{0,4},{4,0},{8,12},{12,8},{1,5},{5,1},{9,13},{13,9},{2,6},{6,2},{1... | collective-permute-start | bytes 835592 | tf_op jit(solution)/shard_map/ppermute | solution.py:346
  18.7 8.6 %collective-permute-start.7 = (bf16[17,64,128]{2,1,0:T(8,128)(2,1)S(1)}, bf16[17,64,128]{2,1,0:T(8,128)(2,1)S(1)}, u32[]{:S(2)}, u32[]{:S(2)}) collective-permute-start(bf16[17,64,128]{2,1,0:T(8,128)(2,1)S(1)} %collective-permute-done.5.refs_0_), channel_id=1, source_target_pairs={{4,8},{8,4},{5,9},{9,5},{6,10},{10,6},{7,11},{11,7},{20,24},{24,20... | collective-permute-start | bytes 835592 | tf_op jit(solution)/shard_map/ppermute | solution.py:346
  23.1 6.4 %collective-permute-start.4 = (bf16[32,64,128]{2,1,0:T(8,128)(2,1)S(1)}, bf16[32,64,128]{2,1,0:T(8,128)(2,1)S(1)}, u32[]{:S(2)}, u32[]{:S(2)}) collective-permute-start(bf16[32,64,128]{2,1,0:T(8,128)(2,1)S(1)} %get-tuple-element.39), channel_id=1, source_target_pairs={{0,1},{1,0},{2,3},{3,2},{4,5},{5,4},{6,7},{7,6},{8,9},{9,8},{10,11... | collective-permute-start | bytes 1572872 | tf_op jit(solution)/shard_map/ppermute | solution.py:342
  23.1 7.8 %collective-permute-start.10 = (bf16[17,64,128]{2,1,0:T(8,128)(2,1)S(1)}, bf16[17,64,128]{2,1,0:T(8,128)(2,1)S(1)}, u32[]{:S(2)}, u32[]{:S(2)}) collective-permute-start(bf16[17,64,128]{2,1,0:T(8,128)(2,1)S(1)} %collective-permute-done.3.refs_1_), channel_id=1, source_target_pairs={{4,8},{8,4},{5,9},{9,5},{6,10},{10,6},{7,11},{11,7},{20,24},{24,20... | collective-permute-start | bytes 835592 | tf_op jit(solution)/shard_map/ppermute | solution.py:346
  23.8 9.6 %collective-permute-start.11 = (bf16[17,64,128]{2,1,0:T(8,128)(2,1)S(1)}, bf16[17,64,128]{2,1,0:T(8,128)(2,1)S(1)}, u32[]{:S(2)}, u32[]{:S(2)}) collective-permute-start(bf16[17,64,128]{2,1,0:T(8,128)(2,1)S(1)} %collective-permute-done.3.refs_1_), channel_id=1, source_target_pairs={{0,4},{4,0},{8,12},{12,8},{1,5},{5,1},{9,13},{13,9},{2,6},{6,2},{1... | collective-permute-start | bytes 835592 | tf_op jit(solution)/shard_map/ppermute | solution.py:346
  27.2 2.1 %collective-permute-start.9 = (bf16[16,64,128]{2,1,0:T(8,128)(2,1)S(1)}, bf16[16,64,128]{2,1,0:T(8,128)(2,1)S(1)}, u32[]{:S(2)}, u32[]{:S(2)}) collective-permute-start(bf16[16,64,128]{2,1,0:T(8,128)(2,1)S(1)} %slice.7), channel_id=1, source_target_pairs={{0,1},{1,0},{2,3},{3,2},{4,5},{5,4},{6,7},{7,6},{8,9},{9,8},{10,11... | collective-permute-start | bytes 786440 | tf_op jit(solution)/shard_map/ppermute | solution.py:342
  27.3 2.2 %collective-permute-start.8 = (bf16[16,64,128]{2,1,0:T(8,128)(2,1)S(1)}, bf16[16,64,128]{2,1,0:T(8,128)(2,1)S(1)}, u32[]{:S(2)}, u32[]{:S(2)}) collective-permute-start(bf16[16,64,128]{2,1,0:T(8,128)(2,1)S(1)} %slice.6), channel_id=1, source_target_pairs={{0,1},{1,0},{2,3},{3,2},{4,5},{5,4},{6,7},{7,6},{8,9},{9,8},{10,11... | collective-permute-start | bytes 786440 | tf_op jit(solution)/shard_map/ppermute | solution.py:342
  29.3 12.0 %collective-permute-start.2 = (bf16[16,64,128]{2,1,0:T(8,128)(2,1)S(1)}, bf16[16,64,128]{2,1,0:T(8,128)(2,1)S(1)}, u32[]{:S(2)}, u32[]{:S(2)}) collective-permute-start(bf16[16,64,128]{2,1,0:T(8,128)(2,1)S(1)} %get-tuple-element.33), channel_id=1, source_target_pairs={{0,1},{1,0},{2,3},{3,2},{4,5},{5,4},{6,7},{7,6},{8,9},{9,8},{10,11... | collective-permute-start | bytes 786440 | tf_op jit(solution)/shard_map/ppermute | solution.py:342
  34.6 8.0 %collective-permute-start.12 = (bf16[16,64,128]{2,1,0:T(8,128)(2,1)S(1)}, bf16[16,64,128]{2,1,0:T(8,128)(2,1)S(1)}, u32[]{:S(2)}, u32[]{:S(2)}) collective-permute-start(bf16[16,64,128]{2,1,0:T(8,128)(2,1)S(1)} %get-tuple-element.51), channel_id=1, source_target_pairs={{0,1},{1,0},{2,3},{3,2},{4,5},{5,4},{6,7},{7,6},{8,9},{9,8},{10,11... | collective-permute-start | bytes 786440 | tf_op jit(solution)/shard_map/ppermute | solution.py:342
  34.6 10.8 %all-to-all-start = ((f32[16,16,128]{2,1,0:T(8,128)}), f32[16,16,128]{2,1,0:T(8,128)S(1)}, u32[]{:S(2)}, u32[]{:S(2)}) async-start(f32[16,16,128]{2,1,0:T(8,128)} %bitcast), calls=%async_computation | async-start | bytes 262144 | tf_op jit(solution)/shard_map/all_to_all | solution.py:413

commit v19 on v17

--- a/solution.py
+++ b/solution.py
@@ -248,7 +248,7 @@
         values.append(first_gram[:, block] + weight * total)
     for slab in range(slabs):
         for owner in range(blocks):
-            start, place = (slab * blocks + owner) * share, (slabs * blocks - 1 - slab * blocks - owner) * share
+            start, place = (slab * blocks + owner) * share, ((slabs - 1 - slab) * blocks + owner) * share
             for k, value in enumerate(values):
                 gram[place:place + share, k * columns:(k + 1) * columns] = value[start:start + share]
 
@@ -294,7 +294,7 @@
     for core in range(CORES):
         sums = []
         for chip in range(chips):
-            last = slabs * blocks - 1 - (CORES * chip + core)
+            last = (slabs - 1) * blocks + CORES * chip + core
             total = shares[last]
             for slab in range(1, slabs):
                 total += shares[last - slab * blocks]
@@ -409,9 +409,10 @@
         (faces, left, first_gram, *partials, *centers, *second_two, *second_one, *images),
     )
     parts = slabs * blocks
+    order = [[slab * blocks + b for slab in reversed(range(slabs)) for b in range(blocks)]]
     shares = gram.reshape(parts, total // parts, chips * columns)
     shares = lax.all_to_all(
-        shares, ("dom", "blk"), split_axis=0, concat_axis=0, tiled=True, axis_index_groups=[[*reversed(range(parts))]]
+        shares, ("dom", "blk"), split_axis=0, concat_axis=0, tiled=True, axis_index_groups=order
     )
     pieces = []
     for k in range(count):

time: 46.3 us -> 46.8 us (1.011)
  waiting for transfers between devices: 10.4 us -> 11.1 us
    all_to_all x1, waiting for transfers between devices: 1.55 us -> 2.34 us  [per_device(): lax.all_to_all(shares, ('dom', 'blk'), split_axis=0, concat_axis=0, tiled...]
where the time goes in v19:
time: 46.8 us; the launch traced here: 46.5 us
  starting transfers between devices  21.7 us (46%)
  waiting for transfers between devices  11.1 us (24%)
  Pallas kernels  10.7 us (23%)
  local copies, waits for them, and re-layouts  2.1 us (4%)
  between operations  0.77 us (2%)
    ppermute x6, starting transfers between devices, exchange(): lax.ppermute(array, 'dom', [(d, to) for d, to in enumerate(partner) if 0...  12.6 us
    pallas_call x9, Pallas kernels, call(): pl.pallas_call(kernel, out_shape=out_shape, in_specs=specs or [VMEM] * le...  8.68 us
    all_to_all x1, starting transfers between devices, per_device(): lax.all_to_all(shares, ('dom', 'blk'), split_axis=0, concat_axis=0, tiled...  6.43 us
    ppermute x7, waiting for transfers between devices, swap(): return lax.ppermute(array, 'blk', [(i, i ^ s) for i in range(blocks)])  5.55 us
    ppermute x6, waiting for transfers between devices, exchange(): lax.ppermute(array, 'dom', [(d, to) for d, to in enumerate(partner) if 0...  3.25 us
    ppermute x7, starting transfers between devices, swap(): return lax.ppermute(array, 'blk', [(i, i ^ s) for i in range(blocks)])  2.74 us
    all_to_all x1, waiting for transfers between devices, per_device(): lax.all_to_all(shares, ('dom', 'blk'), split_axis=0, concat_axis=0, tiled...  2.34 us
    unnamed x6, local copies, waits for them, and re-layouts  2.07 us
  transfers between devices with their start and end apart: 14, of which 5 were waited for; matrix products, arithmetic and copies ran while one was open for 0% of the time, Pallas kernels for 17%

profile of v19, /device:TPU:0, one launch (start us, length us, event | category | flops | bytes accessed | tf_op | source)
XLA Modules:
  0.0 46.5 jit_solution(8361925032402350831)
XLA Ops:
  0.6 2.1 %shard_map.59 = (bf16[33,64,128]{2,1,0:T(8,128)(2,1)S(1)}, bf16[34,64,128]{2,1,0:T(8,128)(2,1)S(1)}, bf16[32,64,128]{2,1,0:T(8,128)(2,1)S(1)}, bf16[17,64,128]{2,1,0:T(8,128)(2,1)S(1)}, bf16[17,64,128]{2,1,0:T(8,128)(2,1)S(1)}) custom-call(bf16[64,1,64,128]{3,2,1,0:T(8,128)(2,1)} %basis_hbm.1, s32[1,64,128]{2,1,0:T(8,128)} %zone_ref.1, f32[16]{0:T(128)} %cond_ref.1), custom_call_target="tpu_custom_call" | custom-call | tf_op jit(solution)/shard_map/pallas_call | solution.py:88
  2.7 0.7 %collective-permute-start.1 = (bf16[33,64,128]{2,1,0:T(8,128)(2,1)S(1)}, bf16[33,64,128]{2,1,0:T(8,128)(2,1)S(1)}, u32[]{:S(2)}, u32[]{:S(2)}) collective-permute-start(bf16[33,64,128]{2,1,0:T(8,128)(2,1)S(1)} %get-tuple-element.31), channel_id=1, source_target_pairs={{4,8},{8,4},{5,9},{9,5},{6,10},{10,6},{7,11},{11,7},{20,24},{24,20... | collective-permute-start | bytes 1622024 | tf_op jit(solution)/shard_map/ppermute | solution.py:346
  3.4 5.9 %collective-permute-start = (bf16[33,64,128]{2,1,0:T(8,128)(2,1)S(1)}, bf16[33,64,128]{2,1,0:T(8,128)(2,1)S(1)}, u32[]{:S(2)}, u32[]{:S(2)}) collective-permute-start(bf16[33,64,128]{2,1,0:T(8,128)(2,1)S(1)} %get-tuple-element.31), channel_id=1, source_target_pairs={{0,4},{4,0},{8,12},{12,8},{1,5},{5,1},{9,13},{13,9},{2,6},{6,2},{1... | collective-permute-start | bytes 1622024 | tf_op jit(solution)/shard_map/ppermute | solution.py:346
  9.3 1.5 %collective-permute-start.5 = (bf16[17,64,128]{2,1,0:T(8,128)(2,1)S(1)}, bf16[17,64,128]{2,1,0:T(8,128)(2,1)S(1)}, u32[]{:S(2)}, u32[]{:S(2)}) collective-permute-start(bf16[17,64,128]{2,1,0:T(8,128)(2,1)S(1)} %get-tuple-element.40), channel_id=1, source_target_pairs={{0,2},{1,3},{2,0},{3,1},{4,6},{5,7},{6,4},{7,5},{8,10},{9,11},{10,... | collective-permute-start | bytes 835592 | tf_op jit(solution)/shard_map/ppermute | solution.py:342
  10.8 0.0 copy-start
  10.8 0.8 %copy-done = s32[1,64,128]{2,1,0:T(8,128)S(1)} copy-done((s32[1,64,128]{2,1,0:T(8,128)S(1)}, s32[1,64,128]{2,1,0:T(8,128)}, u32[]{:S(2)}) %copy-start) | copy-done | bytes 32792
  11.5 0.0 copy-start.1
  11.5 0.7 %copy-done.1 = f32[16]{0:T(128)S(1)} copy-done((f32[16]{0:T(128)S(1)}, f32[16]{0:T(128)}, u32[]{:S(2)}) %copy-start.1) | copy-done | bytes 88
  12.2 0.0 copy-start.2
  12.2 0.7 %copy-done.2 = f32[16]{0:T(128)S(1)} copy-done((f32[16]{0:T(128)S(1)}, f32[16]{0:T(128)}, u32[]{:S(2)}) %copy-start.2) | copy-done | bytes 88
  12.8 1.3 %shard_map.60 = (f32[6,32,128]{2,1,0:T(8,128)S(1)}, f32[32,64,128]{2,1,0:T(8,128)S(1)}) custom-call(s32[1,64,128]{2,1,0:T(8,128)S(1)} %copy-done, f32[16]{0:T(128)S(1)} %copy-done.1, f32[16]{0:T(128)S(1)} %copy-done.2, bf16[34,64,128]{2,1,0:T(8,128)(2,1)S(1)} %get-tuple-element.28.center), custom_call_target="tpu_custom_call" | custom-call | flops 1073741824 | bytes 134217728 | tf_op jit(solution)/shard_map/pallas_call | solution.py:327
  14.2 0.6 %collective-permute-start.3 = (bf16[17,64,128]{2,1,0:T(8,128)(2,1)S(1)}, bf16[17,64,128]{2,1,0:T(8,128)(2,1)S(1)}, u32[]{:S(2)}, u32[]{:S(2)}) collective-permute-start(bf16[17,64,128]{2,1,0:T(8,128)(2,1)S(1)} %get-tuple-element.38), channel_id=1, source_target_pairs={{0,2},{1,3},{2,0},{3,1},{4,6},{5,7},{6,4},{7,5},{8,10},{9,11},{10,... | collective-permute-start | bytes 835592 | tf_op jit(solution)/shard_map/ppermute | solution.py:342
  14.8 3.6 %collective-permute-done.5.refs_0_ = bf16[17,64,128]{2,1,0:T(8,128)(2,1)S(1)} collective-permute-done((bf16[17,64,128]{2,1,0:T(8,128)(2,1)S(1)}, bf16[17,64,128]{2,1,0:T(8,128)(2,1)S(1)}, u32[]{:S(2)}, u32[]{:S(2)}) %collective-permute-start.5) | collective-permute-done | bytes 278560 | tf_op jit(solution)/shard_map/ppermute | solution.py:342
  18.3 0.7 %collective-permute-start.6 = (bf16[17,64,128]{2,1,0:T(8,128)(2,1)S(1)}, bf16[17,64,128]{2,1,0:T(8,128)(2,1)S(1)}, u32[]{:S(2)}, u32[]{:S(2)}) collective-permute-start(bf16[17,64,128]{2,1,0:T(8,128)(2,1)S(1)} %collective-permute-done.5.refs_0_), channel_id=1, source_target_pairs={{4,8},{8,4},{5,9},{9,5},{6,10},{10,6},{7,11},{11,7},{20,24},{24,20... | collective-permute-start | bytes 835592 | tf_op jit(solution)/shard_map/ppermute | solution.py:346
  19.0 2.1 %collective-permute-start.7 = (bf16[17,64,128]{2,1,0:T(8,128)(2,1)S(1)}, bf16[17,64,128]{2,1,0:T(8,128)(2,1)S(1)}, u32[]{:S(2)}, u32[]{:S(2)}) collective-permute-start(bf16[17,64,128]{2,1,0:T(8,128)(2,1)S(1)} %collective-permute-done.5.refs_0_), channel_id=1, source_target_pairs={{0,4},{4,0},{8,12},{12,8},{1,5},{5,1},{9,13},{13,9},{2,6},{6,2},{1... | collective-permute-start | bytes 835592 | tf_op jit(solution)/shard_map/ppermute | solution.py:346
  21.1 2.0 %collective-permute-done.3.refs_1_ = bf16[17,64,128]{2,1,0:T(8,128)(2,1)S(1)} collective-permute-done((bf16[17,64,128]{2,1,0:T(8,128)(2,1)S(1)}, bf16[17,64,128]{2,1,0:T(8,128)(2,1)S(1)}, u32[]{:S(2)}, u32[]{:S(2)}) %collective-permute-start.3) | collective-permute-done | bytes 278560 | tf_op jit(solution)/shard_map/ppermute | solution.py:342
  23.1 0.0 collective-permute-start.4
  23.1 0.0 collective-permute-done.1.two
  23.1 0.7 %collective-permute-start.10 = (bf16[17,64,128]{2,1,0:T(8,128)(2,1)S(1)}, bf16[17,64,128]{2,1,0:T(8,128)(2,1)S(1)}, u32[]{:S(2)}, u32[]{:S(2)}) collective-permute-start(bf16[17,64,128]{2,1,0:T(8,128)(2,1)S(1)} %collective-permute-done.3.refs_1_), channel_id=1, source_target_pairs={{4,8},{8,4},{5,9},{9,5},{6,10},{10,6},{7,11},{11,7},{20,24},{24,20... | collective-permute-start | bytes 835592 | tf_op jit(solution)/shard_map/ppermute | solution.py:346
  23.8 0.0 collective-permute-done.one
  23.8 2.6 %collective-permute-start.11 = (bf16[17,64,128]{2,1,0:T(8,128)(2,1)S(1)}, bf16[17,64,128]{2,1,0:T(8,128)(2,1)S(1)}, u32[]{:S(2)}, u32[]{:S(2)}) collective-permute-start(bf16[17,64,128]{2,1,0:T(8,128)(2,1)S(1)} %collective-permute-done.3.refs_1_), channel_id=1, source_target_pairs={{0,4},{4,0},{8,12},{12,8},{1,5},{5,1},{9,13},{13,9},{2,6},{6,2},{1... | collective-permute-start | bytes 835592 | tf_op jit(solution)/shard_map/ppermute | solution.py:346
  26.3 0.0 collective-permute-done.6.refs_2_
  26.4 0.1 collective-permute-start.9
  26.5 1.0 %collective-permute-done.7.refs_3_ = bf16[17,64,128]{2,1,0:T(8,128)(2,1)S(1)} collective-permute-done((bf16[17,64,128]{2,1,0:T(8,128)(2,1)S(1)}, bf16[17,64,128]{2,1,0:T(8,128)(2,1)S(1)}, u32[]{:S(2)}, u32[]{:S(2)}) %collective-permute-start.7) | collective-permute-done | bytes 278560 | tf_op jit(solution)/shard_map/ppermute | solution.py:346
  27.5 0.0 collective-permute-start.8
  27.5 0.7 %shard_map.63 = (bf16[34,64,128]{2,1,0:T(8,128)(2,1)S(1)}, f32[32,64,128]{2,1,0:T(8,128)S(1)}) custom-call(f32[6,32,128]{2,1,0:T(8,128)S(1)} %get-tuple-element.29.coef, bf16[17,64,128]{2,1,0:T(8,128)(2,1)S(1)} %collective-permute-done.5.refs_0_, bf16[17,64,128]{2,1,0:T(8,128)(2,1)S(1)} %collective-permute-done.3.refs_1_), custom_call_target="tpu_custom_call" | custom-call | flops 1 | bytes 1 | tf_op jit(solution)/shard_map/pallas_call | solution.py:327
  28.2 0.6 %shard_map.61 = (bf16[16,64,128]{2,1,0:T(8,128)(2,1)S(1)}, bf16[16,64,128]{2,1,0:T(8,128)(2,1)S(1)}, f32[2,32,128]{2,1,0:T(8,128)S(1)}, bf16[64,4096]{1,0:T(8,128)(2,1)S(1)}) custom-call(f32[6,32,128]{2,1,0:T(8,128)S(1)} %get-tuple-element.29.coef, f32[32,64,128]{2,1,0:T(8,128)S(1)} %get-tuple-element.30.partial, ...), custom_call_target="tpu_custom_call" | custom-call | flops 1 | bytes 1 | tf_op jit(solution)/shard_map/pallas_call | solution.py:327
  28.8 0.2 shard_map.64
  28.9 0.0 collective-permute-done.9.refs_3_
  29.0 0.6 %collective-permute-start.2 = (bf16[16,64,128]{2,1,0:T(8,128)(2,1)S(1)}, bf16[16,64,128]{2,1,0:T(8,128)(2,1)S(1)}, u32[]{:S(2)}, u32[]{:S(2)}) collective-permute-start(bf16[16,64,128]{2,1,0:T(8,128)(2,1)S(1)} %get-tuple-element.33), channel_id=1, source_target_pairs={{0,1},{1,0},{2,3},{3,2},{4,5},{5,4},{6,7},{7,6},{8,9},{9,8},{10,11... | collective-permute-start | bytes 786440 | tf_op jit(solution)/shard_map/ppermute | solution.py:342
  29.5 0.0 collective-permute-done.8.refs_2_
  29.5 0.0 collective-permute-done.4.plain
  29.5 1.4 %shard_map.65 = (bf16[256,4096]{1,0:T(8,128)(2,1)S(1)}, f32[256,128]{1,0:T(8,128)S(1)}) custom-call(bf16[64,4096]{1,0:T(8,128)(2,1)S(1)} %get-tuple-element.35.flat, bf16[34,64,128]{2,1,0:T(8,128)(2,1)S(1)} %get-tuple-element.28.center, bf16[32,64,128]{2,1,0:T(8,128)(2,1)S(1)} %collective-permute-done.4.plain, ...), custom_call_target="tpu_custom_call" | custom-call | flops 1 | bytes 1 | tf_op jit(solution)/shard_map/pallas_call | solution.py:327
  30.9 0.0 collective-permute-done.10.refs_2_
  30.9 2.3 %collective-permute-done.11.refs_3_ = bf16[17,64,128]{2,1,0:T(8,128)(2,1)S(1)} collective-permute-done((bf16[17,64,128]{2,1,0:T(8,128)(2,1)S(1)}, bf16[17,64,128]{2,1,0:T(8,128)(2,1)S(1)}, u32[]{:S(2)}, u32[]{:S(2)}) %collective-permute-start.11) | collective-permute-done | bytes 278560 | tf_op jit(solution)/shard_map/ppermute | solution.py:346
  33.2 1.2 %shard_map.66 = (bf16[16,64,128]{2,1,0:T(8,128)(2,1)S(1)}, bf16[16,64,128]{2,1,0:T(8,128)(2,1)S(1)}, f32[256,128]{1,0:T(8,128)}) custom-call(f32[2,32,128]{2,1,0:T(8,128)S(1)} %get-tuple-element.34.faces, bf16[256,4096]{1,0:T(8,128)(2,1)S(1)} %get-tuple-element.47.left, f32[256,128]{1,0:T(8,128)S(1)} %get-tuple-element.48.first_gram, ...), custom_call_target="tpu_custom_call" | custom-call | flops 1 | bytes 1 | tf_op jit(solution)/shard_map/pallas_call | solution.py:327
  34.4 0.0 collective-permute-start.12
  34.4 6.4 %all-to-all-start = ((f32[16,16,128]{2,1,0:T(8,128)}), f32[16,16,128]{2,1,0:T(8,128)S(1)}, u32[]{:S(2)}, u32[]{:S(2)}) async-start(f32[16,16,128]{2,1,0:T(8,128)} %bitcast), calls=%async_computation | async-start | bytes 262144 | tf_op jit(solution)/shard_map/all_to_all | solution.py:414
  40.8 0.0 collective-permute-done.2.theirs
  40.8 1.3 %shard_map.62.applied_in = bf16[256,1,16,128]{3,2,1,0:T(8,128)(2,1)} custom-call(bf16[16,64,128]{2,1,0:T(8,128)(2,1)S(1)} %get-tuple-element.32.mine, bf16[16,64,128]{2,1,0:T(8,128)(2,1)S(1)} %collective-permute-done.2.theirs), custom_call_target="tpu_custom_call" | custom-call | flops 1 | bytes 1 | tf_op jit(solution)/shard_map/pallas_call | solution.py:327
  42.1 0.0 collective-permute-done.12.refs_1_
  42.1 1.3 %shard_map.67 = bf16[256,1,16,128]{3,2,1,0:T(8,128)(2,1)} custom-call(bf16[256,1,16,128]{3,2,1,0:T(8,128)(2,1)} %shard_map.62.applied_in, bf16[16,64,128]{2,1,0:T(8,128)(2,1)S(1)} %get-tuple-element.50.refs_0_, bf16[16,64,128]{2,1,0:T(8,128)(2,1)S(1)} %collective-permute-done.12.refs_1_), custom_call_target="tpu_custom_call", output_to_operand_aliasing={{}: (0, {})} | custom-call | flops 1 | bytes 1 | tf_op jit(solution)/shard_map/pallas_call | solution.py:327
  43.4 2.3 %all-to-all-done.shares = f32[16,16,128]{2,1,0:T(8,128)S(1)} async-done(((f32[16,16,128]{2,1,0:T(8,128)}), f32[16,16,128]{2,1,0:T(8,128)S(1)}, u32[]{:S(2)}, u32[]{:S(2)}) %all-to-all-start) | async-done | bytes 131104 | tf_op jit(solution)/shard_map/all_to_all | solution.py:414
  45.7 0.7 %shard_map.68 = f32[16,256]{1,0:T(8,128)} custom-call(f32[16,16,128]{2,1,0:T(8,128)S(1)} %all-to-all-done.shares), custom_call_target="tpu_custom_call" | custom-call | flops 1 | bytes 1 | tf_op jit(solution)/shard_map/pallas_call | solution.py:327
  (2 shorter events, 0.0 us)
Async XLA Ops:
  2.7 20.4 %collective-permute-start.1 = (bf16[33,64,128]{2,1,0:T(8,128)(2,1)S(1)}, bf16[33,64,128]{2,1,0:T(8,128)(2,1)S(1)}, u32[]{:S(2)}, u32[]{:S(2)}) collective-permute-start(bf16[33,64,128]{2,1,0:T(8,128)(2,1)S(1)} %get-tuple-element.31), channel_id=1, source_target_pairs={{4,8},{8,4},{5,9},{9,5},{6,10},{10,6},{7,11},{11,7},{20,24},{24,20... | collective-permute-start | bytes 1622024 | tf_op jit(solution)/shard_map/ppermute | solution.py:346
  3.4 20.4 %collective-permute-start = (bf16[33,64,128]{2,1,0:T(8,128)(2,1)S(1)}, bf16[33,64,128]{2,1,0:T(8,128)(2,1)S(1)}, u32[]{:S(2)}, u32[]{:S(2)}) collective-permute-start(bf16[33,64,128]{2,1,0:T(8,128)(2,1)S(1)} %get-tuple-element.31), channel_id=1, source_target_pairs={{0,4},{4,0},{8,12},{12,8},{1,5},{5,1},{9,13},{13,9},{2,6},{6,2},{1... | collective-permute-start | bytes 1622024 | tf_op jit(solution)/shard_map/ppermute | solution.py:346
  9.3 9.1 %collective-permute-start.5 = (bf16[17,64,128]{2,1,0:T(8,128)(2,1)S(1)}, bf16[17,64,128]{2,1,0:T(8,128)(2,1)S(1)}, u32[]{:S(2)}, u32[]{:S(2)}) collective-permute-start(bf16[17,64,128]{2,1,0:T(8,128)(2,1)S(1)} %get-tuple-element.40), channel_id=1, source_target_pairs={{0,2},{1,3},{2,0},{3,1},{4,6},{5,7},{6,4},{7,5},{8,10},{9,11},{10,... | collective-permute-start | bytes 835592 | tf_op jit(solution)/shard_map/ppermute | solution.py:342
  10.8 0.8 %copy-start = (s32[1,64,128]{2,1,0:T(8,128)S(1)}, s32[1,64,128]{2,1,0:T(8,128)}, u32[]{:S(2)}) copy-start(s32[1,64,128]{2,1,0:T(8,128)} %zone_ref.1) | copy-start | bytes 98308
  11.5 0.7 %copy-start.1 = (f32[16]{0:T(128)S(1)}, f32[16]{0:T(128)}, u32[]{:S(2)}) copy-start(f32[16]{0:T(128)} %cond_ref.1) | copy-start | bytes 196
  12.2 0.7 %copy-start.2 = (f32[16]{0:T(128)S(1)}, f32[16]{0:T(128)}, u32[]{:S(2)}) copy-start(f32[16]{0:T(128)} %heat_ref.1) | copy-start | bytes 196
  14.2 8.9 %collective-permute-start.3 = (bf16[17,64,128]{2,1,0:T(8,128)(2,1)S(1)}, bf16[17,64,128]{2,1,0:T(8,128)(2,1)S(1)}, u32[]{:S(2)}, u32[]{:S(2)}) collective-permute-start(bf16[17,64,128]{2,1,0:T(8,128)(2,1)S(1)} %get-tuple-element.38), channel_id=1, source_target_pairs={{0,2},{1,3},{2,0},{3,1},{4,6},{5,7},{6,4},{7,5},{8,10},{9,11},{10,... | collective-permute-start | bytes 835592 | tf_op jit(solution)/shard_map/ppermute | solution.py:342
  18.3 8.0 %collective-permute-start.6 = (bf16[17,64,128]{2,1,0:T(8,128)(2,1)S(1)}, bf16[17,64,128]{2,1,0:T(8,128)(2,1)S(1)}, u32[]{:S(2)}, u32[]{:S(2)}) collective-permute-start(bf16[17,64,128]{2,1,0:T(8,128)(2,1)S(1)} %collective-permute-done.5.refs_0_), channel_id=1, source_target_pairs={{4,8},{8,4},{5,9},{9,5},{6,10},{10,6},{7,11},{11,7},{20,24},{24,20... | collective-permute-start | bytes 835592 | tf_op jit(solution)/shard_map/ppermute | solution.py:346
  19.0 8.4 %collective-permute-start.7 = (bf16[17,64,128]{2,1,0:T(8,128)(2,1)S(1)}, bf16[17,64,128]{2,1,0:T(8,128)(2,1)S(1)}, u32[]{:S(2)}, u32[]{:S(2)}) collective-permute-start(bf16[17,64,128]{2,1,0:T(8,128)(2,1)S(1)} %collective-permute-done.5.refs_0_), channel_id=1, source_target_pairs={{0,4},{4,0},{8,12},{12,8},{1,5},{5,1},{9,13},{13,9},{2,6},{6,2},{1... | collective-permute-start | bytes 835592 | tf_op jit(solution)/shard_map/ppermute | solution.py:346
  23.1 6.5 %collective-permute-start.4 = (bf16[32,64,128]{2,1,0:T(8,128)(2,1)S(1)}, bf16[32,64,128]{2,1,0:T(8,128)(2,1)S(1)}, u32[]{:S(2)}, u32[]{:S(2)}) collective-permute-start(bf16[32,64,128]{2,1,0:T(8,128)(2,1)S(1)} %get-tuple-element.39), channel_id=1, source_target_pairs={{0,1},{1,0},{2,3},{3,2},{4,5},{5,4},{6,7},{7,6},{8,9},{9,8},{10,11... | collective-permute-start | bytes 1572872 | tf_op jit(solution)/shard_map/ppermute | solution.py:342
  23.1 7.9 %collective-permute-start.10 = (bf16[17,64,128]{2,1,0:T(8,128)(2,1)S(1)}, bf16[17,64,128]{2,1,0:T(8,128)(2,1)S(1)}, u32[]{:S(2)}, u32[]{:S(2)}) collective-permute-start(bf16[17,64,128]{2,1,0:T(8,128)(2,1)S(1)} %collective-permute-done.3.refs_1_), channel_id=1, source_target_pairs={{4,8},{8,4},{5,9},{9,5},{6,10},{10,6},{7,11},{11,7},{20,24},{24,20... | collective-permute-start | bytes 835592 | tf_op jit(solution)/shard_map/ppermute | solution.py:346
  23.8 9.4 %collective-permute-start.11 = (bf16[17,64,128]{2,1,0:T(8,128)(2,1)S(1)}, bf16[17,64,128]{2,1,0:T(8,128)(2,1)S(1)}, u32[]{:S(2)}, u32[]{:S(2)}) collective-permute-start(bf16[17,64,128]{2,1,0:T(8,128)(2,1)S(1)} %collective-permute-done.3.refs_1_), channel_id=1, source_target_pairs={{0,4},{4,0},{8,12},{12,8},{1,5},{5,1},{9,13},{13,9},{2,6},{6,2},{1... | collective-permute-start | bytes 835592 | tf_op jit(solution)/shard_map/ppermute | solution.py:346
  26.4 2.6 %collective-permute-start.9 = (bf16[16,64,128]{2,1,0:T(8,128)(2,1)S(1)}, bf16[16,64,128]{2,1,0:T(8,128)(2,1)S(1)}, u32[]{:S(2)}, u32[]{:S(2)}) collective-permute-start(bf16[16,64,128]{2,1,0:T(8,128)(2,1)S(1)} %slice.7), channel_id=1, source_target_pairs={{0,1},{1,0},{2,3},{3,2},{4,5},{5,4},{6,7},{7,6},{8,9},{9,8},{10,11... | collective-permute-start | bytes 786440 | tf_op jit(solution)/shard_map/ppermute | solution.py:342
  27.5 2.1 %collective-permute-start.8 = (bf16[16,64,128]{2,1,0:T(8,128)(2,1)S(1)}, bf16[16,64,128]{2,1,0:T(8,128)(2,1)S(1)}, u32[]{:S(2)}, u32[]{:S(2)}) collective-permute-start(bf16[16,64,128]{2,1,0:T(8,128)(2,1)S(1)} %slice.6), channel_id=1, source_target_pairs={{0,1},{1,0},{2,3},{3,2},{4,5},{5,4},{6,7},{7,6},{8,9},{9,8},{10,11... | collective-permute-start | bytes 786440 | tf_op jit(solution)/shard_map/ppermute | solution.py:342
  29.0 11.9 %collective-permute-start.2 = (bf16[16,64,128]{2,1,0:T(8,128)(2,1)S(1)}, bf16[16,64,128]{2,1,0:T(8,128)(2,1)S(1)}, u32[]{:S(2)}, u32[]{:S(2)}) collective-permute-start(bf16[16,64,128]{2,1,0:T(8,128)(2,1)S(1)} %get-tuple-element.33), channel_id=1, source_target_pairs={{0,1},{1,0},{2,3},{3,2},{4,5},{5,4},{6,7},{7,6},{8,9},{9,8},{10,11... | collective-permute-start | bytes 786440 | tf_op jit(solution)/shard_map/ppermute | solution.py:342
  34.4 7.7 %collective-permute-start.12 = (bf16[16,64,128]{2,1,0:T(8,128)(2,1)S(1)}, bf16[16,64,128]{2,1,0:T(8,128)(2,1)S(1)}, u32[]{:S(2)}, u32[]{:S(2)}) collective-permute-start(bf16[16,64,128]{2,1,0:T(8,128)(2,1)S(1)} %get-tuple-element.51), channel_id=1, source_target_pairs={{0,1},{1,0},{2,3},{3,2},{4,5},{5,4},{6,7},{7,6},{8,9},{9,8},{10,11... | collective-permute-start | bytes 786440 | tf_op jit(solution)/shard_map/ppermute | solution.py:342
  34.4 11.4 %all-to-all-start = ((f32[16,16,128]{2,1,0:T(8,128)}), f32[16,16,128]{2,1,0:T(8,128)S(1)}, u32[]{:S(2)}, u32[]{:S(2)}) async-start(f32[16,16,128]{2,1,0:T(8,128)} %bitcast), calls=%async_computation | async-start | bytes 262144 | tf_op jit(solution)/shard_map/all_to_all | solution.py:414

commit v20 on v17

--- a/solution.py
+++ b/solution.py
@@ -256,9 +256,9 @@
 def turn_out(image, start, applied, wide, turned, sem):
     rows, columns, _ = image.shape
     for y in range(rows):
-        wide[pl.ds(y, columns, stride=rows), :] = image[y].astype(F32)
+        wide[pl.ds(y, columns, stride=rows + 8), :] = image[y].astype(F32)
     for c in range(columns):
-        turned[c, 0] = wide[c * rows:(c + 1) * rows, :].astype(BF16)
+        turned[c, 0] = wide[c * (rows + 8):c * (rows + 8) + rows, :].astype(BF16)
     copy = pltpu.make_async_copy(turned, applied.at[pl.ds(start, columns)], sem)
     copy.start()
     return copy
@@ -347,7 +347,7 @@
 
     def turning(n):
         return [
-            pltpu.VMEM((n, columns * half, nz), F32),
+            pltpu.VMEM((n, columns * (half + 8), nz), F32),
             pltpu.VMEM((n, columns, 1, half, nz), BF16),
             pltpu.SemaphoreType.DMA((n,)),
         ]

time: 46.3 us -> 46.3 us (level)
  Pallas kernels: 10.7 us -> 10.2 us
  waiting for transfers between devices: 10.4 us -> 10.9 us
    all_to_all x1, waiting for transfers between devices: 1.55 us -> 2.1 us  [per_device(): lax.all_to_all(shares, ('dom', 'blk'), split_axis=0, concat_axis=0, tiled...]
    pallas_call x9, Pallas kernels: 8.68 us -> 8.13 us  [call(): pl.pallas_call(kernel, out_shape=out_shape, in_specs=specs or [VMEM] * le...]
  transfers between devices with their start and end apart: 14 -> 14, of which waited for: 5 -> 5; matrix products, arithmetic and copies ran while one was open for 0% -> 0% of each run, Pallas kernels for 17% -> 16%
where the time goes in v20:
time: 46.3 us; the launch traced here: 45.9 us
  starting transfers between devices  22 us (48%)
  waiting for transfers between devices  10.9 us (24%)
  Pallas kernels  10.2 us (22%)
  local copies, waits for them, and re-layouts  2.1 us (5%)
  between operations  0.77 us (2%)
    ppermute x6, starting transfers between devices, exchange(): lax.ppermute(array, 'dom', [(d, to) for d, to in enumerate(partner) if 0...  12.6 us
    pallas_call x9, Pallas kernels, call(): pl.pallas_call(kernel, out_shape=out_shape, in_specs=specs or [VMEM] * le...  8.13 us
    all_to_all x1, starting transfers between devices, per_device(): lax.all_to_all(shares, ('dom', 'blk'), split_axis=0, concat_axis=0, tiled...  6.65 us
    ppermute x7, waiting for transfers between devices, swap(): return lax.ppermute(array, 'blk', [(i, i ^ s) for i in range(blocks)])  5.55 us
    ppermute x6, waiting for transfers between devices, exchange(): lax.ppermute(array, 'dom', [(d, to) for d, to in enumerate(partner) if 0...  3.25 us
    ppermute x7, starting transfers between devices, swap(): return lax.ppermute(array, 'blk', [(i, i ^ s) for i in range(blocks)])  2.74 us
    all_to_all x1, waiting for transfers between devices, per_device(): lax.all_to_all(shares, ('dom', 'blk'), split_axis=0, concat_axis=0, tiled...  2.1 us
    unnamed x6, local copies, waits for them, and re-layouts  2.07 us
  transfers between devices with their start and end apart: 14, of which 5 were waited for; matrix products, arithmetic and copies ran while one was open for 0% of the time, Pallas kernels for 16%

profile of v20, /device:TPU:0, one launch (start us, length us, event | category | flops | bytes accessed | tf_op | source)
XLA Modules:
  0.0 45.9 jit_solution(6220675350079064262)
XLA Ops:
  0.6 2.1 %shard_map.59 = (bf16[33,64,128]{2,1,0:T(8,128)(2,1)S(1)}, bf16[34,64,128]{2,1,0:T(8,128)(2,1)S(1)}, bf16[32,64,128]{2,1,0:T(8,128)(2,1)S(1)}, bf16[17,64,128]{2,1,0:T(8,128)(2,1)S(1)}, bf16[17,64,128]{2,1,0:T(8,128)(2,1)S(1)}) custom-call(bf16[64,1,64,128]{3,2,1,0:T(8,128)(2,1)} %basis_hbm.1, s32[1,64,128]{2,1,0:T(8,128)} %zone_ref.1, f32[16]{0:T(128)} %cond_ref.1), custom_call_target="tpu_custom_call" | custom-call | tf_op jit(solution)/shard_map/pallas_call | solution.py:88
  2.7 0.7 %collective-permute-start.1 = (bf16[33,64,128]{2,1,0:T(8,128)(2,1)S(1)}, bf16[33,64,128]{2,1,0:T(8,128)(2,1)S(1)}, u32[]{:S(2)}, u32[]{:S(2)}) collective-permute-start(bf16[33,64,128]{2,1,0:T(8,128)(2,1)S(1)} %get-tuple-element.31), channel_id=1, source_target_pairs={{4,8},{8,4},{5,9},{9,5},{6,10},{10,6},{7,11},{11,7},{20,24},{24,20... | collective-permute-start | bytes 1622024 | tf_op jit(solution)/shard_map/ppermute | solution.py:346
  3.4 5.9 %collective-permute-start = (bf16[33,64,128]{2,1,0:T(8,128)(2,1)S(1)}, bf16[33,64,128]{2,1,0:T(8,128)(2,1)S(1)}, u32[]{:S(2)}, u32[]{:S(2)}) collective-permute-start(bf16[33,64,128]{2,1,0:T(8,128)(2,1)S(1)} %get-tuple-element.31), channel_id=1, source_target_pairs={{0,4},{4,0},{8,12},{12,8},{1,5},{5,1},{9,13},{13,9},{2,6},{6,2},{1... | collective-permute-start | bytes 1622024 | tf_op jit(solution)/shard_map/ppermute | solution.py:346
  9.3 1.5 %collective-permute-start.5 = (bf16[17,64,128]{2,1,0:T(8,128)(2,1)S(1)}, bf16[17,64,128]{2,1,0:T(8,128)(2,1)S(1)}, u32[]{:S(2)}, u32[]{:S(2)}) collective-permute-start(bf16[17,64,128]{2,1,0:T(8,128)(2,1)S(1)} %get-tuple-element.40), channel_id=1, source_target_pairs={{0,2},{1,3},{2,0},{3,1},{4,6},{5,7},{6,4},{7,5},{8,10},{9,11},{10,... | collective-permute-start | bytes 835592 | tf_op jit(solution)/shard_map/ppermute | solution.py:342
  10.8 0.0 copy-start
  10.8 0.8 %copy-done = s32[1,64,128]{2,1,0:T(8,128)S(1)} copy-done((s32[1,64,128]{2,1,0:T(8,128)S(1)}, s32[1,64,128]{2,1,0:T(8,128)}, u32[]{:S(2)}) %copy-start) | copy-done | bytes 32792
  11.5 0.0 copy-start.1
  11.5 0.7 %copy-done.1 = f32[16]{0:T(128)S(1)} copy-done((f32[16]{0:T(128)S(1)}, f32[16]{0:T(128)}, u32[]{:S(2)}) %copy-start.1) | copy-done | bytes 88
  12.2 0.0 copy-start.2
  12.2 0.7 %copy-done.2 = f32[16]{0:T(128)S(1)} copy-done((f32[16]{0:T(128)S(1)}, f32[16]{0:T(128)}, u32[]{:S(2)}) %copy-start.2) | copy-done | bytes 88
  12.8 1.3 %shard_map.60 = (f32[6,32,128]{2,1,0:T(8,128)S(1)}, f32[32,64,128]{2,1,0:T(8,128)S(1)}) custom-call(s32[1,64,128]{2,1,0:T(8,128)S(1)} %copy-done, f32[16]{0:T(128)S(1)} %copy-done.1, f32[16]{0:T(128)S(1)} %copy-done.2, bf16[34,64,128]{2,1,0:T(8,128)(2,1)S(1)} %get-tuple-element.28.center), custom_call_target="tpu_custom_call" | custom-call | flops 1073741824 | bytes 134217728 | tf_op jit(solution)/shard_map/pallas_call | solution.py:327
  14.2 0.6 %collective-permute-start.3 = (bf16[17,64,128]{2,1,0:T(8,128)(2,1)S(1)}, bf16[17,64,128]{2,1,0:T(8,128)(2,1)S(1)}, u32[]{:S(2)}, u32[]{:S(2)}) collective-permute-start(bf16[17,64,128]{2,1,0:T(8,128)(2,1)S(1)} %get-tuple-element.38), channel_id=1, source_target_pairs={{0,2},{1,3},{2,0},{3,1},{4,6},{5,7},{6,4},{7,5},{8,10},{9,11},{10,... | collective-permute-start | bytes 835592 | tf_op jit(solution)/shard_map/ppermute | solution.py:342
  14.8 3.6 %collective-permute-done.5.refs_0_ = bf16[17,64,128]{2,1,0:T(8,128)(2,1)S(1)} collective-permute-done((bf16[17,64,128]{2,1,0:T(8,128)(2,1)S(1)}, bf16[17,64,128]{2,1,0:T(8,128)(2,1)S(1)}, u32[]{:S(2)}, u32[]{:S(2)}) %collective-permute-start.5) | collective-permute-done | bytes 278560 | tf_op jit(solution)/shard_map/ppermute | solution.py:342
  18.3 0.7 %collective-permute-start.6 = (bf16[17,64,128]{2,1,0:T(8,128)(2,1)S(1)}, bf16[17,64,128]{2,1,0:T(8,128)(2,1)S(1)}, u32[]{:S(2)}, u32[]{:S(2)}) collective-permute-start(bf16[17,64,128]{2,1,0:T(8,128)(2,1)S(1)} %collective-permute-done.5.refs_0_), channel_id=1, source_target_pairs={{4,8},{8,4},{5,9},{9,5},{6,10},{10,6},{7,11},{11,7},{20,24},{24,20... | collective-permute-start | bytes 835592 | tf_op jit(solution)/shard_map/ppermute | solution.py:346
  19.0 2.1 %collective-permute-start.7 = (bf16[17,64,128]{2,1,0:T(8,128)(2,1)S(1)}, bf16[17,64,128]{2,1,0:T(8,128)(2,1)S(1)}, u32[]{:S(2)}, u32[]{:S(2)}) collective-permute-start(bf16[17,64,128]{2,1,0:T(8,128)(2,1)S(1)} %collective-permute-done.5.refs_0_), channel_id=1, source_target_pairs={{0,4},{4,0},{8,12},{12,8},{1,5},{5,1},{9,13},{13,9},{2,6},{6,2},{1... | collective-permute-start | bytes 835592 | tf_op jit(solution)/shard_map/ppermute | solution.py:346
  21.1 2.0 %collective-permute-done.3.refs_1_ = bf16[17,64,128]{2,1,0:T(8,128)(2,1)S(1)} collective-permute-done((bf16[17,64,128]{2,1,0:T(8,128)(2,1)S(1)}, bf16[17,64,128]{2,1,0:T(8,128)(2,1)S(1)}, u32[]{:S(2)}, u32[]{:S(2)}) %collective-permute-start.3) | collective-permute-done | bytes 278560 | tf_op jit(solution)/shard_map/ppermute | solution.py:342
  23.1 0.0 collective-permute-start.4
  23.1 0.0 collective-permute-done.1.two
  23.1 0.7 %collective-permute-start.10 = (bf16[17,64,128]{2,1,0:T(8,128)(2,1)S(1)}, bf16[17,64,128]{2,1,0:T(8,128)(2,1)S(1)}, u32[]{:S(2)}, u32[]{:S(2)}) collective-permute-start(bf16[17,64,128]{2,1,0:T(8,128)(2,1)S(1)} %collective-permute-done.3.refs_1_), channel_id=1, source_target_pairs={{4,8},{8,4},{5,9},{9,5},{6,10},{10,6},{7,11},{11,7},{20,24},{24,20... | collective-permute-start | bytes 835592 | tf_op jit(solution)/shard_map/ppermute | solution.py:346
  23.8 0.0 collective-permute-done.one
  23.8 2.6 %collective-permute-start.11 = (bf16[17,64,128]{2,1,0:T(8,128)(2,1)S(1)}, bf16[17,64,128]{2,1,0:T(8,128)(2,1)S(1)}, u32[]{:S(2)}, u32[]{:S(2)}) collective-permute-start(bf16[17,64,128]{2,1,0:T(8,128)(2,1)S(1)} %collective-permute-done.3.refs_1_), channel_id=1, source_target_pairs={{0,4},{4,0},{8,12},{12,8},{1,5},{5,1},{9,13},{13,9},{2,6},{6,2},{1... | collective-permute-start | bytes 835592 | tf_op jit(solution)/shard_map/ppermute | solution.py:346
  26.3 0.0 collective-permute-done.6.refs_2_
  26.4 0.1 collective-permute-start.9
  26.5 1.0 %collective-permute-done.7.refs_3_ = bf16[17,64,128]{2,1,0:T(8,128)(2,1)S(1)} collective-permute-done((bf16[17,64,128]{2,1,0:T(8,128)(2,1)S(1)}, bf16[17,64,128]{2,1,0:T(8,128)(2,1)S(1)}, u32[]{:S(2)}, u32[]{:S(2)}) %collective-permute-start.7) | collective-permute-done | bytes 278560 | tf_op jit(solution)/shard_map/ppermute | solution.py:346
  27.5 0.0 collective-permute-start.8
  27.5 0.7 %shard_map.63 = (bf16[34,64,128]{2,1,0:T(8,128)(2,1)S(1)}, f32[32,64,128]{2,1,0:T(8,128)S(1)}) custom-call(f32[6,32,128]{2,1,0:T(8,128)S(1)} %get-tuple-element.29.coef, bf16[17,64,128]{2,1,0:T(8,128)(2,1)S(1)} %collective-permute-done.5.refs_0_, bf16[17,64,128]{2,1,0:T(8,128)(2,1)S(1)} %collective-permute-done.3.refs_1_), custom_call_target="tpu_custom_call" | custom-call | flops 1 | bytes 1 | tf_op jit(solution)/shard_map/pallas_call | solution.py:327
  28.2 0.6 %shard_map.61 = (bf16[16,64,128]{2,1,0:T(8,128)(2,1)S(1)}, bf16[16,64,128]{2,1,0:T(8,128)(2,1)S(1)}, f32[2,32,128]{2,1,0:T(8,128)S(1)}, bf16[64,4096]{1,0:T(8,128)(2,1)S(1)}) custom-call(f32[6,32,128]{2,1,0:T(8,128)S(1)} %get-tuple-element.29.coef, f32[32,64,128]{2,1,0:T(8,128)S(1)} %get-tuple-element.30.partial, ...), custom_call_target="tpu_custom_call" | custom-call | flops 1 | bytes 1 | tf_op jit(solution)/shard_map/pallas_call | solution.py:327
  28.8 0.2 shard_map.64
  28.9 0.0 collective-permute-done.9.refs_3_
  29.0 0.6 %collective-permute-start.2 = (bf16[16,64,128]{2,1,0:T(8,128)(2,1)S(1)}, bf16[16,64,128]{2,1,0:T(8,128)(2,1)S(1)}, u32[]{:S(2)}, u32[]{:S(2)}) collective-permute-start(bf16[16,64,128]{2,1,0:T(8,128)(2,1)S(1)} %get-tuple-element.33), channel_id=1, source_target_pairs={{0,1},{1,0},{2,3},{3,2},{4,5},{5,4},{6,7},{7,6},{8,9},{9,8},{10,11... | collective-permute-start | bytes 786440 | tf_op jit(solution)/shard_map/ppermute | solution.py:342
  29.5 0.0 collective-permute-done.8.refs_2_
  29.5 0.0 collective-permute-done.4.plain
  29.5 1.4 %shard_map.65 = (bf16[256,4096]{1,0:T(8,128)(2,1)S(1)}, f32[256,128]{1,0:T(8,128)S(1)}) custom-call(bf16[64,4096]{1,0:T(8,128)(2,1)S(1)} %get-tuple-element.35.flat, bf16[34,64,128]{2,1,0:T(8,128)(2,1)S(1)} %get-tuple-element.28.center, bf16[32,64,128]{2,1,0:T(8,128)(2,1)S(1)} %collective-permute-done.4.plain, ...), custom_call_target="tpu_custom_call" | custom-call | flops 1 | bytes 1 | tf_op jit(solution)/shard_map/pallas_call | solution.py:327
  30.9 0.0 collective-permute-done.10.refs_2_
  30.9 2.3 %collective-permute-done.11.refs_3_ = bf16[17,64,128]{2,1,0:T(8,128)(2,1)S(1)} collective-permute-done((bf16[17,64,128]{2,1,0:T(8,128)(2,1)S(1)}, bf16[17,64,128]{2,1,0:T(8,128)(2,1)S(1)}, u32[]{:S(2)}, u32[]{:S(2)}) %collective-permute-start.11) | collective-permute-done | bytes 278560 | tf_op jit(solution)/shard_map/ppermute | solution.py:346
  33.2 1.2 %shard_map.66 = (bf16[16,64,128]{2,1,0:T(8,128)(2,1)S(1)}, bf16[16,64,128]{2,1,0:T(8,128)(2,1)S(1)}, f32[256,128]{1,0:T(8,128)}) custom-call(f32[2,32,128]{2,1,0:T(8,128)S(1)} %get-tuple-element.34.faces, bf16[256,4096]{1,0:T(8,128)(2,1)S(1)} %get-tuple-element.47.left, f32[256,128]{1,0:T(8,128)S(1)} %get-tuple-element.48.first_gram, ...), custom_call_target="tpu_custom_call" | custom-call | flops 1 | bytes 1 | tf_op jit(solution)/shard_map/pallas_call | solution.py:327
  34.4 0.0 collective-permute-start.12
  34.4 6.7 %all-to-all-start = ((f32[16,16,128]{2,1,0:T(8,128)}), f32[16,16,128]{2,1,0:T(8,128)S(1)}, u32[]{:S(2)}, u32[]{:S(2)}) async-start(f32[16,16,128]{2,1,0:T(8,128)} %bitcast), calls=%async_computation | async-start | bytes 262144 | tf_op jit(solution)/shard_map/all_to_all | solution.py:413
  41.0 0.0 collective-permute-done.2.theirs
  41.0 1.0 %shard_map.62.applied_in = bf16[256,1,16,128]{3,2,1,0:T(8,128)(2,1)} custom-call(bf16[16,64,128]{2,1,0:T(8,128)(2,1)S(1)} %get-tuple-element.32.mine, bf16[16,64,128]{2,1,0:T(8,128)(2,1)S(1)} %collective-permute-done.2.theirs), custom_call_target="tpu_custom_call" | custom-call | flops 1 | bytes 1 | tf_op jit(solution)/shard_map/pallas_call | solution.py:327
  42.1 0.0 collective-permute-done.12.refs_1_
  42.1 1.0 %shard_map.67 = bf16[256,1,16,128]{3,2,1,0:T(8,128)(2,1)} custom-call(bf16[256,1,16,128]{3,2,1,0:T(8,128)(2,1)} %shard_map.62.applied_in, bf16[16,64,128]{2,1,0:T(8,128)(2,1)S(1)} %get-tuple-element.50.refs_0_, bf16[16,64,128]{2,1,0:T(8,128)(2,1)S(1)} %collective-permute-done.12.refs_1_), custom_call_target="tpu_custom_call", output_to_operand_aliasing={{}: (0, {})} | custom-call | flops 1 | bytes 1 | tf_op jit(solution)/shard_map/pallas_call | solution.py:327
  43.1 2.1 %all-to-all-done.shares = f32[16,16,128]{2,1,0:T(8,128)S(1)} async-done(((f32[16,16,128]{2,1,0:T(8,128)}), f32[16,16,128]{2,1,0:T(8,128)S(1)}, u32[]{:S(2)}, u32[]{:S(2)}) %all-to-all-start) | async-done | bytes 131104 | tf_op jit(solution)/shard_map/all_to_all | solution.py:413
  45.2 0.7 %shard_map.68 = f32[16,256]{1,0:T(8,128)} custom-call(f32[16,16,128]{2,1,0:T(8,128)S(1)} %all-to-all-done.shares), custom_call_target="tpu_custom_call" | custom-call | flops 1 | bytes 1 | tf_op jit(solution)/shard_map/pallas_call | solution.py:327
  (2 shorter events, 0.0 us)
Async XLA Ops:
  2.7 20.4 %collective-permute-start.1 = (bf16[33,64,128]{2,1,0:T(8,128)(2,1)S(1)}, bf16[33,64,128]{2,1,0:T(8,128)(2,1)S(1)}, u32[]{:S(2)}, u32[]{:S(2)}) collective-permute-start(bf16[33,64,128]{2,1,0:T(8,128)(2,1)S(1)} %get-tuple-element.31), channel_id=1, source_target_pairs={{4,8},{8,4},{5,9},{9,5},{6,10},{10,6},{7,11},{11,7},{20,24},{24,20... | collective-permute-start | bytes 1622024 | tf_op jit(solution)/shard_map/ppermute | solution.py:346
  3.4 20.4 %collective-permute-start = (bf16[33,64,128]{2,1,0:T(8,128)(2,1)S(1)}, bf16[33,64,128]{2,1,0:T(8,128)(2,1)S(1)}, u32[]{:S(2)}, u32[]{:S(2)}) collective-permute-start(bf16[33,64,128]{2,1,0:T(8,128)(2,1)S(1)} %get-tuple-element.31), channel_id=1, source_target_pairs={{0,4},{4,0},{8,12},{12,8},{1,5},{5,1},{9,13},{13,9},{2,6},{6,2},{1... | collective-permute-start | bytes 1622024 | tf_op jit(solution)/shard_map/ppermute | solution.py:346
  9.3 9.1 %collective-permute-start.5 = (bf16[17,64,128]{2,1,0:T(8,128)(2,1)S(1)}, bf16[17,64,128]{2,1,0:T(8,128)(2,1)S(1)}, u32[]{:S(2)}, u32[]{:S(2)}) collective-permute-start(bf16[17,64,128]{2,1,0:T(8,128)(2,1)S(1)} %get-tuple-element.40), channel_id=1, source_target_pairs={{0,2},{1,3},{2,0},{3,1},{4,6},{5,7},{6,4},{7,5},{8,10},{9,11},{10,... | collective-permute-start | bytes 835592 | tf_op jit(solution)/shard_map/ppermute | solution.py:342
  10.8 0.8 %copy-start = (s32[1,64,128]{2,1,0:T(8,128)S(1)}, s32[1,64,128]{2,1,0:T(8,128)}, u32[]{:S(2)}) copy-start(s32[1,64,128]{2,1,0:T(8,128)} %zone_ref.1) | copy-start | bytes 98308
  11.5 0.7 %copy-start.1 = (f32[16]{0:T(128)S(1)}, f32[16]{0:T(128)}, u32[]{:S(2)}) copy-start(f32[16]{0:T(128)} %cond_ref.1) | copy-start | bytes 196
  12.2 0.7 %copy-start.2 = (f32[16]{0:T(128)S(1)}, f32[16]{0:T(128)}, u32[]{:S(2)}) copy-start(f32[16]{0:T(128)} %heat_ref.1) | copy-start | bytes 196
  14.2 8.9 %collective-permute-start.3 = (bf16[17,64,128]{2,1,0:T(8,128)(2,1)S(1)}, bf16[17,64,128]{2,1,0:T(8,128)(2,1)S(1)}, u32[]{:S(2)}, u32[]{:S(2)}) collective-permute-start(bf16[17,64,128]{2,1,0:T(8,128)(2,1)S(1)} %get-tuple-element.38), channel_id=1, source_target_pairs={{0,2},{1,3},{2,0},{3,1},{4,6},{5,7},{6,4},{7,5},{8,10},{9,11},{10,... | collective-permute-start | bytes 835592 | tf_op jit(solution)/shard_map/ppermute | solution.py:342
  18.3 8.0 %collective-permute-start.6 = (bf16[17,64,128]{2,1,0:T(8,128)(2,1)S(1)}, bf16[17,64,128]{2,1,0:T(8,128)(2,1)S(1)}, u32[]{:S(2)}, u32[]{:S(2)}) collective-permute-start(bf16[17,64,128]{2,1,0:T(8,128)(2,1)S(1)} %collective-permute-done.5.refs_0_), channel_id=1, source_target_pairs={{4,8},{8,4},{5,9},{9,5},{6,10},{10,6},{7,11},{11,7},{20,24},{24,20... | collective-permute-start | bytes 835592 | tf_op jit(solution)/shard_map/ppermute | solution.py:346
  19.0 8.4 %collective-permute-start.7 = (bf16[17,64,128]{2,1,0:T(8,128)(2,1)S(1)}, bf16[17,64,128]{2,1,0:T(8,128)(2,1)S(1)}, u32[]{:S(2)}, u32[]{:S(2)}) collective-permute-start(bf16[17,64,128]{2,1,0:T(8,128)(2,1)S(1)} %collective-permute-done.5.refs_0_), channel_id=1, source_target_pairs={{0,4},{4,0},{8,12},{12,8},{1,5},{5,1},{9,13},{13,9},{2,6},{6,2},{1... | collective-permute-start | bytes 835592 | tf_op jit(solution)/shard_map/ppermute | solution.py:346
  23.1 6.5 %collective-permute-start.4 = (bf16[32,64,128]{2,1,0:T(8,128)(2,1)S(1)}, bf16[32,64,128]{2,1,0:T(8,128)(2,1)S(1)}, u32[]{:S(2)}, u32[]{:S(2)}) collective-permute-start(bf16[32,64,128]{2,1,0:T(8,128)(2,1)S(1)} %get-tuple-element.39), channel_id=1, source_target_pairs={{0,1},{1,0},{2,3},{3,2},{4,5},{5,4},{6,7},{7,6},{8,9},{9,8},{10,11... | collective-permute-start | bytes 1572872 | tf_op jit(solution)/shard_map/ppermute | solution.py:342
  23.1 7.9 %collective-permute-start.10 = (bf16[17,64,128]{2,1,0:T(8,128)(2,1)S(1)}, bf16[17,64,128]{2,1,0:T(8,128)(2,1)S(1)}, u32[]{:S(2)}, u32[]{:S(2)}) collective-permute-start(bf16[17,64,128]{2,1,0:T(8,128)(2,1)S(1)} %collective-permute-done.3.refs_1_), channel_id=1, source_target_pairs={{4,8},{8,4},{5,9},{9,5},{6,10},{10,6},{7,11},{11,7},{20,24},{24,20... | collective-permute-start | bytes 835592 | tf_op jit(solution)/shard_map/ppermute | solution.py:346
  23.8 9.4 %collective-permute-start.11 = (bf16[17,64,128]{2,1,0:T(8,128)(2,1)S(1)}, bf16[17,64,128]{2,1,0:T(8,128)(2,1)S(1)}, u32[]{:S(2)}, u32[]{:S(2)}) collective-permute-start(bf16[17,64,128]{2,1,0:T(8,128)(2,1)S(1)} %collective-permute-done.3.refs_1_), channel_id=1, source_target_pairs={{0,4},{4,0},{8,12},{12,8},{1,5},{5,1},{9,13},{13,9},{2,6},{6,2},{1... | collective-permute-start | bytes 835592 | tf_op jit(solution)/shard_map/ppermute | solution.py:346
  26.4 2.6 %collective-permute-start.9 = (bf16[16,64,128]{2,1,0:T(8,128)(2,1)S(1)}, bf16[16,64,128]{2,1,0:T(8,128)(2,1)S(1)}, u32[]{:S(2)}, u32[]{:S(2)}) collective-permute-start(bf16[16,64,128]{2,1,0:T(8,128)(2,1)S(1)} %slice.7), channel_id=1, source_target_pairs={{0,1},{1,0},{2,3},{3,2},{4,5},{5,4},{6,7},{7,6},{8,9},{9,8},{10,11... | collective-permute-start | bytes 786440 | tf_op jit(solution)/shard_map/ppermute | solution.py:342
  27.5 2.1 %collective-permute-start.8 = (bf16[16,64,128]{2,1,0:T(8,128)(2,1)S(1)}, bf16[16,64,128]{2,1,0:T(8,128)(2,1)S(1)}, u32[]{:S(2)}, u32[]{:S(2)}) collective-permute-start(bf16[16,64,128]{2,1,0:T(8,128)(2,1)S(1)} %slice.6), channel_id=1, source_target_pairs={{0,1},{1,0},{2,3},{3,2},{4,5},{5,4},{6,7},{7,6},{8,9},{9,8},{10,11... | collective-permute-start | bytes 786440 | tf_op jit(solution)/shard_map/ppermute | solution.py:342
  29.0 12.1 %collective-permute-start.2 = (bf16[16,64,128]{2,1,0:T(8,128)(2,1)S(1)}, bf16[16,64,128]{2,1,0:T(8,128)(2,1)S(1)}, u32[]{:S(2)}, u32[]{:S(2)}) collective-permute-start(bf16[16,64,128]{2,1,0:T(8,128)(2,1)S(1)} %get-tuple-element.33), channel_id=1, source_target_pairs={{0,1},{1,0},{2,3},{3,2},{4,5},{5,4},{6,7},{7,6},{8,9},{9,8},{10,11... | collective-permute-start | bytes 786440 | tf_op jit(solution)/shard_map/ppermute | solution.py:342
  34.4 7.7 %collective-permute-start.12 = (bf16[16,64,128]{2,1,0:T(8,128)(2,1)S(1)}, bf16[16,64,128]{2,1,0:T(8,128)(2,1)S(1)}, u32[]{:S(2)}, u32[]{:S(2)}) collective-permute-start(bf16[16,64,128]{2,1,0:T(8,128)(2,1)S(1)} %get-tuple-element.51), channel_id=1, source_target_pairs={{0,1},{1,0},{2,3},{3,2},{4,5},{5,4},{6,7},{7,6},{8,9},{9,8},{10,11... | collective-permute-start | bytes 786440 | tf_op jit(solution)/shard_map/ppermute | solution.py:342
  34.4 10.8 %all-to-all-start = ((f32[16,16,128]{2,1,0:T(8,128)}), f32[16,16,128]{2,1,0:T(8,128)S(1)}, u32[]{:S(2)}, u32[]{:S(2)}) async-start(f32[16,16,128]{2,1,0:T(8,128)} %bitcast), calls=%async_computation | async-start | bytes 262144 | tf_op jit(solution)/shard_map/all_to_all | solution.py:413
